TPU v7x, 256 devices: a whole 4x4x8 slice. The times are simulated.
256 devices in a mesh: grp: 4 (over z_hi, core), seq: 64 (over x, z_lo, y).
Axes of the slice: x: 4, y: 4, z: 8 (z_hi: 2, z_lo: 4; z = z_hi * 4 + z_lo), core: 2. Of those that a mesh axis runs over, the one named last changes fastest.
Arguments:
- queries: bfloat16 [524288, 128], P(('grp', 'seq')), may hold values from -6 to 6
- keys: bfloat16 [524288, 128], P(('grp', 'seq')), may hold values from -6 to 6
- values: bfloat16 [524288, 128], P(('grp', 'seq')), may hold values from -6 to 6
- cotangent: bfloat16 [524288, 128], P(('grp', 'seq')), may hold values from -640 to 640
Outputs:
- grad_queries: float32 [524288, 128], P(('grp', 'seq'))
- grad_keys: float32 [524288, 128], P(('grp', 'seq'))
- grad_values: float32 [524288, 128], P(('grp', 'seq'))
All inputs are finite; a program needn't handle non-finite values.
Results may differ from a plain program's by a relative error of at most 0.0057.
Values may be sent and summed in bfloat16 or wider, within the bound.
No kernel may reach another device: no remote copies, remote signals or barrier semaphores. Data moves between devices by JAX's collectives and lax.ppermute only.
A program may use at most 128 MiB of HBM per device.

v0:
```python
import jax
import jax.numpy as jnp
from jax import lax
from jax.sharding import PartitionSpec as P

SEG = 2048
LEVELS = 5


NEG_FILL = -1e30


def from_partner(block, axis, apart):
    count = lax.axis_size(axis)
    route = []
    for low in range(count):
        high = low | 1 << apart
        if high != low and high < count:
            route += [(low, high), (high, low)]
    return lax.ppermute(block, axis, route)


def level_rows(field_rows, stride):
    row_count = field_rows.shape[0] // stride
    return field_rows.reshape((row_count, stride) + field_rows.shape[1:])[:, 0]


def spread_rows(part_rows, stride, fill_value):
    row_count = part_rows.shape[0]
    widths = ((0, 0), (0, stride - 1)) + ((0, 0),) * (part_rows.ndim - 1)
    widened = jnp.pad(part_rows[:, None], widths, constant_values=fill_value)
    return widened.reshape((row_count * stride,) + part_rows.shape[1:])


def contract(left, right, left_dim, right_dim):
    return lax.dot_general(
        left, right, (((left_dim,), (right_dim,)), ((), ())), preferred_element_type=jnp.float32
    )


def join_halves(mine_rows, their_rows, high_half):
    return jnp.where(
        high_half,
        jnp.concatenate([their_rows, mine_rows], 0),
        jnp.concatenate([mine_rows, their_rows], 0),
    )


def gather_levels(blocks, depths):
    position = lax.axis_index("seq")
    result = list(blocks)
    for level_bit in range(max(depths + [0])):
        high_half = position // (1 << level_bit) % 2 == 1
        active = [member for member in range(len(result)) if depths[member] > level_bit]
        for member in active:
            incoming = from_partner(result[member], "seq", level_bit)
            result[member] = join_halves(result[member], incoming, high_half)
    return result


def scatter_levels(partials, depths):
    position = lax.axis_index("seq")
    result = list(partials)
    for level_bit in reversed(range(max(depths + [0]))):
        high_half = position // (1 << level_bit) % 2 == 1
        active = [member for member in range(len(result)) if depths[member] > level_bit]
        kept_rows = []
        sent_rows = []
        for member in active:
            half_rows = result[member].shape[0] // 2
            lower_rows = result[member][:half_rows]
            upper_rows = result[member][half_rows:]
            kept_rows.append(jnp.where(high_half, upper_rows, lower_rows))
            sent_rows.append(jnp.where(high_half, lower_rows, upper_rows))
        for member_pos, member in enumerate(active):
            incoming = from_partner(sent_rows[member_pos], "seq", level_bit)
            result[member] = kept_rows[member_pos] + incoming
    return result


def forward_segment(query_seg, kv_seg, score_scale):
    row_count, head_dim = query_seg.shape
    block_rows = min(row_count, 512)

    def one_block(query_block):
        scores = score_scale * contract(query_block, kv_seg[:, 0], 1, 1)
        row_peak = jnp.max(scores, axis=1, keepdims=True)
        log_norm = row_peak[:, 0] + jnp.log(jnp.sum(jnp.exp(scores - row_peak), axis=1))
        prob_low = jnp.exp(scores - log_norm[:, None]).astype(jnp.bfloat16)
        return (log_norm, contract(prob_low, kv_seg[:, 1], 1, 0))

    log_norm, level_out = lax.map(
        one_block, query_seg.reshape(row_count // block_rows, block_rows, head_dim)
    )
    return (log_norm.reshape(row_count), level_out.reshape(row_count, head_dim))


def backward_segment(query_seg, grad_seg, total_seg, delta_seg, kv_seg, score_scale):
    row_count, head_dim = query_seg.shape
    block_rows = min(row_count, 512)
    block_count = row_count // block_rows

    def advance(running, inputs):
        query_block, grad_block, total_block, delta_block = inputs
        scores = score_scale * contract(query_block, kv_seg[:, 0], 1, 1)
        weights = jnp.exp(scores - total_block[:, None])
        grad_probs = contract(grad_block, kv_seg[:, 1], 1, 1)
        grad_scores = (weights * (grad_probs - delta_block[:, None])).astype(jnp.bfloat16)
        grad_query = score_scale * contract(grad_scores, kv_seg[:, 0], 1, 0)
        grad_key = score_scale * contract(grad_scores, query_block, 0, 0)
        grad_value = contract(weights.astype(jnp.bfloat16), grad_block, 0, 0)
        running = running + jnp.stack([grad_key, grad_value], 1)
        return (running, grad_query)

    kv_rows = kv_seg.shape[0]
    initial = jnp.zeros((kv_rows, 2, head_dim), jnp.float32)
    inputs = (
        query_seg.reshape(block_count, block_rows, head_dim),
        grad_seg.reshape(block_count, block_rows, head_dim),
        total_seg.reshape(block_count, block_rows),
        delta_seg.reshape(block_count, block_rows),
    )
    grad_kv, grad_query = lax.scan(advance, initial, inputs)
    return (grad_query.reshape(row_count, head_dim), grad_kv)


def on_device(queries, keys, values, cotangent):
    local_rows, head_dim = queries.shape
    score_scale = head_dim ** (-0.5)
    devices = lax.axis_size("grp") * lax.axis_size("seq")
    strides = [2**level_idx for level_idx in range(LEVELS - 1)] + [local_rows * devices // SEG]
    depths = []
    for stride in strides[:-1]:
        group_span = SEG * stride // local_rows
        depths.append(group_span.bit_length() - 1)
    stacked = jnp.stack([keys, values], 1)
    picked = [level_rows(stacked, stride) for stride in strides]
    segment_kv = gather_levels(picked[:-1], depths)
    segment_kv.append(lax.all_gather(picked[-1], ("grp", "seq"), axis=0, tiled=True))

    def run_forward(segment_pair):
        return forward_segment(segment_pair[0], segment_pair[1], score_scale)

    log_norms = []
    level_outs = []
    for level_idx in range(LEVELS):
        kv_all = segment_kv[level_idx]
        seg_count = kv_all.shape[0] // SEG
        query_sel = level_rows(queries, strides[level_idx])
        log_norm, level_out = lax.map(
            run_forward,
            (
                query_sel.reshape(seg_count, -1, head_dim),
                kv_all.reshape(seg_count, SEG, 2, head_dim),
            ),
        )
        log_norms.append(log_norm.reshape(-1))
        level_outs.append(level_out.reshape(-1, head_dim))
    spread_norms = [
        spread_rows(log_norms[level_idx], strides[level_idx], NEG_FILL)
        for level_idx in range(LEVELS)
    ]
    top_norm = spread_norms[0]
    for norm_field in spread_norms[1:]:
        top_norm = jnp.maximum(top_norm, norm_field)
    norm_sum = jnp.zeros((local_rows,), jnp.float32)
    for norm_field in spread_norms:
        norm_sum = norm_sum + jnp.exp(norm_field - top_norm)
    log_total = top_norm + jnp.log(norm_sum)
    combined = jnp.zeros((local_rows, head_dim), jnp.float32)
    for level_idx in range(LEVELS):
        stride = strides[level_idx]
        level_share = jnp.exp(log_norms[level_idx] - level_rows(log_total, stride))
        combined = combined + spread_rows(level_share[:, None] * level_outs[level_idx], stride, 0.0)
    row_delta = jnp.sum(cotangent.astype(jnp.float32) * combined, axis=1)
    grad_queries = jnp.zeros((local_rows, head_dim), jnp.float32)
    partials = []
    for level_idx in range(LEVELS):
        stride = strides[level_idx]
        kv_all = segment_kv[level_idx]
        seg_count = kv_all.shape[0] // SEG
        with_kv = True

        def run_backward(members, with_kv=with_kv):
            return backward_segment(
                members[0], members[1], members[2], members[3], members[4], score_scale
            )

        members = (
            level_rows(queries, stride).reshape(seg_count, -1, head_dim),
            level_rows(cotangent, stride).reshape(seg_count, -1, head_dim),
            level_rows(log_total, stride).reshape(seg_count, -1),
            level_rows(row_delta, stride).reshape(seg_count, -1),
            kv_all.reshape(seg_count, SEG, 2, head_dim),
        )
        grad_sel, grad_kv = lax.map(run_backward, members)
        grad_queries = grad_queries + spread_rows(grad_sel.reshape(-1, head_dim), stride, 0.0)
        partials.append(grad_kv.reshape(-1, 2, head_dim))
    owned = scatter_levels(partials[:-1], depths)
    owned.append(lax.psum_scatter(partials[-1], ("grp", "seq"), scatter_dimension=0, tiled=True))
    grad_both = jnp.zeros((local_rows, 2, head_dim), jnp.float32)
    for level_idx in range(LEVELS):
        grad_both = grad_both + spread_rows(owned[level_idx], strides[level_idx], 0.0)
    return (grad_queries, grad_both[:, 0], grad_both[:, 1])


def solution(mesh):
    return jax.shard_map(
        on_device,
        mesh=mesh,
        in_specs=(
            P(("grp", "seq"), None),
            P(("grp", "seq"), None),
            P(("grp", "seq"), None),
            P(("grp", "seq"), None),
        ),
        out_specs=(P(("grp", "seq"), None), P(("grp", "seq"), None), P(("grp", "seq"), None)),
        check_vma=False,
    )
```

profile of v0, /device:TPU:1, one launch (start us, length us, event | category | flops | bytes accessed | tf_op | source)
XLA Modules:
  0.0 1995.0 jit_solution(7543077107616612092)
XLA Ops:
  9.0 2.2 collective-permute-start.1
  14.9 4.0 collective-permute-done.3
  19.6 4.0 collective-permute-start.4
  24.7 16.6 while.94
  43.4 1.9 slice.236
  58.4 2.2 collective-permute-start.5
  60.7 2.4 maximum_select_fusion
  63.1 9.2 while.100
  65.8 1.9 fusion.211
  67.8 1.8 multiply_reduce_fusion.5
  70.4 1.9 fusion.211
  99.9 457.3 %all-gather.3.cloned.1.call-done = bf16[2048,1,2,128]{3,1,0,2:T(2,128)(2,1)} async-done(((bf16[8,1,2,128]{3,1,0,2:T(2,128)(2,1)}), bf16[2048,1,2,128]{3,1,0,2:T(2,128)(2,1)}) %all-gather.3.cloned.1.call-update) | async-done | bytes 1048592 | tf_op jit(solution)/shard_map/all_gather | solution.py:139
  569.9 1.9 fusion.164
  575.6 3.8 fusion.97
  585.2 2.1 fusion.106
  590.7 27.7 %while.102 = (s32[]{:T(128)}, f32[2048,2,128]{2,0,1:T(8,128)}, f32[2,512,128]{2,1,0:T(8,128)}, bf16[2,512,128]{2,1,0:T(8,128)(2,1)S(1)}, bf16[2048,2,128]{2,0,1:...) while((s32[]{:T(128)}, f32[2048,2,128]{2,0,1:T(8,128)}, ...), condition=%wide.region_18.19_spmd.clone, body=%wide.region_17.18_spmd.clone.sunk | while | flops 1352466432 | bytes 30686868 | solution.py:123
  592.6 2.2 multiply_convert_fusion.6
  596.6 2.0 convolution_bitcast_fusion.8
  598.7 3.1 maximum_add_fusion.5
  601.8 2.5 fusion.237
  606.1 2.2 multiply_convert_fusion.6
  610.0 2.0 convolution_bitcast_fusion.8
  612.1 3.8 maximum_add_fusion.5
  615.9 2.4 fusion.237
  618.3 2.7 slice_select_fusion
  621.2 3.1 convolution_bitcast_fusion.4
  638.5 50.6 %while.101 = (s32[]{:T(128)}, f32[2048,2,128]{2,0,1:T(8,128)}, f32[4,512,128]{2,1,0:T(8,128)}, bf16[4,512,128]{2,1,0:T(8,128)(2,1)}, bf16[2048,2,128]{2,0,1:T(8,...) while((s32[]{:T(128)}, f32[2048,2,128]{2,0,1:T(8,128)}, ...), condition=%wide.region_16.17_spmd.clone, body=%wide.region_15.16_spmd.clone.sunk | while | flops 1352466432 | bytes 31735444 | solution.py:123
  641.6 2.7 fusion.223
  644.2 2.0 convolution_bitcast_fusion.7
  646.2 3.1 maximum_add_fusion.4
  653.6 2.7 fusion.223
  656.3 2.0 convolution_bitcast_fusion.7
  658.3 3.8 maximum_add_fusion.4
  666.4 2.7 fusion.223
  669.0 2.0 convolution_bitcast_fusion.7
  671.1 3.8 maximum_add_fusion.4
  679.2 2.7 fusion.223
  681.8 2.0 convolution_bitcast_fusion.7
  683.9 3.8 maximum_add_fusion.4
  690.5 2.5 convolution_multiply_fusion.10
  695.1 2.8 fusion.102
  699.6 2.9 collective-permute-start.10
  707.0 2.1 pad.72.clone
  709.1 5.3 collective-permute-done.10
  715.5 11.0 collective-permute-done.8
  728.3 4.0 collective-permute-done.11
  732.3 1250.4 %reduce-scatter.2.cloned.1.call-done = f32[8,2,128]{2,0,1:T(8,128)} async-done(((f32[2048,2,128]{2,0,1:T(8,128)}), f32[8,2,128]{2,0,1:T(8,128)}) %reduce-scatter.2.cloned.1.call-update) | async-done | bytes 8208 | tf_op jit(solution)/shard_map/reduce_scatter | solution.py:200
  1983.6 2.8 fusion.93
  (371 shorter events, 148.2 us)
Async XLA Ops:
  7.2 4.1 copy-start.10
  7.2 4.2 copy-start.9
  7.2 550.0 %all-gather.3.cloned.1.call-start = ((), (), s32[]{:S(2)}) async-start(), calls=%async_computation.2 | async-start | bytes 2105344 | tf_op jit(solution)/shard_map/all_gather | solution.py:139
  9.0 3.4 copy-start.38
  9.0 46.5 %collective-permute-start.1 = (bf16[512,2,128]{2,0,1:T(8,128)(2,1)S(1)}, bf16[512,2,128]{2,0,1:T(8,128)(2,1)}, u32[]{:S(2)}, u32[]{:S(2)}) collective-permute-start(bf16[512,2,128]{2,0,1:T(8,128)(2,1)S(1)} %bitcast.430), channel_id=1, source_target_pairs={{0,1},{1,0},{2,3},{3,2},{4,5},{5,4},{6,7},{7,6},{8,9},{9,8},{10,11... | collective-permute-start | bytes 786440 | tf_op jit(solution)/shard_map/ppermute | solution.py:20
  11.4 7.4 collective-permute-start.3
  12.5 48.1 %collective-permute-start = (bf16[1024,2,128]{2,0,1:T(8,128)(2,1)S(1)}, bf16[1024,2,128]{2,0,1:T(8,128)(2,1)}, u32[]{:S(2)}, u32[]{:S(2)}) collective-permute-start(bf16[1024,2,128]{2,0,1:T(8,128)(2,1)S(1)} %bitcast.425), channel_id=1, source_target_pairs={{0,1},{1,0},{2,3},{3,2},{4,5},{5,4},{6,7},{7,6},{8,9},{9,8},{10,11... | collective-permute-start | bytes 1572872 | tf_op jit(solution)/shard_map/ppermute | solution.py:20
  14.7 1968.0 %reduce-scatter.2.cloned.1.call-start = ((), (), s32[]{:S(2)}) async-start(), calls=%async_computation.1 | async-start | bytes 2105344 | tf_op jit(solution)/shard_map/reduce_scatter | solution.py:200
  19.6 37.4 %collective-permute-start.4 = (bf16[512,2,128]{2,0,1:T(8,128)(2,1)}, bf16[512,2,128]{2,0,1:T(8,128)(2,1)}, u32[]{:S(2)}, u32[]{:S(2)}) collective-permute-start(bf16[512,2,128]{2,0,1:T(8,128)(2,1)} %maximum_select_fusion.5), channel_id=1, source_target_pairs={{0,2},{2,0},{1,3},{3,1},{4,6},{6,4},{5,7},{7,5},{8,10},{10,8},{9,1... | collective-permute-start | bytes 786440 | tf_op jit(solution)/shard_map/ppermute | solution.py:20
  41.2 11.3 copy-start.6
  46.5 43.0 %copy-start.41 = (bf16[256,1,128]{2,1,0:T(2,128)(2,1)}, bf16[256,1,128]{2,1,0:T(2,128)(2,1)S(1)}, u32[]{:S(2)}) copy-start(bf16[256,1,128]{2,1,0:T(2,128)(2,1)S(1)} %slice.238) | copy-start | bytes 196612
  56.9 22.5 %collective-permute-start.2 = (bf16[1024,2,128]{2,0,1:T(8,128)(2,1)S(1)}, bf16[1024,2,128]{2,0,1:T(8,128)(2,1)}, u32[]{:S(2)}, u32[]{:S(2)}) collective-permute-start(bf16[1024,2,128]{2,0,1:T(8,128)(2,1)S(1)} %maximum_select_fusion.3), channel_id=1, source_target_pairs={{0,2},{2,0},{1,3},{3,1},{4,6},{6,4},{5,7},{7,5},{8,10},{10,8},{9,1... | collective-permute-start | bytes 1572872 | tf_op jit(solution)/shard_map/ppermute | solution.py:20
  58.4 29.5 %collective-permute-start.5 = (bf16[1024,2,128]{2,0,1:T(8,128)(2,1)S(1)}, bf16[1024,2,128]{2,0,1:T(8,128)(2,1)}, u32[]{:S(2)}, u32[]{:S(2)}) collective-permute-start(bf16[1024,2,128]{2,0,1:T(8,128)(2,1)S(1)} %maximum_select_fusion.4), channel_id=1, source_target_pairs={{0,4},{4,0},{1,5},{5,1},{2,6},{6,2},{3,7},{7,3},{8,12},{12,8},{9,1... | collective-permute-start | bytes 1572872 | tf_op jit(solution)/shard_map/ppermute | solution.py:20
  75.2 5.6 copy-start.35
  90.0 492.2 %copy-start.4 = (f32[2048,256]{1,0:T(8,128)}, f32[2048,256]{1,0:T(8,128)S(1)}, u32[]{:S(2)}) copy-start(f32[2048,256]{1,0:T(8,128)S(1)} %get-tuple-element.647) | copy-start | bytes 6291460
  96.9 463.0 %copy-start.69 = (bf16[8,1,128]{2,1,0:T(2,128)(2,1)S(1)}, bf16[8,1,128]{2,1,0:T(2,128)(2,1)}, u32[]{:S(2)}) copy-start(bf16[8,1,128]{2,1,0:T(2,128)(2,1)} %slice.240) | copy-start | bytes 6148
  98.2 462.4 %copy-start.44 = (f32[8,256]{1,0:T(8,128)S(1)}, f32[8,256]{1,0:T(8,128)}, u32[]{:S(2)}) copy-start(f32[8,256]{1,0:T(8,128)} %reshape.648) | copy-start | bytes 24580
  98.2 462.4 %copy-start.49 = (f32[8,256]{1,0:T(8,128)S(1)}, f32[8,256]{1,0:T(8,128)}, u32[]{:S(2)}) copy-start(f32[8,256]{1,0:T(8,128)} %reshape.649) | copy-start | bytes 24580
  98.2 462.4 %copy-start.50 = (f32[8,256]{1,0:T(8,128)S(1)}, f32[8,256]{1,0:T(8,128)}, u32[]{:S(2)}) copy-start(f32[8,256]{1,0:T(8,128)} %reshape.650) | copy-start | bytes 24580
  99.9 467.6 %copy-start.45 = (f32[1024,2]{0,1:T(2,128)S(1)}, f32[1024,2]{0,1:T(2,128)}, u32[]{:S(2)}) copy-start(f32[1024,2]{0,1:T(2,128)} %copy.205) | copy-start | bytes 24580
  558.9 14.5 copy-start.48
  560.5 4.4 copy-start.73
  560.6 4.3 copy-start.53
  575.5 3.9 copy-start.51
  575.5 3.9 copy-start.54
  575.5 3.9 copy-start.66
  575.5 4.6 copy-start.27
  575.5 4.6 copy-start.74
  575.5 5.8 copy-start.46
  575.5 5.8 copy-start.47
  575.6 5.8 copy-start.64
  579.4 4.4 copy-start.67
  585.2 4.6 copy-start.68
  621.0 84.5 %collective-permute-start.6 = (f32[1024,2,128]{2,0,1:T(8,128)}, f32[1024,2,128]{2,0,1:T(8,128)}, u32[]{:S(2)}, u32[]{:S(2)}) collective-permute-start(f32[1024,2,128]{2,0,1:T(8,128)} %slice_select_fusion), channel_id=1, source_target_pairs={{0,1},{1,0},{2,3},{3,2},{4,5},{5,4},{6,7},{7,6},{8,9},{9,8},{10,11... | collective-permute-start | bytes 3145736 | tf_op jit(solution)/shard_map/ppermute | solution.py:20
  621.2 3.5 copy-start.1
  621.2 3.7 copy-start.22
  628.0 74.5 %collective-permute-start.7 = (f32[1024,2,128]{2,0,1:T(8,128)}, f32[1024,2,128]{2,0,1:T(8,128)}, u32[]{:S(2)}, u32[]{:S(2)}) collective-permute-start(f32[1024,2,128]{2,0,1:T(8,128)} %broadcast_select_fusion.1), channel_id=1, source_target_pairs={{0,2},{2,0},{1,3},{3,1},{4,6},{6,4},{5,7},{7,5},{8,10},{10,8},{9,1... | collective-permute-start | bytes 3145736 | tf_op jit(solution)/shard_map/ppermute | solution.py:20
  634.5 4.0 copy-start.18
  634.5 2.9 copy-start.55
  634.5 2.9 copy-start.57
  635.8 62.0 %collective-permute-start.9 = (f32[1024,2,128]{2,0,1:T(8,128)}, f32[1024,2,128]{2,0,1:T(8,128)}, u32[]{:S(2)}, u32[]{:S(2)}) collective-permute-start(f32[1024,2,128]{2,0,1:T(8,128)} %broadcast_select_fusion), channel_id=1, source_target_pairs={{0,4},{4,0},{1,5},{5,1},{2,6},{6,2},{3,7},{7,3},{8,12},{12,8},{9,1... | collective-permute-start | bytes 3145736 | tf_op jit(solution)/shard_map/ppermute | solution.py:20
  697.9 4.6 copy-start.13
  697.9 4.6 copy-start.15
  699.6 6.0 copy-start.2
  699.6 14.8 collective-permute-start.10
  704.0 22.5 %collective-permute-start.8 = (f32[512,2,128]{2,0,1:T(8,128)S(1)}, f32[512,2,128]{2,0,1:T(8,128)S(1)}, u32[]{:S(2)}, u32[]{:S(2)}) collective-permute-start(f32[512,2,128]{2,0,1:T(8,128)S(1)} %slice_select_fusion.2), channel_id=1, source_target_pairs={{0,1},{1,0},{2,3},{3,2},{4,5},{5,4},{6,7},{7,6},{8,9},{9,8},{10,11... | collective-permute-start | bytes 1572872 | tf_op jit(solution)/shard_map/ppermute | solution.py:20
  714.5 17.7 collective-permute-start.11
  728.3 1255.3 %copy-start.3 = (f32[2048,2,128]{2,0,1:T(8,128)S(1)}, f32[2048,2,128]{2,0,1:T(8,128)}, u32[]{:S(2)}) copy-start(f32[2048,2,128]{2,0,1:T(8,128)} %get-tuple-element.470) | copy-start | bytes 6291460
  (45 other events, 73.9 us)
Sparse Core Ops, SparseCore 0:
  14.8 542.3 all-gather.2
  631.1 1351.5 reduce-scatter.1
where the time goes:
time: 2000 us; the launch traced here: 1990 us
  waiting for transfers between devices  1730 us (86%)
  matrix products  94.2 us (5%)
  other arithmetic  68.9 us (3%)
  local copies, waits for them, and re-layouts  66.6 us (3%)
    reduce_scatter x1, waiting for transfers between devices, on_device(): lax.psum_scatter(partials[-1], ('grp', 'seq'), scatter_dimension=0, tiled...  1250 us
    all_gather x1, waiting for transfers between devices, on_device(): lax.all_gather(picked[-1], ('grp', 'seq'), axis=0, tiled=True)  457 us
    dot_general x60, matrix products, contract(): lax.dot_general(left, right, (((left_dim,), (right_dim,)), ((), ())), pre...  94.2 us
  transfers between devices with their start and end apart: 14, of which 6 were waited for; matrix products, arithmetic and copies ran while one was open for 8% of the time, Pallas kernels for 0%

commit v1 on v0

v1 whole, which is shorter than its diff:
```python
import functools
import math

import jax
import jax.numpy as jnp
import numpy as np
from jax import lax
from jax.experimental import pallas as pl
from jax.experimental.pallas import tpu as pltpu
from jax.sharding import PartitionSpec as P

ROWS = 2048
HEAD = 128
UNIT = 256
ORDER = (0, 4, 2, 6, 1, 3, 5, 7)
SCALE = HEAD**-0.5
SCALE2 = SCALE * math.log2(math.e)
NEG = -1e30
REMOTE = 5120
SETS = ((0, 1024, 1024), (1024, 1024, 512), (2048, 1024, 256), (3072, 2048, 256))
VMEM = 56 * 1024 * 1024


def unit_level(unit):
    return 3 if unit == 0 else 2 if unit == 1 else 1 if unit < 4 else 0


def own_bias():
    table = np.zeros((8, ROWS), np.float32)
    for key_unit in range(8):
        for query_unit in range(8):
            shared = 1 + min(unit_level(key_unit), unit_level(query_unit))
            table[key_unit, query_unit * UNIT : (query_unit + 1) * UNIT] = math.log2(shared)
    return table


def remote_bias():
    table = np.full((20, 1024), NEG, np.float32)
    for query_unit in range(4):
        lanes = slice(query_unit * UNIT, (query_unit + 1) * UNIT)
        level = unit_level(query_unit)
        for unit in range(4):
            table[unit, lanes] = math.log2(min(unit_level(unit), level))
        for unit in range(4):
            shared = min(unit_level(unit % 2), level) - 1
            if shared > 0:
                table[4 + unit, lanes] = math.log2(shared)
        if level == 3:
            table[8:12, lanes] = 0.0
    table[12:20, :8] = 0.0
    return np.concatenate([table, np.full((4, 1024), NEG, np.float32)], 0)


def dot_nt(left, right):
    return lax.dot_general(left, right, (((1,), (1,)), ((), ())), preferred_element_type=jnp.float32)


def dot_nn(left, right):
    return lax.dot_general(left, right, (((1,), (0,)), ((), ())), preferred_element_type=jnp.float32)


def dot_tn(left, right):
    return lax.dot_general(left, right, (((0,), (0,)), ((), ())), preferred_element_type=jnp.float32)


def call(kernel, outs, args, scratch=(), flops=0, nbytes=0, exps=0, any_inputs=()):
    specs = [
        pl.BlockSpec(memory_space=pl.ANY if at in any_inputs else pltpu.VMEM)
        for at in range(len(args))
    ]
    return pl.pallas_call(
        kernel,
        out_shape=[jax.ShapeDtypeStruct(shape, dtype) for shape, dtype in outs],
        in_specs=specs,
        out_specs=[pl.BlockSpec(memory_space=pltpu.VMEM)] * len(outs),
        scratch_shapes=list(scratch),
        compiler_params=pltpu.CompilerParams(vmem_limit_bytes=VMEM),
        cost_estimate=pl.CostEstimate(flops=flops, bytes_accessed=nbytes, transcendentals=exps),
    )(*args)


def prepare_kernel(q_ref, k_ref, v_ref, g_ref, qp_ref, kv_ref, gp_ref, s1_ref, s2_ref, s3_ref, s4_ref, wide):
    def sort_rows(source, target, lane):
        wide[...] = source[...].astype(jnp.float32)
        for unit, residue in enumerate(ORDER):
            for pair in range(16):
                parts = [
                    wide[pl.ds(8 * (2 * pair + half) + residue, 8, stride=256), :]
                    for half in range(2)
                ]
                rows = slice(unit * UNIT + 16 * pair, unit * UNIT + 16 * pair + 16)
                target[rows, lane : lane + HEAD] = jnp.concatenate(parts, 0).astype(jnp.bfloat16)

    sort_rows(k_ref, kv_ref, 0)
    sort_rows(v_ref, kv_ref, HEAD)
    sort_rows(q_ref, qp_ref, 0)
    sort_rows(g_ref, gp_ref, 0)
    s1_ref[...] = kv_ref[:1024]
    s2_ref[...] = kv_ref[:512]
    s3_ref[...] = kv_ref[:256]
    s4_ref[...] = kv_ref[:16]


def forward_block(q_block, kv_ref, first, units, bias_ref, bias_row, lanes, score_ref):
    count = q_block.shape[0]

    def scores(unit, peak):
        rows = pl.multiple_of(first + unit * UNIT, UNIT)
        block = dot_nt(kv_ref[pl.ds(rows, UNIT), :HEAD], q_block) * SCALE2
        block = block + bias_ref[pl.ds(bias_row + unit, 1), lanes]
        score_ref[pl.ds(pl.multiple_of(unit * UNIT, UNIT), UNIT), :count] = block
        return jnp.maximum(peak, jnp.max(block, axis=0, keepdims=True))

    peak = lax.fori_loop(0, units, scores, jnp.full((1, count), NEG, jnp.float32))

    def values(unit, state):
        total, out = state
        rows = pl.multiple_of(first + unit * UNIT, UNIT)
        block = score_ref[pl.ds(pl.multiple_of(unit * UNIT, UNIT), UNIT), :count]
        prob = jnp.exp2(block - peak)
        total = total + jnp.sum(prob, axis=0, keepdims=True)
        out = out + dot_tn(kv_ref[pl.ds(rows, UNIT), HEAD:], prob.astype(jnp.bfloat16))
        return total, out

    zero = (jnp.zeros((1, count), jnp.float32), jnp.zeros((HEAD, count), jnp.float32))
    total, out = lax.fori_loop(0, units, values, zero)
    return peak, total, out


def own_forward_kernel(q_ref, kv_ref, bias_ref, stat_ref, out_ref, score_ref):
    stat_ref[...] = jnp.zeros_like(stat_ref)

    def block(at, carry):
        start = pl.multiple_of(at * UNIT, UNIT)
        lanes = pl.ds(start, UNIT)
        peak, total, out = forward_block(
            q_ref[pl.ds(start, UNIT), :], kv_ref, 0, 8, bias_ref, 0, lanes, score_ref
        )
        stat_ref[0:1, lanes] = peak
        stat_ref[1:2, lanes] = total
        out_ref[:, lanes] = out
        return carry

    lax.fori_loop(0, ROWS // UNIT, block, 0)


def gather_rows(refs, held, sem):
    copies = []
    at = 0
    for index, ref in enumerate(refs):
        rows = ref.shape[0]
        copies.append(pltpu.make_async_copy(ref, held.at[pl.ds(at, rows)], sem.at[index]))
        at += rows
    for copy in copies:
        copy.start()
    for copy in copies:
        copy.wait()


def remote_forward_kernel(q_ref, g_ref, bias_ref, stat_ref, out_ref, *rest):
    kv_refs, (row_ref, held, score_ref, sem) = rest[:8], rest[8:]
    gather_rows(kv_refs, held, sem)
    row_ref[...] = jnp.zeros_like(row_ref)
    for start, count, units in ((0, 256, 20), (256, 256, 8), (512, 256, 4), (768, 256, 4), (1024, 1024, 0)):
        lanes = slice(start, start + count)
        peak = stat_ref[0:1, lanes]
        total = stat_ref[1:2, lanes]
        out = out_ref[:, lanes]
        if units:
            far_peak, far_total, far_out = forward_block(
                q_ref[lanes, :], held, 0, units, bias_ref, 0, lanes, score_ref
            )
            top = jnp.maximum(peak, far_peak)
            near, far = jnp.exp2(peak - top), jnp.exp2(far_peak - top)
            total = near * total + far * far_total
            out = near * out + far * far_out
            peak = top
        row_ref[0:1, lanes] = peak + jnp.log2(total)
        grad = g_ref[lanes, :].astype(jnp.float32).T
        row_ref[1:2, lanes] = jnp.sum(grad * out, axis=0, keepdims=True) / total


def backward_unit(kv_unit, q_ref, g_ref, row_ref, bias_ref, bias_row, count, step, dq_ref):
    key, value = kv_unit[:, :HEAD], kv_unit[:, HEAD:]
    grad_key = jnp.zeros((UNIT, HEAD), jnp.float32)
    grad_value = jnp.zeros((UNIT, HEAD), jnp.float32)
    for start in range(0, count, step):
        lanes = slice(start, start + step)
        query, grad = q_ref[lanes, :], g_ref[lanes, :]
        offset = bias_ref[pl.ds(bias_row, 1), lanes] - row_ref[0:1, lanes]
        weights = jnp.exp2(dot_nt(key, query) * SCALE2 + offset)
        grad_probs = dot_nt(value, grad)
        grad_scores = (weights * (grad_probs - row_ref[1:2, lanes])).astype(jnp.bfloat16)
        grad_value = grad_value + dot_nn(weights.astype(jnp.bfloat16), grad)
        grad_key = grad_key + dot_nn(grad_scores, query)
        dq_ref[:, lanes] += dot_tn(key, grad_scores)
    return jnp.concatenate([SCALE * grad_key, grad_value], 1)


def remote_backward_kernel(q_ref, g_ref, bias_ref, row_ref, *rest):
    kv_refs, rest = rest[:8], rest[8:]
    out_refs, dq_ref = rest[:8], rest[8]
    dq_ref[...] = jnp.zeros_like(dq_ref)
    bias_row = 0
    for kv_ref, out_ref, count in zip(kv_refs, out_refs, (1024, 512, 512, 256, 256, 256, 256, 256)):
        units = kv_ref.shape[0] // UNIT

        def one(unit, carry, kv_ref=kv_ref, out_ref=out_ref, count=count, bias_row=bias_row):
            rows = pl.ds(pl.multiple_of(unit * UNIT, UNIT), UNIT)
            both = backward_unit(
                kv_ref[rows, :], q_ref, g_ref, row_ref, bias_ref, bias_row + unit, count, min(count, 512), dq_ref
            )
            out_ref[rows, :] = both.astype(jnp.bfloat16)
            return carry

        lax.fori_loop(0, units, one, 0)
        bias_row += units


def own_backward_kernel(q_ref, g_ref, bias_ref, row_ref, kv_ref, far_ref, dq_ref, dkv_ref, acc_ref, tall_ref):
    acc_ref[:, :1024] = far_ref[...]
    acc_ref[:, 1024:] = jnp.zeros((HEAD, 1024), jnp.float32)

    def one(unit, carry):
        rows = pl.ds(pl.multiple_of(unit * UNIT, UNIT), UNIT)
        dkv_ref[rows, :] = backward_unit(
            kv_ref[rows, :], q_ref, g_ref, row_ref, bias_ref, unit, ROWS, 512, acc_ref
        )
        return carry

    lax.fori_loop(0, ROWS // UNIT, one, 0)
    for unit in range(8):
        lanes = slice(unit * UNIT, (unit + 1) * UNIT)
        tall_ref[lanes, :] = acc_ref[:, lanes].T * SCALE
    restore_rows(lambda rows: tall_ref[rows, :], dq_ref)


def restore_rows(read, target):
    for unit, residue in enumerate(ORDER):
        for block in range(32):
            start = unit * UNIT + 8 * block
            target[pl.ds(8 * block + residue, 8, stride=256), :] = read(slice(start, start + 8))


def join_kernel(dkv_ref, *rest):
    far_refs, (dk_ref, dv_ref, sum_ref) = rest[:8], rest[8:]
    sum_ref[...] = dkv_ref[...]
    for ref in far_refs[:7]:
        rows = ref.shape[0]
        sum_ref[:rows, :] += ref[...].astype(jnp.float32)
    whole = far_refs[7]

    def add(at, total):
        piece = whole[pl.ds(pl.multiple_of(at * 16, 16), 16), :].astype(jnp.float32)
        return total + piece[:8] + piece[8:]

    total = lax.fori_loop(0, 128, add, jnp.zeros((8, 2 * HEAD), jnp.float32))
    sum_ref[:8, :] += total
    restore_rows(lambda rows: sum_ref[rows, :HEAD], dk_ref)
    restore_rows(lambda rows: sum_ref[rows, HEAD:], dv_ref)


def swap(block, mask):
    return lax.ppermute(block, "seq", [(at, at ^ mask) for at in range(lax.axis_size("seq"))])


def on_device(queries, keys, values, cotangent):
    f32, bf16 = jnp.float32, jnp.bfloat16
    near_bias = jnp.asarray(own_bias())
    far_bias = jnp.asarray(remote_bias())
    q, kv, g, s1, s2, s3, s4 = call(
        prepare_kernel,
        [((ROWS, HEAD), bf16), ((ROWS, 256), bf16), ((ROWS, HEAD), bf16)]
        + [((rows, 256), bf16) for rows in (1024, 512, 256, 16)],
        (queries, keys, values, cotangent),
        [pltpu.VMEM((ROWS, HEAD), f32)],
        nbytes=5 << 20,
    )
    far = [swap(s1, 1)] + [swap(s2, mask) for mask in (2, 3)] + [swap(s3, mask) for mask in (4, 5, 6, 7)]
    spread = jnp.broadcast_to(s4[None, :8], (256, 8, 256))
    whole = lax.all_to_all(spread, ("grp", "seq"), 0, 0)
    far.append(whole.reshape(2048, 256))
    stat, out = call(
        own_forward_kernel,
        [((8, ROWS), f32), ((HEAD, ROWS), f32)],
        (q, kv, near_bias),
        [pltpu.VMEM((ROWS, UNIT), f32)],
        flops=4 * HEAD * ROWS * ROWS,
        nbytes=3 << 20,
        exps=ROWS * ROWS,
    )
    (row,) = call(
        remote_forward_kernel,
        [((8, ROWS), f32)],
        (q, g, far_bias, stat, out, *far),
        [pltpu.VMEM((REMOTE, 256), bf16), pltpu.VMEM((REMOTE, UNIT), f32), pltpu.SemaphoreType.DMA((8,))],
        flops=2 * HEAD * ROWS * ROWS,
        nbytes=6 << 20,
        exps=ROWS * ROWS // 2,
        any_inputs=range(5, 13),
    )
    *sends, far_dq = call(
        remote_backward_kernel,
        [((block.shape[0], 256), bf16) for block in far] + [((HEAD, 1024), f32)],
        (q, g, far_bias, row, *far),
        flops=5 * HEAD * ROWS * ROWS,
        nbytes=8 << 20,
        exps=ROWS * ROWS // 2,
    )
    back = [swap(block, mask) for block, mask in zip(sends[:7], (1, 2, 3, 4, 5, 6, 7))]
    back.append(lax.all_to_all(sends[7].reshape(256, 8, 256), ("grp", "seq"), 0, 0).reshape(2048, 256))
    dq, dkv = call(
        own_backward_kernel,
        [((ROWS, HEAD), f32), ((ROWS, 256), f32)],
        (q, g, near_bias, row, kv, far_dq),
        [pltpu.VMEM((HEAD, ROWS), f32), pltpu.VMEM((ROWS, HEAD), f32)],
        flops=10 * HEAD * ROWS * ROWS,
        nbytes=8 << 20,
        exps=ROWS * ROWS,
    )
    dk, dv = call(
        join_kernel,
        [((ROWS, HEAD), f32)] * 2,
        (dkv, *back),
        [pltpu.VMEM((ROWS, 256), f32)],
        nbytes=8 << 20,
    )
    return dq, dk, dv


def solution(mesh):
    spec = P(("grp", "seq"), None)
    return jax.shard_map(
        on_device, mesh=mesh, in_specs=(spec,) * 4, out_specs=(spec,) * 3, check_vma=False
    )
```

time: 2000 us -> 187 us (0.09)
  waiting for transfers between devices: 1730 us -> 46.6 us
  matrix products: 94.2 us -> 0 us
  Pallas kernels: 0 us -> 87.7 us
  other arithmetic: 68.9 us -> 0 us
  local copies, waits for them, and re-layouts: 66.6 us -> 4.34 us
  starting transfers between devices: 17.2 us -> 46.9 us
    reduce_scatter x1 -> x0, waiting for transfers between devices: 1250 us -> none  [on_device(): lax.psum_scatter(partials[-1], ('grp', 'seq'), scatter_dimension=0, tiled...]
    all_gather x1 -> x0, waiting for transfers between devices: 457 us -> none  [on_device(): lax.all_gather(picked[-1], ('grp', 'seq'), axis=0, tiled=True)]
    dot_general x60 -> x0, matrix products: 94.2 us -> none  [contract(): lax.dot_general(left, right, (((left_dim,), (right_dim,)), ((), ())), pre...]
    pallas_call x0 -> x6, Pallas kernels: none -> 87.7 us  [call(): pl.pallas_call(kernel, out_shape=[jax.ShapeDtypeStruct(shape, dtype) for...]
    add x25 -> x0, other arithmetic: 33.9 us -> none  [the longest x6 21.5 us: advance(): running = running + jnp.stack([grad_key, grad_value], 1)]
    reshape x42 -> x0, local copies, waits for them, and re-layouts: 30.3 us -> none  [the longest x35 28.1 us: spread_rows(): return widened.reshape((row_count * stride,) + part_rows.shape[1:])]
    all_to_all x0 -> x2, starting transfers between devices: none -> 27.3 us  [the longest x1 15.7 us: on_device(): whole = lax.all_to_all(spread, ('grp', 'seq'), 0, 0)]
    ppermute x12 -> x14, waiting for transfers between devices: 24.3 us -> 46.6 us  [swap(): lax.ppermute(block, 'seq', [(at, at ^ mask) for at in range(lax.axis_size...]
  transfers between devices with their start and end apart: 14 -> 16, of which waited for: 6 -> 5; matrix products, arithmetic and copies ran while one was open for 8% -> 0% of each run, Pallas kernels for 0% -> 24%
where the time goes in v1:
time: 187 us
  Pallas kernels  87.7 us (47%)
  starting transfers between devices  46.9 us (25%)
  waiting for transfers between devices  46.6 us (25%)
  local copies, waits for them, and re-layouts  4.34 us (2%)
    pallas_call x6, Pallas kernels, call(): pl.pallas_call(kernel, out_shape=[jax.ShapeDtypeStruct(shape, dtype) for...  87.7 us
    ppermute x14, waiting for transfers between devices, swap(): lax.ppermute(block, 'seq', [(at, at ^ mask) for at in range(lax.axis_size...  46.6 us
    ppermute x14, starting transfers between devices, swap(): lax.ppermute(block, 'seq', [(at, at ^ mask) for at in range(lax.axis_size...  19.6 us
    all_to_all x1, starting transfers between devices, on_device(): whole = lax.all_to_all(spread, ('grp', 'seq'), 0, 0)  15.7 us
    all_to_all x1, starting transfers between devices, on_device(): lax.all_to_all(sends[7].reshape(256, 8, 256), ('grp', 'seq'), 0, 0)  11.7 us
  transfers between devices with their start and end apart: 16, of which 5 were waited for; matrix products, arithmetic and copies ran while one was open for 0% of the time, Pallas kernels for 24%

profile of v1, /device:TPU:1, one launch (start us, length us, event | category | flops | bytes accessed | tf_op | source)
XLA Modules:
  0.0 186.5 jit_solution(6295298343339036836)
XLA Ops:
  0.6 5.0 %shard_map.85 = (bf16[2048,128]{1,0:T(8,128)(2,1)}, bf16[2048,256]{1,0:T(8,128)(2,1)}, bf16[2048,128]{1,0:T(8,128)(2,1)}, bf16[1024,256]{1,0:T(8,128)(2,1)}, bf1...) custom-call(bf16[2048,128]{1,0:T(8,128)(2,1)} %q_ref.1, bf16[2048,128]{1,0:T(8,128)(2,1)} %k_ref.1, ...), custom_call_target="tpu_custom_call" | custom-call | bytes 5242880 | tf_op jit(solution)/shard_map/pallas_call | solution.py:71
  5.7 0.8 slice.3
  6.5 1.0 broadcast_in_dim.2
  7.5 15.7 %all-to-all-start = ((bf16[256,8,256]{2,1,0:T(8,128)(2,1)}), bf16[256,8,256]{2,1,0:T(8,128)(2,1)S(1)}, u32[]{:S(2)}, u32[]{:S(2)}) async-start(bf16[256,8,256]{2,1,0:T(8,128)(2,1)} %broadcast_in_dim.2), calls=%async_computation | async-start | bytes 2097152 | tf_op jit(solution)/shard_map/all_to_all | solution.py:281
  23.2 1.5 collective-permute-start
  24.7 2.9 %collective-permute-start.6 = (bf16[256,256]{1,0:T(8,128)(2,1)S(1)}, bf16[256,256]{1,0:T(8,128)(2,1)S(1)}, u32[]{:S(2)}, u32[]{:S(2)}) collective-permute-start(bf16[256,256]{1,0:T(8,128)(2,1)S(1)} %copy-done.21), channel_id=1, source_target_pairs={{0,7},{1,6},{2,5},{3,4},{4,3},{5,2},{6,1},{7,0},{8,15},{9,14},{10,... | collective-permute-start | bytes 393224 | tf_op jit(solution)/shard_map/ppermute | solution.py:264
  27.6 0.7 collective-permute-start.5
  28.3 1.8 collective-permute-start.2
  30.1 0.5 collective-permute-start.1
  30.6 22.9 %collective-permute-done.6.rest_6_ = bf16[256,256]{1,0:T(8,128)(2,1)S(1)} collective-permute-done((bf16[256,256]{1,0:T(8,128)(2,1)S(1)}, bf16[256,256]{1,0:T(8,128)(2,1)S(1)}, u32[]{:S(2)}, u32[]{:S(2)}) %collective-permute-start.6) | collective-permute-done | bytes 131104 | tf_op jit(solution)/shard_map/ppermute | solution.py:264
  53.5 0.0 collective-permute-start.4
  53.5 3.2 %collective-permute-done.5.rest_5_ = bf16[256,256]{1,0:T(8,128)(2,1)S(1)} collective-permute-done((bf16[256,256]{1,0:T(8,128)(2,1)S(1)}, bf16[256,256]{1,0:T(8,128)(2,1)S(1)}, u32[]{:S(2)}, u32[]{:S(2)}) %collective-permute-start.5) | collective-permute-done | bytes 131104 | tf_op jit(solution)/shard_map/ppermute | solution.py:264
  56.7 0.0 collective-permute-start.3
  56.7 28.4 %shard_map.86 = (f32[8,2048]{1,0:T(8,128)}, f32[128,2048]{1,0:T(8,128)}) custom-call(bf16[2048,128]{1,0:T(8,128)(2,1)} %get-tuple-element.25.q_ref, bf16[2048,256]{1,0:T(8,128)(2,1)} %get-tuple-element.27.kv_ref, f32[8,2048]{1,0:T(8,128)} %constant.4.clone.bias_ref), custom_call_target="tpu_custom_call" | custom-call | flops 2147483648 | bytes 3145728 | tf_op jit(solution)/shard_map/pallas_call | solution.py:71
  85.1 0.0 collective-permute-done.4.rest_4_
  85.1 0.0 collective-permute-done.3.rest_3_
  85.2 0.0 collective-permute-done.2.rest_2_
  85.2 0.0 collective-permute-done.1.rest_1_
  85.2 0.0 collective-permute-done.rest_0_
  85.2 0.0 copy-start
  85.3 0.6 copy-done.14
  85.8 0.1 copy-done.15
  85.9 0.1 copy-done.4
  86.0 0.1 copy-done.5
  86.0 0.2 copy-done.2
  86.2 0.3 copy-done
  86.5 19.1 %shard_map.87.row_ref = f32[8,2048]{1,0:T(8,128)} custom-call(bf16[2048,128]{1,0:T(8,128)(2,1)} %get-tuple-element.25.q_ref, bf16[2048,128]{1,0:T(8,128)(2,1)} %get-tuple-element.26.g_ref, f32[24,1024]{1,0:T(8,128)} %constant.5.clone.bias_ref, f32[8,2048]{1,0:T(8,128)} %get-tuple-element.28.stat_ref, f32[128,2048]{1,0:T(8,128)} %get-tuple-element.29.out_ref, ...), custom_call_target="tpu_custom_call" | custom-call | flops 1073741824 | bytes 6291456 | tf_op jit(solution)/shard_map/pallas_call | solution.py:71
  105.7 13.4 %shard_map.88 = (bf16[1024,256]{1,0:T(8,128)(2,1)}, bf16[512,256]{1,0:T(8,128)(2,1)}, bf16[512,256]{1,0:T(8,128)(2,1)}, bf16[256,256]{1,0:T(8,128)(2,1)}, bf16[2...) custom-call(bf16[2048,128]{1,0:T(8,128)(2,1)} %get-tuple-element.25., ...), custom_call_target="tpu_custom_call" | custom-call | flops 2684354560 | bytes 8388608 | tf_op jit(solution)/shard_map/pallas_call | solution.py:71
  119.1 11.7 %all-to-all-start.1 = ((bf16[256,8,256]{2,1,0:T(8,128)(2,1)}), bf16[256,8,256]{2,1,0:T(8,128)(2,1)S(1)}, u32[]{:S(2)}, u32[]{:S(2)}) async-start(bf16[256,8,256]{2,1,0:T(8,128)(2,1)} %bitcast.6), calls=%async_computation.1 | async-start | bytes 2097152 | tf_op jit(solution)/shard_map/all_to_all | solution.py:311
  130.8 1.6 collective-permute-start.10
  132.4 1.1 collective-permute-start.11
  133.5 0.3 collective-permute-start.7
  133.8 3.8 %collective-permute-start.12 = (bf16[256,256]{1,0:T(8,128)(2,1)}, bf16[256,256]{1,0:T(8,128)(2,1)S(1)}, u32[]{:S(2)}, u32[]{:S(2)}) collective-permute-start(bf16[256,256]{1,0:T(8,128)(2,1)} %get-tuple-element.42), channel_id=1, source_target_pairs={{0,6},{1,7},{2,4},{3,5},{4,2},{5,3},{6,0},{7,1},{8,14},{9,15},{10,... | collective-permute-start | bytes 393224 | tf_op jit(solution)/shard_map/ppermute | solution.py:264
  137.6 0.6 collective-permute-start.13
  138.3 18.4 %collective-permute-done.10.rest_3_ = bf16[256,256]{1,0:T(8,128)(2,1)S(1)} collective-permute-done((bf16[256,256]{1,0:T(8,128)(2,1)S(1)}, bf16[256,256]{1,0:T(8,128)(2,1)S(1)}, u32[]{:S(2)}, u32[]{:S(2)}) %collective-permute-start.10) | collective-permute-done | bytes 131104 | tf_op jit(solution)/shard_map/ppermute | solution.py:264
  156.7 2.8 %collective-permute-start.8 = (bf16[512,256]{1,0:T(8,128)(2,1)}, bf16[512,256]{1,0:T(8,128)(2,1)S(1)}, u32[]{:S(2)}, u32[]{:S(2)}) collective-permute-start(bf16[512,256]{1,0:T(8,128)(2,1)} %get-tuple-element.38), channel_id=1, source_target_pairs={{0,2},{1,3},{2,0},{3,1},{4,6},{5,7},{6,4},{7,5},{8,10},{9,11},{10,... | collective-permute-start | bytes 786440 | tf_op jit(solution)/shard_map/ppermute | solution.py:264
  159.5 1.0 collective-permute-done.11.rest_4_
  160.5 1.9 %collective-permute-start.9 = (bf16[512,256]{1,0:T(8,128)(2,1)S(1)}, bf16[512,256]{1,0:T(8,128)(2,1)S(1)}, u32[]{:S(2)}, u32[]{:S(2)}) collective-permute-start(bf16[512,256]{1,0:T(8,128)(2,1)S(1)} %copy-done.18), channel_id=1, source_target_pairs={{0,3},{1,2},{2,1},{3,0},{4,7},{5,6},{6,5},{7,4},{8,11},{9,10},{10,... | collective-permute-start | bytes 786440 | tf_op jit(solution)/shard_map/ppermute | solution.py:264
  162.4 16.0 %shard_map.89 = (f32[2048,128]{1,0:T(8,128)}, f32[2048,256]{1,0:T(8,128)}) custom-call(bf16[2048,128]{1,0:T(8,128)(2,1)} %get-tuple-element.25.q_ref, bf16[2048,128]{1,0:T(8,128)(2,1)} %get-tuple-element.26.g_ref, f32[8,2048]{1,0:T(8,128)} %constant.4.clone.bias_ref, f32[8,2048]{1,0:T(8,128)} %shard_map.87.row_ref, ...), custom_call_target="tpu_custom_call" | custom-call | flops 5368709120 | bytes 8388608 | tf_op jit(solution)/shard_map/pallas_call | solution.py:71
  178.4 0.0 collective-permute-done.12.rest_5_
  178.5 0.0 collective-permute-done.8.rest_1_
  178.5 1.1 collective-permute-done.9.rest_2_
  179.6 0.0 collective-permute-done.7.rest_0_
  179.6 0.0 all-to-all-done.1
  179.7 0.7 copy-done.7
  180.3 0.2 copy-done.3
  180.5 0.3 copy-done.1
  180.8 5.7 %shard_map.90 = (f32[2048,128]{1,0:T(8,128)}, f32[2048,128]{1,0:T(8,128)}) custom-call(f32[2048,256]{1,0:T(8,128)} %get-tuple-element.36.dkv_ref, bf16[1024,256]{1,0:T(8,128)(2,1)} %copy-done.3, bf16[512,256]{1,0:T(8,128)(2,1)} %copy-done.6, bf16[512,256]{1,0:T(8,128)(2,1)} %copy-done.7, bf16[256,256]{1,0:T(8,128)(2,1)} %copy-done.8, ...), custom_call_target="tpu_custom_call" | custom-call | bytes 8388608 | tf_op jit(solution)/shard_map/pallas_call | solution.py:71
  (40 shorter events, 0.1 us)
Async XLA Ops:
  5.7 17.5 %copy-start.17 = (bf16[1024,256]{1,0:T(8,128)(2,1)S(1)}, bf16[1024,256]{1,0:T(8,128)(2,1)}, u32[]{:S(2)}) copy-start(bf16[1024,256]{1,0:T(8,128)(2,1)} %get-tuple-element.30) | copy-start | bytes 1572868
  5.7 19.0 %copy-start.21 = (bf16[256,256]{1,0:T(8,128)(2,1)S(1)}, bf16[256,256]{1,0:T(8,128)(2,1)}, u32[]{:S(2)}) copy-start(bf16[256,256]{1,0:T(8,128)(2,1)} %get-tuple-element.32) | copy-start | bytes 393220
  5.7 22.6 %copy-start.19 = (bf16[512,256]{1,0:T(8,128)(2,1)S(1)}, bf16[512,256]{1,0:T(8,128)(2,1)}, u32[]{:S(2)}) copy-start(bf16[512,256]{1,0:T(8,128)(2,1)} %get-tuple-element.31) | copy-start | bytes 786436
  7.5 77.7 %all-to-all-start = ((bf16[256,8,256]{2,1,0:T(8,128)(2,1)}), bf16[256,8,256]{2,1,0:T(8,128)(2,1)S(1)}, u32[]{:S(2)}, u32[]{:S(2)}) async-start(bf16[256,8,256]{2,1,0:T(8,128)(2,1)} %broadcast_in_dim.2), calls=%async_computation | async-start | bytes 2097152 | tf_op jit(solution)/shard_map/all_to_all | solution.py:281
  23.2 62.0 %collective-permute-start = (bf16[1024,256]{1,0:T(8,128)(2,1)S(1)}, bf16[1024,256]{1,0:T(8,128)(2,1)S(1)}, u32[]{:S(2)}, u32[]{:S(2)}) collective-permute-start(bf16[1024,256]{1,0:T(8,128)(2,1)S(1)} %copy-done.17), channel_id=1, source_target_pairs={{0,1},{1,0},{2,3},{3,2},{4,5},{5,4},{6,7},{7,6},{8,9},{9,8},{10,11... | collective-permute-start | bytes 1572872 | tf_op jit(solution)/shard_map/ppermute | solution.py:264
  24.7 28.8 %collective-permute-start.6 = (bf16[256,256]{1,0:T(8,128)(2,1)S(1)}, bf16[256,256]{1,0:T(8,128)(2,1)S(1)}, u32[]{:S(2)}, u32[]{:S(2)}) collective-permute-start(bf16[256,256]{1,0:T(8,128)(2,1)S(1)} %copy-done.21), channel_id=1, source_target_pairs={{0,7},{1,6},{2,5},{3,4},{4,3},{5,2},{6,1},{7,0},{8,15},{9,14},{10,... | collective-permute-start | bytes 393224 | tf_op jit(solution)/shard_map/ppermute | solution.py:264
  27.6 29.1 %collective-permute-start.5 = (bf16[256,256]{1,0:T(8,128)(2,1)S(1)}, bf16[256,256]{1,0:T(8,128)(2,1)S(1)}, u32[]{:S(2)}, u32[]{:S(2)}) collective-permute-start(bf16[256,256]{1,0:T(8,128)(2,1)S(1)} %copy-done.21), channel_id=1, source_target_pairs={{0,6},{1,7},{2,4},{3,5},{4,2},{5,3},{6,0},{7,1},{8,14},{9,15},{10,... | collective-permute-start | bytes 393224 | tf_op jit(solution)/shard_map/ppermute | solution.py:264
  28.3 56.9 %collective-permute-start.2 = (bf16[512,256]{1,0:T(8,128)(2,1)S(1)}, bf16[512,256]{1,0:T(8,128)(2,1)S(1)}, u32[]{:S(2)}, u32[]{:S(2)}) collective-permute-start(bf16[512,256]{1,0:T(8,128)(2,1)S(1)} %copy-done.19), channel_id=1, source_target_pairs={{0,3},{1,2},{2,1},{3,0},{4,7},{5,6},{6,5},{7,4},{8,11},{9,10},{10,... | collective-permute-start | bytes 786440 | tf_op jit(solution)/shard_map/ppermute | solution.py:264
  30.1 55.1 %collective-permute-start.1 = (bf16[512,256]{1,0:T(8,128)(2,1)S(1)}, bf16[512,256]{1,0:T(8,128)(2,1)S(1)}, u32[]{:S(2)}, u32[]{:S(2)}) collective-permute-start(bf16[512,256]{1,0:T(8,128)(2,1)S(1)} %copy-done.19), channel_id=1, source_target_pairs={{0,2},{1,3},{2,0},{3,1},{4,6},{5,7},{6,4},{7,5},{8,10},{9,11},{10,... | collective-permute-start | bytes 786440 | tf_op jit(solution)/shard_map/ppermute | solution.py:264
  53.5 31.6 %copy-start.9 = (bf16[256,256]{1,0:T(8,128)(2,1)}, bf16[256,256]{1,0:T(8,128)(2,1)S(1)}, u32[]{:S(2)}) copy-start(bf16[256,256]{1,0:T(8,128)(2,1)S(1)} %collective-permute-done.6.rest_6_) | copy-start | bytes 393220
  53.5 31.6 %collective-permute-start.4 = (bf16[256,256]{1,0:T(8,128)(2,1)S(1)}, bf16[256,256]{1,0:T(8,128)(2,1)S(1)}, u32[]{:S(2)}, u32[]{:S(2)}) collective-permute-start(bf16[256,256]{1,0:T(8,128)(2,1)S(1)} %copy-done.21), channel_id=1, source_target_pairs={{0,5},{1,4},{2,7},{3,6},{4,1},{5,0},{6,3},{7,2},{8,13},{9,12},{10,... | collective-permute-start | bytes 393224 | tf_op jit(solution)/shard_map/ppermute | solution.py:264
  56.7 28.4 %copy-start.11 = (bf16[256,256]{1,0:T(8,128)(2,1)}, bf16[256,256]{1,0:T(8,128)(2,1)S(1)}, u32[]{:S(2)}) copy-start(bf16[256,256]{1,0:T(8,128)(2,1)S(1)} %collective-permute-done.5.rest_5_) | copy-start | bytes 393220
  56.7 28.4 %collective-permute-start.3 = (bf16[256,256]{1,0:T(8,128)(2,1)S(1)}, bf16[256,256]{1,0:T(8,128)(2,1)S(1)}, u32[]{:S(2)}, u32[]{:S(2)}) collective-permute-start(bf16[256,256]{1,0:T(8,128)(2,1)S(1)} %copy-done.21), channel_id=1, source_target_pairs={{0,4},{1,5},{2,6},{3,7},{4,0},{5,1},{6,2},{7,3},{8,12},{9,13},{10,... | collective-permute-start | bytes 393224 | tf_op jit(solution)/shard_map/ppermute | solution.py:264
  85.1 0.7 copy-start.14
  85.2 0.7 copy-start.15
  85.2 0.8 copy-start.4
  85.2 0.8 copy-start.5
  85.2 1.0 copy-start.2
  85.2 1.3 copy-start
  119.1 11.7 %copy-start.23 = (bf16[256,256]{1,0:T(8,128)(2,1)S(1)}, bf16[256,256]{1,0:T(8,128)(2,1)}, u32[]{:S(2)}) copy-start(bf16[256,256]{1,0:T(8,128)(2,1)} %get-tuple-element.40) | copy-start | bytes 393220
  119.1 13.3 %copy-start.22 = (bf16[256,256]{1,0:T(8,128)(2,1)S(1)}, bf16[256,256]{1,0:T(8,128)(2,1)}, u32[]{:S(2)}) copy-start(bf16[256,256]{1,0:T(8,128)(2,1)} %get-tuple-element.41) | copy-start | bytes 393220
  119.1 14.4 %copy-start.16 = (bf16[1024,256]{1,0:T(8,128)(2,1)S(1)}, bf16[1024,256]{1,0:T(8,128)(2,1)}, u32[]{:S(2)}) copy-start(bf16[1024,256]{1,0:T(8,128)(2,1)} %get-tuple-element.37) | copy-start | bytes 1572868
  119.1 18.5 %copy-start.20 = (bf16[256,256]{1,0:T(8,128)(2,1)S(1)}, bf16[256,256]{1,0:T(8,128)(2,1)}, u32[]{:S(2)}) copy-start(bf16[256,256]{1,0:T(8,128)(2,1)} %get-tuple-element.43) | copy-start | bytes 393220
  119.1 41.4 %copy-start.18 = (bf16[512,256]{1,0:T(8,128)(2,1)S(1)}, bf16[512,256]{1,0:T(8,128)(2,1)}, u32[]{:S(2)}) copy-start(bf16[512,256]{1,0:T(8,128)(2,1)} %get-tuple-element.39) | copy-start | bytes 786436
  119.1 60.5 %all-to-all-start.1 = ((bf16[256,8,256]{2,1,0:T(8,128)(2,1)}), bf16[256,8,256]{2,1,0:T(8,128)(2,1)S(1)}, u32[]{:S(2)}, u32[]{:S(2)}) async-start(bf16[256,8,256]{2,1,0:T(8,128)(2,1)} %bitcast.6), calls=%async_computation.1 | async-start | bytes 2097152 | tf_op jit(solution)/shard_map/all_to_all | solution.py:311
  130.8 25.9 %collective-permute-start.10 = (bf16[256,256]{1,0:T(8,128)(2,1)S(1)}, bf16[256,256]{1,0:T(8,128)(2,1)S(1)}, u32[]{:S(2)}, u32[]{:S(2)}) collective-permute-start(bf16[256,256]{1,0:T(8,128)(2,1)S(1)} %copy-done.23), channel_id=1, source_target_pairs={{0,4},{1,5},{2,6},{3,7},{4,0},{5,1},{6,2},{7,3},{8,12},{9,13},{10,... | collective-permute-start | bytes 393224 | tf_op jit(solution)/shard_map/ppermute | solution.py:264
  132.4 28.0 %collective-permute-start.11 = (bf16[256,256]{1,0:T(8,128)(2,1)S(1)}, bf16[256,256]{1,0:T(8,128)(2,1)S(1)}, u32[]{:S(2)}, u32[]{:S(2)}) collective-permute-start(bf16[256,256]{1,0:T(8,128)(2,1)S(1)} %copy-done.22), channel_id=1, source_target_pairs={{0,5},{1,4},{2,7},{3,6},{4,1},{5,0},{6,3},{7,2},{8,13},{9,12},{10,... | collective-permute-start | bytes 393224 | tf_op jit(solution)/shard_map/ppermute | solution.py:264
  133.5 46.1 %collective-permute-start.7 = (bf16[1024,256]{1,0:T(8,128)(2,1)S(1)}, bf16[1024,256]{1,0:T(8,128)(2,1)S(1)}, u32[]{:S(2)}, u32[]{:S(2)}) collective-permute-start(bf16[1024,256]{1,0:T(8,128)(2,1)S(1)} %copy-done.16), channel_id=1, source_target_pairs={{0,1},{1,0},{2,3},{3,2},{4,5},{5,4},{6,7},{7,6},{8,9},{9,8},{10,11... | collective-permute-start | bytes 1572872 | tf_op jit(solution)/shard_map/ppermute | solution.py:264
  133.8 44.7 %collective-permute-start.12 = (bf16[256,256]{1,0:T(8,128)(2,1)}, bf16[256,256]{1,0:T(8,128)(2,1)S(1)}, u32[]{:S(2)}, u32[]{:S(2)}) collective-permute-start(bf16[256,256]{1,0:T(8,128)(2,1)} %get-tuple-element.42), channel_id=1, source_target_pairs={{0,6},{1,7},{2,4},{3,5},{4,2},{5,3},{6,0},{7,1},{8,14},{9,15},{10,... | collective-permute-start | bytes 393224 | tf_op jit(solution)/shard_map/ppermute | solution.py:264
  137.6 40.8 %collective-permute-start.13 = (bf16[256,256]{1,0:T(8,128)(2,1)S(1)}, bf16[256,256]{1,0:T(8,128)(2,1)S(1)}, u32[]{:S(2)}, u32[]{:S(2)}) collective-permute-start(bf16[256,256]{1,0:T(8,128)(2,1)S(1)} %copy-done.20), channel_id=1, source_target_pairs={{0,7},{1,6},{2,5},{3,4},{4,3},{5,2},{6,1},{7,0},{8,15},{9,14},{10,... | collective-permute-start | bytes 393224 | tf_op jit(solution)/shard_map/ppermute | solution.py:264
  156.7 21.7 %copy-start.8 = (bf16[256,256]{1,0:T(8,128)(2,1)}, bf16[256,256]{1,0:T(8,128)(2,1)S(1)}, u32[]{:S(2)}) copy-start(bf16[256,256]{1,0:T(8,128)(2,1)S(1)} %collective-permute-done.10.rest_3_) | copy-start | bytes 393220
  156.7 21.8 %collective-permute-start.8 = (bf16[512,256]{1,0:T(8,128)(2,1)}, bf16[512,256]{1,0:T(8,128)(2,1)S(1)}, u32[]{:S(2)}, u32[]{:S(2)}) collective-permute-start(bf16[512,256]{1,0:T(8,128)(2,1)} %get-tuple-element.38), channel_id=1, source_target_pairs={{0,2},{1,3},{2,0},{3,1},{4,6},{5,7},{6,4},{7,5},{8,10},{9,11},{10,... | collective-permute-start | bytes 786440 | tf_op jit(solution)/shard_map/ppermute | solution.py:264
  160.5 18.0 %copy-start.10 = (bf16[256,256]{1,0:T(8,128)(2,1)}, bf16[256,256]{1,0:T(8,128)(2,1)S(1)}, u32[]{:S(2)}) copy-start(bf16[256,256]{1,0:T(8,128)(2,1)S(1)} %collective-permute-done.11.rest_4_) | copy-start | bytes 393220
  160.5 19.1 %collective-permute-start.9 = (bf16[512,256]{1,0:T(8,128)(2,1)S(1)}, bf16[512,256]{1,0:T(8,128)(2,1)S(1)}, u32[]{:S(2)}, u32[]{:S(2)}) collective-permute-start(bf16[512,256]{1,0:T(8,128)(2,1)S(1)} %copy-done.18), channel_id=1, source_target_pairs={{0,3},{1,2},{2,1},{3,0},{4,7},{5,6},{6,5},{7,4},{8,11},{9,10},{10,... | collective-permute-start | bytes 786440 | tf_op jit(solution)/shard_map/ppermute | solution.py:264
  178.5 1.2 copy-start.12
  178.5 1.2 copy-start.13
  178.5 1.1 copy-start.6
  179.6 0.7 copy-start.7
  179.6 0.9 copy-start.3
  179.6 1.2 copy-start.1

commit v2 on v1

v2 whole, which is shorter than its diff:
```python
import functools
import math

import jax
import jax.numpy as jnp
import numpy as np
from jax import lax
from jax.experimental import pallas as pl
from jax.experimental.pallas import tpu as pltpu
from jax.sharding import PartitionSpec as P

ROWS = 2048
HEAD = 128
UNIT = 256
ORDER = (0, 4, 2, 6, 1, 3, 5, 7)
SCALE = HEAD**-0.5
SCALE2 = SCALE * math.log2(math.e)
NEG = -1e30
REMOTE = 5120
BLOCK = 512
VMEM = 58 * 1024 * 1024


def unit_level(unit):
    return 3 if unit == 0 else 2 if unit == 1 else 1 if unit < 4 else 0


def own_bias():
    table = np.zeros((8, ROWS), np.float32)
    for key_unit in range(8):
        for query_unit in range(8):
            shared = 1 + min(unit_level(key_unit), unit_level(query_unit))
            table[key_unit, query_unit * UNIT : (query_unit + 1) * UNIT] = math.log2(shared)
    return table


def far_bias():
    table = np.zeros((8, 1024), np.float32)
    for query_unit in range(4):
        lanes = slice(query_unit * UNIT, (query_unit + 1) * UNIT)
        level = unit_level(query_unit)
        table[0, lanes] = math.log2(min(3, level))
        table[1, lanes] = math.log2(min(2, level))
        if level >= 2:
            table[2, lanes] = math.log2(level - 1)
    table[3, 8:] = NEG
    return table


def dot_nt(left, right):
    return lax.dot_general(left, right, (((1,), (1,)), ((), ())), preferred_element_type=jnp.float32)


def dot_nn(left, right):
    return lax.dot_general(left, right, (((1,), (0,)), ((), ())), preferred_element_type=jnp.float32)


def dot_tn(left, right):
    return lax.dot_general(left, right, (((0,), (0,)), ((), ())), preferred_element_type=jnp.float32)


def call(kernel, outs, args, scratch=(), flops=0, nbytes=0, exps=0, any_inputs=(), smem_inputs=()):
    specs = [
        pl.BlockSpec(memory_space=pl.ANY if at in any_inputs else pltpu.SMEM if at in smem_inputs else pltpu.VMEM)
        for at in range(len(args))
    ]
    return pl.pallas_call(
        kernel,
        out_shape=[jax.ShapeDtypeStruct(shape, dtype) for shape, dtype in outs],
        in_specs=specs,
        out_specs=[pl.BlockSpec(memory_space=pltpu.VMEM)] * len(outs),
        scratch_shapes=list(scratch),
        compiler_params=pltpu.CompilerParams(vmem_limit_bytes=VMEM),
        cost_estimate=pl.CostEstimate(flops=flops, bytes_accessed=nbytes, transcendentals=exps),
    )(*args)


def prepare_kernel(q_ref, k_ref, v_ref, g_ref, qp_ref, kv_ref, gp_ref, s1_ref, s4_ref, s8_ref, whole_ref, wide):
    def sort_rows(source, target, lane):
        wide[...] = source[...].astype(jnp.float32)
        for unit, residue in enumerate(ORDER):
            for pair in range(16):
                parts = [
                    wide[pl.ds(8 * (2 * pair + half) + residue, 8, stride=256), :]
                    for half in range(2)
                ]
                rows = slice(unit * UNIT + 16 * pair, unit * UNIT + 16 * pair + 16)
                target[rows, lane : lane + HEAD] = jnp.concatenate(parts, 0).astype(jnp.bfloat16)

    sort_rows(k_ref, kv_ref, 0)
    sort_rows(v_ref, kv_ref, HEAD)
    first = kv_ref[:16].astype(jnp.float32)[:8]
    pair = jnp.concatenate([first, first], 0).astype(jnp.bfloat16)
    for at in range(128):
        whole_ref[16 * at : 16 * at + 16] = pair
    for at in range(8):
        s8_ref[at] = kv_ref[:256]
    for at in range(4):
        s4_ref[at] = kv_ref[256:512]
    s1_ref[...] = kv_ref[512:1024]
    sort_rows(q_ref, qp_ref, 0)
    sort_rows(g_ref, gp_ref, 0)


def add_bias(block, rows):
    if all(row is None for row in rows):
        return block
    parts = []
    for at, row in enumerate(rows):
        part = block[at * UNIT : (at + 1) * UNIT]
        parts.append(part if row is None else part + row)
    return jnp.concatenate(parts, 0)


def attend(query, keys, values, biases):
    scores = [add_bias(dot_nt(key, query) * SCALE2, bias) for key, bias in zip(keys, biases)]
    peak = functools.reduce(jnp.maximum, [jnp.max(block, 0, keepdims=True) for block in scores])
    probs = [jnp.exp2(block - peak) for block in scores]
    total = sum([jnp.sum(block, 0, keepdims=True) for block in probs])
    out = sum([value(block.astype(jnp.bfloat16)) for value, block in zip(values, probs)])
    return peak, total, out


def own_forward_kernel(q_ref, kv_ref, bias_ref, stat_ref, out_ref, vt_ref):
    stat_ref[...] = jnp.zeros_like(stat_ref)
    for unit in range(8):
        rows = slice(unit * UNIT, (unit + 1) * UNIT)
        vt_ref[:, rows] = kv_ref[rows, HEAD:].astype(jnp.float32).T.astype(jnp.bfloat16)
    for start in (0, 1024):
        lanes = slice(start, start + 1024)
        keys, values, biases = [], [], []
        for at in range(0, ROWS, BLOCK):
            rows = slice(at, at + BLOCK)
            keys.append(kv_ref[rows, :HEAD])
            values.append(lambda prob, rows=rows: dot_nn(vt_ref[:, rows], prob))
            unit = at // UNIT
            counted = start == 0 and at < 1024
            biases.append([bias_ref[unit + half : unit + half + 1, lanes] if counted else None for half in (0, 1)])
        peak, total, out = attend(q_ref[lanes, :], keys, values, biases)
        stat_ref[0:1, lanes] = peak
        stat_ref[1:2, lanes] = total
        out_ref[:, lanes] = out


def gather_far(me_ref, s1, s4, s8, whole, held, sem):
    at8, at4 = me_ref[0] % 8, me_ref[0] % 4
    copies = []

    def bring(source, row):
        copies.append(pltpu.make_async_copy(source, held.at[pl.ds(row, source.shape[0])], sem.at[len(copies)]))

    bring(s8.at[at8 ^ 1], 0)
    bring(s4.at[at4 ^ 1], 256)
    bring(s1, 512)
    for peer in (2, 3):
        bring(s8.at[at8 ^ peer], 1024 + 512 * (peer - 2))
        bring(s4.at[at4 ^ peer], 1280 + 512 * (peer - 2))
    for peer in (4, 5, 6, 7):
        bring(s8.at[at8 ^ peer], 1024 + 256 * peer)
    bring(whole, 3072)
    for copy in copies:
        copy.start()
    for copy in copies:
        copy.wait()


SETS = (
    (0, 1024, 1024, ((0, 1), (None, None))),
    (1024, 1024, 512, ((2, None), (2, None))),
    (2048, 1024, 256, ((None, None), (None, None))),
    (3072, 2048, 128, ((3, 3),) * 4),
)


def bias_rows(bias_ref, picks, lanes):
    return [None if pick is None else bias_ref[pick : pick + 1, lanes] for pick in picks]


def remote_forward_kernel(me_ref, q_ref, g_ref, bias_ref, stat_ref, out_ref, s1, s4, s8, whole, row_ref, held, sums, acc, sem):
    gather_far(me_ref, s1, s4, s8, whole, held, sem)
    row_ref[...] = jnp.zeros_like(row_ref)
    sums[...] = stat_ref[...]
    acc[...] = out_ref[...]
    for first, keys, count, picks in SETS:
        lanes = slice(0, count)
        blocks = [slice(first + at, first + at + BLOCK) for at in range(0, keys, BLOCK)]
        far_peak, far_total, far_out = attend(
            q_ref[lanes, :],
            [held[rows, :HEAD] for rows in blocks],
            [lambda prob, rows=rows: dot_tn(held[rows, HEAD:], prob) for rows in blocks],
            [bias_rows(bias_ref, pick, lanes) for pick in picks],
        )
        peak = sums[0:1, lanes]
        top = jnp.maximum(peak, far_peak)
        near, far = jnp.exp2(peak - top), jnp.exp2(far_peak - top)
        sums[0:1, lanes] = top
        sums[1:2, lanes] = near * sums[1:2, lanes] + far * far_total
        acc[:, lanes] = near * acc[:, lanes] + far * far_out
    for unit in range(8):
        lanes = slice(unit * UNIT, (unit + 1) * UNIT)
        total = sums[1:2, lanes]
        row_ref[0:1, lanes] = sums[0:1, lanes] + jnp.log2(total)
        grad = g_ref[lanes, :].astype(jnp.float32).T
        row_ref[1:2, lanes] = jnp.sum(grad * acc[:, lanes], axis=0, keepdims=True) / total


def backward_block(kv_block, q_ref, g_ref, row_ref, bias, count, dq_ref):
    key, value = kv_block[:, :HEAD], kv_block[:, HEAD:]
    lanes = slice(0, count)
    query, grad = q_ref[lanes, :], g_ref[lanes, :]
    scores = add_bias(dot_nt(key, query) * SCALE2, bias)
    weights = jnp.exp2(scores - row_ref[0:1, lanes])
    grad_probs = dot_nt(value, grad)
    grad_scores = (weights * (grad_probs - row_ref[1:2, lanes])).astype(jnp.bfloat16)
    grad_value = dot_nn(weights.astype(jnp.bfloat16), grad)
    grad_key = dot_nn(grad_scores, query)
    dq_ref[:, lanes] += dot_tn(key, grad_scores)
    return SCALE * grad_key, grad_value


def remote_backward_kernel(me_ref, q_ref, g_ref, bias_ref, row_ref, s1, s4, s8, whole, o1, o4, o8, owhole, dq_ref, held, sem):
    gather_far(me_ref, s1, s4, s8, whole, held, sem)
    at8, at4 = me_ref[0] % 8, me_ref[0] % 4
    dq_ref[...] = jnp.zeros_like(dq_ref)
    o8[at8] = jnp.zeros((UNIT, 256), jnp.bfloat16)
    o4[at4] = jnp.zeros((UNIT, 256), jnp.bfloat16)

    def block(first, picks, count):
        bias = bias_rows(bias_ref, picks, slice(0, count))
        rows = pl.ds(pl.multiple_of(first, BLOCK), BLOCK)
        both = backward_block(held[rows, :], q_ref, g_ref, row_ref, bias, count, dq_ref)
        return jnp.concatenate(both, 1).astype(jnp.bfloat16)

    def far(at, carry):
        owhole[pl.ds(pl.multiple_of(at * BLOCK, BLOCK), BLOCK), :] = block(3072 + at * BLOCK, (3, 3), 128)
        return carry

    lax.fori_loop(0, 4, far, 0)

    def third(at, carry):
        both = block(2048 + at * BLOCK, (None, None), 256)
        o8[at8 ^ (4 + 2 * at)] = both[:UNIT]
        o8[at8 ^ (5 + 2 * at)] = both[UNIT:]
        return carry

    lax.fori_loop(0, 2, third, 0)

    def second(at, carry):
        both = block(1024 + at * BLOCK, (2, None), 512)
        o8[at8 ^ (2 + at)] = both[:UNIT]
        o4[at4 ^ (2 + at)] = both[UNIT:]
        return carry

    lax.fori_loop(0, 2, second, 0)
    both = block(0, (0, 1), 1024)
    o8[at8 ^ 1] = both[:UNIT]
    o4[at4 ^ 1] = both[UNIT:]
    o1[...] = block(512, (None, None), 1024)


def own_backward_kernel(q_ref, g_ref, bias_ref, row_ref, kv_ref, far_ref, dq_ref, dkv_ref, acc_ref, tall_ref):
    acc_ref[:, :1024] = far_ref[...]
    acc_ref[:, 1024:] = jnp.zeros((HEAD, 1024), jnp.float32)

    def one(at, carry):
        rows = pl.ds(pl.multiple_of(at * BLOCK, BLOCK), BLOCK)
        bias = [bias_ref[pl.ds(2 * at + half, 1), :] for half in (0, 1)]
        grad_key, grad_value = backward_block(kv_ref[rows, :], q_ref, g_ref, row_ref, bias, ROWS, acc_ref)
        dkv_ref[rows, :HEAD] = grad_key
        dkv_ref[rows, HEAD:] = grad_value
        return carry

    lax.fori_loop(0, ROWS // BLOCK, one, 0)
    for unit in range(8):
        lanes = slice(unit * UNIT, (unit + 1) * UNIT)
        tall_ref[lanes, :] = acc_ref[:, lanes].T * SCALE
    restore_rows(lambda rows: tall_ref[rows, :], dq_ref)


def restore_rows(read, target):
    for unit, residue in enumerate(ORDER):
        for block in range(32):
            start = unit * UNIT + 8 * block
            target[pl.ds(8 * block + residue, 8, stride=256), :] = read(slice(start, start + 8))


def join_kernel(dkv_ref, s1, s4, s8, whole, dk_ref, dv_ref, sum_ref):
    first = dkv_ref[:256, :]
    for at in range(8):
        first = first + s8[at].astype(jnp.float32)
    sum_ref[:256, :] = first
    second = dkv_ref[256:512, :]
    for at in range(4):
        second = second + s4[at].astype(jnp.float32)
    sum_ref[256:512, :] = second
    sum_ref[512:1024, :] = dkv_ref[512:1024, :] + s1[...].astype(jnp.float32)
    sum_ref[1024:, :] = dkv_ref[1024:, :]

    def add(at, total):
        piece = whole[pl.ds(pl.multiple_of(at * 128, 128), 128), :].astype(jnp.float32)
        return total + jnp.sum(piece.reshape(16, 8, 256), 0)

    total = lax.fori_loop(0, 16, add, jnp.zeros((8, 256), jnp.float32))
    sum_ref[:8, :] += total
    restore_rows(lambda rows: sum_ref[rows, :HEAD], dk_ref)
    restore_rows(lambda rows: sum_ref[rows, HEAD:], dv_ref)


def exchange(s1, s4, s8, whole):
    count = lax.axis_size("seq")
    groups = [[list(range(low, low + size)) for low in range(0, count, size)] for size in (4, 8)]
    n1 = lax.ppermute(s1, "seq", [(at, at ^ 1) for at in range(count)])
    n4 = lax.all_to_all(s4, "seq", 0, 0, axis_index_groups=groups[0])
    n8 = lax.all_to_all(s8, "seq", 0, 0, axis_index_groups=groups[1])
    far = lax.all_to_all(whole.reshape(256, 8, 256), ("grp", "seq"), 0, 0).reshape(2048, 256)
    return n1, n4, n8, far


def on_device(queries, keys, values, cotangent):
    f32, bf16 = jnp.float32, jnp.bfloat16
    near_bias, other_bias = jnp.asarray(own_bias()), jnp.asarray(far_bias())
    me = lax.axis_index("seq").astype(jnp.int32).reshape(1)
    parts = [((512, 256), bf16), ((4, 256, 256), bf16), ((8, 256, 256), bf16), ((2048, 256), bf16)]
    q, kv, g, *sends = call(
        prepare_kernel,
        [((ROWS, HEAD), bf16), ((ROWS, 256), bf16), ((ROWS, HEAD), bf16)] + parts,
        (queries, keys, values, cotangent),
        [pltpu.VMEM((ROWS, HEAD), f32)],
        nbytes=5 << 20,
    )
    far = exchange(*sends)
    stat, out = call(
        own_forward_kernel,
        [((8, ROWS), f32), ((HEAD, ROWS), f32)],
        (q, kv, near_bias),
        [pltpu.VMEM((HEAD, ROWS), bf16)],
        flops=4 * HEAD * ROWS * ROWS,
        nbytes=3 << 20,
        exps=ROWS * ROWS,
    )
    (row,) = call(
        remote_forward_kernel,
        [((8, ROWS), f32)],
        (me, q, g, other_bias, stat, out, *far),
        [
            pltpu.VMEM((REMOTE, 256), bf16),
            pltpu.VMEM((8, ROWS), f32),
            pltpu.VMEM((HEAD, ROWS), f32),
            pltpu.SemaphoreType.DMA((12,)),
        ],
        flops=2 * HEAD * ROWS * ROWS,
        nbytes=6 << 20,
        exps=ROWS * ROWS // 2,
        any_inputs=range(6, 10),
        smem_inputs=(0,),
    )
    *sends, far_dq = call(
        remote_backward_kernel,
        parts + [((HEAD, 1024), f32)],
        (me, q, g, other_bias, row, *far),
        [pltpu.VMEM((REMOTE, 256), bf16), pltpu.SemaphoreType.DMA((12,))],
        flops=5 * HEAD * ROWS * ROWS,
        nbytes=8 << 20,
        exps=ROWS * ROWS // 2,
        any_inputs=range(5, 9),
        smem_inputs=(0,),
    )
    back = exchange(*sends)
    dq, dkv = call(
        own_backward_kernel,
        [((ROWS, HEAD), f32), ((ROWS, 256), f32)],
        (q, g, near_bias, row, kv, far_dq),
        [pltpu.VMEM((HEAD, ROWS), f32), pltpu.VMEM((ROWS, HEAD), f32)],
        flops=10 * HEAD * ROWS * ROWS,
        nbytes=8 << 20,
        exps=ROWS * ROWS,
    )
    dk, dv = call(
        join_kernel,
        [((ROWS, HEAD), f32)] * 2,
        (dkv, *back),
        [pltpu.VMEM((ROWS, 256), f32)],
        nbytes=8 << 20,
    )
    return dq, dk, dv


def solution(mesh):
    spec = P(("grp", "seq"), None)
    return jax.shard_map(
        on_device, mesh=mesh, in_specs=(spec,) * 4, out_specs=(spec,) * 3, check_vma=False
    )
```

time: 187 us -> 182 us (0.973)
  blocking collectives: 0 us -> 58.6 us
  Pallas kernels: 87.7 us -> 52 us
  starting transfers between devices: 46.9 us -> 31.5 us
  waiting for transfers between devices: 46.6 us -> 36.1 us
  local copies, waits for them, and re-layouts: 4.34 us -> 1.95 us
    all_to_all x0 -> x4, blocking collectives: none -> 58.6 us  [the longest x2 34.7 us: exchange(): n8 = lax.all_to_all(s8, 'seq', 0, 0, axis_index_groups=groups[1])]
    ppermute x14 -> x2, waiting for transfers between devices: 46.6 us -> 0.98 us  [exchange(): n1 = lax.ppermute(s1, 'seq', [(at, at ^ 1) for at in range(count)])]
    pallas_call x6, Pallas kernels: 87.7 us -> 52 us  [call(): pl.pallas_call(kernel, out_shape=[jax.ShapeDtypeStruct(shape, dtype) for...]
    all_to_all x2, waiting for transfers between devices: 0.01 us -> 35.1 us  [exchange(): lax.all_to_all(whole.reshape(256, 8, 256), ('grp', 'seq'), 0, 0)]
    ppermute x14 -> x2, starting transfers between devices: 19.6 us -> 3.13 us  [exchange(): n1 = lax.ppermute(s1, 'seq', [(at, at ^ 1) for at in range(count)])]
  transfers between devices with their start and end apart: 16 -> 4, of which waited for: 5 -> 3; matrix products, arithmetic and copies ran while one was open for 0% -> 0% of each run, Pallas kernels for 24% -> 13%
where the time goes in v2:
time: 182 us; the launch traced here: 181 us
  blocking collectives  58.6 us (32%)
  Pallas kernels  52 us (29%)
  waiting for transfers between devices  36.1 us (20%)
  starting transfers between devices  31.5 us (17%)
  local copies, waits for them, and re-layouts  1.95 us (1%)
    pallas_call x6, Pallas kernels, call(): pl.pallas_call(kernel, out_shape=[jax.ShapeDtypeStruct(shape, dtype) for...  52 us
    all_to_all x2, waiting for transfers between devices, exchange(): lax.all_to_all(whole.reshape(256, 8, 256), ('grp', 'seq'), 0, 0)  35.1 us
    all_to_all x2, blocking collectives, exchange(): n8 = lax.all_to_all(s8, 'seq', 0, 0, axis_index_groups=groups[1])  34.7 us
    all_to_all x2, starting transfers between devices, exchange(): lax.all_to_all(whole.reshape(256, 8, 256), ('grp', 'seq'), 0, 0)  28.4 us
    all_to_all x2, blocking collectives, exchange(): n4 = lax.all_to_all(s4, 'seq', 0, 0, axis_index_groups=groups[0])  23.9 us
  transfers between devices with their start and end apart: 4, of which 3 were waited for; matrix products, arithmetic and copies ran while one was open for 0% of the time, Pallas kernels for 13%

profile of v2, /device:TPU:1, one launch (start us, length us, event | category | flops | bytes accessed | tf_op | source)
XLA Modules:
  0.0 180.9 jit_solution(4378119965514923048)
XLA Ops:
  0.6 5.1 %shard_map.85 = (bf16[2048,128]{1,0:T(8,128)(2,1)}, bf16[2048,256]{1,0:T(8,128)(2,1)}, bf16[2048,128]{1,0:T(8,128)(2,1)}, bf16[512,256]{1,0:T(8,128)(2,1)}, bf16...) custom-call(bf16[2048,128]{1,0:T(8,128)(2,1)} %q_ref.1, ...), custom_call_target="tpu_custom_call" | custom-call | bytes 5242880 | tf_op jit(solution)/shard_map/pallas_call | solution.py:67
  5.8 12.1 %all_to_all.30.s4 = bf16[4,256,256]{2,1,0:T(8,128)(2,1)} all-to-all(bf16[4,256,256]{2,1,0:T(8,128)(2,1)} %get-tuple-element.27), channel_id=1, replica_groups={{0,1,2,3},{4,5,6,7},{8,9,10,11},{12,13,14,15},{16,17,18,19},{20,21,22,2..., dimensions={0} | all-to-all | bytes 1048576 | tf_op jit(solution)/shard_map/all_to_all | solution.py:313
  17.8 0.0 copy-start.5
  17.8 18.1 %all_to_all.31.s8 = bf16[8,256,256]{2,1,0:T(8,128)(2,1)} all-to-all(bf16[8,256,256]{2,1,0:T(8,128)(2,1)} %get-tuple-element.28), channel_id=1, replica_groups={{0,1,2,3,4,5,6,7},{8,9,10,11,12,13,14,15},{16,17,18,19,20,21,22,23},{24..., dimensions={0} | all-to-all | bytes 2097152 | tf_op jit(solution)/shard_map/all_to_all | solution.py:314
  36.0 16.3 %all-to-all-start.2 = ((bf16[256,8,256]{2,1,0:T(8,128)(2,1)}), bf16[256,8,256]{2,1,0:T(8,128)(2,1)S(1)}, u32[]{:S(2)}, u32[]{:S(2)}) async-start(bf16[256,8,256]{2,1,0:T(8,128)(2,1)} %bitcast.1), calls=%async_computation.2 | async-start | bytes 2097152 | tf_op jit(solution)/shard_map/all_to_all | solution.py:315
  52.3 0.0 copy-done.5
  52.3 1.7 collective-permute-start
  53.9 8.7 %shard_map.86 = (f32[8,2048]{1,0:T(8,128)}, f32[128,2048]{1,0:T(8,128)}) custom-call(bf16[2048,128]{1,0:T(8,128)(2,1)} %get-tuple-element.21.q_ref, bf16[2048,256]{1,0:T(8,128)(2,1)} %get-tuple-element.23.kv_ref, f32[8,2048]{1,0:T(8,128)} %constant.8.clone.bias_ref), custom_call_target="tpu_custom_call" | custom-call | flops 2147483648 | bytes 3145728 | tf_op jit(solution)/shard_map/pallas_call | solution.py:67
  62.7 1.0 collective-permute-done.s1
  63.7 0.0 copy-start.3
  63.7 19.7 %all-to-all-done.2 = bf16[256,8,256]{2,1,0:T(8,128)(2,1)S(1)} async-done(((bf16[256,8,256]{2,1,0:T(8,128)(2,1)}), bf16[256,8,256]{2,1,0:T(8,128)(2,1)S(1)}, u32[]{:S(2)}, u32[]{:S(2)}) %all-to-all-start.2) | async-done | bytes 1048608 | tf_op jit(solution)/shard_map/all_to_all | solution.py:315
  83.4 0.0 copy-start.1
  83.4 0.0 copy-done.3
  83.4 1.0 copy-done.1
  84.4 7.7 %shard_map.87.row_ref = f32[8,2048]{1,0:T(8,128)} custom-call(s32[1]{0:T(128)} %bitcast.me_ref, bf16[2048,128]{1,0:T(8,128)(2,1)} %get-tuple-element.21.q_ref, bf16[2048,128]{1,0:T(8,128)(2,1)} %get-tuple-element.22.g_ref, f32[8,1024]{1,0:T(8,128)} %constant.9.clone.bias_ref, f32[8,2048]{1,0:T(8,128)} %get-tuple-element.24.stat_ref, ...), custom_call_target="tpu_custom_call" | custom-call | flops 1073741824 | bytes 6291456 | tf_op jit(solution)/shard_map/pallas_call | solution.py:67
  92.1 11.0 %shard_map.88 = (bf16[512,256]{1,0:T(8,128)(2,1)}, bf16[4,256,256]{2,1,0:T(8,128)(2,1)}, bf16[8,256,256]{2,1,0:T(8,128)(2,1)}, bf16[2048,256]{1,0:T(8,128)(2,1)}, f32[128,1024]{1,0:T(8,128)}) custom-call(s32[1]{0:T(128)} %bitcast.me_ref, bf16[2048,128]{1,0:T(8,128)(2,1)} %get-tuple-element.21.q_ref, bf16[2048,128]{1,0:T(8,128)(2,1)} %get-tuple-element.22.g_ref, ...), custom_call_target="tpu_custom_call" | custom-call | flops 2684354560 | bytes 8388608 | tf_op jit(solution)/shard_map/pallas_call | solution.py:67
  103.0 11.8 %all_to_all.32.s4 = bf16[4,256,256]{2,1,0:T(8,128)(2,1)} all-to-all(bf16[4,256,256]{2,1,0:T(8,128)(2,1)} %get-tuple-element.34), channel_id=1, replica_groups={{0,1,2,3},{4,5,6,7},{8,9,10,11},{12,13,14,15},{16,17,18,19},{20,21,22,2..., dimensions={0} | all-to-all | bytes 1048576 | tf_op jit(solution)/shard_map/all_to_all | solution.py:313
  114.9 0.0 copy-start.4
  114.9 16.6 %all_to_all.33.s8 = bf16[8,256,256]{2,1,0:T(8,128)(2,1)} all-to-all(bf16[8,256,256]{2,1,0:T(8,128)(2,1)} %get-tuple-element.35), channel_id=1, replica_groups={{0,1,2,3,4,5,6,7},{8,9,10,11,12,13,14,15},{16,17,18,19,20,21,22,23},{24..., dimensions={0} | all-to-all | bytes 2097152 | tf_op jit(solution)/shard_map/all_to_all | solution.py:314
  131.4 12.1 %all-to-all-start.5 = ((bf16[256,8,256]{2,1,0:T(8,128)(2,1)}), bf16[256,8,256]{2,1,0:T(8,128)(2,1)S(1)}, u32[]{:S(2)}, u32[]{:S(2)}) async-start(bf16[256,8,256]{2,1,0:T(8,128)(2,1)} %bitcast.3), calls=%async_computation.5 | async-start | bytes 2097152 | tf_op jit(solution)/shard_map/all_to_all | solution.py:315
  143.5 0.0 copy-done.4
  143.5 1.5 collective-permute-start.1
  145.0 14.2 %shard_map.89 = (f32[2048,128]{1,0:T(8,128)}, f32[2048,256]{1,0:T(8,128)}) custom-call(bf16[2048,128]{1,0:T(8,128)(2,1)} %get-tuple-element.21.q_ref, bf16[2048,128]{1,0:T(8,128)(2,1)} %get-tuple-element.22.g_ref, f32[8,2048]{1,0:T(8,128)} %constant.8.clone.bias_ref, f32[8,2048]{1,0:T(8,128)} %shard_map.87.row_ref, ...), custom_call_target="tpu_custom_call" | custom-call | flops 5368709120 | bytes 8388608 | tf_op jit(solution)/shard_map/pallas_call | solution.py:67
  159.2 0.0 collective-permute-done.1.s1
  159.2 0.0 copy-start.2
  159.2 15.4 %all-to-all-done.5 = bf16[256,8,256]{2,1,0:T(8,128)(2,1)S(1)} async-done(((bf16[256,8,256]{2,1,0:T(8,128)(2,1)}), bf16[256,8,256]{2,1,0:T(8,128)(2,1)S(1)}, u32[]{:S(2)}, u32[]{:S(2)}) %all-to-all-start.5) | async-done | bytes 1048608 | tf_op jit(solution)/shard_map/all_to_all | solution.py:315
  174.6 0.0 copy-start
  174.6 0.0 copy-done.2
  174.6 1.0 copy-done
  175.6 5.3 %shard_map.90 = (f32[2048,128]{1,0:T(8,128)}, f32[2048,128]{1,0:T(8,128)}) custom-call(f32[2048,256]{1,0:T(8,128)} %get-tuple-element.32.dkv_ref, bf16[512,256]{1,0:T(8,128)(2,1)} %copy-done.2, bf16[4,256,256]{2,1,0:T(8,128)(2,1)} %all_to_all.32.s4, bf16[8,256,256]{2,1,0:T(8,128)(2,1)} %all_to_all.33.s8, bf16[2048,256]{1,0:T(8,128)(2,1)} %bitcast.5), custom_call_target="tpu_custom_call" | custom-call | bytes 8388608 | tf_op jit(solution)/shard_map/pallas_call | solution.py:67
Async XLA Ops:
  17.8 34.4 %copy-start.5 = (bf16[512,256]{1,0:T(8,128)(2,1)S(1)}, bf16[512,256]{1,0:T(8,128)(2,1)}, u32[]{:S(2)}) copy-start(bf16[512,256]{1,0:T(8,128)(2,1)} %get-tuple-element.26) | copy-start | bytes 786436
  36.0 47.4 %all-to-all-start.2 = ((bf16[256,8,256]{2,1,0:T(8,128)(2,1)}), bf16[256,8,256]{2,1,0:T(8,128)(2,1)S(1)}, u32[]{:S(2)}, u32[]{:S(2)}) async-start(bf16[256,8,256]{2,1,0:T(8,128)(2,1)} %bitcast.1), calls=%async_computation.2 | async-start | bytes 2097152 | tf_op jit(solution)/shard_map/all_to_all | solution.py:315
  52.3 11.4 %collective-permute-start = (bf16[512,256]{1,0:T(8,128)(2,1)S(1)}, bf16[512,256]{1,0:T(8,128)(2,1)S(1)}, u32[]{:S(2)}, u32[]{:S(2)}) collective-permute-start(bf16[512,256]{1,0:T(8,128)(2,1)S(1)} %copy-done.5), channel_id=1, source_target_pairs={{0,1},{1,0},{2,3},{3,2},{4,5},{5,4},{6,7},{7,6},{8,9},{9,8},{10,11... | collective-permute-start | bytes 786440 | tf_op jit(solution)/shard_map/ppermute | solution.py:312
  63.7 19.7 %copy-start.3 = (bf16[512,256]{1,0:T(8,128)(2,1)}, bf16[512,256]{1,0:T(8,128)(2,1)S(1)}, u32[]{:S(2)}) copy-start(bf16[512,256]{1,0:T(8,128)(2,1)S(1)} %collective-permute-done.s1) | copy-start | bytes 786436
  83.4 1.0 copy-start.1
  114.9 28.6 %copy-start.4 = (bf16[512,256]{1,0:T(8,128)(2,1)S(1)}, bf16[512,256]{1,0:T(8,128)(2,1)}, u32[]{:S(2)}) copy-start(bf16[512,256]{1,0:T(8,128)(2,1)} %get-tuple-element.33) | copy-start | bytes 786436
  131.4 43.2 %all-to-all-start.5 = ((bf16[256,8,256]{2,1,0:T(8,128)(2,1)}), bf16[256,8,256]{2,1,0:T(8,128)(2,1)S(1)}, u32[]{:S(2)}, u32[]{:S(2)}) async-start(bf16[256,8,256]{2,1,0:T(8,128)(2,1)} %bitcast.3), calls=%async_computation.5 | async-start | bytes 2097152 | tf_op jit(solution)/shard_map/all_to_all | solution.py:315
  143.5 15.7 %collective-permute-start.1 = (bf16[512,256]{1,0:T(8,128)(2,1)S(1)}, bf16[512,256]{1,0:T(8,128)(2,1)S(1)}, u32[]{:S(2)}, u32[]{:S(2)}) collective-permute-start(bf16[512,256]{1,0:T(8,128)(2,1)S(1)} %copy-done.4), channel_id=1, source_target_pairs={{0,1},{1,0},{2,3},{3,2},{4,5},{5,4},{6,7},{7,6},{8,9},{9,8},{10,11... | collective-permute-start | bytes 786440 | tf_op jit(solution)/shard_map/ppermute | solution.py:312
  159.2 15.4 %copy-start.2 = (bf16[512,256]{1,0:T(8,128)(2,1)}, bf16[512,256]{1,0:T(8,128)(2,1)S(1)}, u32[]{:S(2)}) copy-start(bf16[512,256]{1,0:T(8,128)(2,1)S(1)} %collective-permute-done.1.s1) | copy-start | bytes 786436
  174.6 1.0 copy-start

commit v3 on v2

v3 whole, which is shorter than its diff:
```python
import functools
import math

import jax
import jax.numpy as jnp
import numpy as np
from jax import lax
from jax.experimental import pallas as pl
from jax.experimental.pallas import tpu as pltpu
from jax.sharding import PartitionSpec as P

ROWS = 2048
HEAD = 128
UNIT = 256
ORDER = (0, 4, 2, 6, 1, 3, 5, 7)
SCALE = HEAD**-0.5
SCALE2 = SCALE * math.log2(math.e)
NEG = -1e30
BLOCK = 512


def unit_level(unit):
    return 3 if unit == 0 else 2 if unit == 1 else 1 if unit < 4 else 0


def own_bias():
    table = np.zeros((8, ROWS), np.float32)
    for key_unit in range(8):
        for query_unit in range(8):
            shared = 1 + min(unit_level(key_unit), unit_level(query_unit))
            table[key_unit, query_unit * UNIT : (query_unit + 1) * UNIT] = math.log2(shared)
    return table


def far_bias():
    table = np.zeros((8, 1024), np.float32)
    for query_unit in range(4):
        lanes = slice(query_unit * UNIT, (query_unit + 1) * UNIT)
        level = unit_level(query_unit)
        table[0, lanes] = math.log2(min(3, level))
        table[1, lanes] = math.log2(min(2, level))
        if level >= 2:
            table[2, lanes] = math.log2(level - 1)
    table[3, 8:] = NEG
    return table


def dot_nt(left, right):
    return lax.dot_general(left, right, (((1,), (1,)), ((), ())), preferred_element_type=jnp.float32)


def dot_nn(left, right):
    return lax.dot_general(left, right, (((1,), (0,)), ((), ())), preferred_element_type=jnp.float32)


def dot_tn(left, right):
    return lax.dot_general(left, right, (((0,), (0,)), ((), ())), preferred_element_type=jnp.float32)


def call(kernel, outs, args, scratch=(), flops=0, nbytes=0, exps=0, vmem=24):
    specs = [pl.BlockSpec(memory_space=pltpu.VMEM)] * len(args)
    return pl.pallas_call(
        kernel,
        out_shape=[jax.ShapeDtypeStruct(shape, dtype) for shape, dtype in outs],
        in_specs=specs,
        out_specs=[pl.BlockSpec(memory_space=pltpu.VMEM)] * len(outs),
        scratch_shapes=list(scratch),
        compiler_params=pltpu.CompilerParams(vmem_limit_bytes=vmem << 20),
        cost_estimate=pl.CostEstimate(flops=flops, bytes_accessed=nbytes, transcendentals=exps),
    )(*args)


def sort_rows(source, target, lane, wide):
    wide[...] = source[...].astype(jnp.float32)
    for unit, residue in enumerate(ORDER):
        for pair in range(16):
            parts = [
                wide[pl.ds(8 * (2 * pair + half) + residue, 8, stride=256), :] for half in range(2)
            ]
            rows = slice(unit * UNIT + 16 * pair, unit * UNIT + 16 * pair + 16)
            target[rows, lane : lane + HEAD] = jnp.concatenate(parts, 0).astype(jnp.bfloat16)


def prepare_keys_kernel(k_ref, v_ref, kv_ref, s1_ref, s2_ref, wide):
    sort_rows(k_ref, kv_ref, 0, wide)
    sort_rows(v_ref, kv_ref, HEAD, wide)
    s1_ref[...] = kv_ref[:1024]
    s2_ref[...] = kv_ref[:512]


def prepare_queries_kernel(q_ref, g_ref, s2_ref, qp_ref, gp_ref, whole_ref, wide):
    first = s2_ref[:16].astype(jnp.float32)[:8]
    pair = jnp.concatenate([first, first], 0).astype(jnp.bfloat16)
    for at in range(128):
        whole_ref[16 * at : 16 * at + 16] = pair
    sort_rows(q_ref, qp_ref, 0, wide)
    sort_rows(g_ref, gp_ref, 0, wide)


def add_bias(block, rows):
    if all(row is None for row in rows):
        return block
    parts = []
    for at, row in enumerate(rows):
        part = block[at * UNIT : (at + 1) * UNIT]
        parts.append(part if row is None else part + row)
    return jnp.concatenate(parts, 0)


def attend(query, keys, values, biases):
    scores = [add_bias(dot_nt(key, query) * SCALE2, bias) for key, bias in zip(keys, biases)]
    peak = functools.reduce(jnp.maximum, [jnp.max(block, 0, keepdims=True) for block in scores])
    probs = [jnp.exp2(block - peak) for block in scores]
    total = sum([jnp.sum(block, 0, keepdims=True) for block in probs])
    out = sum([value(block.astype(jnp.bfloat16)) for value, block in zip(values, probs)])
    return peak, total, out


def own_forward_kernel(q_ref, kv_ref, bias_ref, stat_ref, out_ref, vt_ref):
    stat_ref[...] = jnp.zeros_like(stat_ref)
    for unit in range(8):
        rows = slice(unit * UNIT, (unit + 1) * UNIT)
        vt_ref[:, rows] = kv_ref[rows, HEAD:].astype(jnp.float32).T.astype(jnp.bfloat16)
    for start in (0, 1024):
        lanes = slice(start, start + 1024)
        keys, values, biases = [], [], []
        for at in range(0, ROWS, BLOCK):
            rows = slice(at, at + BLOCK)
            keys.append(kv_ref[rows, :HEAD])
            values.append(lambda prob, rows=rows: dot_nn(vt_ref[:, rows], prob))
            unit = at // UNIT
            counted = start == 0 and at < 1024
            biases.append([bias_ref[unit + half : unit + half + 1, lanes] if counted else None for half in (0, 1)])
        peak, total, out = attend(q_ref[lanes, :], keys, values, biases)
        stat_ref[0:1, lanes] = peak
        stat_ref[1:2, lanes] = total
        out_ref[:, lanes] = out


def bias_rows(bias_ref, picks, count):
    return [None if pick is None else bias_ref[pick : pick + 1, :count] for pick in picks]


PARTNER, PARTNER_REST, SECOND, THIRD, WHOLE = (0, 1), (None, None), (2, None), (None, None), (3, 3)


def attend_far(q_ref, bias_ref, blocks, count, sums, acc):
    lanes = slice(0, count)
    far_peak, far_total, far_out = attend(
        q_ref[lanes, :],
        [ref[first : first + BLOCK, :HEAD] for ref, first, _ in blocks],
        [
            lambda prob, ref=ref, first=first: dot_tn(ref[first : first + BLOCK, HEAD:], prob)
            for ref, first, _ in blocks
        ],
        [bias_rows(bias_ref, picks, count) for _, _, picks in blocks],
    )
    peak = sums[0:1, lanes]
    top = jnp.maximum(peak, far_peak)
    near, far = jnp.exp2(peak - top), jnp.exp2(far_peak - top)
    sums[0:1, lanes] = top
    sums[1:2, lanes] = near * sums[1:2, lanes] + far * far_total
    acc[:, lanes] = near * acc[:, lanes] + far * far_out


def middle_forward_kernel(q_ref, bias_ref, stat_ref, out_ref, r1, r2, r3, sums, acc):
    sums[...] = stat_ref[...]
    acc[...] = out_ref[...]
    attend_far(q_ref, bias_ref, [(r1, 0, PARTNER), (r1, BLOCK, PARTNER_REST)], 1024, sums, acc)
    attend_far(q_ref, bias_ref, [(r2, 0, SECOND), (r3, 0, SECOND)], 512, sums, acc)


def last_forward_kernel(q_ref, g_ref, bias_ref, stat_ref, out_ref, r4, r6, whole, row_ref, sums, acc):
    row_ref[...] = jnp.zeros_like(row_ref)
    sums[...] = stat_ref[:, :256]
    acc[...] = out_ref[:, :256]
    attend_far(q_ref, bias_ref, [(r4, 0, THIRD), (r6, 0, THIRD)], 256, sums, acc)
    attend_far(q_ref, bias_ref, [(whole, at, WHOLE) for at in range(0, ROWS, BLOCK)], 128, sums, acc)
    for unit in range(8):
        lanes = slice(unit * UNIT, (unit + 1) * UNIT)
        peak, total = (sums if unit == 0 else stat_ref)[0:1, lanes], (sums if unit == 0 else stat_ref)[1:2, lanes]
        out = (acc if unit == 0 else out_ref)[:, lanes]
        row_ref[0:1, lanes] = peak + jnp.log2(total)
        grad = g_ref[lanes, :].astype(jnp.float32).T
        row_ref[1:2, lanes] = jnp.sum(grad * out, axis=0, keepdims=True) / total


def backward_block(kv_block, q_ref, g_ref, row_ref, bias, count, dq_ref):
    key, value = kv_block[:, :HEAD], kv_block[:, HEAD:]
    lanes = slice(0, count)
    query, grad = q_ref[lanes, :], g_ref[lanes, :]
    scores = add_bias(dot_nt(key, query) * SCALE2, bias)
    weights = jnp.exp2(scores - row_ref[0:1, lanes])
    grad_probs = dot_nt(value, grad)
    grad_scores = (weights * (grad_probs - row_ref[1:2, lanes])).astype(jnp.bfloat16)
    grad_value = dot_nn(weights.astype(jnp.bfloat16), grad)
    grad_key = dot_nn(grad_scores, query)
    dq_ref[:, lanes] += dot_tn(key, grad_scores)
    return SCALE * grad_key, grad_value


def backward_far(refs, source, first, picks, count, dq_ref):
    q_ref, g_ref, bias_ref, row_ref = refs
    bias = bias_rows(bias_ref, picks, count)
    both = backward_block(source[first : first + BLOCK, :], q_ref, g_ref, row_ref, bias, count, dq_ref)
    return jnp.concatenate(both, 1)


def third_backward_kernel(q_ref, g_ref, bias_ref, row_ref, r4, r6, o4, o6, dq_ref):
    refs = (q_ref, g_ref, bias_ref, row_ref)
    dq_ref[...] = jnp.zeros_like(dq_ref)
    for source, target in ((r4, o4), (r6, o6)):
        target[...] = backward_far(refs, source, 0, THIRD, 256, dq_ref).astype(jnp.bfloat16)


def second_backward_kernel(q_ref, g_ref, bias_ref, row_ref, r2, r3, o2, o3, dq_ref):
    refs = (q_ref, g_ref, bias_ref, row_ref)
    dq_ref[...] = jnp.zeros_like(dq_ref)
    for source, target in ((r2, o2), (r3, o3)):
        target[...] = backward_far(refs, source, 0, SECOND, 512, dq_ref).astype(jnp.bfloat16)


def first_backward_kernel(q_ref, g_ref, bias_ref, row_ref, r1, o1, dq_ref):
    refs = (q_ref, g_ref, bias_ref, row_ref)
    dq_ref[...] = jnp.zeros_like(dq_ref)
    o1[:BLOCK, :] = backward_far(refs, r1, 0, PARTNER, 1024, dq_ref).astype(jnp.bfloat16)
    o1[BLOCK:, :] = backward_far(refs, r1, BLOCK, PARTNER_REST, 1024, dq_ref).astype(jnp.bfloat16)


def relay_kernel(o1, b4, b6, out_ref):
    first = [ref[rows, :].astype(jnp.float32) for ref, rows in ((o1, slice(0, 256)), (b4, slice(256, 512)), (b6, slice(256, 512)))]
    out_ref[:256, :] = sum(first).astype(jnp.bfloat16)
    out_ref[256:, :] = o1[256:, :]


def whole_backward_kernel(q_ref, g_ref, bias_ref, row_ref, whole, dq1, dq2, dq3, out_ref, dq_ref):
    refs = (q_ref, g_ref, bias_ref, row_ref)
    dq_ref[...] = dq1[...]
    dq_ref[:, :512] += dq2[...]
    dq_ref[:, :256] += dq3[...]
    for first in range(0, ROWS, BLOCK):
        both = backward_far(refs, whole, first, WHOLE, 128, dq_ref)
        out_ref[first : first + BLOCK, :] = both.astype(jnp.bfloat16)


def own_backward_kernel(q_ref, g_ref, bias_ref, row_ref, kv_ref, far_ref, dq_ref, dkv_ref, acc_ref, tall_ref):
    acc_ref[:, :1024] = far_ref[...]
    acc_ref[:, 1024:] = jnp.zeros((HEAD, 1024), jnp.float32)

    def one(at, carry):
        rows = pl.ds(pl.multiple_of(at * BLOCK, BLOCK), BLOCK)
        bias = [bias_ref[pl.ds(2 * at + half, 1), :] for half in (0, 1)]
        grad_key, grad_value = backward_block(kv_ref[rows, :], q_ref, g_ref, row_ref, bias, ROWS, acc_ref)
        dkv_ref[rows, :HEAD] = grad_key
        dkv_ref[rows, HEAD:] = grad_value
        return carry

    lax.fori_loop(0, ROWS // BLOCK, one, 0)
    for unit in range(8):
        lanes = slice(unit * UNIT, (unit + 1) * UNIT)
        tall_ref[lanes, :] = acc_ref[:, lanes].T * SCALE
    restore_rows(lambda rows: tall_ref[rows, :], dq_ref)


def restore_rows(read, target):
    for unit, residue in enumerate(ORDER):
        for block in range(32):
            start = unit * UNIT + 8 * block
            target[pl.ds(8 * block + residue, 8, stride=256), :] = read(slice(start, start + 8))


def join_kernel(dkv_ref, b1, b2, b3, b4, b6, whole, dk_ref, dv_ref, sum_ref):
    def wide(ref, rows):
        return ref[rows, :].astype(jnp.float32)

    top, mid, low = slice(0, 256), slice(256, 512), slice(512, 1024)
    near = wide(b1, top) + wide(b2, top) + wide(b3, top)
    sum_ref[top, :] = dkv_ref[top, :] + near + wide(b4, top) + wide(b6, top)
    sum_ref[mid, :] = dkv_ref[mid, :] + wide(b1, mid) + wide(b2, mid) + wide(b3, mid)
    sum_ref[low, :] = dkv_ref[low, :] + wide(b1, low)
    sum_ref[1024:, :] = dkv_ref[1024:, :]

    def add(at, total):
        piece = wide(whole, pl.ds(pl.multiple_of(at * 128, 128), 128))
        return total + jnp.sum(piece.reshape(16, 8, 256), 0)

    total = lax.fori_loop(0, 16, add, jnp.zeros((8, 256), jnp.float32))
    sum_ref[:8, :] += total
    restore_rows(lambda rows: sum_ref[rows, :HEAD], dk_ref)
    restore_rows(lambda rows: sum_ref[rows, HEAD:], dv_ref)


def swap(block, mask):
    return lax.ppermute(block, "seq", [(at, at ^ mask) for at in range(lax.axis_size("seq"))])


def swap_whole(block):
    return lax.all_to_all(block.reshape(256, 8, 256), ("grp", "seq"), 0, 0).reshape(ROWS, 256)


def on_device(queries, keys, values, cotangent):
    f32, bf16 = jnp.float32, jnp.bfloat16
    near_bias, other_bias = jnp.asarray(own_bias()), jnp.asarray(far_bias())

    def both(*rows):
        return [((count, 256), bf16) for count in rows]

    def cost(pairs, products):
        return dict(flops=2 * HEAD * products * pairs, exps=pairs, nbytes=4 << 20)

    kv, s1, s2 = call(
        prepare_keys_kernel, both(ROWS, 1024, 512), (keys, values), [pltpu.VMEM((ROWS, HEAD), f32)], nbytes=8 << 20, vmem=12
    )
    r1, r2, r3 = swap(s1, 1), swap(s2, 2), swap(s2, 3)
    q, g, whole = call(
        prepare_queries_kernel,
        [((ROWS, HEAD), bf16), ((ROWS, HEAD), bf16), *both(ROWS)],
        (queries, cotangent, s2),
        [pltpu.VMEM((ROWS, HEAD), f32)],
        nbytes=8 << 20,
        vmem=12,
    )
    stat, out = call(
        own_forward_kernel,
        [((8, ROWS), f32), ((HEAD, ROWS), f32)],
        (q, kv, near_bias),
        [pltpu.VMEM((HEAD, ROWS), bf16)],
        vmem=28,
        **cost(ROWS * ROWS, 2),
    )
    pair = jnp.concatenate([s2[:256], r1[:256]], 0)
    r1, r2, r3, stat, pair, whole = lax.optimization_barrier((r1, r2, r3, stat, pair, whole))
    r4, r6 = swap(pair, 4), swap(pair, 6)
    whole = swap_whole(whole)
    stat, out = call(
        middle_forward_kernel,
        [((8, ROWS), f32), ((HEAD, ROWS), f32)],
        (q, other_bias, stat, out, r1, r2, r3),
        vmem=20,
        **cost(1536 * 1024, 2),
    )
    (row,) = call(
        last_forward_kernel,
        [((8, ROWS), f32)],
        (q, g, other_bias, stat, out, r4, r6, whole),
        [pltpu.VMEM((8, 256), f32), pltpu.VMEM((HEAD, 256), f32)],
        vmem=16,
        **cost(512 * 1024, 2),
    )
    rows = (q, g, other_bias, row)
    o4, o6, dq3 = call(
        third_backward_kernel, [*both(512, 512), ((HEAD, 256), f32)], (*rows, r4, r6), vmem=12, **cost(256 * 1024, 5)
    )
    b4, b6 = swap(o4, 4), swap(o6, 6)
    o2, o3, dq2 = call(
        second_backward_kernel, [*both(512, 512), ((HEAD, 512), f32)], (*rows, r2, r3), vmem=12, **cost(512 * 1024, 5)
    )
    b2, b3 = swap(o2, 2), swap(o3, 3)
    o1, dq1 = call(
        first_backward_kernel, [*both(1024), ((HEAD, 1024), f32)], (*rows, r1), vmem=16, **cost(1024 * 1024, 5)
    )
    (o1,) = call(relay_kernel, both(1024), (o1, b4, b6), vmem=8, nbytes=1 << 20)
    o1, whole = lax.optimization_barrier((o1, whole))
    b1 = swap(o1, 1)
    whole, far_dq = call(
        whole_backward_kernel,
        [*both(ROWS), ((HEAD, 1024), f32)],
        (*rows, whole, dq1, dq2, dq3),
        vmem=12,
        **cost(256 * 1024, 5),
    )
    b2, b3, whole = lax.optimization_barrier((b2, b3, whole))
    whole = swap_whole(whole)
    dq, dkv = call(
        own_backward_kernel,
        [((ROWS, HEAD), f32), *[((ROWS, 256), f32)]],
        (q, g, near_bias, row, kv, far_dq),
        [pltpu.VMEM((HEAD, ROWS), f32), pltpu.VMEM((ROWS, HEAD), f32)],
        vmem=32,
        **cost(ROWS * ROWS, 5),
    )
    dk, dv = call(
        join_kernel, [((ROWS, HEAD), f32)] * 2, (dkv, b1, b2, b3, b4, b6, whole), [pltpu.VMEM((ROWS, 256), f32)], nbytes=8 << 20, vmem=16
    )
    return dq, dk, dv


def solution(mesh):
    spec = P(("grp", "seq"), None)
    return jax.shard_map(
        on_device, mesh=mesh, in_specs=(spec,) * 4, out_specs=(spec,) * 3, check_vma=False
    )
```

time: 182 us -> 155 us (0.85)
  blocking collectives: 58.6 us -> 0 us
  local copies, waits for them, and re-layouts: 1.95 us -> 24.2 us
  waiting for transfers between devices: 36.1 us -> 53.1 us
  Pallas kernels: 52 us -> 35.3 us
  starting transfers between devices: 31.5 us -> 40.4 us
    all_to_all x4 -> x0, blocking collectives: 58.6 us -> none  [the longest x2 34.7 us: exchange(): n8 = lax.all_to_all(s8, 'seq', 0, 0, axis_index_groups=groups[1])]
    ppermute x2 -> x10, waiting for transfers between devices: 0.98 us -> 43.7 us  [swap(): lax.ppermute(block, 'seq', [(at, at ^ mask) for at in range(lax.axis_size...]
    all_to_all x2, waiting for transfers between devices: 35.1 us -> 9.35 us  [swap_whole(): lax.all_to_all(block.reshape(256, 8, 256), ('grp', 'seq'), 0, 0)]
    unnamed x12 -> x68, local copies, waits for them, and re-layouts: 1.95 us -> 24.1 us
    pallas_call x6 -> x12, Pallas kernels: 52 us -> 35.3 us  [call(): pl.pallas_call(kernel, out_shape=[jax.ShapeDtypeStruct(shape, dtype) for...]
    ppermute x2 -> x10, starting transfers between devices: 3.13 us -> 17.3 us  [swap(): lax.ppermute(block, 'seq', [(at, at ^ mask) for at in range(lax.axis_size...]
    all_to_all x2, starting transfers between devices: 28.4 us -> 23.1 us  [swap_whole(): lax.all_to_all(block.reshape(256, 8, 256), ('grp', 'seq'), 0, 0)]
  transfers between devices with their start and end apart: 4 -> 12, of which waited for: 3 -> 8; matrix products, arithmetic and copies ran while one was open for 0% -> 0% of each run, Pallas kernels for 13% -> 19%
where the time goes in v3:
time: 155 us; the launch traced here: 154 us
  waiting for transfers between devices  53.1 us (34%)
  starting transfers between devices  40.4 us (26%)
  Pallas kernels  35.3 us (23%)
  local copies, waits for them, and re-layouts  24.2 us (16%)
    ppermute x10, waiting for transfers between devices, swap(): lax.ppermute(block, 'seq', [(at, at ^ mask) for at in range(lax.axis_size...  43.7 us
    pallas_call x12, Pallas kernels, call(): pl.pallas_call(kernel, out_shape=[jax.ShapeDtypeStruct(shape, dtype) for...  35.3 us
    unnamed x68, local copies, waits for them, and re-layouts  24.1 us
    all_to_all x2, starting transfers between devices, swap_whole(): lax.all_to_all(block.reshape(256, 8, 256), ('grp', 'seq'), 0, 0)  23.1 us
    ppermute x10, starting transfers between devices, swap(): lax.ppermute(block, 'seq', [(at, at ^ mask) for at in range(lax.axis_size...  17.3 us
    all_to_all x2, waiting for transfers between devices, swap_whole(): lax.all_to_all(block.reshape(256, 8, 256), ('grp', 'seq'), 0, 0)  9.35 us
  transfers between devices with their start and end apart: 12, of which 8 were waited for; matrix products, arithmetic and copies ran while one was open for 0% of the time, Pallas kernels for 19%

profile of v3, /device:TPU:1, one launch (start us, length us, event | category | flops | bytes accessed | tf_op | source)
XLA Modules:
  0.0 154.4 jit_solution(15910214215261930536)
XLA Ops:
  0.6 1.0 copy-done.6
  1.7 1.0 copy-done.7
  2.7 1.4 shard_map.85
  4.1 2.2 %collective-permute-start = (bf16[1024,256]{1,0:T(8,128)(2,1)S(1)}, bf16[1024,256]{1,0:T(8,128)(2,1)S(1)}, u32[]{:S(2)}, u32[]{:S(2)}) collective-permute-start(bf16[1024,256]{1,0:T(8,128)(2,1)S(1)} %get-tuple-element.41), channel_id=1, source_target_pairs={{0,1},{1,0},{2,3},{3,2},{4,5},{5,4},{6,7},{7,6},{8,9},{9,8},{10,11... | collective-permute-start | bytes 1572872 | tf_op jit(solution)/shard_map/ppermute | solution.py:294
  6.3 1.9 %collective-permute-start.2 = (bf16[512,256]{1,0:T(8,128)(2,1)S(1)}, bf16[512,256]{1,0:T(8,128)(2,1)S(1)}, u32[]{:S(2)}, u32[]{:S(2)}) collective-permute-start(bf16[512,256]{1,0:T(8,128)(2,1)S(1)} %get-tuple-element.38.s2_ref), channel_id=1, source_target_pairs={{0,3},{1,2},{2,1},{3,0},{4,7},{5,6},{6,5},{7,4},{8,11},{9,10},{10,... | collective-permute-start | bytes 786440 | tf_op jit(solution)/shard_map/ppermute | solution.py:294
  9.0 1.0 copy-done.8
  10.0 1.0 copy-done.9
  11.0 1.3 shard_map.86
  12.4 6.4 %shard_map.87 = (f32[8,2048]{1,0:T(8,128)S(1)}, f32[128,2048]{1,0:T(8,128)S(1)}) custom-call(bf16[2048,128]{1,0:T(8,128)(2,1)S(1)} %get-tuple-element.39.q_ref, bf16[2048,256]{1,0:T(8,128)(2,1)S(1)} %get-tuple-element.42.kv_ref, f32[8,2048]{1,0:T(8,128)S(1)} %copy-done.28), custom_call_target="tpu_custom_call" | custom-call | flops 2147483648 | bytes 4194304 | tf_op jit(solution)/shard_map/pallas_call | solution.py:62
  18.9 1.0 copy-done.30
  19.9 0.7 pad_maximum_fusion
  21.3 4.6 %collective-permute-done.1.r2 = bf16[512,256]{1,0:T(8,128)(2,1)S(1)} collective-permute-done((bf16[512,256]{1,0:T(8,128)(2,1)S(1)}, bf16[512,256]{1,0:T(8,128)(2,1)S(1)}, u32[]{:S(2)}, u32[]{:S(2)}) %collective-permute-start.1) | collective-permute-done | bytes 262176 | tf_op jit(solution)/shard_map/ppermute | solution.py:294
  26.6 13.1 %all-to-all-start = ((bf16[256,8,256]{2,1,0:T(8,128)(2,1)}), bf16[256,8,256]{2,1,0:T(8,128)(2,1)S(1)}, u32[]{:S(2)}, u32[]{:S(2)}) async-start(bf16[256,8,256]{2,1,0:T(8,128)(2,1)} %bitcast), calls=%async_computation | async-start | bytes 2097152 | tf_op jit(solution)/shard_map/all_to_all | solution.py:298
  39.7 4.1 %collective-permute-start.4 = (bf16[512,256]{1,0:T(8,128)(2,1)}, bf16[512,256]{1,0:T(8,128)(2,1)S(1)}, u32[]{:S(2)}, u32[]{:S(2)}) collective-permute-start(bf16[512,256]{1,0:T(8,128)(2,1)} %pad_maximum_fusion), channel_id=1, source_target_pairs={{0,6},{1,7},{2,4},{3,5},{4,2},{5,3},{6,0},{7,1},{8,14},{9,15},{10,... | collective-permute-start | bytes 786440 | tf_op jit(solution)/shard_map/ppermute | solution.py:294
  43.9 1.0 copy-done.16
  44.9 0.9 copy-done.23
  45.9 0.9 copy-done.26
  46.9 1.2 copy-done.31
  48.1 0.8 copy-done.33
  48.9 2.5 %shard_map.88 = (f32[8,2048]{1,0:T(8,128)S(1)}, f32[128,2048]{1,0:T(8,128)S(1)}) custom-call(bf16[2048,128]{1,0:T(8,128)(2,1)S(1)} %get-tuple-element.39.q_ref, f32[8,1024]{1,0:T(8,128)S(1)} %copy-done.10, f32[8,2048]{1,0:T(8,128)S(1)} %copy-done.33, f32[128,2048]{1,0:T(8,128)S(1)} %copy-done.31, bf16[1024,256]{1,0:T(8,128)(2,1)S(1)} %copy-done.16, ...), custom_call_target="tpu_custom_call" | custom-call | flops 805306368 | bytes 4194304 | tf_op jit(solution)/shard_map/pallas_call | solution.py:62
  52.1 20.1 %collective-permute-done.4.r6 = bf16[512,256]{1,0:T(8,128)(2,1)S(1)} collective-permute-done((bf16[512,256]{1,0:T(8,128)(2,1)}, bf16[512,256]{1,0:T(8,128)(2,1)S(1)}, u32[]{:S(2)}, u32[]{:S(2)}) %collective-permute-start.4) | collective-permute-done | bytes 262176 | tf_op jit(solution)/shard_map/ppermute | solution.py:294
  72.1 2.9 %collective-permute-done.3.r4 = bf16[512,256]{1,0:T(8,128)(2,1)S(1)} collective-permute-done((bf16[512,256]{1,0:T(8,128)(2,1)}, bf16[512,256]{1,0:T(8,128)(2,1)S(1)}, u32[]{:S(2)}, u32[]{:S(2)}) %collective-permute-start.3) | collective-permute-done | bytes 262176 | tf_op jit(solution)/shard_map/ppermute | solution.py:294
  75.8 0.9 copy-done.3
  76.7 0.8 copy-done.14
  77.6 1.3 shard_map.89.row_ref
  78.9 0.9 shard_map.91
  79.8 4.1 %collective-permute-start.6 = (bf16[512,256]{1,0:T(8,128)(2,1)S(1)}, bf16[512,256]{1,0:T(8,128)(2,1)S(1)}, u32[]{:S(2)}, u32[]{:S(2)}) collective-permute-start(bf16[512,256]{1,0:T(8,128)(2,1)S(1)} %get-tuple-element.56), channel_id=1, source_target_pairs={{0,6},{1,7},{2,4},{3,5},{4,2},{5,3},{6,0},{7,1},{8,14},{9,15},{10,... | collective-permute-start | bytes 786440 | tf_op jit(solution)/shard_map/ppermute | solution.py:294
  84.0 1.4 shard_map.93
  85.5 2.5 %collective-permute-start.9 = (bf16[512,256]{1,0:T(8,128)(2,1)S(1)}, bf16[512,256]{1,0:T(8,128)(2,1)S(1)}, u32[]{:S(2)}, u32[]{:S(2)}) collective-permute-start(bf16[512,256]{1,0:T(8,128)(2,1)S(1)} %get-tuple-element.66), channel_id=1, source_target_pairs={{0,3},{1,2},{2,1},{3,0},{4,7},{5,6},{6,5},{7,4},{8,11},{9,10},{10,... | collective-permute-start | bytes 786440 | tf_op jit(solution)/shard_map/ppermute | solution.py:294
  88.0 2.6 %shard_map.90 = (bf16[1024,256]{1,0:T(8,128)(2,1)S(1)}, f32[128,1024]{1,0:T(8,128)S(1)}) custom-call(bf16[2048,128]{1,0:T(8,128)(2,1)S(1)} %get-tuple-element.39.q_ref, bf16[2048,128]{1,0:T(8,128)(2,1)S(1)} %get-tuple-element.40.g_ref, f32[8,1024]{1,0:T(8,128)S(1)} %copy-done.10, f32[8,2048]{1,0:T(8,128)S(1)} %shard_map.89.row_ref, ...), custom_call_target="tpu_custom_call" | custom-call | flops 1342177280 | bytes 4194304 | tf_op jit(solution)/shard_map/pallas_call | solution.py:62
  90.6 4.4 %collective-permute-done.6.b6 = bf16[512,256]{1,0:T(8,128)(2,1)S(1)} collective-permute-done((bf16[512,256]{1,0:T(8,128)(2,1)S(1)}, bf16[512,256]{1,0:T(8,128)(2,1)S(1)}, u32[]{:S(2)}, u32[]{:S(2)}) %collective-permute-start.6) | collective-permute-done | bytes 262176 | tf_op jit(solution)/shard_map/ppermute | solution.py:294
  95.1 2.1 %shard_map.94 = (bf16[2048,256]{1,0:T(8,128)(2,1)}, f32[128,1024]{1,0:T(8,128)S(1)}) custom-call(bf16[2048,128]{1,0:T(8,128)(2,1)S(1)} %get-tuple-element.39.q_ref, bf16[2048,128]{1,0:T(8,128)(2,1)S(1)} %get-tuple-element.40.g_ref, f32[8,1024]{1,0:T(8,128)S(1)} %copy-done.10, f32[8,2048]{1,0:T(8,128)S(1)} %shard_map.89.row_ref, ...), custom_call_target="tpu_custom_call" | custom-call | flops 335544320 | bytes 4194304 | tf_op jit(solution)/shard_map/pallas_call | solution.py:62
  97.3 0.8 copy-done.20
  98.1 1.8 %collective-permute-done.8.b2 = bf16[512,256]{1,0:T(8,128)(2,1)S(1)} collective-permute-done((bf16[512,256]{1,0:T(8,128)(2,1)S(1)}, bf16[512,256]{1,0:T(8,128)(2,1)S(1)}, u32[]{:S(2)}, u32[]{:S(2)}) %collective-permute-start.8) | collective-permute-done | bytes 262176 | tf_op jit(solution)/shard_map/ppermute | solution.py:294
  99.8 6.5 %collective-permute-done.9.b3 = bf16[512,256]{1,0:T(8,128)(2,1)S(1)} collective-permute-done((bf16[512,256]{1,0:T(8,128)(2,1)S(1)}, bf16[512,256]{1,0:T(8,128)(2,1)S(1)}, u32[]{:S(2)}, u32[]{:S(2)}) %collective-permute-start.9) | collective-permute-done | bytes 262176 | tf_op jit(solution)/shard_map/ppermute | solution.py:294
  107.0 9.9 %all-to-all-start.1 = ((bf16[256,8,256]{2,1,0:T(8,128)(2,1)}), bf16[256,8,256]{2,1,0:T(8,128)(2,1)S(1)}, u32[]{:S(2)}, u32[]{:S(2)}) async-start(bf16[256,8,256]{2,1,0:T(8,128)(2,1)} %bitcast.2), calls=%async_computation.1 | async-start | bytes 2097152 | tf_op jit(solution)/shard_map/all_to_all | solution.py:298
  116.9 1.5 collective-permute-start.7
  118.4 1.2 copy-done.19
  119.6 1.0 copy-done.21
  120.7 12.5 %shard_map.95 = (f32[2048,128]{1,0:T(8,128)}, f32[2048,256]{1,0:T(8,128)S(1)}) custom-call(bf16[2048,128]{1,0:T(8,128)(2,1)S(1)} %get-tuple-element.39.q_ref, bf16[2048,128]{1,0:T(8,128)(2,1)S(1)} %get-tuple-element.40.g_ref, f32[8,2048]{1,0:T(8,128)S(1)} %copy-done.29, f32[8,2048]{1,0:T(8,128)S(1)} %shard_map.89.row_ref, bf16[2048,256]{1,0:T(8,128)(2,1)S(1)} %copy-done.19, ...), custom_call_target="tpu_custom_call" | custom-call | flops 5368709120 | bytes 4194304 | tf_op jit(solution)/shard_map/pallas_call | solution.py:62
  133.2 1.3 copy-done
  134.5 3.4 %collective-permute-done.7.b1 = bf16[1024,256]{1,0:T(8,128)(2,1)S(1)} collective-permute-done((bf16[1024,256]{1,0:T(8,128)(2,1)S(1)}, bf16[1024,256]{1,0:T(8,128)(2,1)S(1)}, u32[]{:S(2)}, u32[]{:S(2)}) %collective-permute-start.7) | collective-permute-done | bytes 524320 | tf_op jit(solution)/shard_map/ppermute | solution.py:294
  137.9 0.8 copy-done.4
  138.7 9.3 %all-to-all-done.1 = bf16[256,8,256]{2,1,0:T(8,128)(2,1)S(1)} async-done(((bf16[256,8,256]{2,1,0:T(8,128)(2,1)}), bf16[256,8,256]{2,1,0:T(8,128)(2,1)S(1)}, u32[]{:S(2)}, u32[]{:S(2)}) %all-to-all-start.1) | async-done | bytes 1048608 | tf_op jit(solution)/shard_map/all_to_all | solution.py:298
  148.1 1.6 %copy-done.1 = f32[2048,256]{1,0:T(8,128)S(1)} copy-done((f32[2048,256]{1,0:T(8,128)S(1)}, f32[2048,256]{1,0:T(8,128)}, u32[]{:S(2)}) %copy-start.1) | copy-done | bytes 2097176
  149.6 1.0 copy-done.5
  150.7 0.9 copy-done.12
  151.6 2.8 %shard_map.96 = (f32[2048,128]{1,0:T(8,128)}, f32[2048,128]{1,0:T(8,128)}) custom-call(f32[2048,256]{1,0:T(8,128)S(1)} %copy-done.1, bf16[1024,256]{1,0:T(8,128)(2,1)S(1)} %copy-done.5, bf16[512,256]{1,0:T(8,128)(2,1)S(1)} %collective-permute-done.8.b2, bf16[512,256]{1,0:T(8,128)(2,1)S(1)} %copy-done.12, bf16[512,256]{1,0:T(8,128)(2,1)S(1)} %collective-permute-done.5.b4, ...), custom_call_target="tpu_custom_call" | custom-call | bytes 8388608 | tf_op jit(solution)/shard_map/pallas_call | solution.py:62
  (59 shorter events, 4.5 us)
Async XLA Ops:
  0.6 1.0 copy-start.6
  1.7 1.0 copy-start.7
  2.7 9.7 %copy-start.28 = (f32[8,2048]{1,0:T(8,128)S(1)}, f32[8,2048]{1,0:T(8,128)}, u32[]{:S(2)}) copy-start(f32[8,2048]{1,0:T(8,128)} %constant.4.clone.bias_ref) | copy-start | bytes 196612
  4.1 14.7 %copy-start.18 = (bf16[2048,256]{1,0:T(8,128)(2,1)}, bf16[2048,256]{1,0:T(8,128)(2,1)S(1)}, u32[]{:S(2)}) copy-start(bf16[2048,256]{1,0:T(8,128)(2,1)S(1)} %get-tuple-element.42.kv_ref) | copy-start | bytes 3145732
  4.1 15.7 %collective-permute-start = (bf16[1024,256]{1,0:T(8,128)(2,1)S(1)}, bf16[1024,256]{1,0:T(8,128)(2,1)S(1)}, u32[]{:S(2)}, u32[]{:S(2)}) collective-permute-start(bf16[1024,256]{1,0:T(8,128)(2,1)S(1)} %get-tuple-element.41), channel_id=1, source_target_pairs={{0,1},{1,0},{2,3},{3,2},{4,5},{5,4},{6,7},{7,6},{8,9},{9,8},{10,11... | collective-permute-start | bytes 1572872 | tf_op jit(solution)/shard_map/ppermute | solution.py:294
  6.3 14.3 %collective-permute-start.2 = (bf16[512,256]{1,0:T(8,128)(2,1)S(1)}, bf16[512,256]{1,0:T(8,128)(2,1)S(1)}, u32[]{:S(2)}, u32[]{:S(2)}) collective-permute-start(bf16[512,256]{1,0:T(8,128)(2,1)S(1)} %get-tuple-element.38.s2_ref), channel_id=1, source_target_pairs={{0,3},{1,2},{2,1},{3,0},{4,7},{5,6},{6,5},{7,4},{8,11},{9,10},{10,... | collective-permute-start | bytes 786440 | tf_op jit(solution)/shard_map/ppermute | solution.py:294
  8.2 17.7 %collective-permute-start.1 = (bf16[512,256]{1,0:T(8,128)(2,1)S(1)}, bf16[512,256]{1,0:T(8,128)(2,1)S(1)}, u32[]{:S(2)}, u32[]{:S(2)}) collective-permute-start(bf16[512,256]{1,0:T(8,128)(2,1)S(1)} %get-tuple-element.38.s2_ref), channel_id=1, source_target_pairs={{0,2},{1,3},{2,0},{3,1},{4,6},{5,7},{6,4},{7,5},{8,10},{9,11},{10,... | collective-permute-start | bytes 786440 | tf_op jit(solution)/shard_map/ppermute | solution.py:294
  9.0 1.0 copy-start.8
  10.0 1.0 copy-start.9
  18.8 1.0 copy-start.30
  19.8 6.1 %copy-start.32 = (f32[8,2048]{1,0:T(8,128)}, f32[8,2048]{1,0:T(8,128)S(1)}, u32[]{:S(2)}) copy-start(f32[8,2048]{1,0:T(8,128)S(1)} %get-tuple-element.45.stat_ref) | copy-start | bytes 196612
  19.8 24.1 %copy-start.10 = (f32[8,1024]{1,0:T(8,128)S(1)}, f32[8,1024]{1,0:T(8,128)}, u32[]{:S(2)}) copy-start(f32[8,1024]{1,0:T(8,128)} %constant.5.clone.bias_ref) | copy-start | bytes 98308
  19.8 24.1 %copy-start.15 = (bf16[1024,256]{1,0:T(8,128)(2,1)}, bf16[1024,256]{1,0:T(8,128)(2,1)S(1)}, u32[]{:S(2)}) copy-start(bf16[1024,256]{1,0:T(8,128)(2,1)S(1)} %collective-permute-done.r1) | copy-start | bytes 1572868
  20.6 0.7 copy-start.22
  25.9 0.7 copy-start.25
  26.6 49.2 %all-to-all-start = ((bf16[256,8,256]{2,1,0:T(8,128)(2,1)}), bf16[256,8,256]{2,1,0:T(8,128)(2,1)S(1)}, u32[]{:S(2)}, u32[]{:S(2)}) async-start(bf16[256,8,256]{2,1,0:T(8,128)(2,1)} %bitcast), calls=%async_computation | async-start | bytes 2097152 | tf_op jit(solution)/shard_map/all_to_all | solution.py:298
  39.7 32.4 %collective-permute-start.4 = (bf16[512,256]{1,0:T(8,128)(2,1)}, bf16[512,256]{1,0:T(8,128)(2,1)S(1)}, u32[]{:S(2)}, u32[]{:S(2)}) collective-permute-start(bf16[512,256]{1,0:T(8,128)(2,1)} %pad_maximum_fusion), channel_id=1, source_target_pairs={{0,6},{1,7},{2,4},{3,5},{4,2},{5,3},{6,0},{7,1},{8,14},{9,15},{10,... | collective-permute-start | bytes 786440 | tf_op jit(solution)/shard_map/ppermute | solution.py:294
  43.9 31.2 %collective-permute-start.3 = (bf16[512,256]{1,0:T(8,128)(2,1)}, bf16[512,256]{1,0:T(8,128)(2,1)S(1)}, u32[]{:S(2)}, u32[]{:S(2)}) collective-permute-start(bf16[512,256]{1,0:T(8,128)(2,1)} %pad_maximum_fusion), channel_id=1, source_target_pairs={{0,4},{1,5},{2,6},{3,7},{4,0},{5,1},{6,2},{7,3},{8,12},{9,13},{10,... | collective-permute-start | bytes 786440 | tf_op jit(solution)/shard_map/ppermute | solution.py:294
  43.9 1.0 copy-start.16
  44.9 0.9 copy-start.23
  45.9 0.9 copy-start.26
  46.8 1.2 copy-start.31
  48.1 0.8 copy-start.33
  51.5 0.6 copy-start.13
  75.1 0.7 copy-start.2
  75.8 1.0 copy-start.3
  76.7 0.8 copy-start.14
  77.6 6.4 %copy-start.24 = (bf16[512,256]{1,0:T(8,128)(2,1)S(1)}, bf16[512,256]{1,0:T(8,128)(2,1)}, u32[]{:S(2)}) copy-start(bf16[512,256]{1,0:T(8,128)(2,1)} %copy-done.22) | copy-start | bytes 786436
  77.6 6.4 %copy-start.27 = (bf16[512,256]{1,0:T(8,128)(2,1)S(1)}, bf16[512,256]{1,0:T(8,128)(2,1)}, u32[]{:S(2)}) copy-start(bf16[512,256]{1,0:T(8,128)(2,1)} %copy-done.25) | copy-start | bytes 786436
  78.8 9.1 %copy-start.17 = (bf16[1024,256]{1,0:T(8,128)(2,1)S(1)}, bf16[1024,256]{1,0:T(8,128)(2,1)}, u32[]{:S(2)}) copy-start(bf16[1024,256]{1,0:T(8,128)(2,1)} %copy-done.15) | copy-start | bytes 1572868
  79.7 10.9 %collective-permute-start.5 = (bf16[512,256]{1,0:T(8,128)(2,1)S(1)}, bf16[512,256]{1,0:T(8,128)(2,1)S(1)}, u32[]{:S(2)}, u32[]{:S(2)}) collective-permute-start(bf16[512,256]{1,0:T(8,128)(2,1)S(1)} %get-tuple-element.55), channel_id=1, source_target_pairs={{0,4},{1,5},{2,6},{3,7},{4,0},{5,1},{6,2},{7,3},{8,12},{9,13},{10,... | collective-permute-start | bytes 786440 | tf_op jit(solution)/shard_map/ppermute | solution.py:294
  79.8 15.2 %collective-permute-start.6 = (bf16[512,256]{1,0:T(8,128)(2,1)S(1)}, bf16[512,256]{1,0:T(8,128)(2,1)S(1)}, u32[]{:S(2)}, u32[]{:S(2)}) collective-permute-start(bf16[512,256]{1,0:T(8,128)(2,1)S(1)} %get-tuple-element.56), channel_id=1, source_target_pairs={{0,6},{1,7},{2,4},{3,5},{4,2},{5,3},{6,0},{7,1},{8,14},{9,15},{10,... | collective-permute-start | bytes 786440 | tf_op jit(solution)/shard_map/ppermute | solution.py:294
  85.4 14.5 %collective-permute-start.8 = (bf16[512,256]{1,0:T(8,128)(2,1)S(1)}, bf16[512,256]{1,0:T(8,128)(2,1)S(1)}, u32[]{:S(2)}, u32[]{:S(2)}) collective-permute-start(bf16[512,256]{1,0:T(8,128)(2,1)S(1)} %get-tuple-element.65), channel_id=1, source_target_pairs={{0,2},{1,3},{2,0},{3,1},{4,6},{5,7},{6,4},{7,5},{8,10},{9,11},{10,... | collective-permute-start | bytes 786440 | tf_op jit(solution)/shard_map/ppermute | solution.py:294
  85.5 20.8 %collective-permute-start.9 = (bf16[512,256]{1,0:T(8,128)(2,1)S(1)}, bf16[512,256]{1,0:T(8,128)(2,1)S(1)}, u32[]{:S(2)}, u32[]{:S(2)}) collective-permute-start(bf16[512,256]{1,0:T(8,128)(2,1)S(1)} %get-tuple-element.66), channel_id=1, source_target_pairs={{0,3},{1,2},{2,1},{3,0},{4,7},{5,6},{6,5},{7,4},{8,11},{9,10},{10,... | collective-permute-start | bytes 786440 | tf_op jit(solution)/shard_map/ppermute | solution.py:294
  97.3 0.8 copy-start.20
  98.1 20.4 %copy-start.29 = (f32[8,2048]{1,0:T(8,128)S(1)}, f32[8,2048]{1,0:T(8,128)}, u32[]{:S(2)}) copy-start(f32[8,2048]{1,0:T(8,128)} %constant.4.clone.bias_ref) | copy-start | bytes 196612
  106.3 0.7 copy-start.11
  107.0 41.0 %all-to-all-start.1 = ((bf16[256,8,256]{2,1,0:T(8,128)(2,1)}), bf16[256,8,256]{2,1,0:T(8,128)(2,1)S(1)}, u32[]{:S(2)}, u32[]{:S(2)}) async-start(bf16[256,8,256]{2,1,0:T(8,128)(2,1)} %bitcast.2), calls=%async_computation.1 | async-start | bytes 2097152 | tf_op jit(solution)/shard_map/all_to_all | solution.py:298
  116.9 21.0 %collective-permute-start.7 = (bf16[1024,256]{1,0:T(8,128)(2,1)S(1)}, bf16[1024,256]{1,0:T(8,128)(2,1)S(1)}, u32[]{:S(2)}, u32[]{:S(2)}) collective-permute-start(bf16[1024,256]{1,0:T(8,128)(2,1)S(1)} %shard_map.92), channel_id=1, source_target_pairs={{0,1},{1,0},{2,3},{3,2},{4,5},{5,4},{6,7},{7,6},{8,9},{9,8},{10,11... | collective-permute-start | bytes 1572872 | tf_op jit(solution)/shard_map/ppermute | solution.py:294
  118.4 1.2 copy-start.19
  119.6 1.0 copy-start.21
  133.2 1.3 copy-start
  137.9 0.8 copy-start.4
  148.1 1.6 %copy-start.1 = (f32[2048,256]{1,0:T(8,128)S(1)}, f32[2048,256]{1,0:T(8,128)}, u32[]{:S(2)}) copy-start(f32[2048,256]{1,0:T(8,128)} %copy-done) | copy-start | bytes 6291460
  149.6 1.0 copy-start.5
  150.7 0.9 copy-start.12

commit v4 on v3

v4 whole, which is shorter than its diff:
```python
import functools
import math

import jax
import jax.numpy as jnp
import numpy as np
from jax import lax
from jax.experimental import pallas as pl
from jax.experimental.pallas import tpu as pltpu
from jax.sharding import PartitionSpec as P

ROWS = 2048
HEAD = 128
UNIT = 256
ORDER = (0, 4, 2, 6, 1, 3, 5, 7)
SCALE = HEAD**-0.5
SCALE2 = SCALE * math.log2(math.e)
NEG = -1e30
VMEM = 60 << 20
QUADS = 4
FAR = 64
BLOCK = 512


def unit_level(unit):
    return 3 if unit == 0 else 2 if unit == 1 else 1 if unit < 4 else 0


def own_bias():
    table = np.zeros((8, ROWS), np.float32)
    for key_unit in range(8):
        for query_unit in range(8):
            shared = 1 + min(unit_level(key_unit), unit_level(query_unit))
            table[key_unit, query_unit * UNIT : (query_unit + 1) * UNIT] = math.log2(shared)
    return table


def far_bias():
    table = np.zeros((8, 1024), np.float32)
    for query_unit in range(4):
        lanes = slice(query_unit * UNIT, (query_unit + 1) * UNIT)
        level = unit_level(query_unit)
        table[0, lanes] = math.log2(min(3, level))
        table[1, lanes] = math.log2(min(2, level))
        if level >= 2:
            table[2, lanes] = math.log2(level - 1)
    table[3, 8:] = NEG
    return table


def dot_nt(left, right):
    return lax.dot_general(left, right, (((1,), (1,)), ((), ())), preferred_element_type=jnp.float32)


def dot_nn(left, right):
    return lax.dot_general(left, right, (((1,), (0,)), ((), ())), preferred_element_type=jnp.float32)


def dot_tn(left, right):
    return lax.dot_general(left, right, (((0,), (0,)), ((), ())), preferred_element_type=jnp.float32)


def call(kernel, outs, args, scratch=(), scalars=0):
    return pl.pallas_call(
        kernel,
        out_shape=[jax.ShapeDtypeStruct(shape, dtype) for shape, dtype in outs],
        in_specs=[
            pl.BlockSpec(memory_space=pltpu.SMEM if at < scalars else pltpu.VMEM) for at in range(len(args))
        ],
        out_specs=[pl.BlockSpec(memory_space=pltpu.VMEM)] * len(outs),
        scratch_shapes=list(scratch),
        compiler_params=pltpu.CompilerParams(vmem_limit_bytes=VMEM),
        cost_estimate=pl.CostEstimate(flops=0, bytes_accessed=0, transcendentals=0),
    )(*args)


def sort_rows(source, target, lane, wide):
    wide[...] = source[...].astype(jnp.float32)
    for unit, residue in enumerate(ORDER):
        for pair in range(16):
            parts = [
                wide[pl.ds(8 * (2 * pair + half) + residue, 8, stride=256), :] for half in range(2)
            ]
            rows = slice(unit * UNIT + 16 * pair, unit * UNIT + 16 * pair + 16)
            target[rows, lane : lane + HEAD] = jnp.concatenate(parts, 0).astype(jnp.bfloat16)


def repeat_first(source, target, lane):
    first = source[:16, :].astype(jnp.float32)[:8]
    pair = jnp.concatenate([first, first], 0).astype(jnp.bfloat16)
    for at in range(0, target.shape[0], 16):
        target[at : at + 16, lane : lane + pair.shape[1]] = pair


def prepare_keys_kernel(k_ref, v_ref, q_ref, g_ref, kv_ref, s1_ref, s2_ref, s3_ref, far_ref, wide):
    sort_rows(k_ref, kv_ref, 0, wide)
    sort_rows(v_ref, kv_ref, HEAD, wide)
    s1_ref[:1024] = kv_ref[:1024]
    s2_ref[:512] = kv_ref[:512]
    s3_ref[...] = kv_ref[:256]
    repeat_first(kv_ref, far_ref, 0)
    for lane, ref in ((0, q_ref), (HEAD, g_ref)):
        rows = [ref[at : at + 16, :].astype(jnp.float32)[:1] for at in range(0, ROWS, 256)]
        block = jnp.concatenate(rows + rows, 0).astype(jnp.bfloat16)
        s1_ref[1024:, lane : lane + HEAD] = block
        s2_ref[512:, lane : lane + HEAD] = block


def prepare_queries_kernel(q_ref, g_ref, after_ref, qp_ref, gp_ref, wide):
    sort_rows(q_ref, qp_ref, 0, wide)
    sort_rows(g_ref, gp_ref, 0, wide)


def add_bias(block, rows):
    if all(row is None for row in rows):
        return block
    parts = []
    for at, row in enumerate(rows):
        part = block[at * UNIT : (at + 1) * UNIT]
        parts.append(part if row is None else part + row)
    return jnp.concatenate(parts, 0)


def attend(query, keys, values, biases):
    scores = [add_bias(dot_nt(key, query) * SCALE2, bias) for key, bias in zip(keys, biases)]
    peak = functools.reduce(jnp.maximum, [jnp.max(block, 0, keepdims=True) for block in scores])
    probs = [jnp.exp2(block - peak) for block in scores]
    total = sum([jnp.sum(block, 0, keepdims=True) for block in probs])
    out = sum([value(block.astype(jnp.bfloat16)) for value, block in zip(values, probs)])
    return peak, total, out


def own_forward_kernel(q_ref, kv_ref, bias_ref, stat_ref, out_ref, vt_ref):
    stat_ref[...] = jnp.zeros_like(stat_ref)
    for unit in range(8):
        rows = slice(unit * UNIT, (unit + 1) * UNIT)
        vt_ref[:, rows] = kv_ref[rows, HEAD:].astype(jnp.float32).T.astype(jnp.bfloat16)
    for start in (0, 1024):
        lanes = slice(start, start + 1024)
        keys, values, biases = [], [], []
        for at in range(0, ROWS, BLOCK):
            rows = slice(at, at + BLOCK)
            keys.append(kv_ref[rows, :HEAD])
            values.append(lambda prob, rows=rows: dot_nn(vt_ref[:, rows], prob))
            unit = at // UNIT
            counted = start == 0 and at < 1024
            biases.append([bias_ref[unit + half : unit + half + 1, lanes] if counted else None for half in (0, 1)])
        peak, total, out = attend(q_ref[lanes, :], keys, values, biases)
        stat_ref[0:1, lanes] = peak
        stat_ref[1:2, lanes] = total
        out_ref[:, lanes] = out


def bias_rows(bias_ref, picks, count):
    return [None if pick is None else bias_ref[pick : pick + 1, :count] for pick in picks]


PARTNER, PARTNER_REST, SECOND, THIRD = (0, 1), (None, None), (2, None), (None, None)


def far_blocks(r1, r2, r3):
    return (
        (1024, [((r1, 0), PARTNER), ((r1, BLOCK), PARTNER_REST)]),
        (512, [((ref, 0), SECOND) for ref in r2]),
        (256, [(r3[0:2], THIRD), (r3[2:4], THIRD)]),
    )


def read_block(place, lanes):
    ref, first = place
    if isinstance(first, int):
        return ref[first : first + BLOCK, lanes]
    return jnp.concatenate([ref[:, lanes], first[:, lanes]], 0)


def write_block(place, block):
    ref, first = place
    if isinstance(first, int):
        ref[first : first + BLOCK, :] = block
    else:
        ref[...] = block[:UNIT]
        first[...] = block[UNIT:]


def join_state(sums, acc, lanes, far_peak, far_total, far_out):
    peak = sums[0:1, lanes]
    top = jnp.maximum(peak, far_peak)
    near, far = jnp.exp2(peak - top), jnp.exp2(far_peak - top)
    sums[0:1, lanes] = top
    sums[1:2, lanes] = near * sums[1:2, lanes] + far * far_total
    acc[:, lanes] = near * acc[:, lanes] + far * far_out


def middle_forward_kernel(q_ref, bias_ref, stat_ref, out_ref, *rest):
    r1, r2, r3, (sums, acc) = rest[0], rest[1:3], rest[3:7], rest[7:]
    sums[...] = stat_ref[...]
    acc[...] = out_ref[...]
    for count, blocks in far_blocks(r1, r2, r3):
        lanes = slice(0, count)
        state = attend(
            q_ref[lanes, :],
            [read_block(place, slice(0, HEAD)) for place, _ in blocks],
            [lambda prob, place=place: dot_tn(read_block(place, slice(HEAD, 256)), prob) for place, _ in blocks],
            [bias_rows(bias_ref, picks, count) for _, picks in blocks],
        )
        join_state(sums, acc, lanes, *state)


def whole_forward_kernel(me_ref, own, r1, r2, r3, far_ref, part_ref, quad_ref, rows_ref):
    for mask, ref in enumerate((own, r1, r2, r3)):
        count = ref.shape[0]
        place = pl.multiple_of((me_ref[0] ^ mask) * 8, 8)
        rows_ref[pl.ds(place, 8), :] = ref[count - 16 :, :].astype(jnp.float32)[:8]
    quad_ref[...] = rows_ref[...].astype(jnp.bfloat16)
    scores = dot_nt(quad_ref[:, :HEAD], far_ref[:, :HEAD]) * SCALE2
    peak = jnp.max(scores, 1, keepdims=True)
    prob = jnp.exp2(scores - peak)
    part_ref[:, :HEAD] = dot_nn(prob.astype(jnp.bfloat16), far_ref[:, HEAD:])
    part_ref[:, HEAD : 2 * HEAD] = jnp.broadcast_to(peak, (8 * QUADS, HEAD))
    part_ref[:, 2 * HEAD :] = jnp.broadcast_to(jnp.sum(prob, 1, keepdims=True), (8 * QUADS, HEAD))


def turn(block, fill):
    return jnp.concatenate([block, jnp.full((HEAD - 8, HEAD), fill, jnp.float32)], 0).T


def finish_kernel(g_ref, stat_ref, out_ref, part_ref, row_ref, tall_ref, sums, acc):
    lanes = slice(0, HEAD)
    sums[...] = stat_ref[:, lanes]
    acc[...] = out_ref[:, lanes]
    for at in range(0, 8 * QUADS, 8):
        part = part_ref[at : at + 8, :]
        far_out = turn(part[:, :HEAD], 0.0)
        far_peak = turn(part[:, HEAD : 2 * HEAD], NEG)[0:1]
        far_total = turn(part[:, 2 * HEAD :], 0.0)[0:1]
        join_state(sums, acc, lanes, far_peak, far_total, far_out)
    row_ref[...] = jnp.zeros_like(row_ref)
    for first in range(0, ROWS, HEAD):
        lanes = slice(first, first + HEAD)
        stat, out = (sums[...], acc[...]) if first == 0 else (stat_ref[:, lanes], out_ref[:, lanes])
        total = stat[1:2]
        row_ref[0:1, lanes] = stat[0:1] + jnp.log2(total)
        grad = g_ref[lanes, :].astype(jnp.float32).T
        row_ref[1:2, lanes] = jnp.sum(grad * out, axis=0, keepdims=True) / total
    tall = jnp.concatenate([row_ref[:, :HEAD], jnp.zeros((HEAD - 8, HEAD), jnp.float32)], 0).T
    for at in range(0, 8 * QUADS, 8):
        tall_ref[at : at + 8, :] = tall[:8]


def remote_backward_kernel(q_ref, g_ref, bias_ref, row_ref, *rest):
    far, outs, dq_ref = rest[:7], rest[7:14], rest[14]
    dq_ref[...] = jnp.zeros_like(dq_ref)
    sources, targets = (far_blocks(refs[0], refs[1:3], refs[3:7]) for refs in (far, outs))
    for (count, blocks), (_, places) in zip(sources, targets):
        for (place, picks), (target, _) in zip(blocks, places):
            bias = bias_rows(bias_ref, picks, count)
            both = backward_block(read_block(place, slice(0, 256)), q_ref, g_ref, row_ref, bias, count, dq_ref)
            write_block(target, jnp.concatenate(both, 1).astype(jnp.bfloat16))


def whole_backward_kernel(quad_ref, far_ref, tall_ref, dq_ref, out_ref):
    query, grad = quad_ref[:, :HEAD], quad_ref[:, HEAD:]
    key, value = far_ref[:, :HEAD], far_ref[:, HEAD:]
    weights = jnp.exp2(dot_nt(query, key) * SCALE2 - tall_ref[:, 0:1])
    grad_scores = (weights * (dot_nt(grad, value) - tall_ref[:, 1:2])).astype(jnp.bfloat16)
    dq_ref[...] = dot_nn(grad_scores, key)
    out_ref[:, :HEAD] = (SCALE * dot_tn(grad_scores, query)).astype(jnp.bfloat16)
    out_ref[:, HEAD:] = dot_tn(weights.astype(jnp.bfloat16), grad).astype(jnp.bfloat16)


def backward_block(kv_block, q_ref, g_ref, row_ref, bias, count, dq_ref):
    key, value = kv_block[:, :HEAD], kv_block[:, HEAD:]
    lanes = slice(0, count)
    query, grad = q_ref[lanes, :], g_ref[lanes, :]
    scores = add_bias(dot_nt(key, query) * SCALE2, bias)
    weights = jnp.exp2(scores - row_ref[0:1, lanes])
    grad_probs = dot_nt(value, grad)
    grad_scores = (weights * (grad_probs - row_ref[1:2, lanes])).astype(jnp.bfloat16)
    grad_value = dot_nn(weights.astype(jnp.bfloat16), grad)
    grad_key = dot_nn(grad_scores, query)
    dq_ref[:, lanes] += dot_tn(key, grad_scores)
    return SCALE * grad_key, grad_value


def own_backward_kernel(q_ref, g_ref, bias_ref, row_ref, kv_ref, far_ref, quad_ref, dq_ref, dkv_ref, acc_ref, tall_ref):
    acc_ref[:, :1024] = far_ref[...]
    acc_ref[:, 1024:] = jnp.zeros((HEAD, 1024), jnp.float32)

    def one(at, carry):
        rows = pl.ds(pl.multiple_of(at * BLOCK, BLOCK), BLOCK)
        bias = [bias_ref[pl.ds(2 * at + half, 1), :] for half in (0, 1)]
        grad_key, grad_value = backward_block(kv_ref[rows, :], q_ref, g_ref, row_ref, bias, ROWS, acc_ref)
        dkv_ref[rows, :HEAD] = grad_key
        dkv_ref[rows, HEAD:] = grad_value
        return carry

    lax.fori_loop(0, ROWS // BLOCK, one, 0)
    for unit in range(8):
        lanes = slice(unit * UNIT, (unit + 1) * UNIT)
        tall_ref[lanes, :] = acc_ref[:, lanes].T * SCALE
    for at in range(0, 8 * QUADS, 8):
        tall_ref[:8, :] += SCALE * quad_ref[at : at + 8, :]
    restore_rows(lambda rows: tall_ref[rows, :], dq_ref)


def restore_rows(read, target):
    for unit, residue in enumerate(ORDER):
        for block in range(32):
            start = unit * UNIT + 8 * block
            target[pl.ds(8 * block + residue, 8, stride=256), :] = read(slice(start, start + 8))


def join_kernel(dkv_ref, b1, b2, b3, b4, b5, b6, b7, far_ref, dk_ref, dv_ref, sum_ref):
    def wide(ref, rows=slice(None)):
        return ref[rows, :].astype(jnp.float32)

    top, mid, low = slice(0, 256), slice(256, 512), slice(512, 1024)
    near = wide(b1, top) + wide(b2, top) + wide(b3, top)
    sum_ref[top, :] = dkv_ref[top, :] + near + wide(b4) + wide(b5) + wide(b6) + wide(b7)
    sum_ref[mid, :] = dkv_ref[mid, :] + wide(b1, mid) + wide(b2, mid) + wide(b3, mid)
    sum_ref[low, :] = dkv_ref[low, :] + wide(b1, low)
    sum_ref[1024:, :] = dkv_ref[1024:, :]
    sum_ref[:8, :] += jnp.sum(wide(far_ref).reshape(FAR, 8, 256), 0)
    restore_rows(lambda rows: sum_ref[rows, :HEAD], dk_ref)
    restore_rows(lambda rows: sum_ref[rows, HEAD:], dv_ref)


def swap(block, mask):
    return lax.ppermute(block, ("z", "y"), [(at, at ^ mask) for at in range(16)])


def swap_all(sends):
    near = [swap(block, mask) for block, mask in zip(sends[:5], (1, 2, 3, 4, 5))]
    last = []
    for at, (block, mask) in enumerate(zip(sends[5:], (6, 7))):
        near[3 + at], block = lax.optimization_barrier((near[3 + at], block))
        last.append(swap(block, mask))
    return near + last


def swap_quad(block):
    parts = block.reshape(QUADS, 8, block.shape[1])
    return lax.all_to_all(parts, "y", 0, 0).reshape(block.shape)


def swap_far(block):
    parts = block.reshape(FAR, 8, block.shape[1])
    return lax.all_to_all(parts, ("grp", "x", "z"), 0, 0).reshape(block.shape)


def on_device(queries, keys, values, cotangent):
    f32, bf16 = jnp.float32, jnp.bfloat16
    near_bias, other_bias = jnp.asarray(own_bias()), jnp.asarray(far_bias())
    sizes = (1024, 512, 512, 256, 256, 256, 256)

    def both(*rows):
        return [((count, 256), bf16) for count in rows]

    wide = [pltpu.VMEM((ROWS, HEAD), f32)]
    kv, s1, s2, s3, far = call(
        prepare_keys_kernel, both(ROWS, 1040, 528, 256, 8 * FAR), (keys, values, queries, cotangent), wide
    )
    peers = swap_all([s1, s2, s2, s3, s3, s3, s3])
    far = swap_far(far)
    q, g = call(prepare_queries_kernel, [((ROWS, HEAD), bf16)] * 2, (queries, cotangent, s3), wide)
    state = [((8, ROWS), f32), ((HEAD, ROWS), f32)]
    stat, out = call(own_forward_kernel, state, (q, kv, near_bias), [pltpu.VMEM((HEAD, ROWS), bf16)])
    stat, far = lax.optimization_barrier((stat, far))
    me = lax.axis_index("y").astype(jnp.int32).reshape(1)
    part, quad = call(
        whole_forward_kernel,
        [((8 * QUADS, 3 * HEAD), f32), *both(8 * QUADS)],
        (me, s2, *peers[:3], far),
        [pltpu.VMEM((8 * QUADS, 256), f32)],
        scalars=1,
    )
    part = swap_quad(part)
    stat, out = call(middle_forward_kernel, state, (q, other_bias, stat, out, *peers))
    row, tall = call(
        finish_kernel,
        [((8, ROWS), f32), ((8 * QUADS, HEAD), f32)],
        (g, stat, out, part),
        [pltpu.VMEM((8, HEAD), f32), pltpu.VMEM((HEAD, HEAD), f32)],
    )
    tall = swap_quad(tall)
    *sends, far_dq = call(
        remote_backward_kernel, [*both(*sizes), ((HEAD, 1024), f32)], (q, g, other_bias, row, *peers)
    )
    back = swap_all(sends)
    far_dq, tall = lax.optimization_barrier((far_dq, tall))
    quad_dq, far_dkv = call(
        whole_backward_kernel, [((8 * QUADS, HEAD), f32), *both(8 * FAR)], (quad, far, tall)
    )
    quad_dq = swap_quad(quad_dq)
    far_dkv = swap_far(far_dkv)
    dq, dkv = call(
        own_backward_kernel,
        [((ROWS, HEAD), f32), ((ROWS, 256), f32)],
        (q, g, near_bias, row, kv, far_dq, quad_dq),
        [pltpu.VMEM((HEAD, ROWS), f32), pltpu.VMEM((ROWS, HEAD), f32)],
    )
    dk, dv = call(join_kernel, [((ROWS, HEAD), f32)] * 2, (dkv, *back, far_dkv), [pltpu.VMEM((ROWS, 256), f32)])
    return dq, dk, dv


def solution(mesh):
    axes = ("grp", "x", "z", "y")
    split = jax.sharding.Mesh(mesh.devices.reshape(4, 4, 4, 4), axes)
    spec = P(axes, None)
    return jax.shard_map(
        on_device, mesh=split, in_specs=(spec,) * 4, out_specs=(spec,) * 3, check_vma=False
    )
```

time: 155 us -> 135 us (0.87)
  waiting for transfers between devices: 53.1 us -> 16.5 us
  local copies, waits for them, and re-layouts: 24.2 us -> 4 us
  Pallas kernels: 35.3 us -> 54.8 us
  starting transfers between devices: 40.4 us -> 57.3 us
    ppermute x10 -> x14, waiting for transfers between devices: 43.7 us -> 13.8 us  [swap(): lax.ppermute(block, ('z', 'y'), [(at, at ^ mask) for at in range(16)])]
    unnamed x68 -> x38, local copies, waits for them, and re-layouts: 24.1 us -> 4 us
    pallas_call x12 -> x10, Pallas kernels: 35.3 us -> 54.8 us  [call(): pl.pallas_call(kernel, out_shape=[jax.ShapeDtypeStruct(shape, dtype) for...]
    all_to_all x2 -> x5, starting transfers between devices: 23.1 us -> 37.5 us  [the longest x2 25.7 us: swap_far(): return lax.all_to_all(parts, ('grp', 'x', 'z'), 0, 0).reshape(block.shape)]
    all_to_all x2 -> x5, waiting for transfers between devices: 9.35 us -> 2.76 us  [the longest x3 2.75 us: swap_quad(): return lax.all_to_all(parts, 'y', 0, 0).reshape(block.shape)]
    ppermute x10 -> x14, starting transfers between devices: 17.3 us -> 19.8 us  [swap(): lax.ppermute(block, ('z', 'y'), [(at, at ^ mask) for at in range(16)])]
  transfers between devices with their start and end apart: 12 -> 19, of which waited for: 8 -> 5; matrix products, arithmetic and copies ran while one was open for 0% -> 0% of each run, Pallas kernels for 19% -> 31%
where the time goes in v4:
time: 135 us; the launch traced here: 133 us
  starting transfers between devices  57.3 us (42%)
  Pallas kernels  54.8 us (41%)
  waiting for transfers between devices  16.5 us (12%)
  local copies, waits for them, and re-layouts  4 us (3%)
    pallas_call x10, Pallas kernels, call(): pl.pallas_call(kernel, out_shape=[jax.ShapeDtypeStruct(shape, dtype) for...  54.8 us
    all_to_all x2, starting transfers between devices, swap_far(): return lax.all_to_all(parts, ('grp', 'x', 'z'), 0, 0).reshape(block.shape)  25.7 us
    ppermute x14, starting transfers between devices, swap(): lax.ppermute(block, ('z', 'y'), [(at, at ^ mask) for at in range(16)])  19.8 us
    ppermute x14, waiting for transfers between devices, swap(): lax.ppermute(block, ('z', 'y'), [(at, at ^ mask) for at in range(16)])  13.8 us
    all_to_all x3, starting transfers between devices, swap_quad(): return lax.all_to_all(parts, 'y', 0, 0).reshape(block.shape)  11.7 us
    unnamed x38, local copies, waits for them, and re-layouts  4 us
    all_to_all x3, waiting for transfers between devices, swap_quad(): return lax.all_to_all(parts, 'y', 0, 0).reshape(block.shape)  2.75 us
  transfers between devices with their start and end apart: 19, of which 5 were waited for; matrix products, arithmetic and copies ran while one was open for 0% of the time, Pallas kernels for 31%

profile of v4, /device:TPU:1, one launch (start us, length us, event | category | flops | bytes accessed | tf_op | source)
XLA Modules:
  0.0 133.5 jit_solution(4018175388583234729)
XLA Ops:
  0.6 4.4 %shard_map.85 = (bf16[2048,256]{1,0:T(8,128)(2,1)}, bf16[1040,256]{1,0:T(8,128)(2,1)}, bf16[528,256]{1,0:T(8,128)(2,1)}, bf16[256,256]{1,0:T(8,128)(2,1)}, bf16[512,256]{1,0:T(8,128)(2,1)}) custom-call(bf16[2048,128]{1,0:T(8,128)(2,1)} %k_ref.1, bf16[2048,128]{1,0:T(8,128)(2,1)} %v_ref.1, bf16[2048,128]{1,0:T(8,128)(2,1)} %q_ref.3, bf16[2048,128]{1,0:T(8,128)(2,1)} %g_ref.3), custom_call_target="tpu_custom_call" | custom-call | tf_op jit(solution)/shard_map/pallas_call | solution.py:64
  5.0 2.1 %collective-permute-start = (bf16[1040,256]{1,0:T(8,128)(2,1)}, bf16[1040,256]{1,0:T(8,128)(2,1)S(1)}, u32[]{:S(2)}, u32[]{:S(2)}) collective-permute-start(bf16[1040,256]{1,0:T(8,128)(2,1)} %get-tuple-element.52), channel_id=1, source_target_pairs={{0,1},{1,0},{2,3},{3,2},{4,5},{5,4},{6,7},{7,6},{8,9},{9,8},{10,11... | collective-permute-start | bytes 1597448 | tf_op jit(solution)/shard_map/ppermute | solution.py:329
  7.2 12.4 %all-to-all-start = ((bf16[64,8,256]{2,1,0:T(8,128)(2,1)}), bf16[64,8,256]{2,1,0:T(8,128)(2,1)S(1)}, u32[]{:S(2)}, u32[]{:S(2)}) async-start(bf16[64,8,256]{2,1,0:T(8,128)(2,1)} %bitcast.15), calls=%async_computation | async-start | bytes 524288 | tf_op jit(solution)/shard_map/all_to_all | solution.py:348
  19.6 2.0 %collective-permute-start.2 = (bf16[528,256]{1,0:T(8,128)(2,1)}, bf16[528,256]{1,0:T(8,128)(2,1)S(1)}, u32[]{:S(2)}, u32[]{:S(2)}) collective-permute-start(bf16[528,256]{1,0:T(8,128)(2,1)} %get-tuple-element.53.own), channel_id=1, source_target_pairs={{0,3},{1,2},{2,1},{3,0},{4,7},{5,6},{6,5},{7,4},{8,11},{9,10},{10,... | collective-permute-start | bytes 811016 | tf_op jit(solution)/shard_map/ppermute | solution.py:329
  21.6 0.8 collective-permute-start.1
  22.4 1.6 %collective-permute-start.4 = (bf16[256,256]{1,0:T(8,128)(2,1)}, bf16[256,256]{1,0:T(8,128)(2,1)S(1)}, u32[]{:S(2)}, u32[]{:S(2)}) collective-permute-start(bf16[256,256]{1,0:T(8,128)(2,1)} %get-tuple-element.57.after_ref), channel_id=1, source_target_pairs={{0,5},{1,4},{2,7},{3,6},{4,1},{5,0},{6,3},{7,2},{8,13},{9,12},{10,... | collective-permute-start | bytes 393224 | tf_op jit(solution)/shard_map/ppermute | solution.py:329
  24.0 0.1 collective-permute-start.3
  24.1 5.8 %collective-permute-done.4.rest_4_ = bf16[256,256]{1,0:T(8,128)(2,1)S(1)} collective-permute-done((bf16[256,256]{1,0:T(8,128)(2,1)}, bf16[256,256]{1,0:T(8,128)(2,1)S(1)}, u32[]{:S(2)}, u32[]{:S(2)}) %collective-permute-start.4) | collective-permute-done | bytes 131104 | tf_op jit(solution)/shard_map/ppermute | solution.py:329
  30.0 2.6 %collective-permute-start.6 = (bf16[256,256]{1,0:T(8,128)(2,1)}, bf16[256,256]{1,0:T(8,128)(2,1)S(1)}, u32[]{:S(2)}, u32[]{:S(2)}) collective-permute-start(bf16[256,256]{1,0:T(8,128)(2,1)} %get-tuple-element.57.after_ref), channel_id=1, source_target_pairs={{0,7},{1,6},{2,5},{3,4},{4,3},{5,2},{6,1},{7,0},{8,15},{9,14},{10,... | collective-permute-start | bytes 393224 | tf_op jit(solution)/shard_map/ppermute | solution.py:329
  32.6 0.3 collective-permute-done.3.rest_3_
  32.9 2.7 %collective-permute-start.5 = (bf16[256,256]{1,0:T(8,128)(2,1)}, bf16[256,256]{1,0:T(8,128)(2,1)S(1)}, u32[]{:S(2)}, u32[]{:S(2)}) collective-permute-start(bf16[256,256]{1,0:T(8,128)(2,1)} %get-tuple-element.57.after_ref), channel_id=1, source_target_pairs={{0,6},{1,7},{2,4},{3,5},{4,2},{5,3},{6,0},{7,1},{8,14},{9,15},{10,... | collective-permute-start | bytes 393224 | tf_op jit(solution)/shard_map/ppermute | solution.py:329
  35.6 3.3 %shard_map.86 = (bf16[2048,128]{1,0:T(8,128)(2,1)}, bf16[2048,128]{1,0:T(8,128)(2,1)}) custom-call(bf16[2048,128]{1,0:T(8,128)(2,1)} %q_ref.3, bf16[2048,128]{1,0:T(8,128)(2,1)} %g_ref.3, bf16[256,256]{1,0:T(8,128)(2,1)} %get-tuple-element.57.after_ref), custom_call_target="tpu_custom_call" | custom-call | tf_op jit(solution)/shard_map/pallas_call | solution.py:64
  38.9 8.7 %shard_map.87 = (f32[8,2048]{1,0:T(8,128)}, f32[128,2048]{1,0:T(8,128)}) custom-call(bf16[2048,128]{1,0:T(8,128)(2,1)} %get-tuple-element.45.q_ref, bf16[2048,256]{1,0:T(8,128)(2,1)} %get-tuple-element.47.kv_ref, f32[8,2048]{1,0:T(8,128)} %constant.8.clone.bias_ref), custom_call_target="tpu_custom_call" | custom-call | tf_op jit(solution)/shard_map/pallas_call | solution.py:64
  47.7 0.6 copy-done.3
  48.3 0.1 copy-done.1
  48.4 0.1 copy-done.2
  48.6 0.2 copy-done
  48.7 2.3 %shard_map.89 = (f32[32,384]{1,0:T(8,128)}, bf16[32,256]{1,0:T(8,128)(2,1)}) custom-call(s32[1]{0:T(128)} %bitcast.2.me_ref, bf16[528,256]{1,0:T(8,128)(2,1)} %get-tuple-element.53.own, bf16[1040,256]{1,0:T(8,128)(2,1)} %copy-done, bf16[528,256]{1,0:T(8,128)(2,1)} %copy-done.2, bf16[528,256]{1,0:T(8,128)(2,1)} %copy-done.1, bf16[512,256]{1,0:T(8,128)(2,1)} %bitcast.11), custom_call_target="tpu_custom_call" | custom-call | tf_op jit(solution)/shard_map/pallas_call | solution.py:64
  51.1 3.3 %all-to-all-start.1 = ((f32[4,8,384]{2,1,0:T(8,128)}), f32[4,8,384]{2,1,0:T(8,128)S(1)}, u32[]{:S(2)}, u32[]{:S(2)}) async-start(f32[4,8,384]{2,1,0:T(8,128)} %bitcast.19), calls=%async_computation.1 | async-start | bytes 98304 | tf_op jit(solution)/shard_map/all_to_all | solution.py:343
  54.4 0.6 copy-done.8
  55.0 0.1 copy-done.9
  55.1 5.8 %shard_map.88 = (f32[8,2048]{1,0:T(8,128)}, f32[128,2048]{1,0:T(8,128)}) custom-call(bf16[2048,128]{1,0:T(8,128)(2,1)} %get-tuple-element.45.q_ref, f32[8,1024]{1,0:T(8,128)} %constant.9.clone.bias_ref, f32[8,2048]{1,0:T(8,128)} %get-tuple-element.50.stat_ref, f32[128,2048]{1,0:T(8,128)} %get-tuple-element.51.out_ref, bf16[1040,256]{1,0:T(8,128)(2,1)} %copy-done, ...), custom_call_target="tpu_custom_call" | custom-call | tf_op jit(solution)/shard_map/pallas_call | solution.py:64
  60.9 0.6 copy-done.12
  61.5 2.4 %shard_map.90 = (f32[8,2048]{1,0:T(8,128)}, f32[32,128]{1,0:T(8,128)}) custom-call(bf16[2048,128]{1,0:T(8,128)(2,1)} %get-tuple-element.46.g_ref, f32[8,2048]{1,0:T(8,128)} %get-tuple-element.58.stat_ref, f32[128,2048]{1,0:T(8,128)} %get-tuple-element.59.out_ref, f32[32,384]{1,0:T(8,128)} %bitcast.16), custom_call_target="tpu_custom_call" | custom-call | tf_op jit(solution)/shard_map/pallas_call | solution.py:64
  63.9 4.2 %all-to-all-start.2 = ((f32[4,8,128]{2,1,0:T(8,128)}), f32[4,8,128]{2,1,0:T(8,128)S(1)}, u32[]{:S(2)}, u32[]{:S(2)}) async-start(f32[4,8,128]{2,1,0:T(8,128)} %bitcast.20), calls=%async_computation.2 | async-start | bytes 32768 | tf_op jit(solution)/shard_map/all_to_all | solution.py:343
  68.1 7.1 %shard_map.91 = (bf16[1024,256]{1,0:T(8,128)(2,1)}, bf16[512,256]{1,0:T(8,128)(2,1)}, bf16[512,256]{1,0:T(8,128)(2,1)}, bf16[256,256]{1,0:T(8,128)(2,1)}, bf16[2...) custom-call(bf16[2048,128]{1,0:T(8,128)(2,1)} %get-tuple-element.45.q_ref, ...), custom_call_target="tpu_custom_call" | custom-call | tf_op jit(solution)/shard_map/pallas_call | solution.py:64
  75.2 0.6 copy-done.18
  75.8 2.1 %shard_map.92 = (f32[32,128]{1,0:T(8,128)}, bf16[512,256]{1,0:T(8,128)(2,1)}) custom-call(bf16[32,256]{1,0:T(8,128)(2,1)} %get-tuple-element.66.quad_ref, bf16[512,256]{1,0:T(8,128)(2,1)} %bitcast.12, f32[32,128]{1,0:T(8,128)} %bitcast.18), custom_call_target="tpu_custom_call" | custom-call | tf_op jit(solution)/shard_map/pallas_call | solution.py:64
  77.9 4.2 %all-to-all-start.3 = ((f32[4,8,128]{2,1,0:T(8,128)}), f32[4,8,128]{2,1,0:T(8,128)S(1)}, u32[]{:S(2)}, u32[]{:S(2)}) async-start(f32[4,8,128]{2,1,0:T(8,128)} %bitcast.21), calls=%async_computation.3 | async-start | bytes 32768 | tf_op jit(solution)/shard_map/all_to_all | solution.py:343
  82.2 1.5 %collective-permute-start.7 = (bf16[1024,256]{1,0:T(8,128)(2,1)}, bf16[1024,256]{1,0:T(8,128)(2,1)S(1)}, u32[]{:S(2)}, u32[]{:S(2)}) collective-permute-start(bf16[1024,256]{1,0:T(8,128)(2,1)} %get-tuple-element.71), channel_id=1, source_target_pairs={{0,1},{1,0},{2,3},{3,2},{4,5},{5,4},{6,7},{7,6},{8,9},{9,8},{10,11... | collective-permute-start | bytes 1572872 | tf_op jit(solution)/shard_map/ppermute | solution.py:329
  83.7 2.7 %all-to-all-done.3 = f32[4,8,128]{2,1,0:T(8,128)S(1)} async-done(((f32[4,8,128]{2,1,0:T(8,128)}), f32[4,8,128]{2,1,0:T(8,128)S(1)}, u32[]{:S(2)}, u32[]{:S(2)}) %all-to-all-start.3) | async-done | bytes 16416 | tf_op jit(solution)/shard_map/all_to_all | solution.py:343
  86.4 13.3 %all-to-all-start.4 = ((bf16[64,8,256]{2,1,0:T(8,128)(2,1)}), bf16[64,8,256]{2,1,0:T(8,128)(2,1)S(1)}, u32[]{:S(2)}, u32[]{:S(2)}) async-start(bf16[64,8,256]{2,1,0:T(8,128)(2,1)} %bitcast.14), calls=%async_computation.4 | async-start | bytes 524288 | tf_op jit(solution)/shard_map/all_to_all | solution.py:348
  99.7 1.5 %collective-permute-start.10 = (bf16[256,256]{1,0:T(8,128)(2,1)}, bf16[256,256]{1,0:T(8,128)(2,1)S(1)}, u32[]{:S(2)}, u32[]{:S(2)}) collective-permute-start(bf16[256,256]{1,0:T(8,128)(2,1)} %get-tuple-element.74), channel_id=1, source_target_pairs={{0,4},{1,5},{2,6},{3,7},{4,0},{5,1},{6,2},{7,3},{8,12},{9,13},{10,... | collective-permute-start | bytes 393224 | tf_op jit(solution)/shard_map/ppermute | solution.py:329
  101.2 0.1 collective-permute-start.11
  101.3 1.8 %collective-permute-start.8 = (bf16[512,256]{1,0:T(8,128)(2,1)}, bf16[512,256]{1,0:T(8,128)(2,1)S(1)}, u32[]{:S(2)}, u32[]{:S(2)}) collective-permute-start(bf16[512,256]{1,0:T(8,128)(2,1)} %get-tuple-element.72), channel_id=1, source_target_pairs={{0,2},{1,3},{2,0},{3,1},{4,6},{5,7},{6,4},{7,5},{8,10},{9,11},{10,... | collective-permute-start | bytes 786440 | tf_op jit(solution)/shard_map/ppermute | solution.py:329
  103.1 1.8 %collective-permute-start.9 = (bf16[512,256]{1,0:T(8,128)(2,1)}, bf16[512,256]{1,0:T(8,128)(2,1)S(1)}, u32[]{:S(2)}, u32[]{:S(2)}) collective-permute-start(bf16[512,256]{1,0:T(8,128)(2,1)} %get-tuple-element.73), channel_id=1, source_target_pairs={{0,3},{1,2},{2,1},{3,0},{4,7},{5,6},{6,5},{7,4},{8,11},{9,10},{10,... | collective-permute-start | bytes 786440 | tf_op jit(solution)/shard_map/ppermute | solution.py:329
  104.8 5.3 %collective-permute-done.10.b4 = bf16[256,256]{1,0:T(8,128)(2,1)S(1)} collective-permute-done((bf16[256,256]{1,0:T(8,128)(2,1)}, bf16[256,256]{1,0:T(8,128)(2,1)S(1)}, u32[]{:S(2)}, u32[]{:S(2)}) %collective-permute-start.10) | collective-permute-done | bytes 131104 | tf_op jit(solution)/shard_map/ppermute | solution.py:329
  110.1 0.4 collective-permute-start.12
  110.6 2.4 %collective-permute-done.11.b5 = bf16[256,256]{1,0:T(8,128)(2,1)S(1)} collective-permute-done((bf16[256,256]{1,0:T(8,128)(2,1)}, bf16[256,256]{1,0:T(8,128)(2,1)S(1)}, u32[]{:S(2)}, u32[]{:S(2)}) %collective-permute-start.11) | collective-permute-done | bytes 131104 | tf_op jit(solution)/shard_map/ppermute | solution.py:329
  112.9 0.8 collective-permute-start.13
  113.7 14.2 %shard_map.93 = (f32[2048,128]{1,0:T(8,128)}, f32[2048,256]{1,0:T(8,128)}) custom-call(bf16[2048,128]{1,0:T(8,128)(2,1)} %get-tuple-element.45.q_ref, bf16[2048,128]{1,0:T(8,128)(2,1)} %get-tuple-element.46.g_ref, f32[8,2048]{1,0:T(8,128)} %constant.8.clone.bias_ref, f32[8,2048]{1,0:T(8,128)} %get-tuple-element.62.row_ref, ...), custom_call_target="tpu_custom_call" | custom-call | tf_op jit(solution)/shard_map/pallas_call | solution.py:64
  128.1 0.5 copy-done.15
  128.6 0.0 copy-done.16
  128.6 0.1 copy-done.10
  128.7 0.1 copy-done.11
  128.8 0.2 copy-done.5
  129.0 0.1 copy-done.4
  129.1 4.4 %shard_map.94 = (f32[2048,128]{1,0:T(8,128)}, f32[2048,128]{1,0:T(8,128)}) custom-call(f32[2048,256]{1,0:T(8,128)} %get-tuple-element.70.dkv_ref, bf16[1024,256]{1,0:T(8,128)(2,1)} %copy-done.5, bf16[512,256]{1,0:T(8,128)(2,1)} %copy-done.10, bf16[512,256]{1,0:T(8,128)(2,1)} %copy-done.11, bf16[256,256]{1,0:T(8,128)(2,1)} %copy-done.13, ...), custom_call_target="tpu_custom_call" | custom-call | tf_op jit(solution)/shard_map/pallas_call | solution.py:64
  (38 shorter events, 0.1 us)
Async XLA Ops:
  5.0 42.6 %collective-permute-start = (bf16[1040,256]{1,0:T(8,128)(2,1)}, bf16[1040,256]{1,0:T(8,128)(2,1)S(1)}, u32[]{:S(2)}, u32[]{:S(2)}) collective-permute-start(bf16[1040,256]{1,0:T(8,128)(2,1)} %get-tuple-element.52), channel_id=1, source_target_pairs={{0,1},{1,0},{2,3},{3,2},{4,5},{5,4},{6,7},{7,6},{8,9},{9,8},{10,11... | collective-permute-start | bytes 1597448 | tf_op jit(solution)/shard_map/ppermute | solution.py:329
  7.2 40.5 %all-to-all-start = ((bf16[64,8,256]{2,1,0:T(8,128)(2,1)}), bf16[64,8,256]{2,1,0:T(8,128)(2,1)S(1)}, u32[]{:S(2)}, u32[]{:S(2)}) async-start(bf16[64,8,256]{2,1,0:T(8,128)(2,1)} %bitcast.15), calls=%async_computation | async-start | bytes 524288 | tf_op jit(solution)/shard_map/all_to_all | solution.py:348
  19.6 28.0 %collective-permute-start.2 = (bf16[528,256]{1,0:T(8,128)(2,1)}, bf16[528,256]{1,0:T(8,128)(2,1)S(1)}, u32[]{:S(2)}, u32[]{:S(2)}) collective-permute-start(bf16[528,256]{1,0:T(8,128)(2,1)} %get-tuple-element.53.own), channel_id=1, source_target_pairs={{0,3},{1,2},{2,1},{3,0},{4,7},{5,6},{6,5},{7,4},{8,11},{9,10},{10,... | collective-permute-start | bytes 811016 | tf_op jit(solution)/shard_map/ppermute | solution.py:329
  21.6 26.0 %collective-permute-start.1 = (bf16[528,256]{1,0:T(8,128)(2,1)}, bf16[528,256]{1,0:T(8,128)(2,1)S(1)}, u32[]{:S(2)}, u32[]{:S(2)}) collective-permute-start(bf16[528,256]{1,0:T(8,128)(2,1)} %get-tuple-element.53.own), channel_id=1, source_target_pairs={{0,2},{1,3},{2,0},{3,1},{4,6},{5,7},{6,4},{7,5},{8,10},{9,11},{10,... | collective-permute-start | bytes 811016 | tf_op jit(solution)/shard_map/ppermute | solution.py:329
  22.4 7.5 %collective-permute-start.4 = (bf16[256,256]{1,0:T(8,128)(2,1)}, bf16[256,256]{1,0:T(8,128)(2,1)S(1)}, u32[]{:S(2)}, u32[]{:S(2)}) collective-permute-start(bf16[256,256]{1,0:T(8,128)(2,1)} %get-tuple-element.57.after_ref), channel_id=1, source_target_pairs={{0,5},{1,4},{2,7},{3,6},{4,1},{5,0},{6,3},{7,2},{8,13},{9,12},{10,... | collective-permute-start | bytes 393224 | tf_op jit(solution)/shard_map/ppermute | solution.py:329
  24.0 8.8 %collective-permute-start.3 = (bf16[256,256]{1,0:T(8,128)(2,1)}, bf16[256,256]{1,0:T(8,128)(2,1)S(1)}, u32[]{:S(2)}, u32[]{:S(2)}) collective-permute-start(bf16[256,256]{1,0:T(8,128)(2,1)} %get-tuple-element.57.after_ref), channel_id=1, source_target_pairs={{0,4},{1,5},{2,6},{3,7},{4,0},{5,1},{6,2},{7,3},{8,12},{9,13},{10,... | collective-permute-start | bytes 393224 | tf_op jit(solution)/shard_map/ppermute | solution.py:329
  30.0 21.1 %copy-start.6 = (bf16[256,256]{1,0:T(8,128)(2,1)}, bf16[256,256]{1,0:T(8,128)(2,1)S(1)}, u32[]{:S(2)}) copy-start(bf16[256,256]{1,0:T(8,128)(2,1)S(1)} %collective-permute-done.4.rest_4_) | copy-start | bytes 393220
  30.0 24.4 %collective-permute-start.6 = (bf16[256,256]{1,0:T(8,128)(2,1)}, bf16[256,256]{1,0:T(8,128)(2,1)S(1)}, u32[]{:S(2)}, u32[]{:S(2)}) collective-permute-start(bf16[256,256]{1,0:T(8,128)(2,1)} %get-tuple-element.57.after_ref), channel_id=1, source_target_pairs={{0,7},{1,6},{2,5},{3,4},{4,3},{5,2},{6,1},{7,0},{8,15},{9,14},{10,... | collective-permute-start | bytes 393224 | tf_op jit(solution)/shard_map/ppermute | solution.py:329
  32.9 18.2 %copy-start.7 = (bf16[256,256]{1,0:T(8,128)(2,1)}, bf16[256,256]{1,0:T(8,128)(2,1)S(1)}, u32[]{:S(2)}) copy-start(bf16[256,256]{1,0:T(8,128)(2,1)S(1)} %collective-permute-done.3.rest_3_) | copy-start | bytes 393220
  32.9 21.5 %collective-permute-start.5 = (bf16[256,256]{1,0:T(8,128)(2,1)}, bf16[256,256]{1,0:T(8,128)(2,1)S(1)}, u32[]{:S(2)}, u32[]{:S(2)}) collective-permute-start(bf16[256,256]{1,0:T(8,128)(2,1)} %get-tuple-element.57.after_ref), channel_id=1, source_target_pairs={{0,6},{1,7},{2,4},{3,5},{4,2},{5,3},{6,0},{7,1},{8,14},{9,15},{10,... | collective-permute-start | bytes 393224 | tf_op jit(solution)/shard_map/ppermute | solution.py:329
  47.6 0.7 copy-start.3
  47.6 0.8 copy-start.1
  47.6 0.9 copy-start.2
  47.7 1.1 copy-start
  51.1 9.8 %all-to-all-start.1 = ((f32[4,8,384]{2,1,0:T(8,128)}), f32[4,8,384]{2,1,0:T(8,128)S(1)}, u32[]{:S(2)}, u32[]{:S(2)}) async-start(f32[4,8,384]{2,1,0:T(8,128)} %bitcast.19), calls=%async_computation.1 | async-start | bytes 98304 | tf_op jit(solution)/shard_map/all_to_all | solution.py:343
  54.4 0.7 copy-start.8
  54.4 0.7 copy-start.9
  60.9 0.6 copy-start.12
  63.9 11.3 %all-to-all-start.2 = ((f32[4,8,128]{2,1,0:T(8,128)}), f32[4,8,128]{2,1,0:T(8,128)S(1)}, u32[]{:S(2)}, u32[]{:S(2)}) async-start(f32[4,8,128]{2,1,0:T(8,128)} %bitcast.20), calls=%async_computation.2 | async-start | bytes 32768 | tf_op jit(solution)/shard_map/all_to_all | solution.py:343
  75.2 0.6 copy-start.18
  77.9 8.5 %all-to-all-start.3 = ((f32[4,8,128]{2,1,0:T(8,128)}), f32[4,8,128]{2,1,0:T(8,128)S(1)}, u32[]{:S(2)}, u32[]{:S(2)}) async-start(f32[4,8,128]{2,1,0:T(8,128)} %bitcast.21), calls=%async_computation.3 | async-start | bytes 32768 | tf_op jit(solution)/shard_map/all_to_all | solution.py:343
  82.2 45.8 %collective-permute-start.7 = (bf16[1024,256]{1,0:T(8,128)(2,1)}, bf16[1024,256]{1,0:T(8,128)(2,1)S(1)}, u32[]{:S(2)}, u32[]{:S(2)}) collective-permute-start(bf16[1024,256]{1,0:T(8,128)(2,1)} %get-tuple-element.71), channel_id=1, source_target_pairs={{0,1},{1,0},{2,3},{3,2},{4,5},{5,4},{6,7},{7,6},{8,9},{9,8},{10,11... | collective-permute-start | bytes 1572872 | tf_op jit(solution)/shard_map/ppermute | solution.py:329
  86.4 27.3 %copy-start.17 = (f32[4,8,128]{2,1,0:T(8,128)}, f32[4,8,128]{2,1,0:T(8,128)S(1)}, u32[]{:S(2)}) copy-start(f32[4,8,128]{2,1,0:T(8,128)S(1)} %all-to-all-done.3) | copy-start | bytes 49156
  86.4 41.6 %all-to-all-start.4 = ((bf16[64,8,256]{2,1,0:T(8,128)(2,1)}), bf16[64,8,256]{2,1,0:T(8,128)(2,1)S(1)}, u32[]{:S(2)}, u32[]{:S(2)}) async-start(bf16[64,8,256]{2,1,0:T(8,128)(2,1)} %bitcast.14), calls=%async_computation.4 | async-start | bytes 524288 | tf_op jit(solution)/shard_map/all_to_all | solution.py:348
  99.7 10.4 %collective-permute-start.10 = (bf16[256,256]{1,0:T(8,128)(2,1)}, bf16[256,256]{1,0:T(8,128)(2,1)S(1)}, u32[]{:S(2)}, u32[]{:S(2)}) collective-permute-start(bf16[256,256]{1,0:T(8,128)(2,1)} %get-tuple-element.74), channel_id=1, source_target_pairs={{0,4},{1,5},{2,6},{3,7},{4,0},{5,1},{6,2},{7,3},{8,12},{9,13},{10,... | collective-permute-start | bytes 393224 | tf_op jit(solution)/shard_map/ppermute | solution.py:329
  101.2 11.8 %collective-permute-start.11 = (bf16[256,256]{1,0:T(8,128)(2,1)}, bf16[256,256]{1,0:T(8,128)(2,1)S(1)}, u32[]{:S(2)}, u32[]{:S(2)}) collective-permute-start(bf16[256,256]{1,0:T(8,128)(2,1)} %get-tuple-element.77), channel_id=1, source_target_pairs={{0,5},{1,4},{2,7},{3,6},{4,1},{5,0},{6,3},{7,2},{8,13},{9,12},{10,... | collective-permute-start | bytes 393224 | tf_op jit(solution)/shard_map/ppermute | solution.py:329
  101.3 26.7 %collective-permute-start.8 = (bf16[512,256]{1,0:T(8,128)(2,1)}, bf16[512,256]{1,0:T(8,128)(2,1)S(1)}, u32[]{:S(2)}, u32[]{:S(2)}) collective-permute-start(bf16[512,256]{1,0:T(8,128)(2,1)} %get-tuple-element.72), channel_id=1, source_target_pairs={{0,2},{1,3},{2,0},{3,1},{4,6},{5,7},{6,4},{7,5},{8,10},{9,11},{10,... | collective-permute-start | bytes 786440 | tf_op jit(solution)/shard_map/ppermute | solution.py:329
  103.1 24.9 %collective-permute-start.9 = (bf16[512,256]{1,0:T(8,128)(2,1)}, bf16[512,256]{1,0:T(8,128)(2,1)S(1)}, u32[]{:S(2)}, u32[]{:S(2)}) collective-permute-start(bf16[512,256]{1,0:T(8,128)(2,1)} %get-tuple-element.73), channel_id=1, source_target_pairs={{0,3},{1,2},{2,1},{3,0},{4,7},{5,6},{6,5},{7,4},{8,11},{9,10},{10,... | collective-permute-start | bytes 786440 | tf_op jit(solution)/shard_map/ppermute | solution.py:329
  110.1 17.9 %copy-start.13 = (bf16[256,256]{1,0:T(8,128)(2,1)}, bf16[256,256]{1,0:T(8,128)(2,1)S(1)}, u32[]{:S(2)}) copy-start(bf16[256,256]{1,0:T(8,128)(2,1)S(1)} %collective-permute-done.10.b4) | copy-start | bytes 393220
  110.1 17.8 %collective-permute-start.12 = (bf16[256,256]{1,0:T(8,128)(2,1)}, bf16[256,256]{1,0:T(8,128)(2,1)S(1)}, u32[]{:S(2)}, u32[]{:S(2)}) collective-permute-start(bf16[256,256]{1,0:T(8,128)(2,1)} %get-tuple-element.80), channel_id=1, source_target_pairs={{0,6},{1,7},{2,4},{3,5},{4,2},{5,3},{6,0},{7,1},{8,14},{9,15},{10,... | collective-permute-start | bytes 393224 | tf_op jit(solution)/shard_map/ppermute | solution.py:329
  112.9 15.1 %copy-start.14 = (bf16[256,256]{1,0:T(8,128)(2,1)}, bf16[256,256]{1,0:T(8,128)(2,1)S(1)}, u32[]{:S(2)}) copy-start(bf16[256,256]{1,0:T(8,128)(2,1)S(1)} %collective-permute-done.11.b5) | copy-start | bytes 393220
  112.9 15.0 %collective-permute-start.13 = (bf16[256,256]{1,0:T(8,128)(2,1)}, bf16[256,256]{1,0:T(8,128)(2,1)S(1)}, u32[]{:S(2)}, u32[]{:S(2)}) collective-permute-start(bf16[256,256]{1,0:T(8,128)(2,1)} %get-tuple-element.81), channel_id=1, source_target_pairs={{0,7},{1,6},{2,5},{3,4},{4,3},{5,2},{6,1},{7,0},{8,15},{9,14},{10,... | collective-permute-start | bytes 393224 | tf_op jit(solution)/shard_map/ppermute | solution.py:329
  127.9 0.6 copy-start.15
  128.0 0.7 copy-start.16
  128.0 0.8 copy-start.10
  128.0 0.8 copy-start.11
  128.0 1.0 copy-start.5
  128.0 1.0 copy-start.4

commit v5 on v4

--- a/solution.py
+++ b/solution.py
@@ -20,6 +20,7 @@
 QUADS = 4
 FAR = 64
 BLOCK = 512
+HALF = 1024
 
 
 def unit_level(unit):
@@ -60,15 +61,28 @@
     return lax.dot_general(left, right, (((0,), (0,)), ((), ())), preferred_element_type=jnp.float32)
 
 
-def call(kernel, outs, args, scratch=(), scalars=0):
+def call(kernel, outs, args, scratch=(), scalars=0, steps=(), in_steps=(), out_steps=(), in_place=None):
+    def spec(shape, stepped, at_rest, scalar=False):
+        if at_rest:
+            return pl.BlockSpec(memory_space=pl.ANY)
+        if scalar:
+            return pl.BlockSpec(memory_space=pltpu.SMEM)
+        if not steps:
+            return pl.BlockSpec(memory_space=pltpu.VMEM)
+        if stepped:
+            return pl.BlockSpec((BLOCK, shape[1]), lambda at: (at, 0))
+        return pl.BlockSpec(shape, lambda at: (0, 0))
+
     return pl.pallas_call(
         kernel,
+        grid=steps,
         out_shape=[jax.ShapeDtypeStruct(shape, dtype) for shape, dtype in outs],
-        in_specs=[
-            pl.BlockSpec(memory_space=pltpu.SMEM if at < scalars else pltpu.VMEM) for at in range(len(args))
+        in_specs=[spec(arg.shape, at in in_steps, at == in_place, at < scalars) for at, arg in enumerate(args)],
+        out_specs=[
+            spec(shape, at in out_steps, in_place is not None and at == 0) for at, (shape, _) in enumerate(outs)
         ],
-        out_specs=[pl.BlockSpec(memory_space=pltpu.VMEM)] * len(outs),
         scratch_shapes=list(scratch),
+        input_output_aliases={} if in_place is None else {in_place: 0},
         compiler_params=pltpu.CompilerParams(vmem_limit_bytes=VMEM),
         cost_estimate=pl.CostEstimate(flops=0, bytes_accessed=0, transcendentals=0),
     )(*args)
@@ -130,25 +144,39 @@
     return peak, total, out
 
 
-def own_forward_kernel(q_ref, kv_ref, bias_ref, stat_ref, out_ref, vt_ref):
+def finish_rows(row_ref, target, stat, out, grad):
+    total = stat[1:2]
+    row_ref[0:1, target] = stat[0:1] + jnp.log2(total)
+    row_ref[1:2, target] = jnp.sum(grad.astype(jnp.float32).T * out, axis=0, keepdims=True) / total
+
+
+def own_forward_kernel(q_ref, kv_ref, g_ref, bias_ref, stat_ref, out_ref, odd_ref, vt_ref):
     stat_ref[...] = jnp.zeros_like(stat_ref)
+    odd_ref[...] = jnp.zeros_like(odd_ref)
     for unit in range(8):
         rows = slice(unit * UNIT, (unit + 1) * UNIT)
         vt_ref[:, rows] = kv_ref[rows, HEAD:].astype(jnp.float32).T.astype(jnp.bfloat16)
-    for start in (0, 1024):
-        lanes = slice(start, start + 1024)
+    for start in (0, HALF):
+        lanes = slice(start, start + HALF)
         keys, values, biases = [], [], []
         for at in range(0, ROWS, BLOCK):
             rows = slice(at, at + BLOCK)
             keys.append(kv_ref[rows, :HEAD])
             values.append(lambda prob, rows=rows: dot_nn(vt_ref[:, rows], prob))
             unit = at // UNIT
-            counted = start == 0 and at < 1024
+            counted = start == 0 and at < HALF
             biases.append([bias_ref[unit + half : unit + half + 1, lanes] if counted else None for half in (0, 1)])
         peak, total, out = attend(q_ref[lanes, :], keys, values, biases)
-        stat_ref[0:1, lanes] = peak
-        stat_ref[1:2, lanes] = total
-        out_ref[:, lanes] = out
+        if start == 0:
+            stat_ref[0:1, :] = peak
+            stat_ref[1:2, :] = total
+            out_ref[...] = out
+        else:
+            stat = jnp.concatenate([peak, total], 0)
+            for first in range(0, HALF, UNIT):
+                part = slice(first, first + UNIT)
+                grad = g_ref[HALF + first : HALF + first + UNIT, :]
+                finish_rows(odd_ref, part, stat[:, part], out[:, part], grad)
 
 
 def bias_rows(bias_ref, picks, count):
@@ -224,7 +252,7 @@
     return jnp.concatenate([block, jnp.full((HEAD - 8, HEAD), fill, jnp.float32)], 0).T
 
 
-def finish_kernel(g_ref, stat_ref, out_ref, part_ref, row_ref, tall_ref, sums, acc):
+def finish_kernel(g_ref, stat_ref, out_ref, odd_ref, part_ref, row_ref, tall_ref, sums, acc):
     lanes = slice(0, HEAD)
     sums[...] = stat_ref[:, lanes]
     acc[...] = out_ref[:, lanes]
@@ -235,20 +263,35 @@
         far_total = turn(part[:, 2 * HEAD :], 0.0)[0:1]
         join_state(sums, acc, lanes, far_peak, far_total, far_out)
     row_ref[...] = jnp.zeros_like(row_ref)
-    for first in range(0, ROWS, HEAD):
+    row_ref[:, HALF:] = odd_ref[...]
+    for first in range(0, HALF, HEAD):
         lanes = slice(first, first + HEAD)
         stat, out = (sums[...], acc[...]) if first == 0 else (stat_ref[:, lanes], out_ref[:, lanes])
-        total = stat[1:2]
-        row_ref[0:1, lanes] = stat[0:1] + jnp.log2(total)
-        grad = g_ref[lanes, :].astype(jnp.float32).T
-        row_ref[1:2, lanes] = jnp.sum(grad * out, axis=0, keepdims=True) / total
+        finish_rows(row_ref, lanes, stat, out, g_ref[lanes, :])
     tall = jnp.concatenate([row_ref[:, :HEAD], jnp.zeros((HEAD - 8, HEAD), jnp.float32)], 0).T
     for at in range(0, 8 * QUADS, 8):
         tall_ref[at : at + 8, :] = tall[:8]
 
 
-def remote_backward_kernel(q_ref, g_ref, bias_ref, row_ref, *rest):
-    far, outs, dq_ref = rest[:7], rest[7:14], rest[14]
+def remote_backward_kernel(me_ref, q_ref, g_ref, bias_ref, row_ref, quad_ref, far_ref, tall_ref, *rest):
+    far, outs, (dkv_ref, dq_ref, mine_ref, quad_dq) = rest[:7], rest[7:14], rest[14:]
+    query, grad = quad_ref[:, :HEAD], quad_ref[:, HEAD:]
+    key, value = far_ref[:, :HEAD], far_ref[:, HEAD:]
+    weights = jnp.exp2(dot_nt(query, key) * SCALE2 - tall_ref[:, 0:1])
+    grad_scores = (weights * (dot_nt(grad, value) - tall_ref[:, 1:2])).astype(jnp.bfloat16)
+    dkv_ref[:, :HEAD] = (SCALE * dot_tn(grad_scores, query)).astype(jnp.bfloat16)
+    dkv_ref[:, HEAD:] = dot_tn(weights.astype(jnp.bfloat16), grad).astype(jnp.bfloat16)
+    quad_dq[...] = dot_nn(grad_scores, key)
+    for mask in range(QUADS):
+        place = pl.multiple_of((me_ref[0] ^ mask) * 8, 8)
+        block = quad_dq[pl.ds(place, 8), :]
+        if mask == 0:
+            mine_ref[...] = block
+        else:
+            block = jnp.concatenate([block, jnp.zeros_like(block)], 0)
+            block = jnp.concatenate([block, jnp.zeros_like(block)], 1).astype(jnp.bfloat16)
+            rows = outs[mask - 1].shape[0]
+            outs[mask - 1][rows - 16 :, :] = block
     dq_ref[...] = jnp.zeros_like(dq_ref)
     sources, targets = (far_blocks(refs[0], refs[1:3], refs[3:7]) for refs in (far, outs))
     for (count, blocks), (_, places) in zip(sources, targets):
@@ -256,16 +299,6 @@
             bias = bias_rows(bias_ref, picks, count)
             both = backward_block(read_block(place, slice(0, 256)), q_ref, g_ref, row_ref, bias, count, dq_ref)
             write_block(target, jnp.concatenate(both, 1).astype(jnp.bfloat16))
-
-
-def whole_backward_kernel(quad_ref, far_ref, tall_ref, dq_ref, out_ref):
-    query, grad = quad_ref[:, :HEAD], quad_ref[:, HEAD:]
-    key, value = far_ref[:, :HEAD], far_ref[:, HEAD:]
-    weights = jnp.exp2(dot_nt(query, key) * SCALE2 - tall_ref[:, 0:1])
-    grad_scores = (weights * (dot_nt(grad, value) - tall_ref[:, 1:2])).astype(jnp.bfloat16)
-    dq_ref[...] = dot_nn(grad_scores, key)
-    out_ref[:, :HEAD] = (SCALE * dot_tn(grad_scores, query)).astype(jnp.bfloat16)
-    out_ref[:, HEAD:] = dot_tn(weights.astype(jnp.bfloat16), grad).astype(jnp.bfloat16)
 
 
 def backward_block(kv_block, q_ref, g_ref, row_ref, bias, count, dq_ref):
@@ -282,25 +315,25 @@
     return SCALE * grad_key, grad_value
 
 
-def own_backward_kernel(q_ref, g_ref, bias_ref, row_ref, kv_ref, far_ref, quad_ref, dq_ref, dkv_ref, acc_ref, tall_ref):
-    acc_ref[:, :1024] = far_ref[...]
-    acc_ref[:, 1024:] = jnp.zeros((HEAD, 1024), jnp.float32)
-
-    def one(at, carry):
-        rows = pl.ds(pl.multiple_of(at * BLOCK, BLOCK), BLOCK)
-        bias = [bias_ref[pl.ds(2 * at + half, 1), :] for half in (0, 1)]
-        grad_key, grad_value = backward_block(kv_ref[rows, :], q_ref, g_ref, row_ref, bias, ROWS, acc_ref)
-        dkv_ref[rows, :HEAD] = grad_key
-        dkv_ref[rows, HEAD:] = grad_value
-        return carry
-
-    lax.fori_loop(0, ROWS // BLOCK, one, 0)
-    for unit in range(8):
-        lanes = slice(unit * UNIT, (unit + 1) * UNIT)
-        tall_ref[lanes, :] = acc_ref[:, lanes].T * SCALE
-    for at in range(0, 8 * QUADS, 8):
-        tall_ref[:8, :] += SCALE * quad_ref[at : at + 8, :]
-    restore_rows(lambda rows: tall_ref[rows, :], dq_ref)
+def own_backward_kernel(q_ref, g_ref, bias_ref, row_ref, kv_ref, far_ref, dq_ref, dkv_ref, acc_ref, tall_ref):
+    at = pl.program_id(0)
+
+    @pl.when(at == 0)
+    def _():
+        acc_ref[:, :HALF] = far_ref[...]
+        acc_ref[:, HALF:] = jnp.zeros((HEAD, HALF), jnp.float32)
+
+    bias = [bias_ref[pl.ds(2 * at + half, 1), :] for half in (0, 1)]
+    grad_key, grad_value = backward_block(kv_ref[...], q_ref, g_ref, row_ref, bias, ROWS, acc_ref)
+    dkv_ref[:, :HEAD] = grad_key
+    dkv_ref[:, HEAD:] = grad_value
+
+    @pl.when(at == ROWS // BLOCK - 1)
+    def _():
+        for unit in range(8):
+            lanes = slice(unit * UNIT, (unit + 1) * UNIT)
+            tall_ref[lanes, :] = acc_ref[:, lanes].T * SCALE
+        restore_rows(lambda rows: tall_ref[rows, :], dq_ref)
 
 
 def restore_rows(read, target):
@@ -310,10 +343,25 @@
             target[pl.ds(8 * block + residue, 8, stride=256), :] = read(slice(start, start + 8))
 
 
-def join_kernel(dkv_ref, b1, b2, b3, b4, b5, b6, b7, far_ref, dk_ref, dv_ref, sum_ref):
+def join_kernel(dkv_ref, mine_ref, b1, b2, b3, b4, b5, b6, b7, far_ref, dq_in, dq_out, dk_ref, dv_ref, sum_ref, tiles, sem):
     def wide(ref, rows=slice(None)):
         return ref[rows, :].astype(jnp.float32)
 
+    places = [(pl.ds(256 * at, 8), pl.ds(8 * at, 8)) for at in range(8)]
+    reads = [pltpu.make_async_copy(dq_in.at[rows], tiles.at[spot], sem.at[at]) for at, (rows, spot) in enumerate(places)]
+    for copy in reads:
+        copy.start()
+    mine = mine_ref[...]
+    for ref in (b1, b2, b3):
+        mine = mine + ref[ref.shape[0] - 16 :, :HEAD].astype(jnp.float32)[:8]
+    mine = SCALE * mine
+    for copy in reads:
+        copy.wait()
+    for at in range(8):
+        tiles[8 * at : 8 * at + 1, :] += mine[at : at + 1, :]
+    writes = [pltpu.make_async_copy(tiles.at[spot], dq_out.at[rows], sem.at[8 + at]) for at, (rows, spot) in enumerate(places)]
+    for copy in writes:
+        copy.start()
     top, mid, low = slice(0, 256), slice(256, 512), slice(512, 1024)
     near = wide(b1, top) + wide(b2, top) + wide(b3, top)
     sum_ref[top, :] = dkv_ref[top, :] + near + wide(b4) + wide(b5) + wide(b6) + wide(b7)
@@ -323,6 +371,8 @@
     sum_ref[:8, :] += jnp.sum(wide(far_ref).reshape(FAR, 8, 256), 0)
     restore_rows(lambda rows: sum_ref[rows, :HEAD], dk_ref)
     restore_rows(lambda rows: sum_ref[rows, HEAD:], dv_ref)
+    for copy in writes:
+        copy.wait()
 
 
 def swap(block, mask):
@@ -351,7 +401,6 @@
 def on_device(queries, keys, values, cotangent):
     f32, bf16 = jnp.float32, jnp.bfloat16
     near_bias, other_bias = jnp.asarray(own_bias()), jnp.asarray(far_bias())
-    sizes = (1024, 512, 512, 256, 256, 256, 256)
 
     def both(*rows):
         return [((count, 256), bf16) for count in rows]
@@ -361,10 +410,13 @@
         prepare_keys_kernel, both(ROWS, 1040, 528, 256, 8 * FAR), (keys, values, queries, cotangent), wide
     )
     peers = swap_all([s1, s2, s2, s3, s3, s3, s3])
+    q, g = call(prepare_queries_kernel, [((ROWS, HEAD), bf16)] * 2, (queries, cotangent, s3), wide)
+    q, far, peers[3], peers[4] = lax.optimization_barrier((q, far, peers[3], peers[4]))
     far = swap_far(far)
-    q, g = call(prepare_queries_kernel, [((ROWS, HEAD), bf16)] * 2, (queries, cotangent, s3), wide)
-    state = [((8, ROWS), f32), ((HEAD, ROWS), f32)]
-    stat, out = call(own_forward_kernel, state, (q, kv, near_bias), [pltpu.VMEM((HEAD, ROWS), bf16)])
+    state = [((8, HALF), f32), ((HEAD, HALF), f32)]
+    stat, out, odd = call(
+        own_forward_kernel, [*state, ((8, HALF), f32)], (q, kv, g, near_bias), [pltpu.VMEM((HEAD, ROWS), bf16)]
+    )
     stat, far = lax.optimization_barrier((stat, far))
     me = lax.axis_index("y").astype(jnp.int32).reshape(1)
     part, quad = call(
@@ -379,27 +431,36 @@
     row, tall = call(
         finish_kernel,
         [((8, ROWS), f32), ((8 * QUADS, HEAD), f32)],
-        (g, stat, out, part),
+        (g, stat, out, odd, part),
         [pltpu.VMEM((8, HEAD), f32), pltpu.VMEM((HEAD, HEAD), f32)],
     )
     tall = swap_quad(tall)
-    *sends, far_dq = call(
-        remote_backward_kernel, [*both(*sizes), ((HEAD, 1024), f32)], (q, g, other_bias, row, *peers)
+    *sends, far_dkv, far_dq, mine = call(
+        remote_backward_kernel,
+        [*both(1040, 528, 528, 256, 256, 256, 256, 8 * FAR), ((HEAD, HALF), f32), ((8, HEAD), f32)],
+        (me, q, g, other_bias, row, quad, far, tall, *peers),
+        [pltpu.VMEM((8 * QUADS, HEAD), f32)],
+        scalars=1,
     )
     back = swap_all(sends)
-    far_dq, tall = lax.optimization_barrier((far_dq, tall))
-    quad_dq, far_dkv = call(
-        whole_backward_kernel, [((8 * QUADS, HEAD), f32), *both(8 * FAR)], (quad, far, tall)
-    )
-    quad_dq = swap_quad(quad_dq)
+    back[3], back[4], far_dkv = lax.optimization_barrier((back[3], back[4], far_dkv))
     far_dkv = swap_far(far_dkv)
     dq, dkv = call(
         own_backward_kernel,
         [((ROWS, HEAD), f32), ((ROWS, 256), f32)],
-        (q, g, near_bias, row, kv, far_dq, quad_dq),
+        (q, g, near_bias, row, kv, far_dq),
         [pltpu.VMEM((HEAD, ROWS), f32), pltpu.VMEM((ROWS, HEAD), f32)],
-    )
-    dk, dv = call(join_kernel, [((ROWS, HEAD), f32)] * 2, (dkv, *back, far_dkv), [pltpu.VMEM((ROWS, 256), f32)])
+        steps=(ROWS // BLOCK,),
+        in_steps=(4,),
+        out_steps=(1,),
+    )
+    dq, dk, dv = call(
+        join_kernel,
+        [((ROWS, HEAD), f32)] * 3,
+        (dkv, mine, *back, far_dkv, dq),
+        [pltpu.VMEM((ROWS, 256), f32), pltpu.VMEM((64, HEAD), f32), pltpu.SemaphoreType.DMA((16,))],
+        in_place=10,
+    )
     return dq, dk, dv
 
 

time: 135 us -> 129 us (0.956)
  starting transfers between devices: 57.3 us -> 48.5 us
  blocking collectives: 0 us -> 8.51 us
  waiting for transfers between devices: 16.5 us -> 13.1 us
    all_to_all x0 -> x1, blocking collectives: none -> 8.51 us  [swap_quad(): return lax.all_to_all(parts, 'y', 0, 0).reshape(block.shape)]
    all_to_all x3 -> x1, starting transfers between devices: 11.7 us -> 3.28 us  [swap_quad(): return lax.all_to_all(parts, 'y', 0, 0).reshape(block.shape)]
    all_to_all x3 -> x1, waiting for transfers between devices: 2.75 us -> 0.01 us  [swap_quad(): return lax.all_to_all(parts, 'y', 0, 0).reshape(block.shape)]
    pallas_call x10 -> x9, Pallas kernels: 54.8 us -> 53.8 us  [call(): pl.pallas_call(kernel, grid=steps, out_shape=[jax.ShapeDtypeStruct(shape,...]
    unnamed x38 -> x34, local copies, waits for them, and re-layouts: 4 us -> 3.19 us
  transfers between devices with their start and end apart: 19 -> 17, of which waited for: 5 -> 5; matrix products, arithmetic and copies ran while one was open for 0% -> 0% of each run, Pallas kernels for 31% -> 27%
where the time goes in v5:
time: 129 us; the launch traced here: 128 us
  Pallas kernels  53.8 us (42%)
  starting transfers between devices  48.5 us (38%)
  waiting for transfers between devices  13.1 us (10%)
  blocking collectives  8.51 us (7%)
  local copies, waits for them, and re-layouts  3.19 us (2%)
    pallas_call x9, Pallas kernels, call(): pl.pallas_call(kernel, grid=steps, out_shape=[jax.ShapeDtypeStruct(shape,...  53.8 us
    all_to_all x2, starting transfers between devices, swap_far(): return lax.all_to_all(parts, ('grp', 'x', 'z'), 0, 0).reshape(block.shape)  26.4 us
    ppermute x14, starting transfers between devices, swap(): lax.ppermute(block, ('z', 'y'), [(at, at ^ mask) for at in range(16)])  18.7 us
    ppermute x14, waiting for transfers between devices, swap(): lax.ppermute(block, ('z', 'y'), [(at, at ^ mask) for at in range(16)])  13.1 us
    all_to_all x1, blocking collectives, swap_quad(): return lax.all_to_all(parts, 'y', 0, 0).reshape(block.shape)  8.51 us
    all_to_all x1, starting transfers between devices, swap_quad(): return lax.all_to_all(parts, 'y', 0, 0).reshape(block.shape)  3.28 us
    unnamed x34, local copies, waits for them, and re-layouts  3.19 us
  transfers between devices with their start and end apart: 17, of which 5 were waited for; matrix products, arithmetic and copies ran while one was open for 0% of the time, Pallas kernels for 27%

profile of v5, /device:TPU:1, one launch (start us, length us, event | category | flops | bytes accessed | tf_op | source)
XLA Modules:
  0.0 128.1 jit_solution(17851893705505288953)
XLA Ops:
  0.6 4.4 %shard_map.85 = (bf16[2048,256]{1,0:T(8,128)(2,1)}, bf16[1040,256]{1,0:T(8,128)(2,1)}, bf16[528,256]{1,0:T(8,128)(2,1)}, bf16[256,256]{1,0:T(8,128)(2,1)}, bf16[512,256]{1,0:T(8,128)(2,1)}) custom-call(bf16[2048,128]{1,0:T(8,128)(2,1)} %k_ref.1, bf16[2048,128]{1,0:T(8,128)(2,1)} %v_ref.1, bf16[2048,128]{1,0:T(8,128)(2,1)} %q_ref.3, bf16[2048,128]{1,0:T(8,128)(2,1)} %g_ref.3), custom_call_target="tpu_custom_call" | custom-call | tf_op jit(solution)/shard_map/pallas_call | solution.py:76
  5.0 3.5 %collective-permute-start.1 = (bf16[256,256]{1,0:T(8,128)(2,1)}, bf16[256,256]{1,0:T(8,128)(2,1)S(1)}, u32[]{:S(2)}, u32[]{:S(2)}) collective-permute-start(bf16[256,256]{1,0:T(8,128)(2,1)} %get-tuple-element.65.after_ref), channel_id=1, source_target_pairs={{0,5},{1,4},{2,7},{3,6},{4,1},{5,0},{6,3},{7,2},{8,13},{9,12},{10,... | collective-permute-start | bytes 393224 | tf_op jit(solution)/shard_map/ppermute | solution.py:379
  8.5 0.0 collective-permute-start
  8.5 0.3 collective-permute-start.2
  8.8 3.3 %shard_map.86 = (bf16[2048,128]{1,0:T(8,128)(2,1)}, bf16[2048,128]{1,0:T(8,128)(2,1)}) custom-call(bf16[2048,128]{1,0:T(8,128)(2,1)} %q_ref.3, bf16[2048,128]{1,0:T(8,128)(2,1)} %g_ref.3, bf16[256,256]{1,0:T(8,128)(2,1)} %get-tuple-element.65.after_ref), custom_call_target="tpu_custom_call" | custom-call | tf_op jit(solution)/shard_map/pallas_call | solution.py:76
  12.1 2.1 %collective-permute-done.rest_3_ = bf16[256,256]{1,0:T(8,128)(2,1)S(1)} collective-permute-done((bf16[256,256]{1,0:T(8,128)(2,1)}, bf16[256,256]{1,0:T(8,128)(2,1)S(1)}, u32[]{:S(2)}, u32[]{:S(2)}) %collective-permute-start) | collective-permute-done | bytes 131104 | tf_op jit(solution)/shard_map/ppermute | solution.py:379
  14.2 13.0 %all-to-all-start = ((bf16[64,8,256]{2,1,0:T(8,128)(2,1)}), bf16[64,8,256]{2,1,0:T(8,128)(2,1)S(1)}, u32[]{:S(2)}, u32[]{:S(2)}) async-start(bf16[64,8,256]{2,1,0:T(8,128)(2,1)} %bitcast.13), calls=%async_computation | async-start | bytes 524288 | tf_op jit(solution)/shard_map/all_to_all | solution.py:398
  27.3 2.0 %collective-permute-start.4 = (bf16[528,256]{1,0:T(8,128)(2,1)}, bf16[528,256]{1,0:T(8,128)(2,1)S(1)}, u32[]{:S(2)}, u32[]{:S(2)}) collective-permute-start(bf16[528,256]{1,0:T(8,128)(2,1)} %get-tuple-element.61.own), channel_id=1, source_target_pairs={{0,3},{1,2},{2,1},{3,0},{4,7},{5,6},{6,5},{7,4},{8,11},{9,10},{10,... | collective-permute-start | bytes 811016 | tf_op jit(solution)/shard_map/ppermute | solution.py:379
  29.3 0.8 collective-permute-start.3
  30.1 3.1 %collective-permute-start.6 = (bf16[256,256]{1,0:T(8,128)(2,1)}, bf16[256,256]{1,0:T(8,128)(2,1)S(1)}, u32[]{:S(2)}, u32[]{:S(2)}) collective-permute-start(bf16[256,256]{1,0:T(8,128)(2,1)} %get-tuple-element.65.after_ref), channel_id=1, source_target_pairs={{0,7},{1,6},{2,5},{3,4},{4,3},{5,2},{6,1},{7,0},{8,15},{9,14},{10,... | collective-permute-start | bytes 393224 | tf_op jit(solution)/shard_map/ppermute | solution.py:379
  33.2 0.2 collective-permute-start.5
  33.3 8.6 %shard_map.87 = (f32[8,1024]{1,0:T(8,128)}, f32[128,1024]{1,0:T(8,128)}, f32[8,1024]{1,0:T(8,128)}) custom-call(bf16[2048,128]{1,0:T(8,128)(2,1)} %get-tuple-element.53.q_ref, bf16[2048,256]{1,0:T(8,128)(2,1)} %get-tuple-element.55.kv_ref, bf16[2048,128]{1,0:T(8,128)(2,1)} %get-tuple-element.54.g_ref, f32[8,2048]{1,0:T(8,128)} %constant.8.clone.bias_ref), custom_call_target="tpu_custom_call" | custom-call | tf_op jit(solution)/shard_map/pallas_call | solution.py:76
  42.0 5.8 %collective-permute-done.4.rest_2_.r3 = bf16[528,256]{1,0:T(8,128)(2,1)S(1)} collective-permute-done((bf16[528,256]{1,0:T(8,128)(2,1)}, bf16[528,256]{1,0:T(8,128)(2,1)S(1)}, u32[]{:S(2)}, u32[]{:S(2)}) %collective-permute-start.4) | collective-permute-done | bytes 270368 | tf_op jit(solution)/shard_map/ppermute | solution.py:379
  47.8 0.0 collective-permute-done.3.rest_1_.r2
  47.8 0.0 collective-permute-done.2.rest_0_.r1
  47.8 0.0 copy-start
  47.8 0.7 copy-done.1
  48.5 0.1 copy-done.2
  48.7 0.1 copy-done
  48.8 2.3 %shard_map.89 = (f32[32,384]{1,0:T(8,128)}, bf16[32,256]{1,0:T(8,128)(2,1)}) custom-call(s32[1]{0:T(128)} %bitcast.2.me_ref, bf16[528,256]{1,0:T(8,128)(2,1)} %get-tuple-element.61.own, bf16[1040,256]{1,0:T(8,128)(2,1)} %copy-done, bf16[528,256]{1,0:T(8,128)(2,1)} %copy-done.2, bf16[528,256]{1,0:T(8,128)(2,1)} %copy-done.1, bf16[512,256]{1,0:T(8,128)(2,1)} %bitcast.9), custom_call_target="tpu_custom_call" | custom-call | tf_op jit(solution)/shard_map/pallas_call | solution.py:76
  51.1 3.3 %all-to-all-start.1 = ((f32[4,8,384]{2,1,0:T(8,128)}), f32[4,8,384]{2,1,0:T(8,128)S(1)}, u32[]{:S(2)}, u32[]{:S(2)}) async-start(f32[4,8,384]{2,1,0:T(8,128)} %bitcast.16), calls=%async_computation.1 | async-start | bytes 98304 | tf_op jit(solution)/shard_map/all_to_all | solution.py:393
  54.4 0.0 collective-permute-done.5.rest_5_
  54.5 0.6 copy-done.8
  55.1 0.1 copy-done.9
  55.1 5.5 %shard_map.88 = (f32[8,1024]{1,0:T(8,128)}, f32[128,1024]{1,0:T(8,128)}) custom-call(bf16[2048,128]{1,0:T(8,128)(2,1)} %get-tuple-element.53.q_ref, f32[8,1024]{1,0:T(8,128)} %constant.9.clone.bias_ref, f32[8,1024]{1,0:T(8,128)} %get-tuple-element.58.stat_ref, f32[128,1024]{1,0:T(8,128)} %get-tuple-element.59.out_ref, bf16[1040,256]{1,0:T(8,128)(2,1)} %copy-done, ...), custom_call_target="tpu_custom_call" | custom-call | tf_op jit(solution)/shard_map/pallas_call | solution.py:76
  60.6 0.0 all-to-all-done.1
  60.6 0.6 copy-done.12
  61.2 2.2 %shard_map.90 = (f32[8,2048]{1,0:T(8,128)}, f32[32,128]{1,0:T(8,128)}) custom-call(bf16[2048,128]{1,0:T(8,128)(2,1)} %get-tuple-element.54.g_ref, f32[8,1024]{1,0:T(8,128)} %get-tuple-element.66.stat_ref, f32[128,1024]{1,0:T(8,128)} %get-tuple-element.67.out_ref, f32[8,1024]{1,0:T(8,128)} %get-tuple-element.68.odd_ref, f32[32,384]{1,0:T(8,128)} %bitcast.14), custom_call_target="tpu_custom_call" | custom-call | tf_op jit(solution)/shard_map/pallas_call | solution.py:76
  63.4 8.5 %all_to_all.20 = f32[4,8,128]{2,1,0:T(8,128)} all-to-all(f32[4,8,128]{2,1,0:T(8,128)} %bitcast.17), channel_id=1, replica_groups=mesh['grp'=4,'x'=4,'z'=4,'y'=4] {'y'}, dimensions={0} | all-to-all | bytes 32768 | tf_op jit(solution)/shard_map/all_to_all | solution.py:393
  71.9 7.5 %shard_map.91 = (bf16[1040,256]{1,0:T(8,128)(2,1)}, bf16[528,256]{1,0:T(8,128)(2,1)}, bf16[528,256]{1,0:T(8,128)(2,1)}, bf16[256,256]{1,0:T(8,128)(2,1)}, bf16[2...) custom-call(s32[1]{0:T(128)} %bitcast.2.me_ref, ...), custom_call_target="tpu_custom_call" | custom-call | tf_op jit(solution)/shard_map/pallas_call | solution.py:76
  79.4 1.6 %collective-permute-start.10 = (bf16[256,256]{1,0:T(8,128)(2,1)}, bf16[256,256]{1,0:T(8,128)(2,1)S(1)}, u32[]{:S(2)}, u32[]{:S(2)}) collective-permute-start(bf16[256,256]{1,0:T(8,128)(2,1)} %get-tuple-element.80), channel_id=1, source_target_pairs={{0,4},{1,5},{2,6},{3,7},{4,0},{5,1},{6,2},{7,3},{8,12},{9,13},{10,... | collective-permute-start | bytes 393224 | tf_op jit(solution)/shard_map/ppermute | solution.py:379
  81.0 0.1 collective-permute-start.11
  81.1 1.2 collective-permute-start.7
  82.3 1.3 %collective-permute-done.10.b4 = bf16[256,256]{1,0:T(8,128)(2,1)S(1)} collective-permute-done((bf16[256,256]{1,0:T(8,128)(2,1)}, bf16[256,256]{1,0:T(8,128)(2,1)S(1)}, u32[]{:S(2)}, u32[]{:S(2)}) %collective-permute-start.10) | collective-permute-done | bytes 131104 | tf_op jit(solution)/shard_map/ppermute | solution.py:379
  83.5 2.5 %collective-permute-done.11.b5 = bf16[256,256]{1,0:T(8,128)(2,1)S(1)} collective-permute-done((bf16[256,256]{1,0:T(8,128)(2,1)}, bf16[256,256]{1,0:T(8,128)(2,1)S(1)}, u32[]{:S(2)}, u32[]{:S(2)}) %collective-permute-start.11) | collective-permute-done | bytes 131104 | tf_op jit(solution)/shard_map/ppermute | solution.py:379
  86.1 13.4 %all-to-all-start.3 = ((bf16[64,8,256]{2,1,0:T(8,128)(2,1)}), bf16[64,8,256]{2,1,0:T(8,128)(2,1)S(1)}, u32[]{:S(2)}, u32[]{:S(2)}) async-start(bf16[64,8,256]{2,1,0:T(8,128)(2,1)} %bitcast.12), calls=%async_computation.3 | async-start | bytes 524288 | tf_op jit(solution)/shard_map/all_to_all | solution.py:398
  99.5 1.8 %collective-permute-start.8 = (bf16[528,256]{1,0:T(8,128)(2,1)}, bf16[528,256]{1,0:T(8,128)(2,1)S(1)}, u32[]{:S(2)}, u32[]{:S(2)}) collective-permute-start(bf16[528,256]{1,0:T(8,128)(2,1)} %get-tuple-element.78), channel_id=1, source_target_pairs={{0,2},{1,3},{2,0},{3,1},{4,6},{5,7},{6,4},{7,5},{8,10},{9,11},{10,... | collective-permute-start | bytes 811016 | tf_op jit(solution)/shard_map/ppermute | solution.py:379
  101.3 1.8 %collective-permute-start.9 = (bf16[528,256]{1,0:T(8,128)(2,1)}, bf16[528,256]{1,0:T(8,128)(2,1)S(1)}, u32[]{:S(2)}, u32[]{:S(2)}) collective-permute-start(bf16[528,256]{1,0:T(8,128)(2,1)} %get-tuple-element.79), channel_id=1, source_target_pairs={{0,3},{1,2},{2,1},{3,0},{4,7},{5,6},{6,5},{7,4},{8,11},{9,10},{10,... | collective-permute-start | bytes 811016 | tf_op jit(solution)/shard_map/ppermute | solution.py:379
  103.1 0.8 collective-permute-start.12
  103.9 1.6 %collective-permute-start.13 = (bf16[256,256]{1,0:T(8,128)(2,1)}, bf16[256,256]{1,0:T(8,128)(2,1)S(1)}, u32[]{:S(2)}, u32[]{:S(2)}) collective-permute-start(bf16[256,256]{1,0:T(8,128)(2,1)} %get-tuple-element.90), channel_id=1, source_target_pairs={{0,7},{1,6},{2,5},{3,4},{4,3},{5,2},{6,1},{7,0},{8,15},{9,14},{10,... | collective-permute-start | bytes 393224 | tf_op jit(solution)/shard_map/ppermute | solution.py:379
  105.5 14.3 %shard_map.92 = (f32[2048,128]{1,0:T(8,128)}, f32[2048,256]{1,0:T(8,128)}) custom-call(bf16[2048,128]{1,0:T(8,128)(2,1)} %get-tuple-element.53.q_ref, bf16[2048,128]{1,0:T(8,128)(2,1)} %get-tuple-element.54.g_ref, f32[8,2048]{1,0:T(8,128)} %constant.8.clone.bias_ref, f32[8,2048]{1,0:T(8,128)} %get-tuple-element.71.row_ref, ...), custom_call_target="tpu_custom_call" | custom-call | tf_op jit(solution)/shard_map/pallas_call | solution.py:76
  119.8 1.3 collective-permute-done.9.b3
  121.1 0.0 collective-permute-done.7.b1
  121.1 0.0 all-to-all-done.3
  121.2 0.6 copy-done.11
  121.8 0.2 copy-done.5
  122.0 0.1 copy-done.4
  122.1 5.8 %shard_map.93 = (f32[2048,128]{1,0:T(8,128)}, f32[2048,128]{1,0:T(8,128)}, f32[2048,128]{1,0:T(8,128)}) custom-call(f32[2048,256]{1,0:T(8,128)} %get-tuple-element.75.dkv_ref, f32[8,128]{1,0:T(8,128)} %get-tuple-element.76.mine_ref, bf16[1040,256]{1,0:T(8,128)(2,1)} %copy-done.5, bf16[528,256]{1,0:T(8,128)(2,1)} %copy-done.10, ...), custom_call_target="tpu_custom_call", output_to_operand_aliasing={{0}: (10, {})} | custom-call | tf_op jit(solution)/shard_map/pallas_call | solution.py:76
  (30 shorter events, 0.1 us)
Async XLA Ops:
  5.0 7.1 %collective-permute-start.1 = (bf16[256,256]{1,0:T(8,128)(2,1)}, bf16[256,256]{1,0:T(8,128)(2,1)S(1)}, u32[]{:S(2)}, u32[]{:S(2)}) collective-permute-start(bf16[256,256]{1,0:T(8,128)(2,1)} %get-tuple-element.65.after_ref), channel_id=1, source_target_pairs={{0,5},{1,4},{2,7},{3,6},{4,1},{5,0},{6,3},{7,2},{8,13},{9,12},{10,... | collective-permute-start | bytes 393224 | tf_op jit(solution)/shard_map/ppermute | solution.py:379
  8.5 5.7 %collective-permute-start = (bf16[256,256]{1,0:T(8,128)(2,1)}, bf16[256,256]{1,0:T(8,128)(2,1)S(1)}, u32[]{:S(2)}, u32[]{:S(2)}) collective-permute-start(bf16[256,256]{1,0:T(8,128)(2,1)} %get-tuple-element.65.after_ref), channel_id=1, source_target_pairs={{0,4},{1,5},{2,6},{3,7},{4,0},{5,1},{6,2},{7,3},{8,12},{9,13},{10,... | collective-permute-start | bytes 393224 | tf_op jit(solution)/shard_map/ppermute | solution.py:379
  8.5 39.3 %collective-permute-start.2 = (bf16[1040,256]{1,0:T(8,128)(2,1)}, bf16[1040,256]{1,0:T(8,128)(2,1)S(1)}, u32[]{:S(2)}, u32[]{:S(2)}) collective-permute-start(bf16[1040,256]{1,0:T(8,128)(2,1)} %get-tuple-element.60), channel_id=1, source_target_pairs={{0,1},{1,0},{2,3},{3,2},{4,5},{5,4},{6,7},{7,6},{8,9},{9,8},{10,11... | collective-permute-start | bytes 1597448 | tf_op jit(solution)/shard_map/ppermute | solution.py:379
  12.1 39.0 %copy-start.6 = (bf16[256,256]{1,0:T(8,128)(2,1)}, bf16[256,256]{1,0:T(8,128)(2,1)S(1)}, u32[]{:S(2)}) copy-start(bf16[256,256]{1,0:T(8,128)(2,1)S(1)} %collective-permute-done.1.rest_4_) | copy-start | bytes 393220
  14.2 36.9 %copy-start.7 = (bf16[256,256]{1,0:T(8,128)(2,1)}, bf16[256,256]{1,0:T(8,128)(2,1)S(1)}, u32[]{:S(2)}) copy-start(bf16[256,256]{1,0:T(8,128)(2,1)S(1)} %collective-permute-done.rest_3_) | copy-start | bytes 393220
  14.2 27.7 %all-to-all-start = ((bf16[64,8,256]{2,1,0:T(8,128)(2,1)}), bf16[64,8,256]{2,1,0:T(8,128)(2,1)S(1)}, u32[]{:S(2)}, u32[]{:S(2)}) async-start(bf16[64,8,256]{2,1,0:T(8,128)(2,1)} %bitcast.13), calls=%async_computation | async-start | bytes 524288 | tf_op jit(solution)/shard_map/all_to_all | solution.py:398
  27.3 20.5 %collective-permute-start.4 = (bf16[528,256]{1,0:T(8,128)(2,1)}, bf16[528,256]{1,0:T(8,128)(2,1)S(1)}, u32[]{:S(2)}, u32[]{:S(2)}) collective-permute-start(bf16[528,256]{1,0:T(8,128)(2,1)} %get-tuple-element.61.own), channel_id=1, source_target_pairs={{0,3},{1,2},{2,1},{3,0},{4,7},{5,6},{6,5},{7,4},{8,11},{9,10},{10,... | collective-permute-start | bytes 811016 | tf_op jit(solution)/shard_map/ppermute | solution.py:379
  29.3 18.5 %collective-permute-start.3 = (bf16[528,256]{1,0:T(8,128)(2,1)}, bf16[528,256]{1,0:T(8,128)(2,1)S(1)}, u32[]{:S(2)}, u32[]{:S(2)}) collective-permute-start(bf16[528,256]{1,0:T(8,128)(2,1)} %get-tuple-element.61.own), channel_id=1, source_target_pairs={{0,2},{1,3},{2,0},{3,1},{4,6},{5,7},{6,4},{7,5},{8,10},{9,11},{10,... | collective-permute-start | bytes 811016 | tf_op jit(solution)/shard_map/ppermute | solution.py:379
  30.1 24.3 %collective-permute-start.6 = (bf16[256,256]{1,0:T(8,128)(2,1)}, bf16[256,256]{1,0:T(8,128)(2,1)S(1)}, u32[]{:S(2)}, u32[]{:S(2)}) collective-permute-start(bf16[256,256]{1,0:T(8,128)(2,1)} %get-tuple-element.65.after_ref), channel_id=1, source_target_pairs={{0,7},{1,6},{2,5},{3,4},{4,3},{5,2},{6,1},{7,0},{8,15},{9,14},{10,... | collective-permute-start | bytes 393224 | tf_op jit(solution)/shard_map/ppermute | solution.py:379
  33.2 21.3 %collective-permute-start.5 = (bf16[256,256]{1,0:T(8,128)(2,1)}, bf16[256,256]{1,0:T(8,128)(2,1)S(1)}, u32[]{:S(2)}, u32[]{:S(2)}) collective-permute-start(bf16[256,256]{1,0:T(8,128)(2,1)} %get-tuple-element.65.after_ref), channel_id=1, source_target_pairs={{0,6},{1,7},{2,4},{3,5},{4,2},{5,3},{6,0},{7,1},{8,14},{9,15},{10,... | collective-permute-start | bytes 393224 | tf_op jit(solution)/shard_map/ppermute | solution.py:379
  42.0 5.9 %copy-start.3 = (bf16[64,8,256]{2,1,0:T(8,128)(2,1)}, bf16[64,8,256]{2,1,0:T(8,128)(2,1)S(1)}, u32[]{:S(2)}) copy-start(bf16[64,8,256]{2,1,0:T(8,128)(2,1)S(1)} %all-to-all-done) | copy-start | bytes 786436
  47.8 0.7 copy-start.1
  47.8 0.8 copy-start.2
  47.8 1.0 copy-start
  51.1 9.5 %all-to-all-start.1 = ((f32[4,8,384]{2,1,0:T(8,128)}), f32[4,8,384]{2,1,0:T(8,128)S(1)}, u32[]{:S(2)}, u32[]{:S(2)}) async-start(f32[4,8,384]{2,1,0:T(8,128)} %bitcast.16), calls=%async_computation.1 | async-start | bytes 98304 | tf_op jit(solution)/shard_map/all_to_all | solution.py:393
  54.4 0.6 copy-start.8
  54.5 0.7 copy-start.9
  60.6 0.6 copy-start.12
  79.4 4.1 %collective-permute-start.10 = (bf16[256,256]{1,0:T(8,128)(2,1)}, bf16[256,256]{1,0:T(8,128)(2,1)S(1)}, u32[]{:S(2)}, u32[]{:S(2)}) collective-permute-start(bf16[256,256]{1,0:T(8,128)(2,1)} %get-tuple-element.80), channel_id=1, source_target_pairs={{0,4},{1,5},{2,6},{3,7},{4,0},{5,1},{6,2},{7,3},{8,12},{9,13},{10,... | collective-permute-start | bytes 393224 | tf_op jit(solution)/shard_map/ppermute | solution.py:379
  81.0 5.1 %collective-permute-start.11 = (bf16[256,256]{1,0:T(8,128)(2,1)}, bf16[256,256]{1,0:T(8,128)(2,1)S(1)}, u32[]{:S(2)}, u32[]{:S(2)}) collective-permute-start(bf16[256,256]{1,0:T(8,128)(2,1)} %get-tuple-element.83), channel_id=1, source_target_pairs={{0,5},{1,4},{2,7},{3,6},{4,1},{5,0},{6,3},{7,2},{8,13},{9,12},{10,... | collective-permute-start | bytes 393224 | tf_op jit(solution)/shard_map/ppermute | solution.py:379
  81.1 40.0 %collective-permute-start.7 = (bf16[1040,256]{1,0:T(8,128)(2,1)}, bf16[1040,256]{1,0:T(8,128)(2,1)S(1)}, u32[]{:S(2)}, u32[]{:S(2)}) collective-permute-start(bf16[1040,256]{1,0:T(8,128)(2,1)} %get-tuple-element.77), channel_id=1, source_target_pairs={{0,1},{1,0},{2,3},{3,2},{4,5},{5,4},{6,7},{7,6},{8,9},{9,8},{10,11... | collective-permute-start | bytes 1597448 | tf_op jit(solution)/shard_map/ppermute | solution.py:379
  83.5 37.6 %copy-start.13 = (bf16[256,256]{1,0:T(8,128)(2,1)}, bf16[256,256]{1,0:T(8,128)(2,1)S(1)}, u32[]{:S(2)}) copy-start(bf16[256,256]{1,0:T(8,128)(2,1)S(1)} %collective-permute-done.10.b4) | copy-start | bytes 393220
  86.1 35.1 %copy-start.14 = (bf16[256,256]{1,0:T(8,128)(2,1)}, bf16[256,256]{1,0:T(8,128)(2,1)S(1)}, u32[]{:S(2)}) copy-start(bf16[256,256]{1,0:T(8,128)(2,1)S(1)} %collective-permute-done.11.b5) | copy-start | bytes 393220
  86.1 35.0 %all-to-all-start.3 = ((bf16[64,8,256]{2,1,0:T(8,128)(2,1)}), bf16[64,8,256]{2,1,0:T(8,128)(2,1)S(1)}, u32[]{:S(2)}, u32[]{:S(2)}) async-start(bf16[64,8,256]{2,1,0:T(8,128)(2,1)} %bitcast.12), calls=%async_computation.3 | async-start | bytes 524288 | tf_op jit(solution)/shard_map/all_to_all | solution.py:398
  99.5 20.3 %collective-permute-start.8 = (bf16[528,256]{1,0:T(8,128)(2,1)}, bf16[528,256]{1,0:T(8,128)(2,1)S(1)}, u32[]{:S(2)}, u32[]{:S(2)}) collective-permute-start(bf16[528,256]{1,0:T(8,128)(2,1)} %get-tuple-element.78), channel_id=1, source_target_pairs={{0,2},{1,3},{2,0},{3,1},{4,6},{5,7},{6,4},{7,5},{8,10},{9,11},{10,... | collective-permute-start | bytes 811016 | tf_op jit(solution)/shard_map/ppermute | solution.py:379
  101.3 19.8 %collective-permute-start.9 = (bf16[528,256]{1,0:T(8,128)(2,1)}, bf16[528,256]{1,0:T(8,128)(2,1)S(1)}, u32[]{:S(2)}, u32[]{:S(2)}) collective-permute-start(bf16[528,256]{1,0:T(8,128)(2,1)} %get-tuple-element.79), channel_id=1, source_target_pairs={{0,3},{1,2},{2,1},{3,0},{4,7},{5,6},{6,5},{7,4},{8,11},{9,10},{10,... | collective-permute-start | bytes 811016 | tf_op jit(solution)/shard_map/ppermute | solution.py:379
  103.1 16.7 %collective-permute-start.12 = (bf16[256,256]{1,0:T(8,128)(2,1)}, bf16[256,256]{1,0:T(8,128)(2,1)S(1)}, u32[]{:S(2)}, u32[]{:S(2)}) collective-permute-start(bf16[256,256]{1,0:T(8,128)(2,1)} %get-tuple-element.89), channel_id=1, source_target_pairs={{0,6},{1,7},{2,4},{3,5},{4,2},{5,3},{6,0},{7,1},{8,14},{9,15},{10,... | collective-permute-start | bytes 393224 | tf_op jit(solution)/shard_map/ppermute | solution.py:379
  103.9 15.9 %collective-permute-start.13 = (bf16[256,256]{1,0:T(8,128)(2,1)}, bf16[256,256]{1,0:T(8,128)(2,1)S(1)}, u32[]{:S(2)}, u32[]{:S(2)}) collective-permute-start(bf16[256,256]{1,0:T(8,128)(2,1)} %get-tuple-element.90), channel_id=1, source_target_pairs={{0,7},{1,6},{2,5},{3,4},{4,3},{5,2},{6,1},{7,0},{8,15},{9,14},{10,... | collective-permute-start | bytes 393224 | tf_op jit(solution)/shard_map/ppermute | solution.py:379
  119.8 1.4 %copy-start.15 = (bf16[256,256]{1,0:T(8,128)(2,1)}, bf16[256,256]{1,0:T(8,128)(2,1)S(1)}, u32[]{:S(2)}) copy-start(bf16[256,256]{1,0:T(8,128)(2,1)S(1)} %collective-permute-done.12.b6) | copy-start | bytes 393220
  119.8 1.4 %copy-start.16 = (bf16[256,256]{1,0:T(8,128)(2,1)}, bf16[256,256]{1,0:T(8,128)(2,1)S(1)}, u32[]{:S(2)}) copy-start(bf16[256,256]{1,0:T(8,128)(2,1)S(1)} %collective-permute-done.13.b7) | copy-start | bytes 393220
  119.8 1.3 %copy-start.10 = (bf16[528,256]{1,0:T(8,128)(2,1)}, bf16[528,256]{1,0:T(8,128)(2,1)S(1)}, u32[]{:S(2)}) copy-start(bf16[528,256]{1,0:T(8,128)(2,1)S(1)} %collective-permute-done.8.b2) | copy-start | bytes 811012
  121.1 0.7 copy-start.11
  121.1 0.9 copy-start.5
  121.1 1.0 copy-start.4

commit v6 on v5

--- a/solution.py
+++ b/solution.py
@@ -16,7 +16,6 @@
 SCALE = HEAD**-0.5
 SCALE2 = SCALE * math.log2(math.e)
 NEG = -1e30
-VMEM = 60 << 20
 QUADS = 4
 FAR = 64
 BLOCK = 512
@@ -61,7 +60,7 @@
     return lax.dot_general(left, right, (((0,), (0,)), ((), ())), preferred_element_type=jnp.float32)
 
 
-def call(kernel, outs, args, scratch=(), scalars=0, steps=(), in_steps=(), out_steps=(), in_place=None):
+def call(kernel, outs, args, scratch=(), scalars=0, steps=(), in_steps=(), out_steps=(), in_place=None, vmem=24):
     def spec(shape, stepped, at_rest, scalar=False):
         if at_rest:
             return pl.BlockSpec(memory_space=pl.ANY)
@@ -83,7 +82,7 @@
         ],
         scratch_shapes=list(scratch),
         input_output_aliases={} if in_place is None else {in_place: 0},
-        compiler_params=pltpu.CompilerParams(vmem_limit_bytes=VMEM),
+        compiler_params=pltpu.CompilerParams(vmem_limit_bytes=vmem << 20),
         cost_estimate=pl.CostEstimate(flops=0, bytes_accessed=0, transcendentals=0),
     )(*args)
 
@@ -135,10 +134,20 @@
     return jnp.concatenate(parts, 0)
 
 
-def attend(query, keys, values, biases):
+def longest(rows):
+    wide = rows.astype(jnp.float32)
+    squares = dot_nt(jnp.ones((8, HEAD), jnp.bfloat16), (wide * wide).astype(jnp.bfloat16))
+    return 1.01 * jnp.max(squares)
+
+
+def attend(query, keys, values, biases, small=False):
     scores = [add_bias(dot_nt(key, query) * SCALE2, bias) for key, bias in zip(keys, biases)]
-    peak = functools.reduce(jnp.maximum, [jnp.max(block, 0, keepdims=True) for block in scores])
-    probs = [jnp.exp2(block - peak) for block in scores]
+    if small:
+        peak = jnp.zeros((1, query.shape[0]), jnp.float32)
+        probs = [jnp.exp2(block) for block in scores]
+    else:
+        peak = functools.reduce(jnp.maximum, [jnp.max(block, 0, keepdims=True) for block in scores])
+        probs = [jnp.exp2(block - peak) for block in scores]
     total = sum([jnp.sum(block, 0, keepdims=True) for block in probs])
     out = sum([value(block.astype(jnp.bfloat16)) for value, block in zip(values, probs)])
     return peak, total, out
@@ -156,27 +165,32 @@
     for unit in range(8):
         rows = slice(unit * UNIT, (unit + 1) * UNIT)
         vt_ref[:, rows] = kv_ref[rows, HEAD:].astype(jnp.float32).T.astype(jnp.bfloat16)
-    for start in (0, HALF):
-        lanes = slice(start, start + HALF)
-        keys, values, biases = [], [], []
-        for at in range(0, ROWS, BLOCK):
-            rows = slice(at, at + BLOCK)
-            keys.append(kv_ref[rows, :HEAD])
-            values.append(lambda prob, rows=rows: dot_nn(vt_ref[:, rows], prob))
-            unit = at // UNIT
-            counted = start == 0 and at < HALF
-            biases.append([bias_ref[unit + half : unit + half + 1, lanes] if counted else None for half in (0, 1)])
-        peak, total, out = attend(q_ref[lanes, :], keys, values, biases)
-        if start == 0:
-            stat_ref[0:1, :] = peak
-            stat_ref[1:2, :] = total
-            out_ref[...] = out
-        else:
-            stat = jnp.concatenate([peak, total], 0)
-            for first in range(0, HALF, UNIT):
-                part = slice(first, first + UNIT)
-                grad = g_ref[HALF + first : HALF + first + UNIT, :]
-                finish_rows(odd_ref, part, stat[:, part], out[:, part], grad)
+    def halves(small):
+        for start in (0, HALF):
+            lanes = slice(start, start + HALF)
+            keys, values, biases = [], [], []
+            for at in range(0, ROWS, BLOCK):
+                rows = slice(at, at + BLOCK)
+                keys.append(kv_ref[rows, :HEAD])
+                values.append(lambda prob, rows=rows: dot_nn(vt_ref[:, rows], prob))
+                unit = at // UNIT
+                counted = start == 0 and at < HALF
+                biases.append([bias_ref[unit + half : unit + half + 1, lanes] if counted else None for half in (0, 1)])
+            peak, total, out = attend(q_ref[lanes, :], keys, values, biases, small)
+            if start == 0:
+                stat_ref[0:1, :] = peak
+                stat_ref[1:2, :] = total
+                out_ref[...] = out
+            else:
+                stat = jnp.concatenate([peak, total], 0)
+                for first in range(0, HALF, UNIT):
+                    part = slice(first, first + UNIT)
+                    grad = g_ref[HALF + first : HALF + first + UNIT, :]
+                    finish_rows(odd_ref, part, stat[:, part], out[:, part], grad)
+
+    small = longest(q_ref[...]) * longest(kv_ref[:, :HEAD]) < (60.0 / SCALE2) ** 2
+    pl.when(small)(functools.partial(halves, True))
+    pl.when(jnp.logical_not(small))(functools.partial(halves, False))
 
 
 def bias_rows(bias_ref, picks, count):
@@ -186,12 +200,15 @@
 PARTNER, PARTNER_REST, SECOND, THIRD = (0, 1), (None, None), (2, None), (None, None)
 
 
-def far_blocks(r1, r2, r3):
-    return (
-        (1024, [((r1, 0), PARTNER), ((r1, BLOCK), PARTNER_REST)]),
-        (512, [((ref, 0), SECOND) for ref in r2]),
-        (256, [(r3[0:2], THIRD), (r3[2:4], THIRD)]),
-    )
+def far_blocks(refs):
+    third = (256, [(refs[-4:-2], THIRD), (refs[-2:], THIRD)])
+    if len(refs) == 4:
+        return (third,)
+    near = (
+        (1024, [((refs[0], 0), PARTNER), ((refs[0], BLOCK), PARTNER_REST)]),
+        (512, [((ref, 0), SECOND) for ref in refs[1:3]]),
+    )
+    return near if len(refs) == 3 else (*near, third)
 
 
 def read_block(place, lanes):
@@ -220,10 +237,10 @@
 
 
 def middle_forward_kernel(q_ref, bias_ref, stat_ref, out_ref, *rest):
-    r1, r2, r3, (sums, acc) = rest[0], rest[1:3], rest[3:7], rest[7:]
+    peers, (sums, acc) = rest[:7], rest[7:]
     sums[...] = stat_ref[...]
     acc[...] = out_ref[...]
-    for count, blocks in far_blocks(r1, r2, r3):
+    for count, blocks in far_blocks(peers):
         lanes = slice(0, count)
         state = attend(
             q_ref[lanes, :],
@@ -274,7 +291,7 @@
 
 
 def remote_backward_kernel(me_ref, q_ref, g_ref, bias_ref, row_ref, quad_ref, far_ref, tall_ref, *rest):
-    far, outs, (dkv_ref, dq_ref, mine_ref, quad_dq) = rest[:7], rest[7:14], rest[14:]
+    third_dq, far, outs, (dkv_ref, dq_ref, mine_ref, quad_dq) = rest[0], rest[1:4], rest[4:7], rest[7:]
     query, grad = quad_ref[:, :HEAD], quad_ref[:, HEAD:]
     key, value = far_ref[:, :HEAD], far_ref[:, HEAD:]
     weights = jnp.exp2(dot_nt(query, key) * SCALE2 - tall_ref[:, 0:1])
@@ -293,12 +310,14 @@
             rows = outs[mask - 1].shape[0]
             outs[mask - 1][rows - 16 :, :] = block
     dq_ref[...] = jnp.zeros_like(dq_ref)
-    sources, targets = (far_blocks(refs[0], refs[1:3], refs[3:7]) for refs in (far, outs))
-    for (count, blocks), (_, places) in zip(sources, targets):
-        for (place, picks), (target, _) in zip(blocks, places):
-            bias = bias_rows(bias_ref, picks, count)
-            both = backward_block(read_block(place, slice(0, 256)), q_ref, g_ref, row_ref, bias, count, dq_ref)
-            write_block(target, jnp.concatenate(both, 1).astype(jnp.bfloat16))
+    dq_ref[:, :UNIT] = third_dq[...]
+    backward_far(far, outs, (q_ref, g_ref, bias_ref, row_ref), dq_ref)
+
+
+def third_backward_kernel(q_ref, g_ref, bias_ref, row_ref, *rest):
+    far, outs, dq_ref = rest[:4], rest[4:8], rest[8]
+    dq_ref[...] = jnp.zeros_like(dq_ref)
+    backward_far(far, outs, (q_ref, g_ref, bias_ref, row_ref), dq_ref)
 
 
 def backward_block(kv_block, q_ref, g_ref, row_ref, bias, count, dq_ref):
@@ -313,6 +332,15 @@
     grad_key = dot_nn(grad_scores, query)
     dq_ref[:, lanes] += dot_tn(key, grad_scores)
     return SCALE * grad_key, grad_value
+
+
+def backward_far(far, outs, refs, dq_ref):
+    q_ref, g_ref, bias_ref, row_ref = refs
+    for (count, blocks), (_, places) in zip(far_blocks(far), far_blocks(outs)):
+        for (place, picks), (target, _) in zip(blocks, places):
+            bias = bias_rows(bias_ref, picks, count)
+            both = backward_block(read_block(place, slice(0, 256)), q_ref, g_ref, row_ref, bias, count, dq_ref)
+            write_block(target, jnp.concatenate(both, 1).astype(jnp.bfloat16))
 
 
 def own_backward_kernel(q_ref, g_ref, bias_ref, row_ref, kv_ref, far_ref, dq_ref, dkv_ref, acc_ref, tall_ref):
@@ -415,7 +443,7 @@
     far = swap_far(far)
     state = [((8, HALF), f32), ((HEAD, HALF), f32)]
     stat, out, odd = call(
-        own_forward_kernel, [*state, ((8, HALF), f32)], (q, kv, g, near_bias), [pltpu.VMEM((HEAD, ROWS), bf16)]
+        own_forward_kernel, [*state, ((8, HALF), f32)], (q, kv, g, near_bias), [pltpu.VMEM((HEAD, ROWS), bf16)], vmem=60
     )
     stat, far = lax.optimization_barrier((stat, far))
     me = lax.axis_index("y").astype(jnp.int32).reshape(1)
@@ -435,15 +463,22 @@
         [pltpu.VMEM((8, HEAD), f32), pltpu.VMEM((HEAD, HEAD), f32)],
     )
     tall = swap_quad(tall)
+    *third, third_dq = call(
+        third_backward_kernel,
+        [*both(256, 256, 256, 256), ((HEAD, UNIT), f32)],
+        (q, g, other_bias, row, *peers[3:]),
+    )
+    back = [swap(block, mask) for block, mask in zip(third, (4, 5, 6, 7))]
+    third_dq, tall = lax.optimization_barrier((third_dq, tall))
     *sends, far_dkv, far_dq, mine = call(
         remote_backward_kernel,
-        [*both(1040, 528, 528, 256, 256, 256, 256, 8 * FAR), ((HEAD, HALF), f32), ((8, HEAD), f32)],
-        (me, q, g, other_bias, row, quad, far, tall, *peers),
+        [*both(1040, 528, 528, 8 * FAR), ((HEAD, HALF), f32), ((8, HEAD), f32)],
+        (me, q, g, other_bias, row, quad, far, tall, third_dq, *peers[:3]),
         [pltpu.VMEM((8 * QUADS, HEAD), f32)],
         scalars=1,
     )
-    back = swap_all(sends)
-    back[3], back[4], far_dkv = lax.optimization_barrier((back[3], back[4], far_dkv))
+    far_dkv, *back = lax.optimization_barrier((far_dkv, *back))
+    back = [swap(block, mask) for block, mask in zip(sends, (1, 2, 3))] + back
     far_dkv = swap_far(far_dkv)
     dq, dkv = call(
         own_backward_kernel,
@@ -453,6 +488,7 @@
         steps=(ROWS // BLOCK,),
         in_steps=(4,),
         out_steps=(1,),
+        vmem=60,
     )
     dq, dk, dv = call(
         join_kernel,

time: 129 us -> 124 us (0.961)
  Pallas kernels: 53.8 us -> 40.8 us
  local copies, waits for them, and re-layouts: 3.19 us -> 15.2 us
  waiting for transfers between devices: 13.1 us -> 7.26 us
  starting transfers between devices: 48.5 us -> 50.6 us
    pallas_call x9 -> x10, Pallas kernels: 53.8 us -> 40.8 us  [call(): pl.pallas_call(kernel, grid=steps, out_shape=[jax.ShapeDtypeStruct(shape,...]
    unnamed x34 -> x46, local copies, waits for them, and re-layouts: 3.19 us -> 15.2 us
    ppermute x14, waiting for transfers between devices: 13.1 us -> 7.26 us  [swap(): lax.ppermute(block, ('z', 'y'), [(at, at ^ mask) for at in range(16)])]
    ppermute x14, starting transfers between devices: 18.7 us -> 20 us  [swap(): lax.ppermute(block, ('z', 'y'), [(at, at ^ mask) for at in range(16)])]
  transfers between devices with their start and end apart: 17 -> 17, of which waited for: 5 -> 2; matrix products, arithmetic and copies ran while one was open for 0% -> 0% of each run, Pallas kernels for 27% -> 27%
where the time goes in v6:
time: 124 us; the launch traced here: 123 us
  starting transfers between devices  50.6 us (41%)
  Pallas kernels  40.8 us (33%)
  local copies, waits for them, and re-layouts  15.2 us (12%)
  blocking collectives  8.14 us (7%)
  waiting for transfers between devices  7.26 us (6%)
    pallas_call x10, Pallas kernels, call(): pl.pallas_call(kernel, grid=steps, out_shape=[jax.ShapeDtypeStruct(shape,...  40.8 us
    all_to_all x2, starting transfers between devices, swap_far(): return lax.all_to_all(parts, ('grp', 'x', 'z'), 0, 0).reshape(block.shape)  27.3 us
    ppermute x14, starting transfers between devices, swap(): lax.ppermute(block, ('z', 'y'), [(at, at ^ mask) for at in range(16)])  20 us
    unnamed x46, local copies, waits for them, and re-layouts  15.2 us
    all_to_all x1, blocking collectives, swap_quad(): return lax.all_to_all(parts, 'y', 0, 0).reshape(block.shape)  8.14 us
    ppermute x14, waiting for transfers between devices, swap(): lax.ppermute(block, ('z', 'y'), [(at, at ^ mask) for at in range(16)])  7.26 us
    all_to_all x1, starting transfers between devices, swap_quad(): return lax.all_to_all(parts, 'y', 0, 0).reshape(block.shape)  3.27 us
  transfers between devices with their start and end apart: 17, of which 2 were waited for; matrix products, arithmetic and copies ran while one was open for 0% of the time, Pallas kernels for 27%

profile of v6, /device:TPU:1, one launch (start us, length us, event | category | flops | bytes accessed | tf_op | source)
XLA Modules:
  0.0 123.1 jit_solution(16443945138946111227)
XLA Ops:
  0.6 1.0 copy-done.6
  1.7 1.0 copy-done.8
  2.7 1.0 copy-done.11
  3.8 1.0 copy-done.12
  4.8 2.2 %shard_map.85 = (bf16[2048,256]{1,0:T(8,128)(2,1)S(1)}, bf16[1040,256]{1,0:T(8,128)(2,1)}, bf16[528,256]{1,0:T(8,128)(2,1)S(1)}, bf16[256,256]{1,0:T(8,128)(2,1)S(1)}, bf16[512,256]{1,0:T(8,128)(2,1)}) custom-call(bf16[2048,128]{1,0:T(8,128)(2,1)S(1)} %copy-done.11, bf16[2048,128]{1,0:T(8,128)(2,1)S(1)} %copy-done.12, bf16[2048,128]{1,0:T(8,128)(2,1)S(1)} %copy-done.6, ...), custom_call_target="tpu_custom_call" | custom-call | tf_op jit(solution)/shard_map/pallas_call | solution.py:75
  7.0 1.0 copy-done.4
  8.0 3.5 %collective-permute-start.1 = (bf16[256,256]{1,0:T(8,128)(2,1)S(1)}, bf16[256,256]{1,0:T(8,128)(2,1)S(1)}, u32[]{:S(2)}, u32[]{:S(2)}) collective-permute-start(bf16[256,256]{1,0:T(8,128)(2,1)S(1)} %get-tuple-element.66.after_ref), channel_id=1, source_target_pairs={{0,5},{1,4},{2,7},{3,6},{4,1},{5,0},{6,3},{7,2},{8,13},{9,12},{10,... | collective-permute-start | bytes 393224 | tf_op jit(solution)/shard_map/ppermute | solution.py:407
  11.5 0.0 collective-permute-start
  11.5 0.3 collective-permute-start.2
  11.8 1.3 %shard_map.86 = (bf16[2048,128]{1,0:T(8,128)(2,1)S(1)}, bf16[2048,128]{1,0:T(8,128)(2,1)S(1)}) custom-call(bf16[2048,128]{1,0:T(8,128)(2,1)S(1)} %copy-done.7, bf16[2048,128]{1,0:T(8,128)(2,1)S(1)} %copy-done.9, bf16[256,256]{1,0:T(8,128)(2,1)S(1)} %get-tuple-element.66.after_ref), custom_call_target="tpu_custom_call" | custom-call | tf_op jit(solution)/shard_map/pallas_call | solution.py:75
  13.1 0.8 copy-done
  13.8 0.8 copy-done.2
  14.7 2.4 %collective-permute-done.rest_3_.rest_0_ = bf16[256,256]{1,0:T(8,128)(2,1)S(1)} collective-permute-done((bf16[256,256]{1,0:T(8,128)(2,1)S(1)}, bf16[256,256]{1,0:T(8,128)(2,1)S(1)}, u32[]{:S(2)}, u32[]{:S(2)}) %collective-permute-start) | collective-permute-done | bytes 131104 | tf_op jit(solution)/shard_map/ppermute | solution.py:407
  17.0 13.2 %all-to-all-start = ((bf16[64,8,256]{2,1,0:T(8,128)(2,1)}), bf16[64,8,256]{2,1,0:T(8,128)(2,1)S(1)}, u32[]{:S(2)}, u32[]{:S(2)}) async-start(bf16[64,8,256]{2,1,0:T(8,128)(2,1)} %bitcast), calls=%async_computation | async-start | bytes 524288 | tf_op jit(solution)/shard_map/all_to_all | solution.py:426
  30.2 2.0 %collective-permute-start.4 = (bf16[528,256]{1,0:T(8,128)(2,1)S(1)}, bf16[528,256]{1,0:T(8,128)(2,1)S(1)}, u32[]{:S(2)}, u32[]{:S(2)}) collective-permute-start(bf16[528,256]{1,0:T(8,128)(2,1)S(1)} %get-tuple-element.62.own), channel_id=1, source_target_pairs={{0,3},{1,2},{2,1},{3,0},{4,7},{5,6},{6,5},{7,4},{8,11},{9,10},{10,... | collective-permute-start | bytes 811016 | tf_op jit(solution)/shard_map/ppermute | solution.py:407
  32.2 0.8 collective-permute-start.3
  33.0 3.1 %collective-permute-start.6 = (bf16[256,256]{1,0:T(8,128)(2,1)S(1)}, bf16[256,256]{1,0:T(8,128)(2,1)S(1)}, u32[]{:S(2)}, u32[]{:S(2)}) collective-permute-start(bf16[256,256]{1,0:T(8,128)(2,1)S(1)} %get-tuple-element.66.after_ref), channel_id=1, source_target_pairs={{0,7},{1,6},{2,5},{3,4},{4,3},{5,2},{6,1},{7,0},{8,15},{9,14},{10,... | collective-permute-start | bytes 393224 | tf_op jit(solution)/shard_map/ppermute | solution.py:407
  36.1 0.2 collective-permute-start.5
  36.3 9.4 %shard_map.87 = (f32[8,1024]{1,0:T(8,128)}, f32[128,1024]{1,0:T(8,128)}, f32[8,1024]{1,0:T(8,128)}) custom-call(bf16[2048,128]{1,0:T(8,128)(2,1)} %copy-done, bf16[2048,256]{1,0:T(8,128)(2,1)} %copy-done.4, bf16[2048,128]{1,0:T(8,128)(2,1)} %copy-done.2, f32[8,2048]{1,0:T(8,128)} %constant.8.clone.bias_ref), custom_call_target="tpu_custom_call" | custom-call | tf_op jit(solution)/shard_map/pallas_call | solution.py:75
  45.6 4.9 %collective-permute-done.4.rest_2_.r3.rest_3_ = bf16[528,256]{1,0:T(8,128)(2,1)S(1)} collective-permute-done((bf16[528,256]{1,0:T(8,128)(2,1)S(1)}, bf16[528,256]{1,0:T(8,128)(2,1)S(1)}, u32[]{:S(2)}, u32[]{:S(2)}) %collective-permute-start.4) | collective-permute-done | bytes 270368 | tf_op jit(solution)/shard_map/ppermute | solution.py:407
  50.5 1.0 shard_map.89
  51.5 3.3 %all-to-all-start.1 = ((f32[4,8,384]{2,1,0:T(8,128)}), f32[4,8,384]{2,1,0:T(8,128)S(1)}, u32[]{:S(2)}, u32[]{:S(2)}) async-start(f32[4,8,384]{2,1,0:T(8,128)} %bitcast.3), calls=%async_computation.1 | async-start | bytes 98304 | tf_op jit(solution)/shard_map/all_to_all | solution.py:421
  54.8 0.0 copy-start.14
  54.8 1.0 copy-done.14
  55.9 0.8 copy-done.18
  56.6 3.0 %shard_map.88 = (f32[8,1024]{1,0:T(8,128)S(1)}, f32[128,1024]{1,0:T(8,128)S(1)}) custom-call(bf16[2048,128]{1,0:T(8,128)(2,1)S(1)} %copy-done.1, f32[8,1024]{1,0:T(8,128)S(1)} %copy-done.15, f32[8,1024]{1,0:T(8,128)S(1)} %copy-done.18, f32[128,1024]{1,0:T(8,128)S(1)} %copy-done.14, bf16[1040,256]{1,0:T(8,128)(2,1)S(1)} %collective-permute-done.2.rest_0_.r1.rest_1_, ...), custom_call_target="tpu_custom_call" | custom-call | tf_op jit(solution)/shard_map/pallas_call | solution.py:75
  59.6 0.0 copy-start.20
  59.7 0.6 copy-done.20
  60.3 0.6 copy-done.16
  60.9 0.8 copy-done.17
  61.7 0.8 copy-done.19
  62.4 0.8 copy-done.21
  63.2 0.3 shard_map.90
  63.5 0.9 shard_map.91
  64.4 1.6 %collective-permute-start.10 = (bf16[256,256]{1,0:T(8,128)(2,1)S(1)}, bf16[256,256]{1,0:T(8,128)(2,1)S(1)}, u32[]{:S(2)}, u32[]{:S(2)}) collective-permute-start(bf16[256,256]{1,0:T(8,128)(2,1)S(1)} %get-tuple-element.85), channel_id=1, source_target_pairs={{0,4},{1,5},{2,6},{3,7},{4,0},{5,1},{6,2},{7,3},{8,12},{9,13},{10,... | collective-permute-start | bytes 393224 | tf_op jit(solution)/shard_map/ppermute | solution.py:407
  66.0 1.2 collective-permute-start.11
  67.2 3.5 %collective-permute-start.12 = (bf16[256,256]{1,0:T(8,128)(2,1)S(1)}, bf16[256,256]{1,0:T(8,128)(2,1)S(1)}, u32[]{:S(2)}, u32[]{:S(2)}) collective-permute-start(bf16[256,256]{1,0:T(8,128)(2,1)S(1)} %get-tuple-element.87), channel_id=1, source_target_pairs={{0,6},{1,7},{2,4},{3,5},{4,2},{5,3},{6,0},{7,1},{8,14},{9,15},{10,... | collective-permute-start | bytes 393224 | tf_op jit(solution)/shard_map/ppermute | solution.py:407
  70.7 8.1 %all_to_all.20 = f32[4,8,128]{2,1,0:T(8,128)S(1)} all-to-all(f32[4,8,128]{2,1,0:T(8,128)S(1)} %bitcast.14), channel_id=1, replica_groups=mesh['grp'=4,'x'=4,'z'=4,'y'=4] {'y'}, dimensions={0} | all-to-all | bytes 32768 | tf_op jit(solution)/shard_map/all_to_all | solution.py:421
  78.8 4.8 %shard_map.92 = (bf16[1040,256]{1,0:T(8,128)(2,1)}, bf16[528,256]{1,0:T(8,128)(2,1)S(1)}, bf16[528,256]{1,0:T(8,128)(2,1)S(1)}, bf16[512,256]{1,0:T(8,128)(2,1)}...) custom-call(s32[1]{0:T(128)} %bitcast.2.me_ref, bf16[2048,128]{1,0:T(8,128)(2,1)S(1)} %copy-done.1, ...), custom_call_target="tpu_custom_call" | custom-call | tf_op jit(solution)/shard_map/pallas_call | solution.py:75
  83.6 0.8 copy-done.13
  84.4 0.7 copy-done.22
  85.1 0.3 collective-permute-start.7
  85.4 14.2 %all-to-all-start.3 = ((bf16[64,8,256]{2,1,0:T(8,128)(2,1)}), bf16[64,8,256]{2,1,0:T(8,128)(2,1)S(1)}, u32[]{:S(2)}, u32[]{:S(2)}) async-start(bf16[64,8,256]{2,1,0:T(8,128)(2,1)} %bitcast.7), calls=%async_computation.3 | async-start | bytes 524288 | tf_op jit(solution)/shard_map/all_to_all | solution.py:426
  99.6 1.9 %collective-permute-start.8 = (bf16[528,256]{1,0:T(8,128)(2,1)}, bf16[528,256]{1,0:T(8,128)(2,1)S(1)}, u32[]{:S(2)}, u32[]{:S(2)}) collective-permute-start(bf16[528,256]{1,0:T(8,128)(2,1)} %copy-done.22), channel_id=1, source_target_pairs={{0,2},{1,3},{2,0},{3,1},{4,6},{5,7},{6,4},{7,5},{8,10},{9,11},{10,... | collective-permute-start | bytes 811016 | tf_op jit(solution)/shard_map/ppermute | solution.py:407
  101.5 1.8 %collective-permute-start.9 = (bf16[528,256]{1,0:T(8,128)(2,1)S(1)}, bf16[528,256]{1,0:T(8,128)(2,1)S(1)}, u32[]{:S(2)}, u32[]{:S(2)}) collective-permute-start(bf16[528,256]{1,0:T(8,128)(2,1)S(1)} %get-tuple-element.83), channel_id=1, source_target_pairs={{0,3},{1,2},{2,1},{3,0},{4,7},{5,6},{6,5},{7,4},{8,11},{9,10},{10,... | collective-permute-start | bytes 811016 | tf_op jit(solution)/shard_map/ppermute | solution.py:407
  103.3 14.2 %shard_map.93 = (f32[2048,128]{1,0:T(8,128)}, f32[2048,256]{1,0:T(8,128)}) custom-call(bf16[2048,128]{1,0:T(8,128)(2,1)} %copy-done, bf16[2048,128]{1,0:T(8,128)(2,1)} %copy-done.2, f32[8,2048]{1,0:T(8,128)} %constant.8.clone.bias_ref, f32[8,2048]{1,0:T(8,128)} %copy-done.10, bf16[2048,256]{1,0:T(8,128)(2,1)} %copy-done.4, f32[128,1024]{1,0:T(8,128)} %copy-done.13), custom_call_target="tpu_custom_call" | custom-call | tf_op jit(solution)/shard_map/pallas_call | solution.py:75
  117.5 1.6 %copy-done.5 = f32[2048,256]{1,0:T(8,128)S(1)} copy-done((f32[2048,256]{1,0:T(8,128)S(1)}, f32[2048,256]{1,0:T(8,128)}, u32[]{:S(2)}) %copy-start.5) | copy-done | bytes 2097176
  119.1 3.8 %shard_map.94 = (f32[2048,128]{1,0:T(8,128)}, f32[2048,128]{1,0:T(8,128)}, f32[2048,128]{1,0:T(8,128)}) custom-call(f32[2048,256]{1,0:T(8,128)S(1)} %copy-done.5, f32[8,128]{1,0:T(8,128)S(1)} %get-tuple-element.80.mine_ref, bf16[1040,256]{1,0:T(8,128)(2,1)S(1)} %collective-permute-done.7.b1, ...), custom_call_target="tpu_custom_call", output_to_operand_aliasing={{0}: (10, {})} | custom-call | tf_op jit(solution)/shard_map/pallas_call | solution.py:75
  (43 shorter events, 0.1 us)
Async XLA Ops:
  0.6 1.0 copy-start.6
  1.7 1.0 copy-start.8
  2.7 1.0 copy-start.11
  3.8 1.0 copy-start.12
  4.8 7.0 %copy-start.7 = (bf16[2048,128]{1,0:T(8,128)(2,1)S(1)}, bf16[2048,128]{1,0:T(8,128)(2,1)}, u32[]{:S(2)}) copy-start(bf16[2048,128]{1,0:T(8,128)(2,1)} %q_ref.3) | copy-start | bytes 1572868
  4.8 7.0 %copy-start.9 = (bf16[2048,128]{1,0:T(8,128)(2,1)S(1)}, bf16[2048,128]{1,0:T(8,128)(2,1)}, u32[]{:S(2)}) copy-start(bf16[2048,128]{1,0:T(8,128)(2,1)} %g_ref.3) | copy-start | bytes 1572868
  7.0 1.0 copy-start.4
  8.0 6.7 %collective-permute-start.1 = (bf16[256,256]{1,0:T(8,128)(2,1)S(1)}, bf16[256,256]{1,0:T(8,128)(2,1)S(1)}, u32[]{:S(2)}, u32[]{:S(2)}) collective-permute-start(bf16[256,256]{1,0:T(8,128)(2,1)S(1)} %get-tuple-element.66.after_ref), channel_id=1, source_target_pairs={{0,5},{1,4},{2,7},{3,6},{4,1},{5,0},{6,3},{7,2},{8,13},{9,12},{10,... | collective-permute-start | bytes 393224 | tf_op jit(solution)/shard_map/ppermute | solution.py:407
  11.5 5.5 %collective-permute-start = (bf16[256,256]{1,0:T(8,128)(2,1)S(1)}, bf16[256,256]{1,0:T(8,128)(2,1)S(1)}, u32[]{:S(2)}, u32[]{:S(2)}) collective-permute-start(bf16[256,256]{1,0:T(8,128)(2,1)S(1)} %get-tuple-element.66.after_ref), channel_id=1, source_target_pairs={{0,4},{1,5},{2,6},{3,7},{4,0},{5,1},{6,2},{7,3},{8,12},{9,13},{10,... | collective-permute-start | bytes 393224 | tf_op jit(solution)/shard_map/ppermute | solution.py:407
  11.5 39.0 %collective-permute-start.2 = (bf16[1040,256]{1,0:T(8,128)(2,1)}, bf16[1040,256]{1,0:T(8,128)(2,1)S(1)}, u32[]{:S(2)}, u32[]{:S(2)}) collective-permute-start(bf16[1040,256]{1,0:T(8,128)(2,1)} %get-tuple-element.61), channel_id=1, source_target_pairs={{0,1},{1,0},{2,3},{3,2},{4,5},{5,4},{6,7},{7,6},{8,9},{9,8},{10,11... | collective-permute-start | bytes 1597448 | tf_op jit(solution)/shard_map/ppermute | solution.py:407
  13.0 0.8 copy-start
  13.8 0.8 copy-start.2
  17.0 37.8 %copy-start.1 = (bf16[2048,128]{1,0:T(8,128)(2,1)S(1)}, bf16[2048,128]{1,0:T(8,128)(2,1)}, u32[]{:S(2)}) copy-start(bf16[2048,128]{1,0:T(8,128)(2,1)} %copy-done) | copy-start | bytes 1572868
  17.0 37.8 %copy-start.15 = (f32[8,1024]{1,0:T(8,128)S(1)}, f32[8,1024]{1,0:T(8,128)}, u32[]{:S(2)}) copy-start(f32[8,1024]{1,0:T(8,128)} %constant.9.clone.bias_ref) | copy-start | bytes 98308
  17.0 28.6 %all-to-all-start = ((bf16[64,8,256]{2,1,0:T(8,128)(2,1)}), bf16[64,8,256]{2,1,0:T(8,128)(2,1)S(1)}, u32[]{:S(2)}, u32[]{:S(2)}) async-start(bf16[64,8,256]{2,1,0:T(8,128)(2,1)} %bitcast), calls=%async_computation | async-start | bytes 524288 | tf_op jit(solution)/shard_map/all_to_all | solution.py:426
  30.2 20.3 %collective-permute-start.4 = (bf16[528,256]{1,0:T(8,128)(2,1)S(1)}, bf16[528,256]{1,0:T(8,128)(2,1)S(1)}, u32[]{:S(2)}, u32[]{:S(2)}) collective-permute-start(bf16[528,256]{1,0:T(8,128)(2,1)S(1)} %get-tuple-element.62.own), channel_id=1, source_target_pairs={{0,3},{1,2},{2,1},{3,0},{4,7},{5,6},{6,5},{7,4},{8,11},{9,10},{10,... | collective-permute-start | bytes 811016 | tf_op jit(solution)/shard_map/ppermute | solution.py:407
  32.2 18.3 %collective-permute-start.3 = (bf16[528,256]{1,0:T(8,128)(2,1)S(1)}, bf16[528,256]{1,0:T(8,128)(2,1)S(1)}, u32[]{:S(2)}, u32[]{:S(2)}) collective-permute-start(bf16[528,256]{1,0:T(8,128)(2,1)S(1)} %get-tuple-element.62.own), channel_id=1, source_target_pairs={{0,2},{1,3},{2,0},{3,1},{4,6},{5,7},{6,4},{7,5},{8,10},{9,11},{10,... | collective-permute-start | bytes 811016 | tf_op jit(solution)/shard_map/ppermute | solution.py:407
  33.0 21.8 %collective-permute-start.6 = (bf16[256,256]{1,0:T(8,128)(2,1)S(1)}, bf16[256,256]{1,0:T(8,128)(2,1)S(1)}, u32[]{:S(2)}, u32[]{:S(2)}) collective-permute-start(bf16[256,256]{1,0:T(8,128)(2,1)S(1)} %get-tuple-element.66.after_ref), channel_id=1, source_target_pairs={{0,7},{1,6},{2,5},{3,4},{4,3},{5,2},{6,1},{7,0},{8,15},{9,14},{10,... | collective-permute-start | bytes 393224 | tf_op jit(solution)/shard_map/ppermute | solution.py:407
  36.1 18.7 %collective-permute-start.5 = (bf16[256,256]{1,0:T(8,128)(2,1)S(1)}, bf16[256,256]{1,0:T(8,128)(2,1)S(1)}, u32[]{:S(2)}, u32[]{:S(2)}) collective-permute-start(bf16[256,256]{1,0:T(8,128)(2,1)S(1)} %get-tuple-element.66.after_ref), channel_id=1, source_target_pairs={{0,6},{1,7},{2,4},{3,5},{4,2},{5,3},{6,0},{7,1},{8,14},{9,15},{10,... | collective-permute-start | bytes 393224 | tf_op jit(solution)/shard_map/ppermute | solution.py:407
  50.5 10.4 %copy-start.3 = (bf16[2048,128]{1,0:T(8,128)(2,1)S(1)}, bf16[2048,128]{1,0:T(8,128)(2,1)}, u32[]{:S(2)}) copy-start(bf16[2048,128]{1,0:T(8,128)(2,1)} %copy-done.2) | copy-start | bytes 1572868
  51.5 8.7 %all-to-all-start.1 = ((f32[4,8,384]{2,1,0:T(8,128)}), f32[4,8,384]{2,1,0:T(8,128)S(1)}, u32[]{:S(2)}, u32[]{:S(2)}) async-start(f32[4,8,384]{2,1,0:T(8,128)} %bitcast.3), calls=%async_computation.1 | async-start | bytes 98304 | tf_op jit(solution)/shard_map/all_to_all | solution.py:421
  54.8 1.0 copy-start.14
  55.9 0.8 copy-start.18
  59.6 0.6 copy-start.20
  60.3 0.6 copy-start.16
  60.9 0.8 copy-start.17
  61.7 0.8 copy-start.19
  62.4 0.8 copy-start.21
  63.5 20.1 %copy-start.10 = (f32[8,2048]{1,0:T(8,128)}, f32[8,2048]{1,0:T(8,128)S(1)}, u32[]{:S(2)}) copy-start(f32[8,2048]{1,0:T(8,128)S(1)} %get-tuple-element.72.row_ref) | copy-start | bytes 196612
  64.4 21.0 %collective-permute-start.10 = (bf16[256,256]{1,0:T(8,128)(2,1)S(1)}, bf16[256,256]{1,0:T(8,128)(2,1)S(1)}, u32[]{:S(2)}, u32[]{:S(2)}) collective-permute-start(bf16[256,256]{1,0:T(8,128)(2,1)S(1)} %get-tuple-element.85), channel_id=1, source_target_pairs={{0,4},{1,5},{2,6},{3,7},{4,0},{5,1},{6,2},{7,3},{8,12},{9,13},{10,... | collective-permute-start | bytes 393224 | tf_op jit(solution)/shard_map/ppermute | solution.py:407
  66.0 19.4 %collective-permute-start.11 = (bf16[256,256]{1,0:T(8,128)(2,1)S(1)}, bf16[256,256]{1,0:T(8,128)(2,1)S(1)}, u32[]{:S(2)}, u32[]{:S(2)}) collective-permute-start(bf16[256,256]{1,0:T(8,128)(2,1)S(1)} %get-tuple-element.86), channel_id=1, source_target_pairs={{0,5},{1,4},{2,7},{3,6},{4,1},{5,0},{6,3},{7,2},{8,13},{9,12},{10,... | collective-permute-start | bytes 393224 | tf_op jit(solution)/shard_map/ppermute | solution.py:407
  67.2 18.2 %collective-permute-start.12 = (bf16[256,256]{1,0:T(8,128)(2,1)S(1)}, bf16[256,256]{1,0:T(8,128)(2,1)S(1)}, u32[]{:S(2)}, u32[]{:S(2)}) collective-permute-start(bf16[256,256]{1,0:T(8,128)(2,1)S(1)} %get-tuple-element.87), channel_id=1, source_target_pairs={{0,6},{1,7},{2,4},{3,5},{4,2},{5,3},{6,0},{7,1},{8,14},{9,15},{10,... | collective-permute-start | bytes 393224 | tf_op jit(solution)/shard_map/ppermute | solution.py:407
  70.7 14.8 %collective-permute-start.13 = (bf16[256,256]{1,0:T(8,128)(2,1)S(1)}, bf16[256,256]{1,0:T(8,128)(2,1)S(1)}, u32[]{:S(2)}, u32[]{:S(2)}) collective-permute-start(bf16[256,256]{1,0:T(8,128)(2,1)S(1)} %get-tuple-element.88), channel_id=1, source_target_pairs={{0,7},{1,6},{2,5},{3,4},{4,3},{5,2},{6,1},{7,0},{8,15},{9,14},{10,... | collective-permute-start | bytes 393224 | tf_op jit(solution)/shard_map/ppermute | solution.py:407
  83.6 0.8 copy-start.13
  84.4 0.7 copy-start.22
  85.1 32.4 %collective-permute-start.7 = (bf16[1040,256]{1,0:T(8,128)(2,1)}, bf16[1040,256]{1,0:T(8,128)(2,1)S(1)}, u32[]{:S(2)}, u32[]{:S(2)}) collective-permute-start(bf16[1040,256]{1,0:T(8,128)(2,1)} %get-tuple-element.81), channel_id=1, source_target_pairs={{0,1},{1,0},{2,3},{3,2},{4,5},{5,4},{6,7},{7,6},{8,9},{9,8},{10,11... | collective-permute-start | bytes 1597448 | tf_op jit(solution)/shard_map/ppermute | solution.py:407
  85.4 32.1 %all-to-all-start.3 = ((bf16[64,8,256]{2,1,0:T(8,128)(2,1)}), bf16[64,8,256]{2,1,0:T(8,128)(2,1)S(1)}, u32[]{:S(2)}, u32[]{:S(2)}) async-start(bf16[64,8,256]{2,1,0:T(8,128)(2,1)} %bitcast.7), calls=%async_computation.3 | async-start | bytes 524288 | tf_op jit(solution)/shard_map/all_to_all | solution.py:426
  99.6 17.9 %collective-permute-start.8 = (bf16[528,256]{1,0:T(8,128)(2,1)}, bf16[528,256]{1,0:T(8,128)(2,1)S(1)}, u32[]{:S(2)}, u32[]{:S(2)}) collective-permute-start(bf16[528,256]{1,0:T(8,128)(2,1)} %copy-done.22), channel_id=1, source_target_pairs={{0,2},{1,3},{2,0},{3,1},{4,6},{5,7},{6,4},{7,5},{8,10},{9,11},{10,... | collective-permute-start | bytes 811016 | tf_op jit(solution)/shard_map/ppermute | solution.py:407
  101.5 16.0 %collective-permute-start.9 = (bf16[528,256]{1,0:T(8,128)(2,1)S(1)}, bf16[528,256]{1,0:T(8,128)(2,1)S(1)}, u32[]{:S(2)}, u32[]{:S(2)}) collective-permute-start(bf16[528,256]{1,0:T(8,128)(2,1)S(1)} %get-tuple-element.83), channel_id=1, source_target_pairs={{0,3},{1,2},{2,1},{3,0},{4,7},{5,6},{6,5},{7,4},{8,11},{9,10},{10,... | collective-permute-start | bytes 811016 | tf_op jit(solution)/shard_map/ppermute | solution.py:407
  117.5 1.6 %copy-start.5 = (f32[2048,256]{1,0:T(8,128)S(1)}, f32[2048,256]{1,0:T(8,128)}, u32[]{:S(2)}) copy-start(f32[2048,256]{1,0:T(8,128)} %get-tuple-element.79.dkv_ref) | copy-start | bytes 6291460

commit v7 on v6

--- a/solution.py
+++ b/solution.py
@@ -60,12 +60,17 @@
     return lax.dot_general(left, right, (((0,), (0,)), ((), ())), preferred_element_type=jnp.float32)
 
 
-def call(kernel, outs, args, scratch=(), scalars=0, steps=(), in_steps=(), out_steps=(), in_place=None, vmem=24):
-    def spec(shape, stepped, at_rest, scalar=False):
+def call(kernel, outs, args, scratch=(), scalars=0, steps=(), in_steps=(), out_steps=(), in_place=None, first=None, flops=0):
+    first = first or {}
+    steps = steps or ((1,) if first else ())
+
+    def spec(shape, stepped, at_rest, scalar=False, part=None):
         if at_rest:
             return pl.BlockSpec(memory_space=pl.ANY)
         if scalar:
             return pl.BlockSpec(memory_space=pltpu.SMEM)
+        if part is not None:
+            return pl.BlockSpec(part, lambda *at: (0, 0))
         if not steps:
             return pl.BlockSpec(memory_space=pltpu.VMEM)
         if stepped:
@@ -76,14 +81,14 @@
         kernel,
         grid=steps,
         out_shape=[jax.ShapeDtypeStruct(shape, dtype) for shape, dtype in outs],
-        in_specs=[spec(arg.shape, at in in_steps, at == in_place, at < scalars) for at, arg in enumerate(args)],
+        in_specs=[spec(arg.shape, at in in_steps, at == in_place, at < scalars, first.get(at)) for at, arg in enumerate(args)],
         out_specs=[
             spec(shape, at in out_steps, in_place is not None and at == 0) for at, (shape, _) in enumerate(outs)
         ],
         scratch_shapes=list(scratch),
         input_output_aliases={} if in_place is None else {in_place: 0},
-        compiler_params=pltpu.CompilerParams(vmem_limit_bytes=vmem << 20),
-        cost_estimate=pl.CostEstimate(flops=0, bytes_accessed=0, transcendentals=0),
+        compiler_params=pltpu.CompilerParams(vmem_limit_bytes=60 << 20),
+        cost_estimate=pl.CostEstimate(flops=flops, bytes_accessed=0, transcendentals=0),
     )(*args)
 
 
@@ -439,11 +444,11 @@
     )
     peers = swap_all([s1, s2, s2, s3, s3, s3, s3])
     q, g = call(prepare_queries_kernel, [((ROWS, HEAD), bf16)] * 2, (queries, cotangent, s3), wide)
-    q, far, peers[3], peers[4] = lax.optimization_barrier((q, far, peers[3], peers[4]))
+    q, far = lax.optimization_barrier((q, far))
     far = swap_far(far)
     state = [((8, HALF), f32), ((HEAD, HALF), f32)]
     stat, out, odd = call(
-        own_forward_kernel, [*state, ((8, HALF), f32)], (q, kv, g, near_bias), [pltpu.VMEM((HEAD, ROWS), bf16)], vmem=60
+        own_forward_kernel, [*state, ((8, HALF), f32)], (q, kv, g, near_bias), [pltpu.VMEM((HEAD, ROWS), bf16)], flops=10000000000
     )
     stat, far = lax.optimization_barrier((stat, far))
     me = lax.axis_index("y").astype(jnp.int32).reshape(1)
@@ -455,18 +460,20 @@
         scalars=1,
     )
     part = swap_quad(part)
-    stat, out = call(middle_forward_kernel, state, (q, other_bias, stat, out, *peers))
+    stat, out = call(middle_forward_kernel, state, (q, other_bias, stat, out, *peers), first={0: (HALF, HEAD)})
     row, tall = call(
         finish_kernel,
         [((8, ROWS), f32), ((8 * QUADS, HEAD), f32)],
         (g, stat, out, odd, part),
         [pltpu.VMEM((8, HEAD), f32), pltpu.VMEM((HEAD, HEAD), f32)],
+        first={0: (HALF, HEAD)},
     )
     tall = swap_quad(tall)
     *third, third_dq = call(
         third_backward_kernel,
         [*both(256, 256, 256, 256), ((HEAD, UNIT), f32)],
         (q, g, other_bias, row, *peers[3:]),
+        first={0: (UNIT, HEAD), 1: (UNIT, HEAD), 2: (8, UNIT), 3: (8, UNIT)},
     )
     back = [swap(block, mask) for block, mask in zip(third, (4, 5, 6, 7))]
     third_dq, tall = lax.optimization_barrier((third_dq, tall))
@@ -476,8 +483,8 @@
         (me, q, g, other_bias, row, quad, far, tall, third_dq, *peers[:3]),
         [pltpu.VMEM((8 * QUADS, HEAD), f32)],
         scalars=1,
-    )
-    far_dkv, *back = lax.optimization_barrier((far_dkv, *back))
+        first={1: (HALF, HEAD), 2: (HALF, HEAD), 4: (8, HALF)},
+    )
     back = [swap(block, mask) for block, mask in zip(sends, (1, 2, 3))] + back
     far_dkv = swap_far(far_dkv)
     dq, dkv = call(
@@ -488,7 +495,7 @@
         steps=(ROWS // BLOCK,),
         in_steps=(4,),
         out_steps=(1,),
-        vmem=60,
+        flops=10000000000,
     )
     dq, dk, dv = call(
         join_kernel,

time: 124 us -> 119 us (0.960)
  Pallas kernels: 40.8 us -> 56.3 us
  local copies, waits for them, and re-layouts: 15.2 us -> 3.71 us
  blocking collectives: 8.14 us -> 0 us
  waiting for transfers between devices: 7.26 us -> 1.84 us
  starting transfers between devices: 50.6 us -> 55.4 us
    pallas_call x10, Pallas kernels: 40.8 us -> 56.3 us  [call(): pl.pallas_call(kernel, grid=steps, out_shape=[jax.ShapeDtypeStruct(shape,...]
    unnamed x46 -> x36, local copies, waits for them, and re-layouts: 15.2 us -> 3.71 us
    all_to_all x1 -> x0, blocking collectives: 8.14 us -> none  [swap_quad(): return lax.all_to_all(parts, 'y', 0, 0).reshape(block.shape)]
    ppermute x14, waiting for transfers between devices: 7.26 us -> 1.58 us  [swap(): lax.ppermute(block, ('z', 'y'), [(at, at ^ mask) for at in range(16)])]
    all_to_all x1 -> x2, starting transfers between devices: 3.27 us -> 7.16 us  [swap_quad(): return lax.all_to_all(parts, 'y', 0, 0).reshape(block.shape)]
    ppermute x14, starting transfers between devices: 20 us -> 22.2 us  [swap(): lax.ppermute(block, ('z', 'y'), [(at, at ^ mask) for at in range(16)])]
  transfers between devices with their start and end apart: 17 -> 18, of which waited for: 2 -> 2; matrix products, arithmetic and copies ran while one was open for 0% -> 0% of each run, Pallas kernels for 27% -> 35%
where the time goes in v7:
time: 119 us; the launch traced here: 118 us
  Pallas kernels  56.3 us (47%)
  starting transfers between devices  55.4 us (47%)
  local copies, waits for them, and re-layouts  3.71 us (3%)
  waiting for transfers between devices  1.84 us (2%)
    pallas_call x10, Pallas kernels, call(): pl.pallas_call(kernel, grid=steps, out_shape=[jax.ShapeDtypeStruct(shape,...  56.3 us
    all_to_all x2, starting transfers between devices, swap_far(): return lax.all_to_all(parts, ('grp', 'x', 'z'), 0, 0).reshape(block.shape)  26.1 us
    ppermute x14, starting transfers between devices, swap(): lax.ppermute(block, ('z', 'y'), [(at, at ^ mask) for at in range(16)])  22.2 us
    all_to_all x2, starting transfers between devices, swap_quad(): return lax.all_to_all(parts, 'y', 0, 0).reshape(block.shape)  7.16 us
    unnamed x36, local copies, waits for them, and re-layouts  3.71 us
  transfers between devices with their start and end apart: 18, of which 2 were waited for; matrix products, arithmetic and copies ran while one was open for 0% of the time, Pallas kernels for 35%

profile of v7, /device:TPU:1, one launch (start us, length us, event | category | flops | bytes accessed | tf_op | source)
XLA Modules:
  0.0 118.4 jit_solution(7243443279929933448)
XLA Ops:
  0.6 4.4 %shard_map.85 = (bf16[2048,256]{1,0:T(8,128)(2,1)}, bf16[1040,256]{1,0:T(8,128)(2,1)}, bf16[528,256]{1,0:T(8,128)(2,1)}, bf16[256,256]{1,0:T(8,128)(2,1)}, bf16[512,256]{1,0:T(8,128)(2,1)}) custom-call(bf16[2048,128]{1,0:T(8,128)(2,1)} %k_ref.1, bf16[2048,128]{1,0:T(8,128)(2,1)} %v_ref.1, bf16[2048,128]{1,0:T(8,128)(2,1)} %q_ref.3, bf16[2048,128]{1,0:T(8,128)(2,1)} %g_ref.3), custom_call_target="tpu_custom_call" | custom-call | tf_op jit(solution)/shard_map/pallas_call | solution.py:80
  5.0 3.5 %collective-permute-start.4 = (bf16[256,256]{1,0:T(8,128)(2,1)}, bf16[256,256]{1,0:T(8,128)(2,1)S(1)}, u32[]{:S(2)}, u32[]{:S(2)}) collective-permute-start(bf16[256,256]{1,0:T(8,128)(2,1)} %get-tuple-element.57.after_ref), channel_id=1, source_target_pairs={{0,5},{1,4},{2,7},{3,6},{4,1},{5,0},{6,3},{7,2},{8,13},{9,12},{10,... | collective-permute-start | bytes 393224 | tf_op jit(solution)/shard_map/ppermute | solution.py:412
  8.5 0.0 collective-permute-start.3
  8.5 1.9 %collective-permute-start.2 = (bf16[528,256]{1,0:T(8,128)(2,1)}, bf16[528,256]{1,0:T(8,128)(2,1)S(1)}, u32[]{:S(2)}, u32[]{:S(2)}) collective-permute-start(bf16[528,256]{1,0:T(8,128)(2,1)} %get-tuple-element.53.own), channel_id=1, source_target_pairs={{0,3},{1,2},{2,1},{3,0},{4,7},{5,6},{6,5},{7,4},{8,11},{9,10},{10,... | collective-permute-start | bytes 811016 | tf_op jit(solution)/shard_map/ppermute | solution.py:412
  10.4 0.7 collective-permute-start.1
  11.1 0.6 collective-permute-start
  11.8 3.3 %shard_map.86 = (bf16[2048,128]{1,0:T(8,128)(2,1)}, bf16[2048,128]{1,0:T(8,128)(2,1)}) custom-call(bf16[2048,128]{1,0:T(8,128)(2,1)} %q_ref.3, bf16[2048,128]{1,0:T(8,128)(2,1)} %g_ref.3, bf16[256,256]{1,0:T(8,128)(2,1)} %get-tuple-element.57.after_ref), custom_call_target="tpu_custom_call" | custom-call | tf_op jit(solution)/shard_map/pallas_call | solution.py:80
  15.0 13.4 %all-to-all-start = ((bf16[64,8,256]{2,1,0:T(8,128)(2,1)}), bf16[64,8,256]{2,1,0:T(8,128)(2,1)S(1)}, u32[]{:S(2)}, u32[]{:S(2)}) async-start(bf16[64,8,256]{2,1,0:T(8,128)(2,1)} %bitcast.13), calls=%async_computation | async-start | bytes 524288 | tf_op jit(solution)/shard_map/all_to_all | solution.py:431
  28.4 0.0 collective-permute-done.4.rest_4_.rest_1_
  28.5 3.1 %collective-permute-start.6 = (bf16[256,256]{1,0:T(8,128)(2,1)}, bf16[256,256]{1,0:T(8,128)(2,1)S(1)}, u32[]{:S(2)}, u32[]{:S(2)}) collective-permute-start(bf16[256,256]{1,0:T(8,128)(2,1)} %get-tuple-element.57.after_ref), channel_id=1, source_target_pairs={{0,7},{1,6},{2,5},{3,4},{4,3},{5,2},{6,1},{7,0},{8,15},{9,14},{10,... | collective-permute-start | bytes 393224 | tf_op jit(solution)/shard_map/ppermute | solution.py:412
  31.5 0.0 collective-permute-done.3.rest_3_.rest_0_
  31.6 0.8 collective-permute-start.5
  32.4 9.4 %shard_map.87 = (f32[8,1024]{1,0:T(8,128)}, f32[128,1024]{1,0:T(8,128)}, f32[8,1024]{1,0:T(8,128)}) custom-call(bf16[2048,128]{1,0:T(8,128)(2,1)} %get-tuple-element.45.q_ref, bf16[2048,256]{1,0:T(8,128)(2,1)} %get-tuple-element.47.kv_ref, bf16[2048,128]{1,0:T(8,128)(2,1)} %get-tuple-element.46.g_ref, f32[8,2048]{1,0:T(8,128)} %constant.8.clone.bias_ref), custom_call_target="tpu_custom_call" | custom-call | flops 10000000000 | tf_op jit(solution)/shard_map/pallas_call | solution.py:80
  41.8 0.0 collective-permute-done.2.rest_2_.r3.rest_3_
  41.8 0.0 collective-permute-done.rest_0_.r1.rest_1_
  41.9 0.0 copy-start
  41.9 0.6 copy-done.3
  42.5 0.1 copy-done.1
  42.6 0.1 copy-done.2
  42.7 0.1 copy-done
  42.8 2.3 %shard_map.89 = (f32[32,384]{1,0:T(8,128)}, bf16[32,256]{1,0:T(8,128)(2,1)}) custom-call(s32[1]{0:T(128)} %bitcast.2.me_ref, bf16[528,256]{1,0:T(8,128)(2,1)} %get-tuple-element.53.own, bf16[1040,256]{1,0:T(8,128)(2,1)} %copy-done, bf16[528,256]{1,0:T(8,128)(2,1)} %copy-done.2, bf16[528,256]{1,0:T(8,128)(2,1)} %copy-done.1, bf16[512,256]{1,0:T(8,128)(2,1)} %bitcast.9), custom_call_target="tpu_custom_call" | custom-call | tf_op jit(solution)/shard_map/pallas_call | solution.py:80
  45.2 3.5 %all-to-all-start.1 = ((f32[4,8,384]{2,1,0:T(8,128)}), f32[4,8,384]{2,1,0:T(8,128)S(1)}, u32[]{:S(2)}, u32[]{:S(2)}) async-start(f32[4,8,384]{2,1,0:T(8,128)} %bitcast.16), calls=%async_computation.1 | async-start | bytes 98304 | tf_op jit(solution)/shard_map/all_to_all | solution.py:426
  48.7 0.0 collective-permute-done.5.rest_5_.rest_2_
  48.7 0.6 copy-done.8
  49.4 0.1 copy-done.9
  49.4 5.4 %shard_map.88 = (f32[8,1024]{1,0:T(8,128)}, f32[128,1024]{1,0:T(8,128)}) custom-call(bf16[2048,128]{1,0:T(8,128)(2,1)} %get-tuple-element.45.q_ref, f32[8,1024]{1,0:T(8,128)} %constant.9.clone.bias_ref, f32[8,1024]{1,0:T(8,128)} %get-tuple-element.50.stat_ref, f32[128,1024]{1,0:T(8,128)} %get-tuple-element.51.out_ref, bf16[1040,256]{1,0:T(8,128)(2,1)} %copy-done, ...), custom_call_target="tpu_custom_call" | custom-call | tf_op jit(solution)/shard_map/pallas_call | solution.py:80
  54.8 0.6 copy-done.12
  55.4 2.1 %shard_map.90 = (f32[8,2048]{1,0:T(8,128)}, f32[32,128]{1,0:T(8,128)}) custom-call(bf16[2048,128]{1,0:T(8,128)(2,1)} %get-tuple-element.46.g_ref, f32[8,1024]{1,0:T(8,128)} %get-tuple-element.58.stat_ref, f32[128,1024]{1,0:T(8,128)} %get-tuple-element.59.out_ref, f32[8,1024]{1,0:T(8,128)} %get-tuple-element.60.odd_ref, f32[32,384]{1,0:T(8,128)} %bitcast.14), custom_call_target="tpu_custom_call" | custom-call | tf_op jit(solution)/shard_map/pallas_call | solution.py:80
  57.5 2.7 %shard_map.91 = (bf16[256,256]{1,0:T(8,128)(2,1)}, bf16[256,256]{1,0:T(8,128)(2,1)}, bf16[256,256]{1,0:T(8,128)(2,1)}, bf16[256,256]{1,0:T(8,128)(2,1)}, f32[128,256]{1,0:T(8,128)}) custom-call(bf16[2048,128]{1,0:T(8,128)(2,1)} %get-tuple-element.45.q_ref, bf16[2048,128]{1,0:T(8,128)(2,1)} %get-tuple-element.46.g_ref, f32[8,1024]{1,0:T(8,128)} %constant.9.clone.bias_ref, ...), custom_call_target="tpu_custom_call" | custom-call | tf_op jit(solution)/shard_map/pallas_call | solution.py:80
  60.2 1.1 collective-permute-start.10
  61.3 1.4 %collective-permute-start.11 = (bf16[256,256]{1,0:T(8,128)(2,1)}, bf16[256,256]{1,0:T(8,128)(2,1)S(1)}, u32[]{:S(2)}, u32[]{:S(2)}) collective-permute-start(bf16[256,256]{1,0:T(8,128)(2,1)} %get-tuple-element.76), channel_id=1, source_target_pairs={{0,5},{1,4},{2,7},{3,6},{4,1},{5,0},{6,3},{7,2},{8,13},{9,12},{10,... | collective-permute-start | bytes 393224 | tf_op jit(solution)/shard_map/ppermute | solution.py:412
  62.7 3.7 %all-to-all-start.2 = ((f32[4,8,128]{2,1,0:T(8,128)}), f32[4,8,128]{2,1,0:T(8,128)S(1)}, u32[]{:S(2)}, u32[]{:S(2)}) async-start(f32[4,8,128]{2,1,0:T(8,128)} %bitcast.17), calls=%async_computation.2 | async-start | bytes 32768 | tf_op jit(solution)/shard_map/all_to_all | solution.py:426
  66.4 3.9 %collective-permute-start.12 = (bf16[256,256]{1,0:T(8,128)(2,1)}, bf16[256,256]{1,0:T(8,128)(2,1)S(1)}, u32[]{:S(2)}, u32[]{:S(2)}) collective-permute-start(bf16[256,256]{1,0:T(8,128)(2,1)} %get-tuple-element.77), channel_id=1, source_target_pairs={{0,6},{1,7},{2,4},{3,5},{4,2},{5,3},{6,0},{7,1},{8,14},{9,15},{10,... | collective-permute-start | bytes 393224 | tf_op jit(solution)/shard_map/ppermute | solution.py:412
  70.3 0.8 collective-permute-start.13
  71.1 0.3 all-to-all-done.2
  71.4 0.6 copy-done.17
  72.0 6.6 %shard_map.92 = (bf16[1040,256]{1,0:T(8,128)(2,1)}, bf16[528,256]{1,0:T(8,128)(2,1)}, bf16[528,256]{1,0:T(8,128)(2,1)}, bf16[512,256]{1,0:T(8,128)(2,1)}, f32[128,1024]{1,0:T(8,128)}, /*index=5*/f32[8,128]{1,0:T(8,128)}) custom-call(s32[1]{0:T(128)} %bitcast.2.me_ref, bf16[2048,128]{1,0:T(8,128)(2,1)} %get-tuple-element.45.q_ref, ...), custom_call_target="tpu_custom_call" | custom-call | tf_op jit(solution)/shard_map/pallas_call | solution.py:80
  78.6 12.7 %all-to-all-start.3 = ((bf16[64,8,256]{2,1,0:T(8,128)(2,1)}), bf16[64,8,256]{2,1,0:T(8,128)(2,1)S(1)}, u32[]{:S(2)}, u32[]{:S(2)}) async-start(bf16[64,8,256]{2,1,0:T(8,128)(2,1)} %bitcast.12), calls=%async_computation.3 | async-start | bytes 524288 | tf_op jit(solution)/shard_map/all_to_all | solution.py:431
  91.3 1.3 %collective-permute-start.8 = (bf16[528,256]{1,0:T(8,128)(2,1)}, bf16[528,256]{1,0:T(8,128)(2,1)S(1)}, u32[]{:S(2)}, u32[]{:S(2)}) collective-permute-start(bf16[528,256]{1,0:T(8,128)(2,1)} %get-tuple-element.73), channel_id=1, source_target_pairs={{0,2},{1,3},{2,0},{3,1},{4,6},{5,7},{6,4},{7,5},{8,10},{9,11},{10,... | collective-permute-start | bytes 811016 | tf_op jit(solution)/shard_map/ppermute | solution.py:412
  92.6 3.0 %collective-permute-start.9 = (bf16[528,256]{1,0:T(8,128)(2,1)}, bf16[528,256]{1,0:T(8,128)(2,1)S(1)}, u32[]{:S(2)}, u32[]{:S(2)}) collective-permute-start(bf16[528,256]{1,0:T(8,128)(2,1)} %get-tuple-element.74), channel_id=1, source_target_pairs={{0,3},{1,2},{2,1},{3,0},{4,7},{5,6},{6,5},{7,4},{8,11},{9,10},{10,... | collective-permute-start | bytes 811016 | tf_op jit(solution)/shard_map/ppermute | solution.py:412
  95.6 0.0 collective-permute-start.7
  95.6 14.3 %shard_map.93 = (f32[2048,128]{1,0:T(8,128)}, f32[2048,256]{1,0:T(8,128)}) custom-call(bf16[2048,128]{1,0:T(8,128)(2,1)} %get-tuple-element.45.q_ref, bf16[2048,128]{1,0:T(8,128)(2,1)} %get-tuple-element.46.g_ref, f32[8,2048]{1,0:T(8,128)} %constant.8.clone.bias_ref, f32[8,2048]{1,0:T(8,128)} %get-tuple-element.63.row_ref, ...), custom_call_target="tpu_custom_call" | custom-call | flops 10000000000 | tf_op jit(solution)/shard_map/pallas_call | solution.py:80
  109.9 0.0 collective-permute-done.13.b7
  110.0 0.0 collective-permute-done.8.b2
  110.0 0.0 all-to-all-done.3
  110.0 1.5 %collective-permute-done.7.b1 = bf16[1040,256]{1,0:T(8,128)(2,1)S(1)} collective-permute-done((bf16[1040,256]{1,0:T(8,128)(2,1)}, bf16[1040,256]{1,0:T(8,128)(2,1)S(1)}, u32[]{:S(2)}, u32[]{:S(2)}) %collective-permute-start.7) | collective-permute-done | bytes 532512 | tf_op jit(solution)/shard_map/ppermute | solution.py:412
  111.6 0.8 copy-done.5
  112.4 5.8 %shard_map.94 = (f32[2048,128]{1,0:T(8,128)}, f32[2048,128]{1,0:T(8,128)}, f32[2048,128]{1,0:T(8,128)}) custom-call(f32[2048,256]{1,0:T(8,128)} %get-tuple-element.70.dkv_ref, f32[8,128]{1,0:T(8,128)} %get-tuple-element.71.mine_ref, bf16[1040,256]{1,0:T(8,128)(2,1)} %copy-done.5, bf16[528,256]{1,0:T(8,128)(2,1)} %copy-done.10, ...), custom_call_target="tpu_custom_call", output_to_operand_aliasing={{0}: (10, {})} | custom-call | tf_op jit(solution)/shard_map/pallas_call | solution.py:80
  (34 shorter events, 0.1 us)
Async XLA Ops:
  5.0 23.4 %collective-permute-start.4 = (bf16[256,256]{1,0:T(8,128)(2,1)}, bf16[256,256]{1,0:T(8,128)(2,1)S(1)}, u32[]{:S(2)}, u32[]{:S(2)}) collective-permute-start(bf16[256,256]{1,0:T(8,128)(2,1)} %get-tuple-element.57.after_ref), channel_id=1, source_target_pairs={{0,5},{1,4},{2,7},{3,6},{4,1},{5,0},{6,3},{7,2},{8,13},{9,12},{10,... | collective-permute-start | bytes 393224 | tf_op jit(solution)/shard_map/ppermute | solution.py:412
  8.5 23.1 %collective-permute-start.3 = (bf16[256,256]{1,0:T(8,128)(2,1)}, bf16[256,256]{1,0:T(8,128)(2,1)S(1)}, u32[]{:S(2)}, u32[]{:S(2)}) collective-permute-start(bf16[256,256]{1,0:T(8,128)(2,1)} %get-tuple-element.57.after_ref), channel_id=1, source_target_pairs={{0,4},{1,5},{2,6},{3,7},{4,0},{5,1},{6,2},{7,3},{8,12},{9,13},{10,... | collective-permute-start | bytes 393224 | tf_op jit(solution)/shard_map/ppermute | solution.py:412
  8.5 33.3 %collective-permute-start.2 = (bf16[528,256]{1,0:T(8,128)(2,1)}, bf16[528,256]{1,0:T(8,128)(2,1)S(1)}, u32[]{:S(2)}, u32[]{:S(2)}) collective-permute-start(bf16[528,256]{1,0:T(8,128)(2,1)} %get-tuple-element.53.own), channel_id=1, source_target_pairs={{0,3},{1,2},{2,1},{3,0},{4,7},{5,6},{6,5},{7,4},{8,11},{9,10},{10,... | collective-permute-start | bytes 811016 | tf_op jit(solution)/shard_map/ppermute | solution.py:412
  10.4 31.4 %collective-permute-start.1 = (bf16[528,256]{1,0:T(8,128)(2,1)}, bf16[528,256]{1,0:T(8,128)(2,1)S(1)}, u32[]{:S(2)}, u32[]{:S(2)}) collective-permute-start(bf16[528,256]{1,0:T(8,128)(2,1)} %get-tuple-element.53.own), channel_id=1, source_target_pairs={{0,2},{1,3},{2,0},{3,1},{4,6},{5,7},{6,4},{7,5},{8,10},{9,11},{10,... | collective-permute-start | bytes 811016 | tf_op jit(solution)/shard_map/ppermute | solution.py:412
  11.1 30.7 %collective-permute-start = (bf16[1040,256]{1,0:T(8,128)(2,1)}, bf16[1040,256]{1,0:T(8,128)(2,1)S(1)}, u32[]{:S(2)}, u32[]{:S(2)}) collective-permute-start(bf16[1040,256]{1,0:T(8,128)(2,1)} %get-tuple-element.52), channel_id=1, source_target_pairs={{0,1},{1,0},{2,3},{3,2},{4,5},{5,4},{6,7},{7,6},{8,9},{9,8},{10,11... | collective-permute-start | bytes 1597448 | tf_op jit(solution)/shard_map/ppermute | solution.py:412
  15.0 26.7 %all-to-all-start = ((bf16[64,8,256]{2,1,0:T(8,128)(2,1)}), bf16[64,8,256]{2,1,0:T(8,128)(2,1)S(1)}, u32[]{:S(2)}, u32[]{:S(2)}) async-start(bf16[64,8,256]{2,1,0:T(8,128)(2,1)} %bitcast.13), calls=%async_computation | async-start | bytes 524288 | tf_op jit(solution)/shard_map/all_to_all | solution.py:431
  28.5 13.3 %copy-start.6 = (bf16[256,256]{1,0:T(8,128)(2,1)}, bf16[256,256]{1,0:T(8,128)(2,1)S(1)}, u32[]{:S(2)}) copy-start(bf16[256,256]{1,0:T(8,128)(2,1)S(1)} %collective-permute-done.4.rest_4_.rest_1_) | copy-start | bytes 393220
  28.5 20.2 %collective-permute-start.6 = (bf16[256,256]{1,0:T(8,128)(2,1)}, bf16[256,256]{1,0:T(8,128)(2,1)S(1)}, u32[]{:S(2)}, u32[]{:S(2)}) collective-permute-start(bf16[256,256]{1,0:T(8,128)(2,1)} %get-tuple-element.57.after_ref), channel_id=1, source_target_pairs={{0,7},{1,6},{2,5},{3,4},{4,3},{5,2},{6,1},{7,0},{8,15},{9,14},{10,... | collective-permute-start | bytes 393224 | tf_op jit(solution)/shard_map/ppermute | solution.py:412
  31.6 10.2 %copy-start.7 = (bf16[256,256]{1,0:T(8,128)(2,1)}, bf16[256,256]{1,0:T(8,128)(2,1)S(1)}, u32[]{:S(2)}) copy-start(bf16[256,256]{1,0:T(8,128)(2,1)S(1)} %collective-permute-done.3.rest_3_.rest_0_) | copy-start | bytes 393220
  31.6 17.2 %collective-permute-start.5 = (bf16[256,256]{1,0:T(8,128)(2,1)}, bf16[256,256]{1,0:T(8,128)(2,1)S(1)}, u32[]{:S(2)}, u32[]{:S(2)}) collective-permute-start(bf16[256,256]{1,0:T(8,128)(2,1)} %get-tuple-element.57.after_ref), channel_id=1, source_target_pairs={{0,6},{1,7},{2,4},{3,5},{4,2},{5,3},{6,0},{7,1},{8,14},{9,15},{10,... | collective-permute-start | bytes 393224 | tf_op jit(solution)/shard_map/ppermute | solution.py:412
  41.8 0.7 copy-start.3
  41.8 0.8 copy-start.1
  41.8 0.9 copy-start.2
  41.9 1.0 copy-start
  45.2 9.6 %all-to-all-start.1 = ((f32[4,8,384]{2,1,0:T(8,128)}), f32[4,8,384]{2,1,0:T(8,128)S(1)}, u32[]{:S(2)}, u32[]{:S(2)}) async-start(f32[4,8,384]{2,1,0:T(8,128)} %bitcast.16), calls=%async_computation.1 | async-start | bytes 98304 | tf_op jit(solution)/shard_map/all_to_all | solution.py:426
  48.7 0.7 copy-start.8
  48.7 0.7 copy-start.9
  54.8 0.6 copy-start.12
  60.2 32.4 %collective-permute-start.10 = (bf16[256,256]{1,0:T(8,128)(2,1)}, bf16[256,256]{1,0:T(8,128)(2,1)S(1)}, u32[]{:S(2)}, u32[]{:S(2)}) collective-permute-start(bf16[256,256]{1,0:T(8,128)(2,1)} %get-tuple-element.75), channel_id=1, source_target_pairs={{0,4},{1,5},{2,6},{3,7},{4,0},{5,1},{6,2},{7,3},{8,12},{9,13},{10,... | collective-permute-start | bytes 393224 | tf_op jit(solution)/shard_map/ppermute | solution.py:412
  61.3 34.3 %collective-permute-start.11 = (bf16[256,256]{1,0:T(8,128)(2,1)}, bf16[256,256]{1,0:T(8,128)(2,1)S(1)}, u32[]{:S(2)}, u32[]{:S(2)}) collective-permute-start(bf16[256,256]{1,0:T(8,128)(2,1)} %get-tuple-element.76), channel_id=1, source_target_pairs={{0,5},{1,4},{2,7},{3,6},{4,1},{5,0},{6,3},{7,2},{8,13},{9,12},{10,... | collective-permute-start | bytes 393224 | tf_op jit(solution)/shard_map/ppermute | solution.py:412
  62.7 8.7 %all-to-all-start.2 = ((f32[4,8,128]{2,1,0:T(8,128)}), f32[4,8,128]{2,1,0:T(8,128)S(1)}, u32[]{:S(2)}, u32[]{:S(2)}) async-start(f32[4,8,128]{2,1,0:T(8,128)} %bitcast.17), calls=%async_computation.2 | async-start | bytes 32768 | tf_op jit(solution)/shard_map/all_to_all | solution.py:426
  66.4 43.6 %collective-permute-start.12 = (bf16[256,256]{1,0:T(8,128)(2,1)}, bf16[256,256]{1,0:T(8,128)(2,1)S(1)}, u32[]{:S(2)}, u32[]{:S(2)}) collective-permute-start(bf16[256,256]{1,0:T(8,128)(2,1)} %get-tuple-element.77), channel_id=1, source_target_pairs={{0,6},{1,7},{2,4},{3,5},{4,2},{5,3},{6,0},{7,1},{8,14},{9,15},{10,... | collective-permute-start | bytes 393224 | tf_op jit(solution)/shard_map/ppermute | solution.py:412
  70.3 39.7 %collective-permute-start.13 = (bf16[256,256]{1,0:T(8,128)(2,1)}, bf16[256,256]{1,0:T(8,128)(2,1)S(1)}, u32[]{:S(2)}, u32[]{:S(2)}) collective-permute-start(bf16[256,256]{1,0:T(8,128)(2,1)} %get-tuple-element.78), channel_id=1, source_target_pairs={{0,7},{1,6},{2,5},{3,4},{4,3},{5,2},{6,1},{7,0},{8,15},{9,14},{10,... | collective-permute-start | bytes 393224 | tf_op jit(solution)/shard_map/ppermute | solution.py:412
  71.4 0.6 copy-start.17
  78.6 31.4 %all-to-all-start.3 = ((bf16[64,8,256]{2,1,0:T(8,128)(2,1)}), bf16[64,8,256]{2,1,0:T(8,128)(2,1)S(1)}, u32[]{:S(2)}, u32[]{:S(2)}) async-start(bf16[64,8,256]{2,1,0:T(8,128)(2,1)} %bitcast.12), calls=%async_computation.3 | async-start | bytes 524288 | tf_op jit(solution)/shard_map/all_to_all | solution.py:431
  91.3 18.7 %collective-permute-start.8 = (bf16[528,256]{1,0:T(8,128)(2,1)}, bf16[528,256]{1,0:T(8,128)(2,1)S(1)}, u32[]{:S(2)}, u32[]{:S(2)}) collective-permute-start(bf16[528,256]{1,0:T(8,128)(2,1)} %get-tuple-element.73), channel_id=1, source_target_pairs={{0,2},{1,3},{2,0},{3,1},{4,6},{5,7},{6,4},{7,5},{8,10},{9,11},{10,... | collective-permute-start | bytes 811016 | tf_op jit(solution)/shard_map/ppermute | solution.py:412
  92.6 17.3 %copy-start.13 = (bf16[256,256]{1,0:T(8,128)(2,1)}, bf16[256,256]{1,0:T(8,128)(2,1)S(1)}, u32[]{:S(2)}) copy-start(bf16[256,256]{1,0:T(8,128)(2,1)S(1)} %collective-permute-done.10.b4) | copy-start | bytes 393220
  92.6 17.4 %collective-permute-start.9 = (bf16[528,256]{1,0:T(8,128)(2,1)}, bf16[528,256]{1,0:T(8,128)(2,1)S(1)}, u32[]{:S(2)}, u32[]{:S(2)}) collective-permute-start(bf16[528,256]{1,0:T(8,128)(2,1)} %get-tuple-element.74), channel_id=1, source_target_pairs={{0,3},{1,2},{2,1},{3,0},{4,7},{5,6},{6,5},{7,4},{8,11},{9,10},{10,... | collective-permute-start | bytes 811016 | tf_op jit(solution)/shard_map/ppermute | solution.py:412
  95.6 14.3 %copy-start.14 = (bf16[256,256]{1,0:T(8,128)(2,1)}, bf16[256,256]{1,0:T(8,128)(2,1)S(1)}, u32[]{:S(2)}) copy-start(bf16[256,256]{1,0:T(8,128)(2,1)S(1)} %collective-permute-done.11.b5) | copy-start | bytes 393220
  95.6 16.0 %collective-permute-start.7 = (bf16[1040,256]{1,0:T(8,128)(2,1)}, bf16[1040,256]{1,0:T(8,128)(2,1)S(1)}, u32[]{:S(2)}, u32[]{:S(2)}) collective-permute-start(bf16[1040,256]{1,0:T(8,128)(2,1)} %get-tuple-element.72), channel_id=1, source_target_pairs={{0,1},{1,0},{2,3},{3,2},{4,5},{5,4},{6,7},{7,6},{8,9},{9,8},{10,11... | collective-permute-start | bytes 1597448 | tf_op jit(solution)/shard_map/ppermute | solution.py:412
  109.9 1.6 %copy-start.15 = (bf16[256,256]{1,0:T(8,128)(2,1)}, bf16[256,256]{1,0:T(8,128)(2,1)S(1)}, u32[]{:S(2)}) copy-start(bf16[256,256]{1,0:T(8,128)(2,1)S(1)} %collective-permute-done.12.b6) | copy-start | bytes 393220
  110.0 1.6 %copy-start.16 = (bf16[256,256]{1,0:T(8,128)(2,1)}, bf16[256,256]{1,0:T(8,128)(2,1)S(1)}, u32[]{:S(2)}) copy-start(bf16[256,256]{1,0:T(8,128)(2,1)S(1)} %collective-permute-done.13.b7) | copy-start | bytes 393220
  110.0 1.6 %copy-start.10 = (bf16[528,256]{1,0:T(8,128)(2,1)}, bf16[528,256]{1,0:T(8,128)(2,1)S(1)}, u32[]{:S(2)}) copy-start(bf16[528,256]{1,0:T(8,128)(2,1)S(1)} %collective-permute-done.8.b2) | copy-start | bytes 811012
  110.0 1.6 %copy-start.11 = (bf16[528,256]{1,0:T(8,128)(2,1)}, bf16[528,256]{1,0:T(8,128)(2,1)S(1)}, u32[]{:S(2)}) copy-start(bf16[528,256]{1,0:T(8,128)(2,1)S(1)} %collective-permute-done.9.b3) | copy-start | bytes 811012
  110.0 1.6 %copy-start.4 = (bf16[64,8,256]{2,1,0:T(8,128)(2,1)}, bf16[64,8,256]{2,1,0:T(8,128)(2,1)S(1)}, u32[]{:S(2)}) copy-start(bf16[64,8,256]{2,1,0:T(8,128)(2,1)S(1)} %all-to-all-done.3) | copy-start | bytes 786436
  111.6 0.8 copy-start.5

commit v8 on v7

--- a/solution.py
+++ b/solution.py
@@ -20,6 +20,7 @@
 FAR = 64
 BLOCK = 512
 HALF = 1024
+LARGE = 10**10
 
 
 def unit_level(unit):
@@ -60,15 +61,17 @@
     return lax.dot_general(left, right, (((0,), (0,)), ((), ())), preferred_element_type=jnp.float32)
 
 
-def call(kernel, outs, args, scratch=(), scalars=0, steps=(), in_steps=(), out_steps=(), in_place=None, first=None, flops=0):
+def call(kernel, outs, args, scratch=(), scalars=0, steps=(), in_steps=(), out_steps=(), lane_steps=(), in_place=None, first=None, flops=0, vmem=60):
     first = first or {}
     steps = steps or ((1,) if first else ())
 
-    def spec(shape, stepped, at_rest, scalar=False, part=None):
+    def spec(shape, stepped, at_rest, scalar=False, part=None, by_lanes=False):
         if at_rest:
             return pl.BlockSpec(memory_space=pl.ANY)
         if scalar:
             return pl.BlockSpec(memory_space=pltpu.SMEM)
+        if by_lanes:
+            return pl.BlockSpec((shape[0], HEAD), lambda at: (0, at))
         if part is not None:
             return pl.BlockSpec(part, lambda *at: (0, 0))
         if not steps:
@@ -81,13 +84,13 @@
         kernel,
         grid=steps,
         out_shape=[jax.ShapeDtypeStruct(shape, dtype) for shape, dtype in outs],
-        in_specs=[spec(arg.shape, at in in_steps, at == in_place, at < scalars, first.get(at)) for at, arg in enumerate(args)],
+        in_specs=[spec(arg.shape, at in in_steps, at == in_place, at < scalars, first.get(at), at in lane_steps) for at, arg in enumerate(args)],
         out_specs=[
-            spec(shape, at in out_steps, in_place is not None and at == 0) for at, (shape, _) in enumerate(outs)
+            spec(shape, at in out_steps, bool(lane_steps)) for at, (shape, _) in enumerate(outs)
         ],
         scratch_shapes=list(scratch),
         input_output_aliases={} if in_place is None else {in_place: 0},
-        compiler_params=pltpu.CompilerParams(vmem_limit_bytes=60 << 20),
+        compiler_params=pltpu.CompilerParams(vmem_limit_bytes=vmem << 20),
         cost_estimate=pl.CostEstimate(flops=flops, bytes_accessed=0, transcendentals=0),
     )(*args)
 
@@ -124,11 +127,6 @@
         s2_ref[512:, lane : lane + HEAD] = block
 
 
-def prepare_queries_kernel(q_ref, g_ref, after_ref, qp_ref, gp_ref, wide):
-    sort_rows(q_ref, qp_ref, 0, wide)
-    sort_rows(g_ref, gp_ref, 0, wide)
-
-
 def add_bias(block, rows):
     if all(row is None for row in rows):
         return block
@@ -164,7 +162,9 @@
     row_ref[1:2, target] = jnp.sum(grad.astype(jnp.float32).T * out, axis=0, keepdims=True) / total
 
 
-def own_forward_kernel(q_ref, kv_ref, g_ref, bias_ref, stat_ref, out_ref, odd_ref, vt_ref):
+def own_forward_kernel(raw_q, raw_g, kv_ref, bias_ref, stat_ref, out_ref, odd_ref, q_ref, g_ref, vt_ref, wide):
+    sort_rows(raw_q, q_ref, 0, wide)
+    sort_rows(raw_g, g_ref, 0, wide)
     stat_ref[...] = jnp.zeros_like(stat_ref)
     odd_ref[...] = jnp.zeros_like(odd_ref)
     for unit in range(8):
@@ -274,7 +274,8 @@
     return jnp.concatenate([block, jnp.full((HEAD - 8, HEAD), fill, jnp.float32)], 0).T
 
 
-def finish_kernel(g_ref, stat_ref, out_ref, odd_ref, part_ref, row_ref, tall_ref, sums, acc):
+def finish_kernel(q_ref, g_ref, bias_ref, stat_ref, out_ref, odd_ref, part_ref, *rest):
+    far, third, (dq_ref, row_ref, tall_ref, sums, acc) = rest[:4], rest[4:8], rest[8:]
     lanes = slice(0, HEAD)
     sums[...] = stat_ref[:, lanes]
     acc[...] = out_ref[:, lanes]
@@ -293,6 +294,8 @@
     tall = jnp.concatenate([row_ref[:, :HEAD], jnp.zeros((HEAD - 8, HEAD), jnp.float32)], 0).T
     for at in range(0, 8 * QUADS, 8):
         tall_ref[at : at + 8, :] = tall[:8]
+    dq_ref[...] = jnp.zeros_like(dq_ref)
+    backward_far(far, third, (q_ref, g_ref, bias_ref, row_ref), dq_ref)
 
 
 def remote_backward_kernel(me_ref, q_ref, g_ref, bias_ref, row_ref, quad_ref, far_ref, tall_ref, *rest):
@@ -319,12 +322,6 @@
     backward_far(far, outs, (q_ref, g_ref, bias_ref, row_ref), dq_ref)
 
 
-def third_backward_kernel(q_ref, g_ref, bias_ref, row_ref, *rest):
-    far, outs, dq_ref = rest[:4], rest[4:8], rest[8]
-    dq_ref[...] = jnp.zeros_like(dq_ref)
-    backward_far(far, outs, (q_ref, g_ref, bias_ref, row_ref), dq_ref)
-
-
 def backward_block(kv_block, q_ref, g_ref, row_ref, bias, count, dq_ref):
     key, value = kv_block[:, :HEAD], kv_block[:, HEAD:]
     lanes = slice(0, count)
@@ -376,36 +373,51 @@
             target[pl.ds(8 * block + residue, 8, stride=256), :] = read(slice(start, start + 8))
 
 
-def join_kernel(dkv_ref, mine_ref, b1, b2, b3, b4, b5, b6, b7, far_ref, dq_in, dq_out, dk_ref, dv_ref, sum_ref, tiles, sem):
+def join_kernel(dkv_ref, mine_ref, b1, b2, b3, b4, b5, b6, b7, far_ref, dq_in, dq_out, dk_out, dv_out, sum_ref, done_ref, tiles, sem):
+    at = pl.program_id(0)
+
     def wide(ref, rows=slice(None)):
         return ref[rows, :].astype(jnp.float32)
 
-    places = [(pl.ds(256 * at, 8), pl.ds(8 * at, 8)) for at in range(8)]
-    reads = [pltpu.make_async_copy(dq_in.at[rows], tiles.at[spot], sem.at[at]) for at, (rows, spot) in enumerate(places)]
-    for copy in reads:
-        copy.start()
-    mine = mine_ref[...]
-    for ref in (b1, b2, b3):
-        mine = mine + ref[ref.shape[0] - 16 :, :HEAD].astype(jnp.float32)[:8]
-    mine = SCALE * mine
-    for copy in reads:
-        copy.wait()
-    for at in range(8):
-        tiles[8 * at : 8 * at + 1, :] += mine[at : at + 1, :]
-    writes = [pltpu.make_async_copy(tiles.at[spot], dq_out.at[rows], sem.at[8 + at]) for at, (rows, spot) in enumerate(places)]
-    for copy in writes:
-        copy.start()
+    places = [(pl.ds(256 * step, 8), pl.ds(8 * step, 8)) for step in range(8)]
+    reads = [pltpu.make_async_copy(dq_in.at[rows], tiles.at[spot], sem.at[n]) for n, (rows, spot) in enumerate(places)]
+    writes = [pltpu.make_async_copy(tiles.at[spot], dq_out.at[rows], sem.at[8 + n]) for n, (rows, spot) in enumerate(places)]
+    sends = [pltpu.make_async_copy(done_ref.at[n], out, sem.at[16 + n]) for n, out in enumerate((dk_out, dv_out))]
+
+    @pl.when(at == 0)
+    def _():
+        for copy in reads:
+            copy.start()
+
     top, mid, low = slice(0, 256), slice(256, 512), slice(512, 1024)
     near = wide(b1, top) + wide(b2, top) + wide(b3, top)
     sum_ref[top, :] = dkv_ref[top, :] + near + wide(b4) + wide(b5) + wide(b6) + wide(b7)
     sum_ref[mid, :] = dkv_ref[mid, :] + wide(b1, mid) + wide(b2, mid) + wide(b3, mid)
     sum_ref[low, :] = dkv_ref[low, :] + wide(b1, low)
-    sum_ref[1024:, :] = dkv_ref[1024:, :]
-    sum_ref[:8, :] += jnp.sum(wide(far_ref).reshape(FAR, 8, 256), 0)
-    restore_rows(lambda rows: sum_ref[rows, :HEAD], dk_ref)
-    restore_rows(lambda rows: sum_ref[rows, HEAD:], dv_ref)
-    for copy in writes:
-        copy.wait()
+    sum_ref[HALF:, :] = dkv_ref[HALF:, :]
+    sum_ref[:8, :] += jnp.sum(wide(far_ref).reshape(FAR, 8, HEAD), 0)
+
+    @pl.when(at == 0)
+    def _():
+        restore_rows(lambda rows: sum_ref[rows, :], done_ref.at[0])
+        sends[0].start()
+        mine = mine_ref[...]
+        for ref in (b1, b2, b3):
+            mine = mine + ref[ref.shape[0] - 16 :, :].astype(jnp.float32)[:8]
+        mine = SCALE * mine
+        for copy in reads:
+            copy.wait()
+        for step in range(8):
+            tiles[8 * step : 8 * step + 1, :] += mine[step : step + 1, :]
+        for copy in writes:
+            copy.start()
+
+    @pl.when(at == 1)
+    def _():
+        restore_rows(lambda rows: sum_ref[rows, :], done_ref.at[1])
+        sends[1].start()
+        for copy in writes + sends:
+            copy.wait()
 
 
 def swap(block, mask):
@@ -443,12 +455,14 @@
         prepare_keys_kernel, both(ROWS, 1040, 528, 256, 8 * FAR), (keys, values, queries, cotangent), wide
     )
     peers = swap_all([s1, s2, s2, s3, s3, s3, s3])
-    q, g = call(prepare_queries_kernel, [((ROWS, HEAD), bf16)] * 2, (queries, cotangent, s3), wide)
-    q, far = lax.optimization_barrier((q, far))
     far = swap_far(far)
     state = [((8, HALF), f32), ((HEAD, HALF), f32)]
-    stat, out, odd = call(
-        own_forward_kernel, [*state, ((8, HALF), f32)], (q, kv, g, near_bias), [pltpu.VMEM((HEAD, ROWS), bf16)], flops=10000000000
+    stat, out, odd, q, g = call(
+        own_forward_kernel,
+        [*state, ((8, HALF), f32), ((ROWS, HEAD), bf16), ((ROWS, HEAD), bf16)],
+        (queries, cotangent, kv, near_bias),
+        [pltpu.VMEM((HEAD, ROWS), bf16), *wide],
+        flops=LARGE,
     )
     stat, far = lax.optimization_barrier((stat, far))
     me = lax.axis_index("y").astype(jnp.int32).reshape(1)
@@ -458,23 +472,18 @@
         (me, s2, *peers[:3], far),
         [pltpu.VMEM((8 * QUADS, 256), f32)],
         scalars=1,
+        vmem=24,
     )
     part = swap_quad(part)
     stat, out = call(middle_forward_kernel, state, (q, other_bias, stat, out, *peers), first={0: (HALF, HEAD)})
-    row, tall = call(
+    *third, third_dq, row, tall = call(
         finish_kernel,
-        [((8, ROWS), f32), ((8 * QUADS, HEAD), f32)],
-        (g, stat, out, odd, part),
+        [*both(256, 256, 256, 256), ((HEAD, UNIT), f32), ((8, ROWS), f32), ((8 * QUADS, HEAD), f32)],
+        (q, g, other_bias, stat, out, odd, part, *peers[3:]),
         [pltpu.VMEM((8, HEAD), f32), pltpu.VMEM((HEAD, HEAD), f32)],
-        first={0: (HALF, HEAD)},
+        first={0: (UNIT, HEAD), 1: (HALF, HEAD), 2: (8, UNIT)},
     )
     tall = swap_quad(tall)
-    *third, third_dq = call(
-        third_backward_kernel,
-        [*both(256, 256, 256, 256), ((HEAD, UNIT), f32)],
-        (q, g, other_bias, row, *peers[3:]),
-        first={0: (UNIT, HEAD), 1: (UNIT, HEAD), 2: (8, UNIT), 3: (8, UNIT)},
-    )
     back = [swap(block, mask) for block, mask in zip(third, (4, 5, 6, 7))]
     third_dq, tall = lax.optimization_barrier((third_dq, tall))
     *sends, far_dkv, far_dq, mine = call(
@@ -495,13 +504,20 @@
         steps=(ROWS // BLOCK,),
         in_steps=(4,),
         out_steps=(1,),
-        flops=10000000000,
+        flops=LARGE,
     )
     dq, dk, dv = call(
         join_kernel,
         [((ROWS, HEAD), f32)] * 3,
         (dkv, mine, *back, far_dkv, dq),
-        [pltpu.VMEM((ROWS, 256), f32), pltpu.VMEM((64, HEAD), f32), pltpu.SemaphoreType.DMA((16,))],
+        [
+            pltpu.VMEM((ROWS, HEAD), f32),
+            pltpu.VMEM((2, ROWS, HEAD), f32),
+            pltpu.VMEM((64, HEAD), f32),
+            pltpu.SemaphoreType.DMA((18,)),
+        ],
+        steps=(2,),
+        lane_steps=(0, *range(2, 10)),
         in_place=10,
     )
     return dq, dk, dv

time: 119 us -> 114 us (0.958)
  Pallas kernels: 56.3 us -> 50.1 us
    pallas_call x10 -> x8, Pallas kernels: 56.3 us -> 50.1 us  [call(): pl.pallas_call(kernel, grid=steps, out_shape=[jax.ShapeDtypeStruct(shape,...]
    unnamed x36 -> x40, local copies, waits for them, and re-layouts: 3.71 us -> 3.31 us
  transfers between devices with their start and end apart: 18 -> 18, of which waited for: 2 -> 3; matrix products, arithmetic and copies ran while one was open for 0% -> 0% of each run, Pallas kernels for 35% -> 34%
where the time goes in v8:
time: 114 us; the launch traced here: 113 us
  starting transfers between devices  56.1 us (49%)
  Pallas kernels  50.1 us (44%)
  local copies, waits for them, and re-layouts  3.31 us (3%)
  waiting for transfers between devices  2.38 us (2%)
    pallas_call x8, Pallas kernels, call(): pl.pallas_call(kernel, grid=steps, out_shape=[jax.ShapeDtypeStruct(shape,...  50.1 us
    all_to_all x2, starting transfers between devices, swap_far(): return lax.all_to_all(parts, ('grp', 'x', 'z'), 0, 0).reshape(block.shape)  26 us
    ppermute x14, starting transfers between devices, swap(): lax.ppermute(block, ('z', 'y'), [(at, at ^ mask) for at in range(16)])  22.5 us
    all_to_all x2, starting transfers between devices, swap_quad(): return lax.all_to_all(parts, 'y', 0, 0).reshape(block.shape)  7.46 us
    unnamed x40, local copies, waits for them, and re-layouts  3.31 us
  transfers between devices with their start and end apart: 18, of which 3 were waited for; matrix products, arithmetic and copies ran while one was open for 0% of the time, Pallas kernels for 34%

profile of v8, /device:TPU:1, one launch (start us, length us, event | category | flops | bytes accessed | tf_op | source)
XLA Modules:
  0.0 112.9 jit_solution(16639589741972252155)
XLA Ops:
  0.6 4.4 %shard_map.85 = (bf16[2048,256]{1,0:T(8,128)(2,1)}, bf16[1040,256]{1,0:T(8,128)(2,1)}, bf16[528,256]{1,0:T(8,128)(2,1)}, bf16[256,256]{1,0:T(8,128)(2,1)}, bf16[512,256]{1,0:T(8,128)(2,1)}) custom-call(bf16[2048,128]{1,0:T(8,128)(2,1)} %k_ref.1, bf16[2048,128]{1,0:T(8,128)(2,1)} %v_ref.1, bf16[2048,128]{1,0:T(8,128)(2,1)} %raw_q.1, bf16[2048,128]{1,0:T(8,128)(2,1)} %raw_g.1), custom_call_target="tpu_custom_call" | custom-call | tf_op jit(solution)/shard_map/pallas_call | solution.py:83
  5.0 3.5 %collective-permute-start.4 = (bf16[256,256]{1,0:T(8,128)(2,1)}, bf16[256,256]{1,0:T(8,128)(2,1)S(1)}, u32[]{:S(2)}, u32[]{:S(2)}) collective-permute-start(bf16[256,256]{1,0:T(8,128)(2,1)} %get-tuple-element.53), channel_id=1, source_target_pairs={{0,5},{1,4},{2,7},{3,6},{4,1},{5,0},{6,3},{7,2},{8,13},{9,12},{10,... | collective-permute-start | bytes 393224 | tf_op jit(solution)/shard_map/ppermute | solution.py:424
  8.5 0.0 collective-permute-start.3
  8.5 1.9 %collective-permute-start.2 = (bf16[528,256]{1,0:T(8,128)(2,1)}, bf16[528,256]{1,0:T(8,128)(2,1)S(1)}, u32[]{:S(2)}, u32[]{:S(2)}) collective-permute-start(bf16[528,256]{1,0:T(8,128)(2,1)} %get-tuple-element.48.own), channel_id=1, source_target_pairs={{0,3},{1,2},{2,1},{3,0},{4,7},{5,6},{6,5},{7,4},{8,11},{9,10},{10,... | collective-permute-start | bytes 811016 | tf_op jit(solution)/shard_map/ppermute | solution.py:424
  10.4 0.7 collective-permute-start.1
  11.1 12.8 %all-to-all-start = ((bf16[64,8,256]{2,1,0:T(8,128)(2,1)}), bf16[64,8,256]{2,1,0:T(8,128)(2,1)S(1)}, u32[]{:S(2)}, u32[]{:S(2)}) async-start(bf16[64,8,256]{2,1,0:T(8,128)(2,1)} %bitcast.13), calls=%async_computation | async-start | bytes 524288 | tf_op jit(solution)/shard_map/all_to_all | solution.py:443
  24.0 1.0 collective-permute-start
  25.0 0.0 collective-permute-done.4.rest_4_.rest_1_
  25.0 3.0 %collective-permute-start.6 = (bf16[256,256]{1,0:T(8,128)(2,1)}, bf16[256,256]{1,0:T(8,128)(2,1)S(1)}, u32[]{:S(2)}, u32[]{:S(2)}) collective-permute-start(bf16[256,256]{1,0:T(8,128)(2,1)} %get-tuple-element.53), channel_id=1, source_target_pairs={{0,7},{1,6},{2,5},{3,4},{4,3},{5,2},{6,1},{7,0},{8,15},{9,14},{10,... | collective-permute-start | bytes 393224 | tf_op jit(solution)/shard_map/ppermute | solution.py:424
  28.0 0.0 collective-permute-done.3.rest_3_.rest_0_
  28.0 0.8 collective-permute-start.5
  28.8 11.0 %shard_map.86 = (f32[8,1024]{1,0:T(8,128)}, f32[128,1024]{1,0:T(8,128)}, f32[8,1024]{1,0:T(8,128)}, bf16[2048,128]{1,0:T(8,128)(2,1)}, bf16[2048,128]{1,0:T(8,128)(2,1)}) custom-call(bf16[2048,128]{1,0:T(8,128)(2,1)} %raw_q.1, bf16[2048,128]{1,0:T(8,128)(2,1)} %raw_g.1, bf16[2048,256]{1,0:T(8,128)(2,1)} %get-tuple-element.40.kv_ref, ...), custom_call_target="tpu_custom_call" | custom-call | flops 10000000000 | tf_op jit(solution)/shard_map/pallas_call | solution.py:83
  39.8 0.0 all-to-all-done
  39.8 0.0 collective-permute-done.2.rest_2_.r3.rest_3_
  39.9 0.0 collective-permute-done.1.rest_1_.r2.rest_2_
  39.9 0.4 collective-permute-done.rest_0_.r1.rest_1_
  40.3 1.0 shard_map.88
  41.3 0.6 copy-done.5
  41.9 3.8 %all-to-all-start.1 = ((f32[4,8,384]{2,1,0:T(8,128)}), f32[4,8,384]{2,1,0:T(8,128)S(1)}, u32[]{:S(2)}, u32[]{:S(2)}) async-start(f32[4,8,384]{2,1,0:T(8,128)} %bitcast.3), calls=%async_computation.1 | async-start | bytes 98304 | tf_op jit(solution)/shard_map/all_to_all | solution.py:438
  45.7 0.0 collective-permute-done.6.rest_6_.rest_3_
  45.7 0.0 collective-permute-done.5.rest_5_.rest_2_
  45.7 0.6 copy-done.10
  46.3 0.1 copy-done.11
  46.4 5.4 %shard_map.87 = (f32[8,1024]{1,0:T(8,128)}, f32[128,1024]{1,0:T(8,128)}) custom-call(bf16[2048,128]{1,0:T(8,128)(2,1)} %get-tuple-element.41.q_ref, f32[8,1024]{1,0:T(8,128)} %constant.9.clone.bias_ref, f32[8,1024]{1,0:T(8,128)} %get-tuple-element.45.stat_ref, f32[128,1024]{1,0:T(8,128)} %get-tuple-element.46.out_ref, bf16[1040,256]{1,0:T(8,128)(2,1)} %copy-done, ...), custom_call_target="tpu_custom_call" | custom-call | tf_op jit(solution)/shard_map/pallas_call | solution.py:83
  51.8 0.0 all-to-all-done.1
  51.8 0.6 copy-done.14
  52.4 3.0 %shard_map.89 = (bf16[256,256]{1,0:T(8,128)(2,1)}, bf16[256,256]{1,0:T(8,128)(2,1)}, bf16[256,256]{1,0:T(8,128)(2,1)}, bf16[256,256]{1,0:T(8,128)(2,1)}, f32[128...) custom-call(bf16[2048,128]{1,0:T(8,128)(2,1)} %get-tuple-element.41.q_ref, ...), custom_call_target="tpu_custom_call" | custom-call | tf_op jit(solution)/shard_map/pallas_call | solution.py:83
  55.4 1.5 %collective-permute-start.10 = (bf16[256,256]{1,0:T(8,128)(2,1)}, bf16[256,256]{1,0:T(8,128)(2,1)S(1)}, u32[]{:S(2)}, u32[]{:S(2)}) collective-permute-start(bf16[256,256]{1,0:T(8,128)(2,1)} %get-tuple-element.71), channel_id=1, source_target_pairs={{0,4},{1,5},{2,6},{3,7},{4,0},{5,1},{6,2},{7,3},{8,12},{9,13},{10,... | collective-permute-start | bytes 393224 | tf_op jit(solution)/shard_map/ppermute | solution.py:424
  56.8 1.3 %collective-permute-start.11 = (bf16[256,256]{1,0:T(8,128)(2,1)}, bf16[256,256]{1,0:T(8,128)(2,1)S(1)}, u32[]{:S(2)}, u32[]{:S(2)}) collective-permute-start(bf16[256,256]{1,0:T(8,128)(2,1)} %get-tuple-element.72), channel_id=1, source_target_pairs={{0,5},{1,4},{2,7},{3,6},{4,1},{5,0},{6,3},{7,2},{8,13},{9,12},{10,... | collective-permute-start | bytes 393224 | tf_op jit(solution)/shard_map/ppermute | solution.py:424
  58.1 3.7 %all-to-all-start.2 = ((f32[4,8,128]{2,1,0:T(8,128)}), f32[4,8,128]{2,1,0:T(8,128)S(1)}, u32[]{:S(2)}, u32[]{:S(2)}) async-start(f32[4,8,128]{2,1,0:T(8,128)} %bitcast.16), calls=%async_computation.2 | async-start | bytes 32768 | tf_op jit(solution)/shard_map/all_to_all | solution.py:438
  61.8 4.1 %collective-permute-start.12 = (bf16[256,256]{1,0:T(8,128)(2,1)}, bf16[256,256]{1,0:T(8,128)(2,1)S(1)}, u32[]{:S(2)}, u32[]{:S(2)}) collective-permute-start(bf16[256,256]{1,0:T(8,128)(2,1)} %get-tuple-element.73), channel_id=1, source_target_pairs={{0,6},{1,7},{2,4},{3,5},{4,2},{5,3},{6,0},{7,1},{8,14},{9,15},{10,... | collective-permute-start | bytes 393224 | tf_op jit(solution)/shard_map/ppermute | solution.py:424
  65.8 0.7 collective-permute-start.13
  66.5 0.3 all-to-all-done.2
  66.8 0.6 copy-done.19
  67.4 6.6 %shard_map.90 = (bf16[1040,256]{1,0:T(8,128)(2,1)}, bf16[528,256]{1,0:T(8,128)(2,1)}, bf16[528,256]{1,0:T(8,128)(2,1)}, bf16[512,256]{1,0:T(8,128)(2,1)}, f32[128,1024]{1,0:T(8,128)}, /*index=5*/f32[8,128]{1,0:T(8,128)}) custom-call(s32[1]{0:T(128)} %bitcast.2.me_ref, bf16[2048,128]{1,0:T(8,128)(2,1)} %get-tuple-element.41.q_ref, ...), custom_call_target="tpu_custom_call" | custom-call | tf_op jit(solution)/shard_map/pallas_call | solution.py:83
  74.0 13.2 %all-to-all-start.3 = ((bf16[64,8,256]{2,1,0:T(8,128)(2,1)}), bf16[64,8,256]{2,1,0:T(8,128)(2,1)S(1)}, u32[]{:S(2)}, u32[]{:S(2)}) async-start(bf16[64,8,256]{2,1,0:T(8,128)(2,1)} %bitcast.12), calls=%async_computation.3 | async-start | bytes 524288 | tf_op jit(solution)/shard_map/all_to_all | solution.py:443
  87.2 1.3 %collective-permute-start.8 = (bf16[528,256]{1,0:T(8,128)(2,1)}, bf16[528,256]{1,0:T(8,128)(2,1)S(1)}, u32[]{:S(2)}, u32[]{:S(2)}) collective-permute-start(bf16[528,256]{1,0:T(8,128)(2,1)} %get-tuple-element.69), channel_id=1, source_target_pairs={{0,2},{1,3},{2,0},{3,1},{4,6},{5,7},{6,4},{7,5},{8,10},{9,11},{10,... | collective-permute-start | bytes 811016 | tf_op jit(solution)/shard_map/ppermute | solution.py:424
  88.5 0.0 collective-permute-done.10.b4
  88.5 2.9 %collective-permute-start.9 = (bf16[528,256]{1,0:T(8,128)(2,1)}, bf16[528,256]{1,0:T(8,128)(2,1)S(1)}, u32[]{:S(2)}, u32[]{:S(2)}) collective-permute-start(bf16[528,256]{1,0:T(8,128)(2,1)} %get-tuple-element.70), channel_id=1, source_target_pairs={{0,3},{1,2},{2,1},{3,0},{4,7},{5,6},{6,5},{7,4},{8,11},{9,10},{10,... | collective-permute-start | bytes 811016 | tf_op jit(solution)/shard_map/ppermute | solution.py:424
  91.3 0.0 collective-permute-done.11.b5
  91.3 0.0 collective-permute-start.7
  91.3 14.3 %shard_map.91 = (f32[2048,128]{1,0:T(8,128)}, f32[2048,256]{1,0:T(8,128)}) custom-call(bf16[2048,128]{1,0:T(8,128)(2,1)} %get-tuple-element.41.q_ref, bf16[2048,128]{1,0:T(8,128)(2,1)} %get-tuple-element.42.g_ref, f32[8,2048]{1,0:T(8,128)} %constant.8.clone.bias_ref, f32[8,2048]{1,0:T(8,128)} %get-tuple-element.59.row_ref, ...), custom_call_target="tpu_custom_call" | custom-call | flops 10000000000 | tf_op jit(solution)/shard_map/pallas_call | solution.py:83
  105.7 0.0 collective-permute-done.12.b6
  105.7 0.0 collective-permute-done.13.b7
  105.7 0.0 collective-permute-done.9.b3
  105.8 1.7 %collective-permute-done.7.b1 = bf16[1040,256]{1,0:T(8,128)(2,1)S(1)} collective-permute-done((bf16[1040,256]{1,0:T(8,128)(2,1)}, bf16[1040,256]{1,0:T(8,128)(2,1)S(1)}, u32[]{:S(2)}, u32[]{:S(2)}) %collective-permute-start.7) | collective-permute-done | bytes 532512 | tf_op jit(solution)/shard_map/ppermute | solution.py:424
  107.5 0.8 copy-done.7
  108.3 4.5 %shard_map.92 = (f32[2048,128]{1,0:T(8,128)}, f32[2048,128]{1,0:T(8,128)}, f32[2048,128]{1,0:T(8,128)}) custom-call(f32[2048,256]{1,0:T(8,128)} %get-tuple-element.66.dkv_ref, f32[8,128]{1,0:T(8,128)} %get-tuple-element.67.mine_ref, bf16[1040,256]{1,0:T(8,128)(2,1)} %copy-done.7, bf16[528,256]{1,0:T(8,128)(2,1)} %copy-done.12, ...), custom_call_target="tpu_custom_call", output_to_operand_aliasing={{0}: (10, {})} | custom-call | tf_op jit(solution)/shard_map/pallas_call | solution.py:83
  (36 shorter events, 0.1 us)
Async XLA Ops:
  5.0 19.9 %collective-permute-start.4 = (bf16[256,256]{1,0:T(8,128)(2,1)}, bf16[256,256]{1,0:T(8,128)(2,1)S(1)}, u32[]{:S(2)}, u32[]{:S(2)}) collective-permute-start(bf16[256,256]{1,0:T(8,128)(2,1)} %get-tuple-element.53), channel_id=1, source_target_pairs={{0,5},{1,4},{2,7},{3,6},{4,1},{5,0},{6,3},{7,2},{8,13},{9,12},{10,... | collective-permute-start | bytes 393224 | tf_op jit(solution)/shard_map/ppermute | solution.py:424
  8.5 19.5 %collective-permute-start.3 = (bf16[256,256]{1,0:T(8,128)(2,1)}, bf16[256,256]{1,0:T(8,128)(2,1)S(1)}, u32[]{:S(2)}, u32[]{:S(2)}) collective-permute-start(bf16[256,256]{1,0:T(8,128)(2,1)} %get-tuple-element.53), channel_id=1, source_target_pairs={{0,4},{1,5},{2,6},{3,7},{4,0},{5,1},{6,2},{7,3},{8,12},{9,13},{10,... | collective-permute-start | bytes 393224 | tf_op jit(solution)/shard_map/ppermute | solution.py:424
  8.5 31.3 %collective-permute-start.2 = (bf16[528,256]{1,0:T(8,128)(2,1)}, bf16[528,256]{1,0:T(8,128)(2,1)S(1)}, u32[]{:S(2)}, u32[]{:S(2)}) collective-permute-start(bf16[528,256]{1,0:T(8,128)(2,1)} %get-tuple-element.48.own), channel_id=1, source_target_pairs={{0,3},{1,2},{2,1},{3,0},{4,7},{5,6},{6,5},{7,4},{8,11},{9,10},{10,... | collective-permute-start | bytes 811016 | tf_op jit(solution)/shard_map/ppermute | solution.py:424
  10.4 29.5 %collective-permute-start.1 = (bf16[528,256]{1,0:T(8,128)(2,1)}, bf16[528,256]{1,0:T(8,128)(2,1)S(1)}, u32[]{:S(2)}, u32[]{:S(2)}) collective-permute-start(bf16[528,256]{1,0:T(8,128)(2,1)} %get-tuple-element.48.own), channel_id=1, source_target_pairs={{0,2},{1,3},{2,0},{3,1},{4,6},{5,7},{6,4},{7,5},{8,10},{9,11},{10,... | collective-permute-start | bytes 811016 | tf_op jit(solution)/shard_map/ppermute | solution.py:424
  11.1 28.7 %all-to-all-start = ((bf16[64,8,256]{2,1,0:T(8,128)(2,1)}), bf16[64,8,256]{2,1,0:T(8,128)(2,1)S(1)}, u32[]{:S(2)}, u32[]{:S(2)}) async-start(bf16[64,8,256]{2,1,0:T(8,128)(2,1)} %bitcast.13), calls=%async_computation | async-start | bytes 524288 | tf_op jit(solution)/shard_map/all_to_all | solution.py:443
  24.0 16.3 %collective-permute-start = (bf16[1040,256]{1,0:T(8,128)(2,1)}, bf16[1040,256]{1,0:T(8,128)(2,1)S(1)}, u32[]{:S(2)}, u32[]{:S(2)}) collective-permute-start(bf16[1040,256]{1,0:T(8,128)(2,1)} %get-tuple-element.47), channel_id=1, source_target_pairs={{0,1},{1,0},{2,3},{3,2},{4,5},{5,4},{6,7},{7,6},{8,9},{9,8},{10,11... | collective-permute-start | bytes 1597448 | tf_op jit(solution)/shard_map/ppermute | solution.py:424
  25.0 14.9 %copy-start.8 = (bf16[256,256]{1,0:T(8,128)(2,1)}, bf16[256,256]{1,0:T(8,128)(2,1)S(1)}, u32[]{:S(2)}) copy-start(bf16[256,256]{1,0:T(8,128)(2,1)S(1)} %collective-permute-done.4.rest_4_.rest_1_) | copy-start | bytes 393220
  25.0 20.7 %collective-permute-start.6 = (bf16[256,256]{1,0:T(8,128)(2,1)}, bf16[256,256]{1,0:T(8,128)(2,1)S(1)}, u32[]{:S(2)}, u32[]{:S(2)}) collective-permute-start(bf16[256,256]{1,0:T(8,128)(2,1)} %get-tuple-element.53), channel_id=1, source_target_pairs={{0,7},{1,6},{2,5},{3,4},{4,3},{5,2},{6,1},{7,0},{8,15},{9,14},{10,... | collective-permute-start | bytes 393224 | tf_op jit(solution)/shard_map/ppermute | solution.py:424
  28.0 11.9 %copy-start.9 = (bf16[256,256]{1,0:T(8,128)(2,1)}, bf16[256,256]{1,0:T(8,128)(2,1)S(1)}, u32[]{:S(2)}) copy-start(bf16[256,256]{1,0:T(8,128)(2,1)S(1)} %collective-permute-done.3.rest_3_.rest_0_) | copy-start | bytes 393220
  28.0 17.7 %collective-permute-start.5 = (bf16[256,256]{1,0:T(8,128)(2,1)}, bf16[256,256]{1,0:T(8,128)(2,1)S(1)}, u32[]{:S(2)}, u32[]{:S(2)}) collective-permute-start(bf16[256,256]{1,0:T(8,128)(2,1)} %get-tuple-element.53), channel_id=1, source_target_pairs={{0,6},{1,7},{2,4},{3,5},{4,2},{5,3},{6,0},{7,1},{8,14},{9,15},{10,... | collective-permute-start | bytes 393224 | tf_op jit(solution)/shard_map/ppermute | solution.py:424
  28.8 11.5 %copy-start.4 = (bf16[528,256]{1,0:T(8,128)(2,1)S(1)}, bf16[528,256]{1,0:T(8,128)(2,1)}, u32[]{:S(2)}) copy-start(bf16[528,256]{1,0:T(8,128)(2,1)} %get-tuple-element.48.own) | copy-start | bytes 811012
  39.8 11.9 %copy-start.3 = (bf16[64,8,256]{2,1,0:T(8,128)(2,1)}, bf16[64,8,256]{2,1,0:T(8,128)(2,1)S(1)}, u32[]{:S(2)}) copy-start(bf16[64,8,256]{2,1,0:T(8,128)(2,1)S(1)} %all-to-all-done) | copy-start | bytes 786436
  39.9 5.8 %copy-start.1 = (bf16[528,256]{1,0:T(8,128)(2,1)}, bf16[528,256]{1,0:T(8,128)(2,1)S(1)}, u32[]{:S(2)}) copy-start(bf16[528,256]{1,0:T(8,128)(2,1)S(1)} %collective-permute-done.2.rest_2_.r3.rest_3_) | copy-start | bytes 811012
  39.9 5.8 %copy-start.2 = (bf16[528,256]{1,0:T(8,128)(2,1)}, bf16[528,256]{1,0:T(8,128)(2,1)S(1)}, u32[]{:S(2)}) copy-start(bf16[528,256]{1,0:T(8,128)(2,1)S(1)} %collective-permute-done.1.rest_1_.r2.rest_2_) | copy-start | bytes 811012
  40.3 5.4 %copy-start = (bf16[1040,256]{1,0:T(8,128)(2,1)}, bf16[1040,256]{1,0:T(8,128)(2,1)S(1)}, u32[]{:S(2)}) copy-start(bf16[1040,256]{1,0:T(8,128)(2,1)S(1)} %collective-permute-done.rest_0_.r1.rest_1_) | copy-start | bytes 1597444
  41.3 0.6 copy-start.5
  41.9 9.9 %all-to-all-start.1 = ((f32[4,8,384]{2,1,0:T(8,128)}), f32[4,8,384]{2,1,0:T(8,128)S(1)}, u32[]{:S(2)}, u32[]{:S(2)}) async-start(f32[4,8,384]{2,1,0:T(8,128)} %bitcast.3), calls=%async_computation.1 | async-start | bytes 98304 | tf_op jit(solution)/shard_map/all_to_all | solution.py:438
  45.7 0.7 copy-start.10
  45.7 0.7 copy-start.11
  51.8 0.6 copy-start.14
  55.4 33.1 %collective-permute-start.10 = (bf16[256,256]{1,0:T(8,128)(2,1)}, bf16[256,256]{1,0:T(8,128)(2,1)S(1)}, u32[]{:S(2)}, u32[]{:S(2)}) collective-permute-start(bf16[256,256]{1,0:T(8,128)(2,1)} %get-tuple-element.71), channel_id=1, source_target_pairs={{0,4},{1,5},{2,6},{3,7},{4,0},{5,1},{6,2},{7,3},{8,12},{9,13},{10,... | collective-permute-start | bytes 393224 | tf_op jit(solution)/shard_map/ppermute | solution.py:424
  56.8 34.5 %collective-permute-start.11 = (bf16[256,256]{1,0:T(8,128)(2,1)}, bf16[256,256]{1,0:T(8,128)(2,1)S(1)}, u32[]{:S(2)}, u32[]{:S(2)}) collective-permute-start(bf16[256,256]{1,0:T(8,128)(2,1)} %get-tuple-element.72), channel_id=1, source_target_pairs={{0,5},{1,4},{2,7},{3,6},{4,1},{5,0},{6,3},{7,2},{8,13},{9,12},{10,... | collective-permute-start | bytes 393224 | tf_op jit(solution)/shard_map/ppermute | solution.py:424
  58.1 8.7 %all-to-all-start.2 = ((f32[4,8,128]{2,1,0:T(8,128)}), f32[4,8,128]{2,1,0:T(8,128)S(1)}, u32[]{:S(2)}, u32[]{:S(2)}) async-start(f32[4,8,128]{2,1,0:T(8,128)} %bitcast.16), calls=%async_computation.2 | async-start | bytes 32768 | tf_op jit(solution)/shard_map/all_to_all | solution.py:438
  61.8 43.9 %collective-permute-start.12 = (bf16[256,256]{1,0:T(8,128)(2,1)}, bf16[256,256]{1,0:T(8,128)(2,1)S(1)}, u32[]{:S(2)}, u32[]{:S(2)}) collective-permute-start(bf16[256,256]{1,0:T(8,128)(2,1)} %get-tuple-element.73), channel_id=1, source_target_pairs={{0,6},{1,7},{2,4},{3,5},{4,2},{5,3},{6,0},{7,1},{8,14},{9,15},{10,... | collective-permute-start | bytes 393224 | tf_op jit(solution)/shard_map/ppermute | solution.py:424
  65.8 39.9 %collective-permute-start.13 = (bf16[256,256]{1,0:T(8,128)(2,1)}, bf16[256,256]{1,0:T(8,128)(2,1)S(1)}, u32[]{:S(2)}, u32[]{:S(2)}) collective-permute-start(bf16[256,256]{1,0:T(8,128)(2,1)} %get-tuple-element.74), channel_id=1, source_target_pairs={{0,7},{1,6},{2,5},{3,4},{4,3},{5,2},{6,1},{7,0},{8,15},{9,14},{10,... | collective-permute-start | bytes 393224 | tf_op jit(solution)/shard_map/ppermute | solution.py:424
  66.8 0.6 copy-start.19
  74.0 31.8 %all-to-all-start.3 = ((bf16[64,8,256]{2,1,0:T(8,128)(2,1)}), bf16[64,8,256]{2,1,0:T(8,128)(2,1)S(1)}, u32[]{:S(2)}, u32[]{:S(2)}) async-start(bf16[64,8,256]{2,1,0:T(8,128)(2,1)} %bitcast.12), calls=%async_computation.3 | async-start | bytes 524288 | tf_op jit(solution)/shard_map/all_to_all | solution.py:443
  87.2 18.5 %collective-permute-start.8 = (bf16[528,256]{1,0:T(8,128)(2,1)}, bf16[528,256]{1,0:T(8,128)(2,1)S(1)}, u32[]{:S(2)}, u32[]{:S(2)}) collective-permute-start(bf16[528,256]{1,0:T(8,128)(2,1)} %get-tuple-element.69), channel_id=1, source_target_pairs={{0,2},{1,3},{2,0},{3,1},{4,6},{5,7},{6,4},{7,5},{8,10},{9,11},{10,... | collective-permute-start | bytes 811016 | tf_op jit(solution)/shard_map/ppermute | solution.py:424
  88.5 17.2 %copy-start.15 = (bf16[256,256]{1,0:T(8,128)(2,1)}, bf16[256,256]{1,0:T(8,128)(2,1)S(1)}, u32[]{:S(2)}) copy-start(bf16[256,256]{1,0:T(8,128)(2,1)S(1)} %collective-permute-done.10.b4) | copy-start | bytes 393220
  88.5 17.3 %collective-permute-start.9 = (bf16[528,256]{1,0:T(8,128)(2,1)}, bf16[528,256]{1,0:T(8,128)(2,1)S(1)}, u32[]{:S(2)}, u32[]{:S(2)}) collective-permute-start(bf16[528,256]{1,0:T(8,128)(2,1)} %get-tuple-element.70), channel_id=1, source_target_pairs={{0,3},{1,2},{2,1},{3,0},{4,7},{5,6},{6,5},{7,4},{8,11},{9,10},{10,... | collective-permute-start | bytes 811016 | tf_op jit(solution)/shard_map/ppermute | solution.py:424
  91.3 14.3 %copy-start.16 = (bf16[256,256]{1,0:T(8,128)(2,1)}, bf16[256,256]{1,0:T(8,128)(2,1)S(1)}, u32[]{:S(2)}) copy-start(bf16[256,256]{1,0:T(8,128)(2,1)S(1)} %collective-permute-done.11.b5) | copy-start | bytes 393220
  91.3 16.1 %collective-permute-start.7 = (bf16[1040,256]{1,0:T(8,128)(2,1)}, bf16[1040,256]{1,0:T(8,128)(2,1)S(1)}, u32[]{:S(2)}, u32[]{:S(2)}) collective-permute-start(bf16[1040,256]{1,0:T(8,128)(2,1)} %get-tuple-element.68), channel_id=1, source_target_pairs={{0,1},{1,0},{2,3},{3,2},{4,5},{5,4},{6,7},{7,6},{8,9},{9,8},{10,11... | collective-permute-start | bytes 1597448 | tf_op jit(solution)/shard_map/ppermute | solution.py:424
  105.7 1.8 %copy-start.17 = (bf16[256,256]{1,0:T(8,128)(2,1)}, bf16[256,256]{1,0:T(8,128)(2,1)S(1)}, u32[]{:S(2)}) copy-start(bf16[256,256]{1,0:T(8,128)(2,1)S(1)} %collective-permute-done.12.b6) | copy-start | bytes 393220
  105.7 1.8 %copy-start.18 = (bf16[256,256]{1,0:T(8,128)(2,1)}, bf16[256,256]{1,0:T(8,128)(2,1)S(1)}, u32[]{:S(2)}) copy-start(bf16[256,256]{1,0:T(8,128)(2,1)S(1)} %collective-permute-done.13.b7) | copy-start | bytes 393220
  105.7 1.7 %copy-start.12 = (bf16[528,256]{1,0:T(8,128)(2,1)}, bf16[528,256]{1,0:T(8,128)(2,1)S(1)}, u32[]{:S(2)}) copy-start(bf16[528,256]{1,0:T(8,128)(2,1)S(1)} %collective-permute-done.8.b2) | copy-start | bytes 811012
  105.8 1.7 %copy-start.13 = (bf16[528,256]{1,0:T(8,128)(2,1)}, bf16[528,256]{1,0:T(8,128)(2,1)S(1)}, u32[]{:S(2)}) copy-start(bf16[528,256]{1,0:T(8,128)(2,1)S(1)} %collective-permute-done.9.b3) | copy-start | bytes 811012
  105.8 1.7 %copy-start.6 = (bf16[64,8,256]{2,1,0:T(8,128)(2,1)}, bf16[64,8,256]{2,1,0:T(8,128)(2,1)S(1)}, u32[]{:S(2)}) copy-start(bf16[64,8,256]{2,1,0:T(8,128)(2,1)S(1)} %all-to-all-done.3) | copy-start | bytes 786436
  107.5 0.8 copy-start.7

commit v9 on v8

--- a/solution.py
+++ b/solution.py
@@ -424,15 +424,6 @@
     return lax.ppermute(block, ("z", "y"), [(at, at ^ mask) for at in range(16)])
 
 
-def swap_all(sends):
-    near = [swap(block, mask) for block, mask in zip(sends[:5], (1, 2, 3, 4, 5))]
-    last = []
-    for at, (block, mask) in enumerate(zip(sends[5:], (6, 7))):
-        near[3 + at], block = lax.optimization_barrier((near[3 + at], block))
-        last.append(swap(block, mask))
-    return near + last
-
-
 def swap_quad(block):
     parts = block.reshape(QUADS, 8, block.shape[1])
     return lax.all_to_all(parts, "y", 0, 0).reshape(block.shape)
@@ -454,7 +445,7 @@
     kv, s1, s2, s3, far = call(
         prepare_keys_kernel, both(ROWS, 1040, 528, 256, 8 * FAR), (keys, values, queries, cotangent), wide
     )
-    peers = swap_all([s1, s2, s2, s3, s3, s3, s3])
+    peers = [swap(block, mask) for block, mask in zip((s1, s2, s2, s3, s3), (1, 2, 3, 4, 5))]
     far = swap_far(far)
     state = [((8, HALF), f32), ((HEAD, HALF), f32)]
     stat, out, odd, q, g = call(
@@ -464,7 +455,8 @@
         [pltpu.VMEM((HEAD, ROWS), bf16), *wide],
         flops=LARGE,
     )
-    stat, far = lax.optimization_barrier((stat, far))
+    stat, far, s3, peers[3], peers[4] = lax.optimization_barrier((stat, far, s3, peers[3], peers[4]))
+    peers += [swap(s3, mask) for mask in (6, 7)]
     me = lax.axis_index("y").astype(jnp.int32).reshape(1)
     part, quad = call(
         whole_forward_kernel,

time: 114 us -> 113 us (level)
  starting transfers between devices: 56.1 us -> 54.4 us
    unnamed x40 -> x42, local copies, waits for them, and re-layouts: 3.31 us -> 3.25 us
  transfers between devices with their start and end apart: 18 -> 18, of which waited for: 3 -> 4; matrix products, arithmetic and copies ran while one was open for 0% -> 0% of each run, Pallas kernels for 34% -> 34%
where the time goes in v9:
time: 113 us; the launch traced here: 112 us
  starting transfers between devices  54.4 us (48%)
  Pallas kernels  50.2 us (44%)
  local copies, waits for them, and re-layouts  3.25 us (3%)
  waiting for transfers between devices  3.08 us (3%)
    pallas_call x8, Pallas kernels, call(): pl.pallas_call(kernel, grid=steps, out_shape=[jax.ShapeDtypeStruct(shape,...  50.2 us
    all_to_all x2, starting transfers between devices, swap_far(): return lax.all_to_all(parts, ('grp', 'x', 'z'), 0, 0).reshape(block.shape)  25.2 us
    ppermute x14, starting transfers between devices, swap(): lax.ppermute(block, ('z', 'y'), [(at, at ^ mask) for at in range(16)])  21.6 us
    all_to_all x2, starting transfers between devices, swap_quad(): return lax.all_to_all(parts, 'y', 0, 0).reshape(block.shape)  7.55 us
    unnamed x42, local copies, waits for them, and re-layouts  3.25 us
    ppermute x14, waiting for transfers between devices, swap(): lax.ppermute(block, ('z', 'y'), [(at, at ^ mask) for at in range(16)])  2.38 us
  transfers between devices with their start and end apart: 18, of which 4 were waited for; matrix products, arithmetic and copies ran while one was open for 0% of the time, Pallas kernels for 34%

profile of v9, /device:TPU:1, one launch (start us, length us, event | category | flops | bytes accessed | tf_op | source)
XLA Modules:
  0.0 111.9 jit_solution(15758802357932985313)
XLA Ops:
  0.6 4.4 %shard_map.85 = (bf16[2048,256]{1,0:T(8,128)(2,1)}, bf16[1040,256]{1,0:T(8,128)(2,1)}, bf16[528,256]{1,0:T(8,128)(2,1)}, bf16[256,256]{1,0:T(8,128)(2,1)}, bf16[512,256]{1,0:T(8,128)(2,1)}) custom-call(bf16[2048,128]{1,0:T(8,128)(2,1)} %k_ref.1, bf16[2048,128]{1,0:T(8,128)(2,1)} %v_ref.1, bf16[2048,128]{1,0:T(8,128)(2,1)} %raw_q.1, bf16[2048,128]{1,0:T(8,128)(2,1)} %raw_g.1), custom_call_target="tpu_custom_call" | custom-call | tf_op jit(solution)/shard_map/pallas_call | solution.py:83
  5.0 3.5 %collective-permute-start.1 = (bf16[256,256]{1,0:T(8,128)(2,1)}, bf16[256,256]{1,0:T(8,128)(2,1)S(1)}, u32[]{:S(2)}, u32[]{:S(2)}) collective-permute-start(bf16[256,256]{1,0:T(8,128)(2,1)} %get-tuple-element.51), channel_id=1, source_target_pairs={{0,5},{1,4},{2,7},{3,6},{4,1},{5,0},{6,3},{7,2},{8,13},{9,12},{10,... | collective-permute-start | bytes 393224 | tf_op jit(solution)/shard_map/ppermute | solution.py:424
  8.5 0.0 collective-permute-start
  8.5 1.9 %collective-permute-start.4 = (bf16[528,256]{1,0:T(8,128)(2,1)}, bf16[528,256]{1,0:T(8,128)(2,1)S(1)}, u32[]{:S(2)}, u32[]{:S(2)}) collective-permute-start(bf16[528,256]{1,0:T(8,128)(2,1)} %get-tuple-element.48.own), channel_id=1, source_target_pairs={{0,3},{1,2},{2,1},{3,0},{4,7},{5,6},{6,5},{7,4},{8,11},{9,10},{10,... | collective-permute-start | bytes 811016 | tf_op jit(solution)/shard_map/ppermute | solution.py:424
  10.4 0.7 collective-permute-start.3
  11.1 12.8 %all-to-all-start = ((bf16[64,8,256]{2,1,0:T(8,128)(2,1)}), bf16[64,8,256]{2,1,0:T(8,128)(2,1)S(1)}, u32[]{:S(2)}, u32[]{:S(2)}) async-start(bf16[64,8,256]{2,1,0:T(8,128)(2,1)} %bitcast.13), calls=%async_computation | async-start | bytes 524288 | tf_op jit(solution)/shard_map/all_to_all | solution.py:434
  24.0 1.0 collective-permute-start.2
  25.0 11.0 %shard_map.86 = (f32[8,1024]{1,0:T(8,128)}, f32[128,1024]{1,0:T(8,128)}, f32[8,1024]{1,0:T(8,128)}, bf16[2048,128]{1,0:T(8,128)(2,1)}, bf16[2048,128]{1,0:T(8,128)(2,1)}) custom-call(bf16[2048,128]{1,0:T(8,128)(2,1)} %raw_q.1, bf16[2048,128]{1,0:T(8,128)(2,1)} %raw_g.1, bf16[2048,256]{1,0:T(8,128)(2,1)} %get-tuple-element.39.kv_ref, ...), custom_call_target="tpu_custom_call" | custom-call | flops 10000000000 | tf_op jit(solution)/shard_map/pallas_call | solution.py:83
  36.0 0.0 collective-permute-done.1.rest_4_.rest_1_
  36.0 0.0 collective-permute-done.rest_3_.rest_0_
  36.0 0.6 all-to-all-done
  36.6 2.9 %collective-permute-start.6 = (bf16[256,256]{1,0:T(8,128)(2,1)S(1)}, bf16[256,256]{1,0:T(8,128)(2,1)S(1)}, u32[]{:S(2)}, u32[]{:S(2)}) collective-permute-start(bf16[256,256]{1,0:T(8,128)(2,1)S(1)} %copy-done.20), channel_id=1, source_target_pairs={{0,7},{1,6},{2,5},{3,4},{4,3},{5,2},{6,1},{7,0},{8,15},{9,14},{10,... | collective-permute-start | bytes 393224 | tf_op jit(solution)/shard_map/ppermute | solution.py:424
  39.5 0.7 collective-permute-start.5
  40.2 0.0 collective-permute-done.4.rest_2_.r3.rest_3_
  40.2 0.0 collective-permute-done.3.rest_1_.r2.rest_2_
  40.2 0.0 collective-permute-done.2.rest_0_.r1.rest_1_
  40.3 0.0 copy-start
  40.3 1.0 shard_map.88
  41.3 0.6 copy-done.5
  41.9 3.9 %all-to-all-start.1 = ((f32[4,8,384]{2,1,0:T(8,128)}), f32[4,8,384]{2,1,0:T(8,128)S(1)}, u32[]{:S(2)}, u32[]{:S(2)}) async-start(f32[4,8,384]{2,1,0:T(8,128)} %bitcast.3), calls=%async_computation.1 | async-start | bytes 98304 | tf_op jit(solution)/shard_map/all_to_all | solution.py:429
  45.8 0.0 collective-permute-done.6.rest_6_.rest_3_
  45.8 0.6 collective-permute-done.5.rest_5_.rest_2_
  46.5 0.6 copy-done.11
  47.1 5.4 %shard_map.87 = (f32[8,1024]{1,0:T(8,128)}, f32[128,1024]{1,0:T(8,128)}) custom-call(bf16[2048,128]{1,0:T(8,128)(2,1)} %get-tuple-element.40.q_ref, f32[8,1024]{1,0:T(8,128)} %constant.9.clone.bias_ref, f32[8,1024]{1,0:T(8,128)} %get-tuple-element.45.stat_ref, f32[128,1024]{1,0:T(8,128)} %get-tuple-element.46.out_ref, bf16[1040,256]{1,0:T(8,128)(2,1)} %copy-done, ...), custom_call_target="tpu_custom_call" | custom-call | tf_op jit(solution)/shard_map/pallas_call | solution.py:83
  52.5 0.0 all-to-all-done.1
  52.5 0.6 copy-done.14
  53.1 3.0 %shard_map.89 = (bf16[256,256]{1,0:T(8,128)(2,1)}, bf16[256,256]{1,0:T(8,128)(2,1)}, bf16[256,256]{1,0:T(8,128)(2,1)}, bf16[256,256]{1,0:T(8,128)(2,1)}, f32[128...) custom-call(bf16[2048,128]{1,0:T(8,128)(2,1)} %get-tuple-element.40.q_ref, ...), custom_call_target="tpu_custom_call" | custom-call | tf_op jit(solution)/shard_map/pallas_call | solution.py:83
  56.0 0.6 collective-permute-start.10
  56.6 1.5 %collective-permute-start.11 = (bf16[256,256]{1,0:T(8,128)(2,1)}, bf16[256,256]{1,0:T(8,128)(2,1)S(1)}, u32[]{:S(2)}, u32[]{:S(2)}) collective-permute-start(bf16[256,256]{1,0:T(8,128)(2,1)} %get-tuple-element.70), channel_id=1, source_target_pairs={{0,5},{1,4},{2,7},{3,6},{4,1},{5,0},{6,3},{7,2},{8,13},{9,12},{10,... | collective-permute-start | bytes 393224 | tf_op jit(solution)/shard_map/ppermute | solution.py:424
  58.1 3.7 %all-to-all-start.2 = ((f32[4,8,128]{2,1,0:T(8,128)}), f32[4,8,128]{2,1,0:T(8,128)S(1)}, u32[]{:S(2)}, u32[]{:S(2)}) async-start(f32[4,8,128]{2,1,0:T(8,128)} %bitcast.16), calls=%async_computation.2 | async-start | bytes 32768 | tf_op jit(solution)/shard_map/all_to_all | solution.py:429
  61.8 3.5 %collective-permute-start.12 = (bf16[256,256]{1,0:T(8,128)(2,1)}, bf16[256,256]{1,0:T(8,128)(2,1)S(1)}, u32[]{:S(2)}, u32[]{:S(2)}) collective-permute-start(bf16[256,256]{1,0:T(8,128)(2,1)} %get-tuple-element.71), channel_id=1, source_target_pairs={{0,6},{1,7},{2,4},{3,5},{4,2},{5,3},{6,0},{7,1},{8,14},{9,15},{10,... | collective-permute-start | bytes 393224 | tf_op jit(solution)/shard_map/ppermute | solution.py:424
  65.3 1.3 %collective-permute-start.13 = (bf16[256,256]{1,0:T(8,128)(2,1)}, bf16[256,256]{1,0:T(8,128)(2,1)S(1)}, u32[]{:S(2)}, u32[]{:S(2)}) collective-permute-start(bf16[256,256]{1,0:T(8,128)(2,1)} %get-tuple-element.72), channel_id=1, source_target_pairs={{0,7},{1,6},{2,5},{3,4},{4,3},{5,2},{6,1},{7,0},{8,15},{9,14},{10,... | collective-permute-start | bytes 393224 | tf_op jit(solution)/shard_map/ppermute | solution.py:424
  66.5 0.1 all-to-all-done.2
  66.6 0.6 copy-done.19
  67.2 6.6 %shard_map.90 = (bf16[1040,256]{1,0:T(8,128)(2,1)}, bf16[528,256]{1,0:T(8,128)(2,1)}, bf16[528,256]{1,0:T(8,128)(2,1)}, bf16[512,256]{1,0:T(8,128)(2,1)}, f32[128,1024]{1,0:T(8,128)}, /*index=5*/f32[8,128]{1,0:T(8,128)}) custom-call(s32[1]{0:T(128)} %bitcast.2.me_ref, bf16[2048,128]{1,0:T(8,128)(2,1)} %get-tuple-element.40.q_ref, ...), custom_call_target="tpu_custom_call" | custom-call | tf_op jit(solution)/shard_map/pallas_call | solution.py:83
  73.8 12.4 %all-to-all-start.3 = ((bf16[64,8,256]{2,1,0:T(8,128)(2,1)}), bf16[64,8,256]{2,1,0:T(8,128)(2,1)S(1)}, u32[]{:S(2)}, u32[]{:S(2)}) async-start(bf16[64,8,256]{2,1,0:T(8,128)(2,1)} %bitcast.12), calls=%async_computation.3 | async-start | bytes 524288 | tf_op jit(solution)/shard_map/all_to_all | solution.py:434
  86.2 1.3 %collective-permute-start.8 = (bf16[528,256]{1,0:T(8,128)(2,1)}, bf16[528,256]{1,0:T(8,128)(2,1)S(1)}, u32[]{:S(2)}, u32[]{:S(2)}) collective-permute-start(bf16[528,256]{1,0:T(8,128)(2,1)} %get-tuple-element.67), channel_id=1, source_target_pairs={{0,2},{1,3},{2,0},{3,1},{4,6},{5,7},{6,4},{7,5},{8,10},{9,11},{10,... | collective-permute-start | bytes 811016 | tf_op jit(solution)/shard_map/ppermute | solution.py:424
  87.4 0.0 collective-permute-done.10.b4
  87.4 2.8 %collective-permute-start.9 = (bf16[528,256]{1,0:T(8,128)(2,1)}, bf16[528,256]{1,0:T(8,128)(2,1)S(1)}, u32[]{:S(2)}, u32[]{:S(2)}) collective-permute-start(bf16[528,256]{1,0:T(8,128)(2,1)} %get-tuple-element.68), channel_id=1, source_target_pairs={{0,3},{1,2},{2,1},{3,0},{4,7},{5,6},{6,5},{7,4},{8,11},{9,10},{10,... | collective-permute-start | bytes 811016 | tf_op jit(solution)/shard_map/ppermute | solution.py:424
  90.3 0.0 collective-permute-done.11.b5
  90.3 0.0 collective-permute-start.7
  90.3 14.3 %shard_map.91 = (f32[2048,128]{1,0:T(8,128)}, f32[2048,256]{1,0:T(8,128)}) custom-call(bf16[2048,128]{1,0:T(8,128)(2,1)} %get-tuple-element.40.q_ref, bf16[2048,128]{1,0:T(8,128)(2,1)} %get-tuple-element.41.g_ref, f32[8,2048]{1,0:T(8,128)} %constant.8.clone.bias_ref, f32[8,2048]{1,0:T(8,128)} %get-tuple-element.57.row_ref, ...), custom_call_target="tpu_custom_call" | custom-call | flops 10000000000 | tf_op jit(solution)/shard_map/pallas_call | solution.py:83
  104.6 0.0 collective-permute-done.13.b7
  104.7 0.0 collective-permute-done.8.b2
  104.7 0.0 all-to-all-done.3
  104.7 1.7 %collective-permute-done.7.b1 = bf16[1040,256]{1,0:T(8,128)(2,1)S(1)} collective-permute-done((bf16[1040,256]{1,0:T(8,128)(2,1)}, bf16[1040,256]{1,0:T(8,128)(2,1)S(1)}, u32[]{:S(2)}, u32[]{:S(2)}) %collective-permute-start.7) | collective-permute-done | bytes 532512 | tf_op jit(solution)/shard_map/ppermute | solution.py:424
  106.5 0.8 copy-done.7
  107.2 4.5 %shard_map.92 = (f32[2048,128]{1,0:T(8,128)}, f32[2048,128]{1,0:T(8,128)}, f32[2048,128]{1,0:T(8,128)}) custom-call(f32[2048,256]{1,0:T(8,128)} %get-tuple-element.64.dkv_ref, f32[8,128]{1,0:T(8,128)} %get-tuple-element.65.mine_ref, bf16[1040,256]{1,0:T(8,128)(2,1)} %copy-done.7, bf16[528,256]{1,0:T(8,128)(2,1)} %copy-done.12, ...), custom_call_target="tpu_custom_call", output_to_operand_aliasing={{0}: (10, {})} | custom-call | tf_op jit(solution)/shard_map/pallas_call | solution.py:83
  (38 shorter events, 0.1 us)
Async XLA Ops:
  5.0 31.0 %collective-permute-start.1 = (bf16[256,256]{1,0:T(8,128)(2,1)}, bf16[256,256]{1,0:T(8,128)(2,1)S(1)}, u32[]{:S(2)}, u32[]{:S(2)}) collective-permute-start(bf16[256,256]{1,0:T(8,128)(2,1)} %get-tuple-element.51), channel_id=1, source_target_pairs={{0,5},{1,4},{2,7},{3,6},{4,1},{5,0},{6,3},{7,2},{8,13},{9,12},{10,... | collective-permute-start | bytes 393224 | tf_op jit(solution)/shard_map/ppermute | solution.py:424
  8.5 27.5 %collective-permute-start = (bf16[256,256]{1,0:T(8,128)(2,1)}, bf16[256,256]{1,0:T(8,128)(2,1)S(1)}, u32[]{:S(2)}, u32[]{:S(2)}) collective-permute-start(bf16[256,256]{1,0:T(8,128)(2,1)} %get-tuple-element.51), channel_id=1, source_target_pairs={{0,4},{1,5},{2,6},{3,7},{4,0},{5,1},{6,2},{7,3},{8,12},{9,13},{10,... | collective-permute-start | bytes 393224 | tf_op jit(solution)/shard_map/ppermute | solution.py:424
  8.5 31.7 %collective-permute-start.4 = (bf16[528,256]{1,0:T(8,128)(2,1)}, bf16[528,256]{1,0:T(8,128)(2,1)S(1)}, u32[]{:S(2)}, u32[]{:S(2)}) collective-permute-start(bf16[528,256]{1,0:T(8,128)(2,1)} %get-tuple-element.48.own), channel_id=1, source_target_pairs={{0,3},{1,2},{2,1},{3,0},{4,7},{5,6},{6,5},{7,4},{8,11},{9,10},{10,... | collective-permute-start | bytes 811016 | tf_op jit(solution)/shard_map/ppermute | solution.py:424
  10.4 29.8 %collective-permute-start.3 = (bf16[528,256]{1,0:T(8,128)(2,1)}, bf16[528,256]{1,0:T(8,128)(2,1)S(1)}, u32[]{:S(2)}, u32[]{:S(2)}) collective-permute-start(bf16[528,256]{1,0:T(8,128)(2,1)} %get-tuple-element.48.own), channel_id=1, source_target_pairs={{0,2},{1,3},{2,0},{3,1},{4,6},{5,7},{6,4},{7,5},{8,10},{9,11},{10,... | collective-permute-start | bytes 811016 | tf_op jit(solution)/shard_map/ppermute | solution.py:424
  11.1 25.5 %all-to-all-start = ((bf16[64,8,256]{2,1,0:T(8,128)(2,1)}), bf16[64,8,256]{2,1,0:T(8,128)(2,1)S(1)}, u32[]{:S(2)}, u32[]{:S(2)}) async-start(bf16[64,8,256]{2,1,0:T(8,128)(2,1)} %bitcast.13), calls=%async_computation | async-start | bytes 524288 | tf_op jit(solution)/shard_map/all_to_all | solution.py:434
  24.0 16.3 %collective-permute-start.2 = (bf16[1040,256]{1,0:T(8,128)(2,1)}, bf16[1040,256]{1,0:T(8,128)(2,1)S(1)}, u32[]{:S(2)}, u32[]{:S(2)}) collective-permute-start(bf16[1040,256]{1,0:T(8,128)(2,1)} %get-tuple-element.47), channel_id=1, source_target_pairs={{0,1},{1,0},{2,3},{3,2},{4,5},{5,4},{6,7},{7,6},{8,9},{9,8},{10,11... | collective-permute-start | bytes 1597448 | tf_op jit(solution)/shard_map/ppermute | solution.py:424
  25.0 11.7 %copy-start.20 = (bf16[256,256]{1,0:T(8,128)(2,1)S(1)}, bf16[256,256]{1,0:T(8,128)(2,1)}, u32[]{:S(2)}) copy-start(bf16[256,256]{1,0:T(8,128)(2,1)} %get-tuple-element.51) | copy-start | bytes 393220
  25.0 15.3 %copy-start.4 = (bf16[528,256]{1,0:T(8,128)(2,1)S(1)}, bf16[528,256]{1,0:T(8,128)(2,1)}, u32[]{:S(2)}) copy-start(bf16[528,256]{1,0:T(8,128)(2,1)} %get-tuple-element.48.own) | copy-start | bytes 811012
  36.0 10.4 %copy-start.8 = (bf16[256,256]{1,0:T(8,128)(2,1)}, bf16[256,256]{1,0:T(8,128)(2,1)S(1)}, u32[]{:S(2)}) copy-start(bf16[256,256]{1,0:T(8,128)(2,1)S(1)} %collective-permute-done.1.rest_4_.rest_1_) | copy-start | bytes 393220
  36.0 10.4 %copy-start.9 = (bf16[256,256]{1,0:T(8,128)(2,1)}, bf16[256,256]{1,0:T(8,128)(2,1)S(1)}, u32[]{:S(2)}) copy-start(bf16[256,256]{1,0:T(8,128)(2,1)S(1)} %collective-permute-done.rest_3_.rest_0_) | copy-start | bytes 393220
  36.6 15.8 %copy-start.3 = (bf16[64,8,256]{2,1,0:T(8,128)(2,1)}, bf16[64,8,256]{2,1,0:T(8,128)(2,1)S(1)}, u32[]{:S(2)}) copy-start(bf16[64,8,256]{2,1,0:T(8,128)(2,1)S(1)} %all-to-all-done) | copy-start | bytes 786436
  36.6 9.2 %collective-permute-start.6 = (bf16[256,256]{1,0:T(8,128)(2,1)S(1)}, bf16[256,256]{1,0:T(8,128)(2,1)S(1)}, u32[]{:S(2)}, u32[]{:S(2)}) collective-permute-start(bf16[256,256]{1,0:T(8,128)(2,1)S(1)} %copy-done.20), channel_id=1, source_target_pairs={{0,7},{1,6},{2,5},{3,4},{4,3},{5,2},{6,1},{7,0},{8,15},{9,14},{10,... | collective-permute-start | bytes 393224 | tf_op jit(solution)/shard_map/ppermute | solution.py:424
  39.5 6.9 %collective-permute-start.5 = (bf16[256,256]{1,0:T(8,128)(2,1)S(1)}, bf16[256,256]{1,0:T(8,128)(2,1)S(1)}, u32[]{:S(2)}, u32[]{:S(2)}) collective-permute-start(bf16[256,256]{1,0:T(8,128)(2,1)S(1)} %copy-done.20), channel_id=1, source_target_pairs={{0,6},{1,7},{2,4},{3,5},{4,2},{5,3},{6,0},{7,1},{8,14},{9,15},{10,... | collective-permute-start | bytes 393224 | tf_op jit(solution)/shard_map/ppermute | solution.py:424
  40.2 6.2 %copy-start.1 = (bf16[528,256]{1,0:T(8,128)(2,1)}, bf16[528,256]{1,0:T(8,128)(2,1)S(1)}, u32[]{:S(2)}) copy-start(bf16[528,256]{1,0:T(8,128)(2,1)S(1)} %collective-permute-done.4.rest_2_.r3.rest_3_) | copy-start | bytes 811012
  40.2 6.2 %copy-start.2 = (bf16[528,256]{1,0:T(8,128)(2,1)}, bf16[528,256]{1,0:T(8,128)(2,1)S(1)}, u32[]{:S(2)}) copy-start(bf16[528,256]{1,0:T(8,128)(2,1)S(1)} %collective-permute-done.3.rest_1_.r2.rest_2_) | copy-start | bytes 811012
  40.3 6.2 %copy-start = (bf16[1040,256]{1,0:T(8,128)(2,1)}, bf16[1040,256]{1,0:T(8,128)(2,1)S(1)}, u32[]{:S(2)}) copy-start(bf16[1040,256]{1,0:T(8,128)(2,1)S(1)} %collective-permute-done.2.rest_0_.r1.rest_1_) | copy-start | bytes 1597444
  41.3 0.6 copy-start.5
  41.9 10.6 %all-to-all-start.1 = ((f32[4,8,384]{2,1,0:T(8,128)}), f32[4,8,384]{2,1,0:T(8,128)S(1)}, u32[]{:S(2)}, u32[]{:S(2)}) async-start(f32[4,8,384]{2,1,0:T(8,128)} %bitcast.3), calls=%async_computation.1 | async-start | bytes 98304 | tf_op jit(solution)/shard_map/all_to_all | solution.py:429
  45.8 0.7 copy-start.10
  46.4 0.6 copy-start.11
  52.5 0.6 copy-start.14
  56.0 31.4 %collective-permute-start.10 = (bf16[256,256]{1,0:T(8,128)(2,1)}, bf16[256,256]{1,0:T(8,128)(2,1)S(1)}, u32[]{:S(2)}, u32[]{:S(2)}) collective-permute-start(bf16[256,256]{1,0:T(8,128)(2,1)} %get-tuple-element.69), channel_id=1, source_target_pairs={{0,4},{1,5},{2,6},{3,7},{4,0},{5,1},{6,2},{7,3},{8,12},{9,13},{10,... | collective-permute-start | bytes 393224 | tf_op jit(solution)/shard_map/ppermute | solution.py:424
  56.6 33.6 %collective-permute-start.11 = (bf16[256,256]{1,0:T(8,128)(2,1)}, bf16[256,256]{1,0:T(8,128)(2,1)S(1)}, u32[]{:S(2)}, u32[]{:S(2)}) collective-permute-start(bf16[256,256]{1,0:T(8,128)(2,1)} %get-tuple-element.70), channel_id=1, source_target_pairs={{0,5},{1,4},{2,7},{3,6},{4,1},{5,0},{6,3},{7,2},{8,13},{9,12},{10,... | collective-permute-start | bytes 393224 | tf_op jit(solution)/shard_map/ppermute | solution.py:424
  58.1 8.5 %all-to-all-start.2 = ((f32[4,8,128]{2,1,0:T(8,128)}), f32[4,8,128]{2,1,0:T(8,128)S(1)}, u32[]{:S(2)}, u32[]{:S(2)}) async-start(f32[4,8,128]{2,1,0:T(8,128)} %bitcast.16), calls=%async_computation.2 | async-start | bytes 32768 | tf_op jit(solution)/shard_map/all_to_all | solution.py:429
  61.8 42.9 %collective-permute-start.12 = (bf16[256,256]{1,0:T(8,128)(2,1)}, bf16[256,256]{1,0:T(8,128)(2,1)S(1)}, u32[]{:S(2)}, u32[]{:S(2)}) collective-permute-start(bf16[256,256]{1,0:T(8,128)(2,1)} %get-tuple-element.71), channel_id=1, source_target_pairs={{0,6},{1,7},{2,4},{3,5},{4,2},{5,3},{6,0},{7,1},{8,14},{9,15},{10,... | collective-permute-start | bytes 393224 | tf_op jit(solution)/shard_map/ppermute | solution.py:424
  65.3 39.4 %collective-permute-start.13 = (bf16[256,256]{1,0:T(8,128)(2,1)}, bf16[256,256]{1,0:T(8,128)(2,1)S(1)}, u32[]{:S(2)}, u32[]{:S(2)}) collective-permute-start(bf16[256,256]{1,0:T(8,128)(2,1)} %get-tuple-element.72), channel_id=1, source_target_pairs={{0,7},{1,6},{2,5},{3,4},{4,3},{5,2},{6,1},{7,0},{8,15},{9,14},{10,... | collective-permute-start | bytes 393224 | tf_op jit(solution)/shard_map/ppermute | solution.py:424
  66.6 0.6 copy-start.19
  73.8 30.9 %all-to-all-start.3 = ((bf16[64,8,256]{2,1,0:T(8,128)(2,1)}), bf16[64,8,256]{2,1,0:T(8,128)(2,1)S(1)}, u32[]{:S(2)}, u32[]{:S(2)}) async-start(bf16[64,8,256]{2,1,0:T(8,128)(2,1)} %bitcast.12), calls=%async_computation.3 | async-start | bytes 524288 | tf_op jit(solution)/shard_map/all_to_all | solution.py:434
  86.2 18.5 %collective-permute-start.8 = (bf16[528,256]{1,0:T(8,128)(2,1)}, bf16[528,256]{1,0:T(8,128)(2,1)S(1)}, u32[]{:S(2)}, u32[]{:S(2)}) collective-permute-start(bf16[528,256]{1,0:T(8,128)(2,1)} %get-tuple-element.67), channel_id=1, source_target_pairs={{0,2},{1,3},{2,0},{3,1},{4,6},{5,7},{6,4},{7,5},{8,10},{9,11},{10,... | collective-permute-start | bytes 811016 | tf_op jit(solution)/shard_map/ppermute | solution.py:424
  87.4 17.2 %copy-start.15 = (bf16[256,256]{1,0:T(8,128)(2,1)}, bf16[256,256]{1,0:T(8,128)(2,1)S(1)}, u32[]{:S(2)}) copy-start(bf16[256,256]{1,0:T(8,128)(2,1)S(1)} %collective-permute-done.10.b4) | copy-start | bytes 393220
  87.4 17.2 %collective-permute-start.9 = (bf16[528,256]{1,0:T(8,128)(2,1)}, bf16[528,256]{1,0:T(8,128)(2,1)S(1)}, u32[]{:S(2)}, u32[]{:S(2)}) collective-permute-start(bf16[528,256]{1,0:T(8,128)(2,1)} %get-tuple-element.68), channel_id=1, source_target_pairs={{0,3},{1,2},{2,1},{3,0},{4,7},{5,6},{6,5},{7,4},{8,11},{9,10},{10,... | collective-permute-start | bytes 811016 | tf_op jit(solution)/shard_map/ppermute | solution.py:424
  90.3 14.3 %copy-start.16 = (bf16[256,256]{1,0:T(8,128)(2,1)}, bf16[256,256]{1,0:T(8,128)(2,1)S(1)}, u32[]{:S(2)}) copy-start(bf16[256,256]{1,0:T(8,128)(2,1)S(1)} %collective-permute-done.11.b5) | copy-start | bytes 393220
  90.3 16.1 %collective-permute-start.7 = (bf16[1040,256]{1,0:T(8,128)(2,1)}, bf16[1040,256]{1,0:T(8,128)(2,1)S(1)}, u32[]{:S(2)}, u32[]{:S(2)}) collective-permute-start(bf16[1040,256]{1,0:T(8,128)(2,1)} %get-tuple-element.66), channel_id=1, source_target_pairs={{0,1},{1,0},{2,3},{3,2},{4,5},{5,4},{6,7},{7,6},{8,9},{9,8},{10,11... | collective-permute-start | bytes 1597448 | tf_op jit(solution)/shard_map/ppermute | solution.py:424
  104.6 1.8 %copy-start.17 = (bf16[256,256]{1,0:T(8,128)(2,1)}, bf16[256,256]{1,0:T(8,128)(2,1)S(1)}, u32[]{:S(2)}) copy-start(bf16[256,256]{1,0:T(8,128)(2,1)S(1)} %collective-permute-done.12.b6) | copy-start | bytes 393220
  104.7 1.8 %copy-start.18 = (bf16[256,256]{1,0:T(8,128)(2,1)}, bf16[256,256]{1,0:T(8,128)(2,1)S(1)}, u32[]{:S(2)}) copy-start(bf16[256,256]{1,0:T(8,128)(2,1)S(1)} %collective-permute-done.13.b7) | copy-start | bytes 393220
  104.7 1.8 %copy-start.12 = (bf16[528,256]{1,0:T(8,128)(2,1)}, bf16[528,256]{1,0:T(8,128)(2,1)S(1)}, u32[]{:S(2)}) copy-start(bf16[528,256]{1,0:T(8,128)(2,1)S(1)} %collective-permute-done.8.b2) | copy-start | bytes 811012
  104.7 1.7 %copy-start.13 = (bf16[528,256]{1,0:T(8,128)(2,1)}, bf16[528,256]{1,0:T(8,128)(2,1)S(1)}, u32[]{:S(2)}) copy-start(bf16[528,256]{1,0:T(8,128)(2,1)S(1)} %collective-permute-done.9.b3) | copy-start | bytes 811012
  104.7 1.7 %copy-start.6 = (bf16[64,8,256]{2,1,0:T(8,128)(2,1)}, bf16[64,8,256]{2,1,0:T(8,128)(2,1)S(1)}, u32[]{:S(2)}) copy-start(bf16[64,8,256]{2,1,0:T(8,128)(2,1)S(1)} %all-to-all-done.3) | copy-start | bytes 786436
  106.4 0.8 copy-start.7

commit v10 on v9

--- a/solution.py
+++ b/solution.py
@@ -61,7 +61,7 @@
     return lax.dot_general(left, right, (((0,), (0,)), ((), ())), preferred_element_type=jnp.float32)
 
 
-def call(kernel, outs, args, scratch=(), scalars=0, steps=(), in_steps=(), out_steps=(), lane_steps=(), in_place=None, first=None, flops=0, vmem=60):
+def call(kernel, outs, args, scratch=(), scalars=0, steps=(), in_steps=(), out_steps=(), lane_steps=(), in_place=None, at_home=(), first=None, flops=0, vmem=60):
     first = first or {}
     steps = steps or ((1,) if first else ())
 
@@ -84,7 +84,7 @@
         kernel,
         grid=steps,
         out_shape=[jax.ShapeDtypeStruct(shape, dtype) for shape, dtype in outs],
-        in_specs=[spec(arg.shape, at in in_steps, at == in_place, at < scalars, first.get(at), at in lane_steps) for at, arg in enumerate(args)],
+        in_specs=[spec(arg.shape, at in in_steps, at == in_place or at in at_home, at < scalars, first.get(at), at in lane_steps) for at, arg in enumerate(args)],
         out_specs=[
             spec(shape, at in out_steps, bool(lane_steps)) for at, (shape, _) in enumerate(outs)
         ],
@@ -113,15 +113,24 @@
         target[at : at + 16, lane : lane + pair.shape[1]] = pair
 
 
-def prepare_keys_kernel(k_ref, v_ref, q_ref, g_ref, kv_ref, s1_ref, s2_ref, s3_ref, far_ref, wide):
+def prepare_keys_kernel(k_ref, v_ref, q_ref, g_ref, kv_ref, s1_ref, s2_ref, s3_ref, far_ref, wide, tiles, sem):
+    copies = []
+    for index, ref in enumerate((q_ref, g_ref)):
+        for at in range(8):
+            source, target = ref.at[pl.ds(256 * at, 16)], tiles.at[index, pl.ds(16 * at, 16)]
+            copies.append(pltpu.make_async_copy(source, target, sem.at[8 * index + at]))
+    for copy in copies:
+        copy.start()
     sort_rows(k_ref, kv_ref, 0, wide)
     sort_rows(v_ref, kv_ref, HEAD, wide)
     s1_ref[:1024] = kv_ref[:1024]
     s2_ref[:512] = kv_ref[:512]
     s3_ref[...] = kv_ref[:256]
     repeat_first(kv_ref, far_ref, 0)
-    for lane, ref in ((0, q_ref), (HEAD, g_ref)):
-        rows = [ref[at : at + 16, :].astype(jnp.float32)[:1] for at in range(0, ROWS, 256)]
+    for copy in copies:
+        copy.wait()
+    for index, lane in enumerate((0, HEAD)):
+        rows = [tiles[index, at : at + 16, :].astype(jnp.float32)[:1] for at in range(0, 128, 16)]
         block = jnp.concatenate(rows + rows, 0).astype(jnp.bfloat16)
         s1_ref[1024:, lane : lane + HEAD] = block
         s2_ref[512:, lane : lane + HEAD] = block
@@ -443,7 +452,9 @@
 
     wide = [pltpu.VMEM((ROWS, HEAD), f32)]
     kv, s1, s2, s3, far = call(
-        prepare_keys_kernel, both(ROWS, 1040, 528, 256, 8 * FAR), (keys, values, queries, cotangent), wide
+        prepare_keys_kernel, both(ROWS, 1040, 528, 256, 8 * FAR), (keys, values, queries, cotangent),
+        [*wide, pltpu.VMEM((2, 128, HEAD), bf16), pltpu.SemaphoreType.DMA((16,))],
+        at_home=(2, 3),
     )
     peers = [swap(block, mask) for block, mask in zip((s1, s2, s2, s3, s3), (1, 2, 3, 4, 5))]
     far = swap_far(far)

time: 113 us -> 112 us (level)
  no operation moved by 1% of the time
where the time goes in v10:
time: 112 us
  starting transfers between devices  54.4 us (49%)
  Pallas kernels  49.9 us (45%)
  local copies, waits for them, and re-layouts  3.25 us (3%)
  waiting for transfers between devices  3.08 us (3%)
    pallas_call x8, Pallas kernels, call(): pl.pallas_call(kernel, grid=steps, out_shape=[jax.ShapeDtypeStruct(shape,...  49.9 us
    all_to_all x2, starting transfers between devices, swap_far(): return lax.all_to_all(parts, ('grp', 'x', 'z'), 0, 0).reshape(block.shape)  25.2 us
    ppermute x14, starting transfers between devices, swap(): lax.ppermute(block, ('z', 'y'), [(at, at ^ mask) for at in range(16)])  21.7 us
    all_to_all x2, starting transfers between devices, swap_quad(): return lax.all_to_all(parts, 'y', 0, 0).reshape(block.shape)  7.55 us
    unnamed x42, local copies, waits for them, and re-layouts  3.25 us
    ppermute x14, waiting for transfers between devices, swap(): lax.ppermute(block, ('z', 'y'), [(at, at ^ mask) for at in range(16)])  2.38 us
  transfers between devices with their start and end apart: 18, of which 4 were waited for; matrix products, arithmetic and copies ran while one was open for 0% of the time, Pallas kernels for 34%

profile of v10, /device:TPU:1, one launch (start us, length us, event | category | flops | bytes accessed | tf_op | source)
XLA Modules:
  0.0 111.8 jit_solution(16468667222735672669)
XLA Ops:
  0.6 4.1 %shard_map.85 = (bf16[2048,256]{1,0:T(8,128)(2,1)}, bf16[1040,256]{1,0:T(8,128)(2,1)}, bf16[528,256]{1,0:T(8,128)(2,1)}, bf16[256,256]{1,0:T(8,128)(2,1)}, bf16[512,256]{1,0:T(8,128)(2,1)}) custom-call(bf16[2048,128]{1,0:T(8,128)(2,1)} %k_ref.1, bf16[2048,128]{1,0:T(8,128)(2,1)} %v_ref.1, bf16[2048,128]{1,0:T(8,128)(2,1)} %raw_q.1, bf16[2048,128]{1,0:T(8,128)(2,1)} %raw_g.1), custom_call_target="tpu_custom_call" | custom-call | tf_op jit(solution)/shard_map/pallas_call | solution.py:83
  4.8 3.6 %collective-permute-start.1 = (bf16[256,256]{1,0:T(8,128)(2,1)}, bf16[256,256]{1,0:T(8,128)(2,1)S(1)}, u32[]{:S(2)}, u32[]{:S(2)}) collective-permute-start(bf16[256,256]{1,0:T(8,128)(2,1)} %get-tuple-element.51), channel_id=1, source_target_pairs={{0,5},{1,4},{2,7},{3,6},{4,1},{5,0},{6,3},{7,2},{8,13},{9,12},{10,... | collective-permute-start | bytes 393224 | tf_op jit(solution)/shard_map/ppermute | solution.py:433
  8.3 0.0 collective-permute-start
  8.3 1.9 %collective-permute-start.4 = (bf16[528,256]{1,0:T(8,128)(2,1)}, bf16[528,256]{1,0:T(8,128)(2,1)S(1)}, u32[]{:S(2)}, u32[]{:S(2)}) collective-permute-start(bf16[528,256]{1,0:T(8,128)(2,1)} %get-tuple-element.48.own), channel_id=1, source_target_pairs={{0,3},{1,2},{2,1},{3,0},{4,7},{5,6},{6,5},{7,4},{8,11},{9,10},{10,... | collective-permute-start | bytes 811016 | tf_op jit(solution)/shard_map/ppermute | solution.py:433
  10.2 0.7 collective-permute-start.3
  11.0 12.8 %all-to-all-start = ((bf16[64,8,256]{2,1,0:T(8,128)(2,1)}), bf16[64,8,256]{2,1,0:T(8,128)(2,1)S(1)}, u32[]{:S(2)}, u32[]{:S(2)}) async-start(bf16[64,8,256]{2,1,0:T(8,128)(2,1)} %bitcast.13), calls=%async_computation | async-start | bytes 524288 | tf_op jit(solution)/shard_map/all_to_all | solution.py:443
  23.8 1.0 collective-permute-start.2
  24.8 11.0 %shard_map.86 = (f32[8,1024]{1,0:T(8,128)}, f32[128,1024]{1,0:T(8,128)}, f32[8,1024]{1,0:T(8,128)}, bf16[2048,128]{1,0:T(8,128)(2,1)}, bf16[2048,128]{1,0:T(8,128)(2,1)}) custom-call(bf16[2048,128]{1,0:T(8,128)(2,1)} %raw_q.1, bf16[2048,128]{1,0:T(8,128)(2,1)} %raw_g.1, bf16[2048,256]{1,0:T(8,128)(2,1)} %get-tuple-element.39.kv_ref, ...), custom_call_target="tpu_custom_call" | custom-call | flops 10000000000 | tf_op jit(solution)/shard_map/pallas_call | solution.py:83
  35.8 0.0 collective-permute-done.1.rest_4_.rest_1_
  35.8 0.0 collective-permute-done.rest_3_.rest_0_
  35.9 0.6 all-to-all-done
  36.5 2.9 %collective-permute-start.6 = (bf16[256,256]{1,0:T(8,128)(2,1)S(1)}, bf16[256,256]{1,0:T(8,128)(2,1)S(1)}, u32[]{:S(2)}, u32[]{:S(2)}) collective-permute-start(bf16[256,256]{1,0:T(8,128)(2,1)S(1)} %copy-done.20), channel_id=1, source_target_pairs={{0,7},{1,6},{2,5},{3,4},{4,3},{5,2},{6,1},{7,0},{8,15},{9,14},{10,... | collective-permute-start | bytes 393224 | tf_op jit(solution)/shard_map/ppermute | solution.py:433
  39.3 0.7 collective-permute-start.5
  40.1 0.0 collective-permute-done.4.rest_2_.r3.rest_3_
  40.1 0.0 collective-permute-done.3.rest_1_.r2.rest_2_
  40.1 0.0 collective-permute-done.2.rest_0_.r1.rest_1_
  40.1 0.0 copy-start
  40.1 1.0 shard_map.88
  41.1 0.6 copy-done.5
  41.7 3.9 %all-to-all-start.1 = ((f32[4,8,384]{2,1,0:T(8,128)}), f32[4,8,384]{2,1,0:T(8,128)S(1)}, u32[]{:S(2)}, u32[]{:S(2)}) async-start(f32[4,8,384]{2,1,0:T(8,128)} %bitcast.3), calls=%async_computation.1 | async-start | bytes 98304 | tf_op jit(solution)/shard_map/all_to_all | solution.py:438
  45.6 0.0 collective-permute-done.6.rest_6_.rest_3_
  45.6 0.6 collective-permute-done.5.rest_5_.rest_2_
  46.3 0.6 copy-done.11
  46.9 5.4 %shard_map.87 = (f32[8,1024]{1,0:T(8,128)}, f32[128,1024]{1,0:T(8,128)}) custom-call(bf16[2048,128]{1,0:T(8,128)(2,1)} %get-tuple-element.40.q_ref, f32[8,1024]{1,0:T(8,128)} %constant.9.clone.bias_ref, f32[8,1024]{1,0:T(8,128)} %get-tuple-element.45.stat_ref, f32[128,1024]{1,0:T(8,128)} %get-tuple-element.46.out_ref, bf16[1040,256]{1,0:T(8,128)(2,1)} %copy-done, ...), custom_call_target="tpu_custom_call" | custom-call | tf_op jit(solution)/shard_map/pallas_call | solution.py:83
  52.3 0.0 all-to-all-done.1
  52.3 0.6 copy-done.14
  52.9 3.0 %shard_map.89 = (bf16[256,256]{1,0:T(8,128)(2,1)}, bf16[256,256]{1,0:T(8,128)(2,1)}, bf16[256,256]{1,0:T(8,128)(2,1)}, bf16[256,256]{1,0:T(8,128)(2,1)}, f32[128...) custom-call(bf16[2048,128]{1,0:T(8,128)(2,1)} %get-tuple-element.40.q_ref, ...), custom_call_target="tpu_custom_call" | custom-call | tf_op jit(solution)/shard_map/pallas_call | solution.py:83
  55.9 0.6 collective-permute-start.10
  56.5 1.5 %collective-permute-start.11 = (bf16[256,256]{1,0:T(8,128)(2,1)}, bf16[256,256]{1,0:T(8,128)(2,1)S(1)}, u32[]{:S(2)}, u32[]{:S(2)}) collective-permute-start(bf16[256,256]{1,0:T(8,128)(2,1)} %get-tuple-element.70), channel_id=1, source_target_pairs={{0,5},{1,4},{2,7},{3,6},{4,1},{5,0},{6,3},{7,2},{8,13},{9,12},{10,... | collective-permute-start | bytes 393224 | tf_op jit(solution)/shard_map/ppermute | solution.py:433
  57.9 3.7 %all-to-all-start.2 = ((f32[4,8,128]{2,1,0:T(8,128)}), f32[4,8,128]{2,1,0:T(8,128)S(1)}, u32[]{:S(2)}, u32[]{:S(2)}) async-start(f32[4,8,128]{2,1,0:T(8,128)} %bitcast.16), calls=%async_computation.2 | async-start | bytes 32768 | tf_op jit(solution)/shard_map/all_to_all | solution.py:438
  61.6 3.5 %collective-permute-start.12 = (bf16[256,256]{1,0:T(8,128)(2,1)}, bf16[256,256]{1,0:T(8,128)(2,1)S(1)}, u32[]{:S(2)}, u32[]{:S(2)}) collective-permute-start(bf16[256,256]{1,0:T(8,128)(2,1)} %get-tuple-element.71), channel_id=1, source_target_pairs={{0,6},{1,7},{2,4},{3,5},{4,2},{5,3},{6,0},{7,1},{8,14},{9,15},{10,... | collective-permute-start | bytes 393224 | tf_op jit(solution)/shard_map/ppermute | solution.py:433
  65.1 1.3 %collective-permute-start.13 = (bf16[256,256]{1,0:T(8,128)(2,1)}, bf16[256,256]{1,0:T(8,128)(2,1)S(1)}, u32[]{:S(2)}, u32[]{:S(2)}) collective-permute-start(bf16[256,256]{1,0:T(8,128)(2,1)} %get-tuple-element.72), channel_id=1, source_target_pairs={{0,7},{1,6},{2,5},{3,4},{4,3},{5,2},{6,1},{7,0},{8,15},{9,14},{10,... | collective-permute-start | bytes 393224 | tf_op jit(solution)/shard_map/ppermute | solution.py:433
  66.4 0.1 all-to-all-done.2
  66.5 0.6 copy-done.19
  67.1 6.6 %shard_map.90 = (bf16[1040,256]{1,0:T(8,128)(2,1)}, bf16[528,256]{1,0:T(8,128)(2,1)}, bf16[528,256]{1,0:T(8,128)(2,1)}, bf16[512,256]{1,0:T(8,128)(2,1)}, f32[128,1024]{1,0:T(8,128)}, /*index=5*/f32[8,128]{1,0:T(8,128)}) custom-call(s32[1]{0:T(128)} %bitcast.2.me_ref, bf16[2048,128]{1,0:T(8,128)(2,1)} %get-tuple-element.40.q_ref, ...), custom_call_target="tpu_custom_call" | custom-call | tf_op jit(solution)/shard_map/pallas_call | solution.py:83
  73.7 12.4 %all-to-all-start.3 = ((bf16[64,8,256]{2,1,0:T(8,128)(2,1)}), bf16[64,8,256]{2,1,0:T(8,128)(2,1)S(1)}, u32[]{:S(2)}, u32[]{:S(2)}) async-start(bf16[64,8,256]{2,1,0:T(8,128)(2,1)} %bitcast.12), calls=%async_computation.3 | async-start | bytes 524288 | tf_op jit(solution)/shard_map/all_to_all | solution.py:443
  86.0 1.3 %collective-permute-start.8 = (bf16[528,256]{1,0:T(8,128)(2,1)}, bf16[528,256]{1,0:T(8,128)(2,1)S(1)}, u32[]{:S(2)}, u32[]{:S(2)}) collective-permute-start(bf16[528,256]{1,0:T(8,128)(2,1)} %get-tuple-element.67), channel_id=1, source_target_pairs={{0,2},{1,3},{2,0},{3,1},{4,6},{5,7},{6,4},{7,5},{8,10},{9,11},{10,... | collective-permute-start | bytes 811016 | tf_op jit(solution)/shard_map/ppermute | solution.py:433
  87.3 0.0 collective-permute-done.10.b4
  87.3 2.8 %collective-permute-start.9 = (bf16[528,256]{1,0:T(8,128)(2,1)}, bf16[528,256]{1,0:T(8,128)(2,1)S(1)}, u32[]{:S(2)}, u32[]{:S(2)}) collective-permute-start(bf16[528,256]{1,0:T(8,128)(2,1)} %get-tuple-element.68), channel_id=1, source_target_pairs={{0,3},{1,2},{2,1},{3,0},{4,7},{5,6},{6,5},{7,4},{8,11},{9,10},{10,... | collective-permute-start | bytes 811016 | tf_op jit(solution)/shard_map/ppermute | solution.py:433
  90.1 0.0 collective-permute-done.11.b5
  90.1 0.0 collective-permute-start.7
  90.1 14.3 %shard_map.91 = (f32[2048,128]{1,0:T(8,128)}, f32[2048,256]{1,0:T(8,128)}) custom-call(bf16[2048,128]{1,0:T(8,128)(2,1)} %get-tuple-element.40.q_ref, bf16[2048,128]{1,0:T(8,128)(2,1)} %get-tuple-element.41.g_ref, f32[8,2048]{1,0:T(8,128)} %constant.8.clone.bias_ref, f32[8,2048]{1,0:T(8,128)} %get-tuple-element.57.row_ref, ...), custom_call_target="tpu_custom_call" | custom-call | flops 10000000000 | tf_op jit(solution)/shard_map/pallas_call | solution.py:83
  104.5 0.0 collective-permute-done.13.b7
  104.5 0.0 collective-permute-done.8.b2
  104.6 0.0 all-to-all-done.3
  104.6 1.7 %collective-permute-done.7.b1 = bf16[1040,256]{1,0:T(8,128)(2,1)S(1)} collective-permute-done((bf16[1040,256]{1,0:T(8,128)(2,1)}, bf16[1040,256]{1,0:T(8,128)(2,1)S(1)}, u32[]{:S(2)}, u32[]{:S(2)}) %collective-permute-start.7) | collective-permute-done | bytes 532512 | tf_op jit(solution)/shard_map/ppermute | solution.py:433
  106.3 0.8 copy-done.7
  107.1 4.5 %shard_map.92 = (f32[2048,128]{1,0:T(8,128)}, f32[2048,128]{1,0:T(8,128)}, f32[2048,128]{1,0:T(8,128)}) custom-call(f32[2048,256]{1,0:T(8,128)} %get-tuple-element.64.dkv_ref, f32[8,128]{1,0:T(8,128)} %get-tuple-element.65.mine_ref, bf16[1040,256]{1,0:T(8,128)(2,1)} %copy-done.7, bf16[528,256]{1,0:T(8,128)(2,1)} %copy-done.12, ...), custom_call_target="tpu_custom_call", output_to_operand_aliasing={{0}: (10, {})} | custom-call | tf_op jit(solution)/shard_map/pallas_call | solution.py:83
  (38 shorter events, 0.1 us)
Async XLA Ops:
  4.8 31.1 %collective-permute-start.1 = (bf16[256,256]{1,0:T(8,128)(2,1)}, bf16[256,256]{1,0:T(8,128)(2,1)S(1)}, u32[]{:S(2)}, u32[]{:S(2)}) collective-permute-start(bf16[256,256]{1,0:T(8,128)(2,1)} %get-tuple-element.51), channel_id=1, source_target_pairs={{0,5},{1,4},{2,7},{3,6},{4,1},{5,0},{6,3},{7,2},{8,13},{9,12},{10,... | collective-permute-start | bytes 393224 | tf_op jit(solution)/shard_map/ppermute | solution.py:433
  8.3 27.5 %collective-permute-start = (bf16[256,256]{1,0:T(8,128)(2,1)}, bf16[256,256]{1,0:T(8,128)(2,1)S(1)}, u32[]{:S(2)}, u32[]{:S(2)}) collective-permute-start(bf16[256,256]{1,0:T(8,128)(2,1)} %get-tuple-element.51), channel_id=1, source_target_pairs={{0,4},{1,5},{2,6},{3,7},{4,0},{5,1},{6,2},{7,3},{8,12},{9,13},{10,... | collective-permute-start | bytes 393224 | tf_op jit(solution)/shard_map/ppermute | solution.py:433
  8.3 31.7 %collective-permute-start.4 = (bf16[528,256]{1,0:T(8,128)(2,1)}, bf16[528,256]{1,0:T(8,128)(2,1)S(1)}, u32[]{:S(2)}, u32[]{:S(2)}) collective-permute-start(bf16[528,256]{1,0:T(8,128)(2,1)} %get-tuple-element.48.own), channel_id=1, source_target_pairs={{0,3},{1,2},{2,1},{3,0},{4,7},{5,6},{6,5},{7,4},{8,11},{9,10},{10,... | collective-permute-start | bytes 811016 | tf_op jit(solution)/shard_map/ppermute | solution.py:433
  10.2 29.8 %collective-permute-start.3 = (bf16[528,256]{1,0:T(8,128)(2,1)}, bf16[528,256]{1,0:T(8,128)(2,1)S(1)}, u32[]{:S(2)}, u32[]{:S(2)}) collective-permute-start(bf16[528,256]{1,0:T(8,128)(2,1)} %get-tuple-element.48.own), channel_id=1, source_target_pairs={{0,2},{1,3},{2,0},{3,1},{4,6},{5,7},{6,4},{7,5},{8,10},{9,11},{10,... | collective-permute-start | bytes 811016 | tf_op jit(solution)/shard_map/ppermute | solution.py:433
  11.0 25.5 %all-to-all-start = ((bf16[64,8,256]{2,1,0:T(8,128)(2,1)}), bf16[64,8,256]{2,1,0:T(8,128)(2,1)S(1)}, u32[]{:S(2)}, u32[]{:S(2)}) async-start(bf16[64,8,256]{2,1,0:T(8,128)(2,1)} %bitcast.13), calls=%async_computation | async-start | bytes 524288 | tf_op jit(solution)/shard_map/all_to_all | solution.py:443
  23.8 16.3 %collective-permute-start.2 = (bf16[1040,256]{1,0:T(8,128)(2,1)}, bf16[1040,256]{1,0:T(8,128)(2,1)S(1)}, u32[]{:S(2)}, u32[]{:S(2)}) collective-permute-start(bf16[1040,256]{1,0:T(8,128)(2,1)} %get-tuple-element.47), channel_id=1, source_target_pairs={{0,1},{1,0},{2,3},{3,2},{4,5},{5,4},{6,7},{7,6},{8,9},{9,8},{10,11... | collective-permute-start | bytes 1597448 | tf_op jit(solution)/shard_map/ppermute | solution.py:433
  24.8 11.7 %copy-start.20 = (bf16[256,256]{1,0:T(8,128)(2,1)S(1)}, bf16[256,256]{1,0:T(8,128)(2,1)}, u32[]{:S(2)}) copy-start(bf16[256,256]{1,0:T(8,128)(2,1)} %get-tuple-element.51) | copy-start | bytes 393220
  24.8 15.3 %copy-start.4 = (bf16[528,256]{1,0:T(8,128)(2,1)S(1)}, bf16[528,256]{1,0:T(8,128)(2,1)}, u32[]{:S(2)}) copy-start(bf16[528,256]{1,0:T(8,128)(2,1)} %get-tuple-element.48.own) | copy-start | bytes 811012
  35.8 10.4 %copy-start.8 = (bf16[256,256]{1,0:T(8,128)(2,1)}, bf16[256,256]{1,0:T(8,128)(2,1)S(1)}, u32[]{:S(2)}) copy-start(bf16[256,256]{1,0:T(8,128)(2,1)S(1)} %collective-permute-done.1.rest_4_.rest_1_) | copy-start | bytes 393220
  35.8 10.4 %copy-start.9 = (bf16[256,256]{1,0:T(8,128)(2,1)}, bf16[256,256]{1,0:T(8,128)(2,1)S(1)}, u32[]{:S(2)}) copy-start(bf16[256,256]{1,0:T(8,128)(2,1)S(1)} %collective-permute-done.rest_3_.rest_0_) | copy-start | bytes 393220
  36.5 15.8 %copy-start.3 = (bf16[64,8,256]{2,1,0:T(8,128)(2,1)}, bf16[64,8,256]{2,1,0:T(8,128)(2,1)S(1)}, u32[]{:S(2)}) copy-start(bf16[64,8,256]{2,1,0:T(8,128)(2,1)S(1)} %all-to-all-done) | copy-start | bytes 786436
  36.5 9.2 %collective-permute-start.6 = (bf16[256,256]{1,0:T(8,128)(2,1)S(1)}, bf16[256,256]{1,0:T(8,128)(2,1)S(1)}, u32[]{:S(2)}, u32[]{:S(2)}) collective-permute-start(bf16[256,256]{1,0:T(8,128)(2,1)S(1)} %copy-done.20), channel_id=1, source_target_pairs={{0,7},{1,6},{2,5},{3,4},{4,3},{5,2},{6,1},{7,0},{8,15},{9,14},{10,... | collective-permute-start | bytes 393224 | tf_op jit(solution)/shard_map/ppermute | solution.py:433
  39.3 6.9 %collective-permute-start.5 = (bf16[256,256]{1,0:T(8,128)(2,1)S(1)}, bf16[256,256]{1,0:T(8,128)(2,1)S(1)}, u32[]{:S(2)}, u32[]{:S(2)}) collective-permute-start(bf16[256,256]{1,0:T(8,128)(2,1)S(1)} %copy-done.20), channel_id=1, source_target_pairs={{0,6},{1,7},{2,4},{3,5},{4,2},{5,3},{6,0},{7,1},{8,14},{9,15},{10,... | collective-permute-start | bytes 393224 | tf_op jit(solution)/shard_map/ppermute | solution.py:433
  40.1 6.2 %copy-start.1 = (bf16[528,256]{1,0:T(8,128)(2,1)}, bf16[528,256]{1,0:T(8,128)(2,1)S(1)}, u32[]{:S(2)}) copy-start(bf16[528,256]{1,0:T(8,128)(2,1)S(1)} %collective-permute-done.4.rest_2_.r3.rest_3_) | copy-start | bytes 811012
  40.1 6.2 %copy-start.2 = (bf16[528,256]{1,0:T(8,128)(2,1)}, bf16[528,256]{1,0:T(8,128)(2,1)S(1)}, u32[]{:S(2)}) copy-start(bf16[528,256]{1,0:T(8,128)(2,1)S(1)} %collective-permute-done.3.rest_1_.r2.rest_2_) | copy-start | bytes 811012
  40.1 6.2 %copy-start = (bf16[1040,256]{1,0:T(8,128)(2,1)}, bf16[1040,256]{1,0:T(8,128)(2,1)S(1)}, u32[]{:S(2)}) copy-start(bf16[1040,256]{1,0:T(8,128)(2,1)S(1)} %collective-permute-done.2.rest_0_.r1.rest_1_) | copy-start | bytes 1597444
  41.1 0.6 copy-start.5
  41.7 10.6 %all-to-all-start.1 = ((f32[4,8,384]{2,1,0:T(8,128)}), f32[4,8,384]{2,1,0:T(8,128)S(1)}, u32[]{:S(2)}, u32[]{:S(2)}) async-start(f32[4,8,384]{2,1,0:T(8,128)} %bitcast.3), calls=%async_computation.1 | async-start | bytes 98304 | tf_op jit(solution)/shard_map/all_to_all | solution.py:438
  45.6 0.7 copy-start.10
  46.3 0.6 copy-start.11
  52.3 0.6 copy-start.14
  55.9 31.4 %collective-permute-start.10 = (bf16[256,256]{1,0:T(8,128)(2,1)}, bf16[256,256]{1,0:T(8,128)(2,1)S(1)}, u32[]{:S(2)}, u32[]{:S(2)}) collective-permute-start(bf16[256,256]{1,0:T(8,128)(2,1)} %get-tuple-element.69), channel_id=1, source_target_pairs={{0,4},{1,5},{2,6},{3,7},{4,0},{5,1},{6,2},{7,3},{8,12},{9,13},{10,... | collective-permute-start | bytes 393224 | tf_op jit(solution)/shard_map/ppermute | solution.py:433
  56.5 33.7 %collective-permute-start.11 = (bf16[256,256]{1,0:T(8,128)(2,1)}, bf16[256,256]{1,0:T(8,128)(2,1)S(1)}, u32[]{:S(2)}, u32[]{:S(2)}) collective-permute-start(bf16[256,256]{1,0:T(8,128)(2,1)} %get-tuple-element.70), channel_id=1, source_target_pairs={{0,5},{1,4},{2,7},{3,6},{4,1},{5,0},{6,3},{7,2},{8,13},{9,12},{10,... | collective-permute-start | bytes 393224 | tf_op jit(solution)/shard_map/ppermute | solution.py:433
  57.9 8.5 %all-to-all-start.2 = ((f32[4,8,128]{2,1,0:T(8,128)}), f32[4,8,128]{2,1,0:T(8,128)S(1)}, u32[]{:S(2)}, u32[]{:S(2)}) async-start(f32[4,8,128]{2,1,0:T(8,128)} %bitcast.16), calls=%async_computation.2 | async-start | bytes 32768 | tf_op jit(solution)/shard_map/all_to_all | solution.py:438
  61.6 42.9 %collective-permute-start.12 = (bf16[256,256]{1,0:T(8,128)(2,1)}, bf16[256,256]{1,0:T(8,128)(2,1)S(1)}, u32[]{:S(2)}, u32[]{:S(2)}) collective-permute-start(bf16[256,256]{1,0:T(8,128)(2,1)} %get-tuple-element.71), channel_id=1, source_target_pairs={{0,6},{1,7},{2,4},{3,5},{4,2},{5,3},{6,0},{7,1},{8,14},{9,15},{10,... | collective-permute-start | bytes 393224 | tf_op jit(solution)/shard_map/ppermute | solution.py:433
  65.1 39.4 %collective-permute-start.13 = (bf16[256,256]{1,0:T(8,128)(2,1)}, bf16[256,256]{1,0:T(8,128)(2,1)S(1)}, u32[]{:S(2)}, u32[]{:S(2)}) collective-permute-start(bf16[256,256]{1,0:T(8,128)(2,1)} %get-tuple-element.72), channel_id=1, source_target_pairs={{0,7},{1,6},{2,5},{3,4},{4,3},{5,2},{6,1},{7,0},{8,15},{9,14},{10,... | collective-permute-start | bytes 393224 | tf_op jit(solution)/shard_map/ppermute | solution.py:433
  66.5 0.6 copy-start.19
  73.7 30.9 %all-to-all-start.3 = ((bf16[64,8,256]{2,1,0:T(8,128)(2,1)}), bf16[64,8,256]{2,1,0:T(8,128)(2,1)S(1)}, u32[]{:S(2)}, u32[]{:S(2)}) async-start(bf16[64,8,256]{2,1,0:T(8,128)(2,1)} %bitcast.12), calls=%async_computation.3 | async-start | bytes 524288 | tf_op jit(solution)/shard_map/all_to_all | solution.py:443
  86.0 18.5 %collective-permute-start.8 = (bf16[528,256]{1,0:T(8,128)(2,1)}, bf16[528,256]{1,0:T(8,128)(2,1)S(1)}, u32[]{:S(2)}, u32[]{:S(2)}) collective-permute-start(bf16[528,256]{1,0:T(8,128)(2,1)} %get-tuple-element.67), channel_id=1, source_target_pairs={{0,2},{1,3},{2,0},{3,1},{4,6},{5,7},{6,4},{7,5},{8,10},{9,11},{10,... | collective-permute-start | bytes 811016 | tf_op jit(solution)/shard_map/ppermute | solution.py:433
  87.3 17.2 %copy-start.15 = (bf16[256,256]{1,0:T(8,128)(2,1)}, bf16[256,256]{1,0:T(8,128)(2,1)S(1)}, u32[]{:S(2)}) copy-start(bf16[256,256]{1,0:T(8,128)(2,1)S(1)} %collective-permute-done.10.b4) | copy-start | bytes 393220
  87.3 17.2 %collective-permute-start.9 = (bf16[528,256]{1,0:T(8,128)(2,1)}, bf16[528,256]{1,0:T(8,128)(2,1)S(1)}, u32[]{:S(2)}, u32[]{:S(2)}) collective-permute-start(bf16[528,256]{1,0:T(8,128)(2,1)} %get-tuple-element.68), channel_id=1, source_target_pairs={{0,3},{1,2},{2,1},{3,0},{4,7},{5,6},{6,5},{7,4},{8,11},{9,10},{10,... | collective-permute-start | bytes 811016 | tf_op jit(solution)/shard_map/ppermute | solution.py:433
  90.1 14.3 %copy-start.16 = (bf16[256,256]{1,0:T(8,128)(2,1)}, bf16[256,256]{1,0:T(8,128)(2,1)S(1)}, u32[]{:S(2)}) copy-start(bf16[256,256]{1,0:T(8,128)(2,1)S(1)} %collective-permute-done.11.b5) | copy-start | bytes 393220
  90.1 16.1 %collective-permute-start.7 = (bf16[1040,256]{1,0:T(8,128)(2,1)}, bf16[1040,256]{1,0:T(8,128)(2,1)S(1)}, u32[]{:S(2)}, u32[]{:S(2)}) collective-permute-start(bf16[1040,256]{1,0:T(8,128)(2,1)} %get-tuple-element.66), channel_id=1, source_target_pairs={{0,1},{1,0},{2,3},{3,2},{4,5},{5,4},{6,7},{7,6},{8,9},{9,8},{10,11... | collective-permute-start | bytes 1597448 | tf_op jit(solution)/shard_map/ppermute | solution.py:433
  104.5 1.8 %copy-start.17 = (bf16[256,256]{1,0:T(8,128)(2,1)}, bf16[256,256]{1,0:T(8,128)(2,1)S(1)}, u32[]{:S(2)}) copy-start(bf16[256,256]{1,0:T(8,128)(2,1)S(1)} %collective-permute-done.12.b6) | copy-start | bytes 393220
  104.5 1.8 %copy-start.18 = (bf16[256,256]{1,0:T(8,128)(2,1)}, bf16[256,256]{1,0:T(8,128)(2,1)S(1)}, u32[]{:S(2)}) copy-start(bf16[256,256]{1,0:T(8,128)(2,1)S(1)} %collective-permute-done.13.b7) | copy-start | bytes 393220
  104.5 1.8 %copy-start.12 = (bf16[528,256]{1,0:T(8,128)(2,1)}, bf16[528,256]{1,0:T(8,128)(2,1)S(1)}, u32[]{:S(2)}) copy-start(bf16[528,256]{1,0:T(8,128)(2,1)S(1)} %collective-permute-done.8.b2) | copy-start | bytes 811012
  104.5 1.7 %copy-start.13 = (bf16[528,256]{1,0:T(8,128)(2,1)}, bf16[528,256]{1,0:T(8,128)(2,1)S(1)}, u32[]{:S(2)}) copy-start(bf16[528,256]{1,0:T(8,128)(2,1)S(1)} %collective-permute-done.9.b3) | copy-start | bytes 811012
  104.6 1.7 %copy-start.6 = (bf16[64,8,256]{2,1,0:T(8,128)(2,1)}, bf16[64,8,256]{2,1,0:T(8,128)(2,1)S(1)}, u32[]{:S(2)}) copy-start(bf16[64,8,256]{2,1,0:T(8,128)(2,1)S(1)} %all-to-all-done.3) | copy-start | bytes 786436
  106.3 0.8 copy-start.7
